TPU v7x, 1024 devices: a whole 4x8x16 slice. The times are simulated.
1024 devices in a mesh: dp: 32 (over z_hi, y, core), mp: 32 (over z_lo, x).
Axes of the slice: x: 4, y: 8, z: 16 (z_hi: 2, z_lo: 8; z = z_hi * 8 + z_lo), core: 2. Of those that a mesh axis runs over, the one named last changes fastest.
Arguments:
- tokens: bfloat16 [8192, 4096], P(('dp', 'mp')), may hold values from -24 to 24
- cotangent: bfloat16 [8192, 4096], P(('dp', 'mp')), may hold values from -24 to 24
- w_qkv: bfloat16 [4096, 32, 384], P(None, 'mp'), may hold values from -0.09375 to 0.09375
- w_out: bfloat16 [32, 128, 4096], P('mp'), may hold values from -0.09375 to 0.09375
Outputs:
- grad_qkv: float32 [4096, 32, 384], P('dp', 'mp')
- grad_out: float32 [32, 128, 4096], P('mp', None, 'dp')
All inputs are finite; a program needn't handle non-finite values.
Results may differ from a plain program's by a relative error of at most 0.02.
Values may be sent and summed in bfloat16 or wider, within the bound.
No kernel may reach another device: no remote copies, remote signals or barrier semaphores. Data moves between devices by JAX's collectives and lax.ppermute only.
A program may use at most 32 MiB of HBM per device.

v0:
```python
import jax
import jax.numpy as jnp
from jax import lax
from jax.sharding import PartitionSpec as P

PATCHES = 256


highest_precision = lax.Precision.HIGHEST


def normalize(values):
    centred = values - jnp.mean(values, -1, keepdims=True)
    spread = lax.rsqrt(jnp.mean(centred * centred, -1, keepdims=True) + 1e-06)
    return (centred * spread, spread)


def normalize_back(grad, normed, spread):
    inner = jnp.mean(grad * normed, -1, keepdims=True)
    return spread * (grad - jnp.mean(grad, -1, keepdims=True) - normed * inner)


def attend(normed, w_head, patches):
    width = w_head.shape[1] // 3
    qkv = jnp.dot(normed, w_head, preferred_element_type=jnp.float32)
    count = qkv.shape[0] // patches
    qkv = qkv.reshape(count, patches, 3 * width)
    query_rows, query_spread = normalize(qkv[..., :width])
    key, key_spread = normalize(qkv[..., width : 2 * width])
    value_rows = qkv[..., 2 * width :]
    score_scale = width ** (-0.5)
    attention_scores = (
        jnp.einsum("omx,oex->ome", query_rows, key, precision=highest_precision) * score_scale
    )
    weights = jnp.exp(attention_scores)
    attention_probabilities = weights / jnp.sum(weights, -1, keepdims=True)
    attended_values = jnp.einsum(
        "mut,mtw->muw", attention_probabilities, value_rows, precision=highest_precision
    )
    attended_values = attended_values.reshape(count * patches, width).astype(jnp.bfloat16)
    return (
        attended_values,
        (query_rows, query_spread, key, key_spread, value_rows, attention_probabilities),
    )


def attend_back(attended_gradient, saved):
    query_rows, query_spread, key, key_spread, value_rows, attention_probabilities = saved
    count, patches, width = value_rows.shape
    attended_gradient = attended_gradient.reshape(count, patches, width)
    score_scale = width ** (-0.5)
    value_gradient = jnp.einsum(
        "wth,wtg->whg", attention_probabilities, attended_gradient, precision=highest_precision
    )
    probability_gradient = jnp.einsum(
        "omx,oex->ome", attended_gradient, value_rows, precision=highest_precision
    )
    score_gradient = (
        attention_probabilities
        * (
            probability_gradient
            - jnp.sum(probability_gradient * attention_probabilities, -1, keepdims=True)
        )
        * score_scale
    )
    query_gradient = jnp.einsum("mut,mtw->muw", score_gradient, key, precision=highest_precision)
    key_gradient = jnp.einsum(
        "wth,wtg->whg", score_gradient, query_rows, precision=highest_precision
    )
    d_qkv = jnp.concatenate(
        [
            normalize_back(query_gradient, query_rows, query_spread),
            normalize_back(key_gradient, key, key_spread),
            value_gradient,
        ],
        -1,
    )
    return d_qkv.reshape(count * patches, 3 * width).astype(jnp.bfloat16)


def forward_part(rows, w_head):
    normed = normalize(rows.astype(jnp.float32))[0].astype(jnp.bfloat16)
    attended_values, saved = attend(normed, w_head, PATCHES)
    return (normed, attended_values, saved)


def qkv_term_of(normed, attended_gradient, saved):
    d_qkv = attend_back(attended_gradient, saved)
    return lax.dot_general(
        normed, d_qkv, (((0,), (0,)), ((), ())), preferred_element_type=jnp.float32
    )


def local(tokens, cotangent, w_qkv, w_out):
    w_head = w_qkv[:, 0, :]
    w_back = w_out[0]
    rows, grads = (
        lax.all_gather(tokens, "mp", axis=0, tiled=True),
        lax.all_gather(cotangent, "mp", axis=0, tiled=True),
    )
    normed, attended_values, saved = forward_part(rows, w_head)
    out_term = lax.dot_general(
        grads, attended_values, (((0,), (0,)), ((), ())), preferred_element_type=jnp.float32
    )
    attended_gradient = lax.dot_general(
        grads, w_back, (((1,), (1,)), ((), ())), preferred_element_type=jnp.float32
    )
    qkv_term = qkv_term_of(normed, attended_gradient, saved)
    columns = qkv_term.shape[1]
    both = lax.psum_scatter(
        jnp.concatenate([qkv_term, out_term], 1).astype(jnp.bfloat16),
        "dp",
        scatter_dimension=0,
        tiled=True,
    ).astype(jnp.float32)
    qkv_sum = both[:, :columns]
    out_sum = both[:, columns:]
    return (qkv_sum[:, None, :], jnp.transpose(out_sum)[None])


def solution(mesh):
    in_specs = (
        P(("dp", "mp"), None),
        P(("dp", "mp"), None),
        P(None, "mp", None),
        P("mp", None, None),
    )
    out_specs = (P("dp", "mp", None), P("mp", None, "dp"))
    return jax.shard_map(local, mesh=mesh, in_specs=in_specs, out_specs=out_specs, check_vma=False)
```

profile of v0, /device:TPU:6, one launch (start us, length us, event | category | flops | bytes accessed | tf_op | source)
XLA Modules:
  0.0 705.0 jit_solution(15758304111434105160)
XLA Ops:
  7.2 0.7 all-gather.3.cloned.1.call-update
  8.0 0.7 all-gather.5.cloned.1.call-update
  8.7 227.8 %all-gather.3.cloned.1.call-done = bf16[256,4096]{1,0:T(8,128)(2,1)} async-done(((bf16[8,4096]{1,0:T(8,128)(2,1)}), bf16[256,4096]{1,0:T(8,128)(2,1)}) %all-gather.3.cloned.1.call-update) | async-done | bytes 2097168 | tf_op jit(solution)/shard_map/all_gather | solution.py:98
  236.5 2.1 convert_reduce_fusion
  238.6 0.1 copy-done.1
  238.8 0.7 fusion.3
  239.5 1.3 fusion.7
  240.8 0.1 slice_reduce_fusion.1
  241.0 0.2 multiply_reduce_fusion.2
  241.3 0.5 fusion.42
  241.8 0.7 copy-done.3
  242.5 1.2 convolution_convert_fusion.2
  243.7 220.6 %all-gather.5.cloned.1.call-done = bf16[256,4096]{1,0:T(8,128)(2,1)} async-done(((bf16[8,4096]{1,0:T(8,128)(2,1)}), bf16[256,4096]{1,0:T(8,128)(2,1)}) %all-gather.5.cloned.1.call-update) | async-done | bytes 2097168 | tf_op jit(solution)/shard_map/all_gather | solution.py:99
  464.3 2.6 fusion.12
  466.9 1.0 fusion.11
  467.9 0.4 multiply_reduce_fusion
  468.3 1.1 fusion.44
  469.5 1.2 fusion.43
  470.6 0.6 broadcast_multiply_fusion.3
  471.2 0.6 broadcast_multiply_fusion.1
  471.8 1.6 copy.14
  473.4 1.6 copy.12
  475.1 1.4 fusion.21
  476.5 1.3 fusion.23
  477.9 2.1 fusion.2
  480.0 1.9 convolution_convert_fusion
  481.9 2.2 pad_maximum_fusion
  484.1 6.5 copy.19
  490.6 205.4 %reduce-scatter.4.cloned.1.call-done = bf16[128,512]{1,0:T(8,128)(2,1)} async-done(((bf16[4096,512]{1,0:T(8,128)(2,1)}), bf16[128,512]{1,0:T(8,128)(2,1)}) %reduce-scatter.4.cloned.1.call-update) | async-done | bytes 131088
  696.0 1.0 copy.20
  697.0 0.6 slice_bitcast_fusion.4
  697.7 0.8 copy.17
  (31 shorter events, 0.2 us)
Async XLA Ops:
  7.2 232.3 %copy-start = (bf16[4096,1,384]{2,0,1:T(8,128)(2,1)S(1)}, bf16[4096,1,384]{2,0,1:T(8,128)(2,1)}, u32[]{:S(2)}) copy-start(bf16[4096,1,384]{2,0,1:T(8,128)(2,1)} %param.6) | copy-start | bytes 9437188
  7.2 229.3 %all-gather.3.cloned.1.call-start = ((), (), s32[]{:S(2)}) async-start(), calls=%async_computation.1 | async-start | bytes 2162688 | tf_op jit(solution)/shard_map/all_gather | solution.py:98
  7.9 456.4 %all-gather.5.cloned.1.call-start = ((), (), s32[]{:S(2)}) async-start(), calls=%async_computation.2 | async-start | bytes 2162688 | tf_op jit(solution)/shard_map/all_gather | solution.py:99
  8.7 687.3 %reduce-scatter.4.cloned.1.call-start = ((), (), s32[]{:S(2)}) async-start(), calls=%async_computation.3 | async-start | bytes 4325376
  236.5 2.2 copy-start.1
  238.7 2.1 copy-start.5
  239.5 1.4 copy-start.8
  241.8 0.7 copy-start.3
  241.8 0.7 copy-start.6
  464.3 2.6 copy-start.4
  464.3 2.6 copy-start.7
  475.1 4.9 copy-start.2
  475.1 4.9 copy-start.9
Sparse Core Ops, SparseCore 0:
  10.7 225.8 all-gather.2
  239.2 225.0 all-gather.4
  490.7 205.1 reduce-scatter.3
where the time goes:
time: 705 us
  waiting for transfers between devices  655 us (93%)
  between operations  13.9 us (2%)
  matrix products  13.4 us (2%)
  local copies, waits for them, and re-layouts  13 us (2%)
  other arithmetic  9.4 us (1%)
    all_gather x1, waiting for transfers between devices, local(): lax.all_gather(tokens, 'mp', axis=0, tiled=True)  228 us
    all_gather x1, waiting for transfers between devices, local(): lax.all_gather(cotangent, 'mp', axis=0, tiled=True)  221 us
    unnamed x4, waiting for transfers between devices  207 us
  transfers between devices with their start and end apart: 3, of which 3 were waited for; matrix products, arithmetic and copies ran while one was open for 1% of the time, Pallas kernels for 0%

commit v1 on v0

v1 whole, which is shorter than its diff:
```python
import functools

import jax
import jax.numpy as jnp
from jax import lax
from jax.experimental import pallas as pl
from jax.experimental.pallas import tpu as pltpu
from jax.sharding import Mesh
from jax.sharding import PartitionSpec as P

HIGHEST = lax.Precision.HIGHEST
BF16 = jnp.bfloat16
F32 = jnp.float32
EPS = 1e-6
TM = (((0,), (0,)), ((), ()))
NT = (((1,), (1,)), ((), ()))
NN = (((1,), (0,)), ((), ()))
VMEM = pl.BlockSpec(memory_space=pltpu.VMEM)
SMEM = pl.BlockSpec(memory_space=pltpu.SMEM)
PARAMS = pltpu.CompilerParams(vmem_limit_bytes=40 * 1024 * 1024)


def normalize(values):
    centred = values - jnp.mean(values, -1, keepdims=True)
    spread = lax.rsqrt(jnp.mean(centred * centred, -1, keepdims=True) + EPS)
    return centred * spread, spread


def normalize_back(grad, normed, spread):
    inner = jnp.mean(grad * normed, -1, keepdims=True)
    return spread * (grad - jnp.mean(grad, -1, keepdims=True) - normed * inner)


def exact(a, b, dims):
    return lax.dot_general(a, b, dims, precision=HIGHEST, preferred_element_type=F32)


def forward_kernel(*refs, rows):
    pieces = refs[: len(rows)]
    w_ref, normed_ref, att_ref, q_ref, k_ref, v_ref, prob_ref, sq_ref, sk_ref = refs[len(rows) :]
    step = 16
    at = 0
    for piece, count in zip(pieces, rows):

        def body(i, carry, piece=piece, at=at):
            part = pl.ds(pl.multiple_of(i * step, step), step)
            x = piece[part, :].astype(F32)
            centred = x - jnp.mean(x, -1, keepdims=True)
            spread = lax.rsqrt(jnp.mean(centred * centred, -1, keepdims=True) + EPS)
            normed_ref[pl.ds(pl.multiple_of(at + i * step, step), step), :] = (
                centred * spread
            ).astype(BF16)
            return carry

        lax.fori_loop(0, count // step, body, 0)
        at += count
    width = w_ref.shape[1] // 3
    qkv = jnp.dot(normed_ref[...], w_ref[...], preferred_element_type=F32)
    q, sq = normalize(qkv[:, :width])
    k, sk = normalize(qkv[:, width : 2 * width])
    v = qkv[:, 2 * width :]
    weights = jnp.exp(exact(q, k, NT) * width ** (-0.5))
    probs = weights / jnp.sum(weights, -1, keepdims=True)
    att_ref[...] = exact(probs, v, NN).T.astype(BF16)
    q_ref[...] = q
    k_ref[...] = k
    v_ref[...] = v
    prob_ref[...] = probs
    sq_ref[...] = jnp.broadcast_to(sq, q.shape)
    sk_ref[...] = jnp.broadcast_to(sk, k.shape)


def backward_kernel(*refs, rows):
    pieces = refs[: len(rows)]
    w_ref, q_ref, k_ref, v_ref, prob_ref, sq_ref, sk_ref, out_ref = refs[len(rows) :]
    width = w_ref.shape[0]
    cot = jnp.concatenate([piece[...] for piece in pieces], 0)
    d_att = lax.dot_general(cot, w_ref[...], NT, preferred_element_type=F32)
    q, k, v, probs = q_ref[...], k_ref[...], v_ref[...], prob_ref[...]
    d_value = exact(probs, d_att, TM)
    d_probs = exact(d_att, v, NT)
    inner = jnp.sum(d_probs * probs, -1, keepdims=True)
    d_scores = probs * (d_probs - inner) * width ** (-0.5)
    d_q = normalize_back(exact(d_scores, k, NN), q, sq_ref[...])
    d_k = normalize_back(exact(d_scores, q, TM), k, sk_ref[...])
    out_ref[:width, :] = d_q.T.astype(BF16)
    out_ref[width : 2 * width, :] = d_k.T.astype(BF16)
    out_ref[2 * width :, :] = d_value.T.astype(BF16)


def terms_kernel(*refs, count, blocks, adds):
    core_ref, normed_ref = refs[:2]
    pieces = refs[2 : 2 + count]
    d_ref, att_ref = refs[2 + count : 4 + count]
    out_ref = refs[-1]
    far, near, width = blocks
    core = core_ref[0]
    d_all, att = d_ref[...], att_ref[...]
    split = d_all.shape[0]
    for y in range(near):
        cols = [
            pl.ds(pl.multiple_of(((zh * near + y) * 2 + core) * width, width), width)
            for zh in range(far)
        ]
        rhs = jnp.concatenate([normed_ref[:, c] for c in cols], 1)
        cot = jnp.concatenate(
            [jnp.concatenate([p[:, c] for p in pieces], 0) for c in cols], 1
        )
        top = jnp.dot(d_all, rhs, preferred_element_type=F32)
        low = jnp.dot(att, cot, preferred_element_type=F32)
        for zh in range(far):
            a = top[:, zh * width : (zh + 1) * width]
            b = low[:, zh * width : (zh + 1) * width]
            if adds:
                other = refs[4 + count]
                a = a + other[y * far + zh, :split, :].astype(F32)
                b = b + other[y * far + zh, split:, :].astype(F32)
            out_ref[y * far + zh, :split, :] = a.astype(BF16)
            out_ref[y * far + zh, split:, :] = b.astype(BF16)


def swap(n, s):
    return [(i, i ^ s) for i in range(n)]


def gather_z(rows, n):
    s = n // 2
    while s:
        rows = jnp.concatenate([rows, lax.ppermute(rows, "zl", swap(n, s))], 0)
        s //= 2
    return rows


def gather_x(rows, n):
    up = [(i, (i + 1) % n) for i in range(n)]
    down = [(i, (i - 1) % n) for i in range(n)]
    half = rows.shape[0] // 2
    left = lax.ppermute(rows, "x", up)
    right = lax.ppermute(rows, "x", down)
    far_top = lax.ppermute(left[:half], "x", up)
    far_low = lax.ppermute(right[half:], "x", down)
    return [rows, left, right, far_top, far_low]


def local(sizes, tokens, cotangent, w_qkv, w_out):
    far, near, cores, n_z, n_x = sizes
    w_head = w_qkv[:, 0, :]
    w_back = w_out[0]
    model, width = w_head.shape[0], w_back.shape[0]
    t_pieces = gather_x(gather_z(tokens, n_z), n_x)
    c_pieces = gather_x(gather_z(cotangent, n_z), n_x)
    rows = tuple(p.shape[0] for p in t_pieces)
    total = sum(rows)
    small = jax.ShapeDtypeStruct((total, width), F32)
    normed, att, q, k, v, probs, sq, sk = pl.pallas_call(
        functools.partial(forward_kernel, rows=rows),
        out_shape=[
            jax.ShapeDtypeStruct((total, model), BF16),
            jax.ShapeDtypeStruct((width, total), BF16),
            small,
            small,
            small,
            jax.ShapeDtypeStruct((total, total), F32),
            small,
            small,
        ],
        in_specs=[VMEM] * (len(rows) + 1),
        out_specs=[VMEM] * 8,
        compiler_params=PARAMS,
    )(*t_pieces, w_head)
    d_qkv = pl.pallas_call(
        functools.partial(backward_kernel, rows=rows),
        out_shape=jax.ShapeDtypeStruct((3 * width, total), BF16),
        in_specs=[VMEM] * (len(rows) + 7),
        out_specs=VMEM,
        compiler_params=PARAMS,
    )(*c_pieces, w_back, q, k, v, probs, sq, sk)
    blocks = (far, near, model // (far * near * cores))

    def terms(core, *other):
        return pl.pallas_call(
            functools.partial(terms_kernel, count=len(rows), blocks=blocks, adds=len(other) > 0),
            out_shape=jax.ShapeDtypeStruct((far * near, 4 * width, blocks[2]), BF16),
            in_specs=[SMEM] + [VMEM] * (len(rows) + 3 + len(other)),
            out_specs=VMEM,
            compiler_params=PARAMS,
        )(core.reshape(1), normed, *c_pieces, d_qkv, att, *other)

    core = lax.axis_index("c").astype(jnp.int32)
    theirs = lax.ppermute(terms(1 - core), "c", swap(cores, 1))
    pair = terms(core, theirs)
    summed = lax.psum_scatter(pair, "y", scatter_dimension=0, tiled=True)
    zh = lax.axis_index("zh")
    own = lax.dynamic_index_in_dim(summed, zh, 0, keepdims=False)
    away = lax.dynamic_index_in_dim(summed, 1 - zh, 0, keepdims=False)
    both = own.astype(F32) + lax.ppermute(away, "zh", swap(far, 1)).astype(F32)
    return both[: 3 * width].T[:, None, :], both[3 * width :][None]


def solution(mesh):
    sizes = (2, mesh.shape["dp"] // 4, 2, mesh.shape["mp"] // 4, 4)
    fine = Mesh(mesh.devices.reshape(sizes), ("zh", "y", "c", "zl", "x"))
    dp, mp = ("zh", "y", "c"), ("zl", "x")
    in_specs = (P(dp + mp, None), P(dp + mp, None), P(None, mp, None), P(mp, None, None))
    out_specs = (P(dp, mp, None), P(mp, None, dp))
    return jax.shard_map(
        functools.partial(local, sizes),
        mesh=fine,
        in_specs=in_specs,
        out_specs=out_specs,
        check_vma=False,
    )
```

time: 705 us -> 196 us (0.28)
  waiting for transfers between devices: 655 us -> 75.7 us
  starting transfers between devices: 0.11 us -> 77.1 us
  Pallas kernels: 0 us -> 13.7 us
  matrix products: 13.4 us -> 0 us
    all_gather x2 -> x0, waiting for transfers between devices: 448 us -> none  [the longest x1 228 us: local(): lax.all_gather(tokens, 'mp', axis=0, tiled=True)]
    unnamed x4 -> x1, waiting for transfers between devices: 207 us -> 0.02 us
    ppermute x0 -> x16, starting transfers between devices: none -> 77 us  [the longest x6 34.2 us: gather_z(): rows = jnp.concatenate([rows, lax.ppermute(rows, 'zl', swap(n, s))], 0)]
    reduce_scatter x0 -> x1, waiting for transfers between devices: none -> 53.8 us  [local(): summed = lax.psum_scatter(pair, 'y', scatter_dimension=0, tiled=True)]
    ppermute x0 -> x16, waiting for transfers between devices: none -> 21.8 us  [the longest x1 6.97 us: local(): both = own.astype(F32) + lax.ppermute(away, 'zh', swap(far, 1)).astype(F32)]
    pallas_call x0 -> x4, Pallas kernels: none -> 13.7 us  [the longest x1 7.63 us: local(): pl.pallas_call(functools.partial(forward_kernel, rows=rows), out_shape=[j...]
    dot_general x10 -> x0, matrix products: 13.4 us -> none  [the longest x1 2.6 us: local(): lax.dot_general(grads, w_back, (((1,), (1,)), ((), ())), preferred_elemen...]
  transfers between devices with their start and end apart: 3 -> 17, of which waited for: 3 -> 7; matrix products, arithmetic and copies ran while one was open for 1% -> 4% of each run, Pallas kernels for 0% -> 4%
where the time goes in v1:
time: 196 us; the launch traced here: 195 us
  starting transfers between devices  77.1 us (39%)
  waiting for transfers between devices  75.7 us (39%)
  between operations  14.3 us (7%)
  Pallas kernels  13.7 us (7%)
  local copies, waits for them, and re-layouts  9.93 us (5%)
  other arithmetic  4.35 us (2%)
    reduce_scatter x1, waiting for transfers between devices, local(): summed = lax.psum_scatter(pair, 'y', scatter_dimension=0, tiled=True)  53.8 us
    ppermute x6, starting transfers between devices, gather_z(): rows = jnp.concatenate([rows, lax.ppermute(rows, 'zl', swap(n, s))], 0)  34.2 us
    ppermute x1, starting transfers between devices, local(): both = own.astype(F32) + lax.ppermute(away, 'zh', swap(far, 1)).astype(F32)  13.6 us
    ppermute x2, starting transfers between devices, gather_x(): left = lax.ppermute(rows, 'x', up)  10.2 us
    ppermute x2, starting transfers between devices, gather_x(): far_top = lax.ppermute(left[:half], 'x', up)  9.44 us
    pallas_call x1, Pallas kernels, local(): pl.pallas_call(functools.partial(forward_kernel, rows=rows), out_shape=[j...  7.63 us
    ppermute x1, waiting for transfers between devices, local(): both = own.astype(F32) + lax.ppermute(away, 'zh', swap(far, 1)).astype(F32)  6.97 us
    unnamed x15, local copies, waits for them, and re-layouts  5.47 us
  transfers between devices with their start and end apart: 17, of which 7 were waited for; matrix products, arithmetic and copies ran while one was open for 4% of the time, Pallas kernels for 4%

profile of v1, /device:TPU:6, one launch (start us, length us, event | category | flops | bytes accessed | tf_op | source)
XLA Modules:
  0.0 195.1 jit_solution(1317273427235070204)
XLA Ops:
  7.2 10.9 %collective-permute-start = (bf16[8,4096]{1,0:T(8,128)(2,1)}, bf16[8,4096]{1,0:T(8,128)(2,1)S(1)}, u32[]{:S(2)}, u32[]{:S(2)}) collective-permute-start(bf16[8,4096]{1,0:T(8,128)(2,1)} %param.4), channel_id=1, source_target_pairs={{0,16},{4,20},{8,24},{12,28},{16,0},{20,4},{24,8},{28,12},{1,17},{... | collective-permute-start | bytes 196616 | tf_op jit(solution)/shard_map/ppermute | solution.py:129
  18.1 1.9 collective-permute-start.7
  22.6 8.2 %collective-permute-start.1 = (bf16[16,4096]{1,0:T(8,128)(2,1)S(1)}, bf16[16,4096]{1,0:T(8,128)(2,1)S(1)}, u32[]{:S(2)}, u32[]{:S(2)}) collective-permute-start(bf16[16,4096]{1,0:T(8,128)(2,1)S(1)} %pad_maximum_fusion.2), channel_id=1, source_target_pairs={{0,8},{4,12},{8,0},{12,4},{16,24},{20,28},{24,16},{28,20},{1,9},{5... | collective-permute-start | bytes 393224 | tf_op jit(solution)/shard_map/ppermute | solution.py:129
  31.7 4.3 %collective-permute-start.8 = (bf16[16,4096]{1,0:T(8,128)(2,1)S(1)}, bf16[16,4096]{1,0:T(8,128)(2,1)S(1)}, u32[]{:S(2)}, u32[]{:S(2)}) collective-permute-start(bf16[16,4096]{1,0:T(8,128)(2,1)S(1)} %pad_maximum_fusion.3), channel_id=1, source_target_pairs={{0,8},{4,12},{8,0},{12,4},{16,24},{20,28},{24,16},{28,20},{1,9},{5... | collective-permute-start | bytes 393224 | tf_op jit(solution)/shard_map/ppermute | solution.py:129
  36.1 0.9 pad_maximum_fusion
  37.0 6.8 %collective-permute-start.2 = (bf16[32,4096]{1,0:T(8,128)(2,1)S(1)}, bf16[32,4096]{1,0:T(8,128)(2,1)S(1)}, u32[]{:S(2)}, u32[]{:S(2)}) collective-permute-start(bf16[32,4096]{1,0:T(8,128)(2,1)S(1)} %pad_maximum_fusion), channel_id=1, source_target_pairs={{0,4},{4,0},{8,12},{12,8},{16,20},{20,16},{24,28},{28,24},{1,5},{5... | collective-permute-start | bytes 786440 | tf_op jit(solution)/shard_map/ppermute | solution.py:129
  44.7 1.9 collective-permute-start.9
  46.7 3.9 %collective-permute-done.2 = bf16[32,4096]{1,0:T(8,128)(2,1)S(1)} collective-permute-done((bf16[32,4096]{1,0:T(8,128)(2,1)S(1)}, bf16[32,4096]{1,0:T(8,128)(2,1)S(1)}, u32[]{:S(2)}, u32[]{:S(2)}) %collective-permute-start.2) | collective-permute-done | bytes 262176 | tf_op jit(solution)/shard_map/ppermute | solution.py:129
  50.6 5.1 %collective-permute-start.3 = (bf16[64,4096]{1,0:T(8,128)(2,1)S(1)}, bf16[64,4096]{1,0:T(8,128)(2,1)S(1)}, u32[]{:S(2)}, u32[]{:S(2)}) collective-permute-start(bf16[64,4096]{1,0:T(8,128)(2,1)S(1)} %constant_dynamic-update-slice_fusion.refs_0_), channel_id=1, source_target_pairs={{0,1},{1,2},{2,3},{3,0},{4,5},{5,6},{6,7},{7,4},{8,9},{9,10},{10,1... | collective-permute-start | bytes 1572872 | tf_op jit(solution)/shard_map/ppermute | solution.py:138
  55.7 1.9 collective-permute-start.4
  57.6 5.1 %collective-permute-start.10 = (bf16[64,4096]{1,0:T(8,128)(2,1)S(1)}, bf16[64,4096]{1,0:T(8,128)(2,1)S(1)}, u32[]{:S(2)}, u32[]{:S(2)}) collective-permute-start(bf16[64,4096]{1,0:T(8,128)(2,1)S(1)} %constant_dynamic-update-slice_fusion.4.refs_0_.refs_2_), channel_id=1, source_target_pairs={{0,1},{1,2},{2,3},{3,0},{4,5},{5,6},{6,7},{7,4},{8,9},{9,10},{10,1... | collective-permute-start | bytes 1572872 | tf_op jit(solution)/shard_map/ppermute | solution.py:138
  62.8 1.9 collective-permute-start.11
  64.7 2.6 %collective-permute-done.3.refs_1_ = bf16[64,4096]{1,0:T(8,128)(2,1)S(1)} collective-permute-done((bf16[64,4096]{1,0:T(8,128)(2,1)S(1)}, bf16[64,4096]{1,0:T(8,128)(2,1)S(1)}, u32[]{:S(2)}, u32[]{:S(2)}) %collective-permute-start.3) | collective-permute-done | bytes 524320 | tf_op jit(solution)/shard_map/ppermute | solution.py:138
  68.1 5.5 %collective-permute-start.5 = (bf16[32,4096]{1,0:T(8,128)(2,1)}, bf16[32,4096]{1,0:T(8,128)(2,1)S(1)}, u32[]{:S(2)}, u32[]{:S(2)}) collective-permute-start(bf16[32,4096]{1,0:T(8,128)(2,1)} %slice.24), channel_id=1, source_target_pairs={{0,1},{1,2},{2,3},{3,0},{4,5},{5,6},{6,7},{7,4},{8,9},{9,10},{10,1... | collective-permute-start | bytes 786440 | tf_op jit(solution)/shard_map/ppermute | solution.py:140
  74.3 1.9 collective-permute-start.6
  76.2 2.3 %collective-permute-done.10.refs_1_.refs_3_ = bf16[64,4096]{1,0:T(8,128)(2,1)S(1)} collective-permute-done((bf16[64,4096]{1,0:T(8,128)(2,1)S(1)}, bf16[64,4096]{1,0:T(8,128)(2,1)S(1)}, u32[]{:S(2)}, u32[]{:S(2)}) %collective-permute-start.10) | collective-permute-done | bytes 524320 | tf_op jit(solution)/shard_map/ppermute | solution.py:138
  79.3 3.9 %collective-permute-start.12 = (bf16[32,4096]{1,0:T(8,128)(2,1)}, bf16[32,4096]{1,0:T(8,128)(2,1)S(1)}, u32[]{:S(2)}, u32[]{:S(2)}) collective-permute-start(bf16[32,4096]{1,0:T(8,128)(2,1)} %slice.26), channel_id=1, source_target_pairs={{0,1},{1,2},{2,3},{3,0},{4,5},{5,6},{6,7},{7,4},{8,9},{9,10},{10,1... | collective-permute-start | bytes 786440 | tf_op jit(solution)/shard_map/ppermute | solution.py:140
  83.9 1.9 collective-permute-start.13
  85.9 1.8 collective-permute-done.6.refs_4_
  87.7 1.9 copy-done
  89.6 1.0 copy-done.3
  90.6 7.6 %shard_map.59 = (bf16[256,4096]{1,0:T(8,128)(2,1)S(1)}, bf16[128,256]{1,0:T(8,128)(2,1)S(1)}, f32[256,128]{1,0:T(8,128)S(1)}, f32[256,128]{1,0:T(8,128)S(1)}, f3...) custom-call(bf16[64,4096]{1,0:T(8,128)(2,1)S(1)} %copy-done.3, ...), custom_call_target="tpu_custom_call" | custom-call | tf_op jit(solution)/shard_map/pallas_call | solution.py:155
  98.3 2.9 %shard_map.60.refs_7_ = bf16[384,256]{1,0:T(8,128)(2,1)S(1)} custom-call(bf16[64,4096]{1,0:T(8,128)(2,1)S(1)} %constant_dynamic-update-slice_fusion.4.refs_0_.refs_2_, bf16[64,4096]{1,0:T(8,128)(2,1)S(1)} %collective-permute-done.10.refs_1_.refs_3_, bf16[64,4096]{1,0:T(8,128)(2,1)S(1)} %collective-permute-done.11.refs_2_.refs_4_, ...), custom_call_target="tpu_custom_call" | custom-call | tf_op jit(solution)/shard_map/pallas_call | solution.py:171
  101.2 0.9 shard_map.61
  102.2 1.9 collective-permute-start.14
  104.1 4.1 %collective-permute-done.14.refs_9_ = bf16[16,512,128]{2,1,0:T(8,128)(2,1)S(1)} collective-permute-done((bf16[16,512,128]{2,1,0:T(8,128)(2,1)S(1)}, bf16[16,512,128]{2,1,0:T(8,128)(2,1)S(1)}, u32[]{:S(2)}, u32[]{:S(2)}) %collective-permute-start.14) | collective-permute-done | bytes 2097184 | tf_op jit(solution)/shard_map/ppermute | solution.py:190
  108.2 2.3 %shard_map.62 = bf16[16,512,128]{2,1,0:T(8,128)(2,1)} custom-call(s32[1]{0:T(128)} %bitcast.refs_0_, bf16[256,4096]{1,0:T(8,128)(2,1)S(1)} %get-tuple-element.10.refs_1_, bf16[64,4096]{1,0:T(8,128)(2,1)S(1)} %constant_dynamic-update-slice_fusion.4.refs_0_.refs_2_, bf16[64,4096]{1,0:T(8,128)(2,1)S(1)} %collective-permute-done.10.refs_1_.refs_3_, ...), custom_call_target="tpu_custom_call" | custom-call | tf_op jit(solution)/shard_map/pallas_call | solution.py:181
  110.5 53.8 %reduce-scatter.2.cloned.1.call-done = bf16[2,512,128]{2,1,0:T(8,128)(2,1)} async-done(((bf16[16,512,128]{2,1,0:T(8,128)(2,1)}), bf16[2,512,128]{2,1,0:T(8,128)(2,1)}) %reduce-scatter.2.cloned.1.call-update) | async-done | bytes 262160 | tf_op jit(solution)/shard_map/reduce_scatter | solution.py:192
  164.3 0.9 dynamic-slice_bitcast_fusion
  165.3 13.6 %collective-permute-start.15 = (bf16[512,128]{1,0:T(8,128)(2,1)S(1)}, bf16[512,128]{1,0:T(8,128)(2,1)S(1)}, u32[]{:S(2)}, u32[]{:S(2)}) collective-permute-start(bf16[512,128]{1,0:T(8,128)(2,1)S(1)} %dynamic-slice_bitcast_fusion), channel_id=1, source_target_pairs={{0,512},{512,0},{1,513},{513,1},{2,514},{514,2},{3,515},{515,3},{4... | collective-permute-start | bytes 393224 | tf_op jit(solution)/shard_map/ppermute | solution.py:196
  178.9 7.0 %collective-permute-done.15 = bf16[512,128]{1,0:T(8,128)(2,1)S(1)} collective-permute-done((bf16[512,128]{1,0:T(8,128)(2,1)S(1)}, bf16[512,128]{1,0:T(8,128)(2,1)S(1)}, u32[]{:S(2)}, u32[]{:S(2)}) %collective-permute-start.15) | collective-permute-done | bytes 131104 | tf_op jit(solution)/shard_map/ppermute | solution.py:196
  185.9 0.9 convert_add_fusion
  (36 shorter events, 8.7 us)
Async XLA Ops:
  7.2 157.2 %reduce-scatter.2.cloned.1.call-start = ((), (), s32[]{:S(2)}) async-start(), calls=%async_computation.1 | async-start | bytes 2359296 | tf_op jit(solution)/shard_map/reduce_scatter | solution.py:192
  7.2 14.6 %collective-permute-start = (bf16[8,4096]{1,0:T(8,128)(2,1)}, bf16[8,4096]{1,0:T(8,128)(2,1)S(1)}, u32[]{:S(2)}, u32[]{:S(2)}) collective-permute-start(bf16[8,4096]{1,0:T(8,128)(2,1)} %param.4), channel_id=1, source_target_pairs={{0,16},{4,20},{8,24},{12,28},{16,0},{20,4},{24,8},{28,12},{1,17},{... | collective-permute-start | bytes 196616 | tf_op jit(solution)/shard_map/ppermute | solution.py:129
  18.1 12.7 %collective-permute-start.7 = (bf16[8,4096]{1,0:T(8,128)(2,1)}, bf16[8,4096]{1,0:T(8,128)(2,1)S(1)}, u32[]{:S(2)}, u32[]{:S(2)}) collective-permute-start(bf16[8,4096]{1,0:T(8,128)(2,1)} %param.5), channel_id=1, source_target_pairs={{0,16},{4,20},{8,24},{12,28},{16,0},{20,4},{24,8},{28,12},{1,17},{... | collective-permute-start | bytes 196616 | tf_op jit(solution)/shard_map/ppermute | solution.py:129
  22.6 13.5 %collective-permute-start.1 = (bf16[16,4096]{1,0:T(8,128)(2,1)S(1)}, bf16[16,4096]{1,0:T(8,128)(2,1)S(1)}, u32[]{:S(2)}, u32[]{:S(2)}) collective-permute-start(bf16[16,4096]{1,0:T(8,128)(2,1)S(1)} %pad_maximum_fusion.2), channel_id=1, source_target_pairs={{0,8},{4,12},{8,0},{12,4},{16,24},{20,28},{24,16},{28,20},{1,9},{5... | collective-permute-start | bytes 393224 | tf_op jit(solution)/shard_map/ppermute | solution.py:129
  31.7 12.1 %collective-permute-start.8 = (bf16[16,4096]{1,0:T(8,128)(2,1)S(1)}, bf16[16,4096]{1,0:T(8,128)(2,1)S(1)}, u32[]{:S(2)}, u32[]{:S(2)}) collective-permute-start(bf16[16,4096]{1,0:T(8,128)(2,1)S(1)} %pad_maximum_fusion.3), channel_id=1, source_target_pairs={{0,8},{4,12},{8,0},{12,4},{16,24},{20,28},{24,16},{28,20},{1,9},{5... | collective-permute-start | bytes 393224 | tf_op jit(solution)/shard_map/ppermute | solution.py:129
  37.0 13.6 %collective-permute-start.2 = (bf16[32,4096]{1,0:T(8,128)(2,1)S(1)}, bf16[32,4096]{1,0:T(8,128)(2,1)S(1)}, u32[]{:S(2)}, u32[]{:S(2)}) collective-permute-start(bf16[32,4096]{1,0:T(8,128)(2,1)S(1)} %pad_maximum_fusion), channel_id=1, source_target_pairs={{0,4},{4,0},{8,12},{12,8},{16,20},{20,16},{24,28},{28,24},{1,5},{5... | collective-permute-start | bytes 786440 | tf_op jit(solution)/shard_map/ppermute | solution.py:129
  44.7 12.9 %collective-permute-start.9 = (bf16[32,4096]{1,0:T(8,128)(2,1)S(1)}, bf16[32,4096]{1,0:T(8,128)(2,1)S(1)}, u32[]{:S(2)}, u32[]{:S(2)}) collective-permute-start(bf16[32,4096]{1,0:T(8,128)(2,1)S(1)} %pad_maximum_fusion.1), channel_id=1, source_target_pairs={{0,4},{4,0},{8,12},{12,8},{16,20},{20,16},{24,28},{28,24},{1,5},{5... | collective-permute-start | bytes 786440 | tf_op jit(solution)/shard_map/ppermute | solution.py:129
  50.6 28.0 %copy-start.2 = (bf16[64,4096]{1,0:T(8,128)(2,1)}, bf16[64,4096]{1,0:T(8,128)(2,1)S(1)}, u32[]{:S(2)}) copy-start(bf16[64,4096]{1,0:T(8,128)(2,1)S(1)} %constant_dynamic-update-slice_fusion.refs_0_) | copy-start | bytes 1572868
  50.6 16.8 %collective-permute-start.3 = (bf16[64,4096]{1,0:T(8,128)(2,1)S(1)}, bf16[64,4096]{1,0:T(8,128)(2,1)S(1)}, u32[]{:S(2)}, u32[]{:S(2)}) collective-permute-start(bf16[64,4096]{1,0:T(8,128)(2,1)S(1)} %constant_dynamic-update-slice_fusion.refs_0_), channel_id=1, source_target_pairs={{0,1},{1,2},{2,3},{3,0},{4,5},{5,6},{6,7},{7,4},{8,9},{9,10},{10,1... | collective-permute-start | bytes 1572872 | tf_op jit(solution)/shard_map/ppermute | solution.py:138
  55.7 17.9 %collective-permute-start.4 = (bf16[64,4096]{1,0:T(8,128)(2,1)S(1)}, bf16[64,4096]{1,0:T(8,128)(2,1)S(1)}, u32[]{:S(2)}, u32[]{:S(2)}) collective-permute-start(bf16[64,4096]{1,0:T(8,128)(2,1)S(1)} %constant_dynamic-update-slice_fusion.refs_0_), channel_id=1, source_target_pairs={{0,3},{1,0},{2,1},{3,2},{4,7},{5,4},{6,5},{7,6},{8,11},{9,8},{10,9... | collective-permute-start | bytes 1572872 | tf_op jit(solution)/shard_map/ppermute | solution.py:139
  57.6 20.9 %collective-permute-start.10 = (bf16[64,4096]{1,0:T(8,128)(2,1)S(1)}, bf16[64,4096]{1,0:T(8,128)(2,1)S(1)}, u32[]{:S(2)}, u32[]{:S(2)}) collective-permute-start(bf16[64,4096]{1,0:T(8,128)(2,1)S(1)} %constant_dynamic-update-slice_fusion.4.refs_0_.refs_2_), channel_id=1, source_target_pairs={{0,1},{1,2},{2,3},{3,0},{4,5},{5,6},{6,7},{7,4},{8,9},{9,10},{10,1... | collective-permute-start | bytes 1572872 | tf_op jit(solution)/shard_map/ppermute | solution.py:138
  62.8 20.4 %collective-permute-start.11 = (bf16[64,4096]{1,0:T(8,128)(2,1)S(1)}, bf16[64,4096]{1,0:T(8,128)(2,1)S(1)}, u32[]{:S(2)}, u32[]{:S(2)}) collective-permute-start(bf16[64,4096]{1,0:T(8,128)(2,1)S(1)} %constant_dynamic-update-slice_fusion.4.refs_0_.refs_2_), channel_id=1, source_target_pairs={{0,3},{1,0},{2,1},{3,2},{4,7},{5,4},{6,5},{7,6},{8,11},{9,8},{10,9... | collective-permute-start | bytes 1572872 | tf_op jit(solution)/shard_map/ppermute | solution.py:139
  68.1 17.8 %collective-permute-start.5 = (bf16[32,4096]{1,0:T(8,128)(2,1)}, bf16[32,4096]{1,0:T(8,128)(2,1)S(1)}, u32[]{:S(2)}, u32[]{:S(2)}) collective-permute-start(bf16[32,4096]{1,0:T(8,128)(2,1)} %slice.24), channel_id=1, source_target_pairs={{0,1},{1,2},{2,3},{3,0},{4,5},{5,6},{6,7},{7,4},{8,9},{9,10},{10,1... | collective-permute-start | bytes 786440 | tf_op jit(solution)/shard_map/ppermute | solution.py:140
  74.3 13.4 %collective-permute-start.6 = (bf16[32,4096]{1,0:T(8,128)(2,1)}, bf16[32,4096]{1,0:T(8,128)(2,1)}, u32[]{:S(2)}, u32[]{:S(2)}) collective-permute-start(bf16[32,4096]{1,0:T(8,128)(2,1)} %slice.25), channel_id=1, source_target_pairs={{0,3},{1,0},{2,1},{3,2},{4,7},{5,4},{6,5},{7,6},{8,11},{9,8},{10,9... | collective-permute-start | bytes 786440 | tf_op jit(solution)/shard_map/ppermute | solution.py:141
  79.3 19.0 %collective-permute-start.12 = (bf16[32,4096]{1,0:T(8,128)(2,1)}, bf16[32,4096]{1,0:T(8,128)(2,1)S(1)}, u32[]{:S(2)}, u32[]{:S(2)}) collective-permute-start(bf16[32,4096]{1,0:T(8,128)(2,1)} %slice.26), channel_id=1, source_target_pairs={{0,1},{1,2},{2,3},{3,0},{4,5},{5,6},{6,7},{7,4},{8,9},{9,10},{10,1... | collective-permute-start | bytes 786440 | tf_op jit(solution)/shard_map/ppermute | solution.py:140
  83.9 14.4 %collective-permute-start.13 = (bf16[32,4096]{1,0:T(8,128)(2,1)}, bf16[32,4096]{1,0:T(8,128)(2,1)S(1)}, u32[]{:S(2)}, u32[]{:S(2)}) collective-permute-start(bf16[32,4096]{1,0:T(8,128)(2,1)} %slice.27), channel_id=1, source_target_pairs={{0,3},{1,0},{2,1},{3,2},{4,7},{5,4},{6,5},{7,6},{8,11},{9,8},{10,9... | collective-permute-start | bytes 786440 | tf_op jit(solution)/shard_map/ppermute | solution.py:141
  87.7 1.9 copy-start
  89.6 1.0 copy-start.3
  90.6 7.7 %copy-start.1 = (bf16[1,128,4096]{2,1,0:T(8,128)(2,1)S(1)}, bf16[1,128,4096]{2,1,0:T(8,128)(2,1)}, u32[]{:S(2)}) copy-start(bf16[1,128,4096]{2,1,0:T(8,128)(2,1)} %param.7) | copy-start | bytes 3145732
  102.2 6.1 %collective-permute-start.14 = (bf16[16,512,128]{2,1,0:T(8,128)(2,1)S(1)}, bf16[16,512,128]{2,1,0:T(8,128)(2,1)S(1)}, u32[]{:S(2)}, u32[]{:S(2)}) collective-permute-start(bf16[16,512,128]{2,1,0:T(8,128)(2,1)S(1)} %shard_map.61), channel_id=1, source_target_pairs={{0,32},{32,0},{1,33},{33,1},{2,34},{34,2},{3,35},{35,3},{4,36},{36... | collective-permute-start | bytes 6291464 | tf_op jit(solution)/shard_map/ppermute | solution.py:190
  165.3 20.6 %collective-permute-start.15 = (bf16[512,128]{1,0:T(8,128)(2,1)S(1)}, bf16[512,128]{1,0:T(8,128)(2,1)S(1)}, u32[]{:S(2)}, u32[]{:S(2)}) collective-permute-start(bf16[512,128]{1,0:T(8,128)(2,1)S(1)} %dynamic-slice_bitcast_fusion), channel_id=1, source_target_pairs={{0,512},{512,0},{1,513},{513,1},{2,514},{514,2},{3,515},{515,3},{4... | collective-permute-start | bytes 393224 | tf_op jit(solution)/shard_map/ppermute | solution.py:196
Sparse Core Ops, SparseCore 0:
  110.6 53.6 reduce-scatter.1

commit v2 on v1

--- a/solution.py
+++ b/solution.py
@@ -17,7 +17,7 @@
 NN = (((1,), (0,)), ((), ()))
 VMEM = pl.BlockSpec(memory_space=pltpu.VMEM)
 SMEM = pl.BlockSpec(memory_space=pltpu.SMEM)
-PARAMS = pltpu.CompilerParams(vmem_limit_bytes=40 * 1024 * 1024)
+PARAMS = pltpu.CompilerParams(vmem_limit_bytes=16 * 1024 * 1024)
 
 
 def normalize(values):
@@ -88,58 +88,113 @@
     out_ref[2 * width :, :] = d_value.T.astype(BF16)
 
 
-def terms_kernel(*refs, count, blocks, adds):
-    core_ref, normed_ref = refs[:2]
+def terms_kernel(*refs, count, blocks, slots):
+    place_ref, normed_ref = refs[:2]
     pieces = refs[2 : 2 + count]
     d_ref, att_ref = refs[2 + count : 4 + count]
-    out_ref = refs[-1]
+    rest = refs[4 + count :]
     far, near, width = blocks
-    core = core_ref[0]
+    core, here = place_ref[0], place_ref[1]
     d_all, att = d_ref[...], att_ref[...]
     split = d_all.shape[0]
-    for y in range(near):
+    order = distances(near)
+    for slot, distance in enumerate(order):
+        y = lax.rem(here + distance + near, near)
         cols = [
             pl.ds(pl.multiple_of(((zh * near + y) * 2 + core) * width, width), width)
             for zh in range(far)
         ]
         rhs = jnp.concatenate([normed_ref[:, c] for c in cols], 1)
-        cot = jnp.concatenate(
-            [jnp.concatenate([p[:, c] for p in pieces], 0) for c in cols], 1
-        )
+        cot = jnp.concatenate([jnp.concatenate([p[:, c] for p in pieces], 0) for c in cols], 1)
         top = jnp.dot(d_all, rhs, preferred_element_type=F32)
         low = jnp.dot(att, cot, preferred_element_type=F32)
         for zh in range(far):
             a = top[:, zh * width : (zh + 1) * width]
             b = low[:, zh * width : (zh + 1) * width]
-            if adds:
-                other = refs[4 + count]
-                a = a + other[y * far + zh, :split, :].astype(F32)
-                b = b + other[y * far + zh, split:, :].astype(F32)
-            out_ref[y * far + zh, :split, :] = a.astype(BF16)
-            out_ref[y * far + zh, split:, :] = b.astype(BF16)
+            at = slot * far + zh
+            if slots:
+                other = rest[0]
+                a = a + other[at, :split, :].astype(F32)
+                b = b + other[at, split:, :].astype(F32)
+                out = rest[1 + zh] if slot == 0 else rest[far + slot].at[zh]
+            else:
+                out = rest[0].at[at]
+            out[:split, :] = a.astype(BF16)
+            out[split:, :] = b.astype(BF16)
+
+
+def distances(n):
+    order = [n // 2]
+    for d in range(n // 2 - 1, 0, -1):
+        order += [d, -d]
+    return order + [0]
+
+
+def last_kernel(zh_ref, own_ref, up_ref, down_ref, away_ref, kept_ref):
+    def total(at):
+        return (
+            own_ref[at, :, :].astype(F32)
+            + up_ref[at, :, :].astype(F32)
+            + down_ref[at, :, :].astype(F32)
+        )
+
+    zh = zh_ref[0]
+    away_ref[...] = total(1 - zh).astype(BF16)
+    kept_ref[...] = total(zh)
+
+
+def finish_kernel(kept_ref, other_ref, qkv_ref, out_ref):
+    both = kept_ref[...] + other_ref[...].astype(F32)
+    split = qkv_ref.shape[1]
+    qkv_ref[...] = both[:split].T
+    out_ref[...] = both[split:]
 
 
 def swap(n, s):
     return [(i, i ^ s) for i in range(n)]
 
 
-def gather_z(rows, n):
-    s = n // 2
-    while s:
-        rows = jnp.concatenate([rows, lax.ppermute(rows, "zl", swap(n, s))], 0)
+def turn(n, s):
+    return [(i, (i + s) % n) for i in range(n)]
+
+
+def after(value, *done):
+    return lax.optimization_barrier((value, *done))[0]
+
+
+def gather(tokens, cotangent, n_z, n_x):
+    up, down = turn(n_x, 1), turn(n_x, -1)
+
+    def join(rows, s, *done):
+        other = lax.ppermute(after(rows, *done), "zl", swap(n_z, s))
+        return lax.optimization_barrier(jnp.concatenate([rows, other], 0)), other
+
+    t, t_done = tokens, ()
+    c, c_done = cotangent, ()
+    s = n_z // 2
+    while s > 1:
+        t, other = join(t, s)
+        c, last = join(c, s, *t_done)
+        t_done = (other,)
         s //= 2
-    return rows
-
-
-def gather_x(rows, n):
-    up = [(i, (i + 1) % n) for i in range(n)]
-    down = [(i, (i - 1) % n) for i in range(n)]
-    half = rows.shape[0] // 2
-    left = lax.ppermute(rows, "x", up)
-    right = lax.ppermute(rows, "x", down)
-    far_top = lax.ppermute(left[:half], "x", up)
-    far_low = lax.ppermute(right[half:], "x", down)
-    return [rows, left, right, far_top, far_low]
+    tb = lax.ppermute(t, "zl", swap(n_z, 1))
+    ta_left = lax.ppermute(t, "x", up)
+    ta_right = lax.ppermute(t, "x", down)
+    tb_right = lax.ppermute(tb, "x", down)
+    tb_left = lax.ppermute(tb, "x", up)
+    ta_far = lax.ppermute(ta_left, "x", up)
+    tb_far = lax.ppermute(tb_right, "x", down)
+    cb = lax.ppermute(after(c, tb, ta_left, ta_right), "zl", swap(n_z, 1))
+    ca_left = lax.ppermute(after(c, ta_left, tb_left), "x", up)
+    cb_right = lax.ppermute(after(cb, tb_right, tb_left), "x", down)
+    ca_right = lax.ppermute(after(c, tb_right, tb_left), "x", down)
+    cb_left = lax.ppermute(cb, "x", up)
+    ca_far = lax.ppermute(ca_left, "x", up)
+    cb_far = lax.ppermute(cb_right, "x", down)
+    return (
+        [t, ta_left, ta_right, tb, tb_left, tb_right, ta_far, tb_far],
+        [c, ca_left, ca_right, cb, cb_left, cb_right, ca_far, cb_far],
+    )
 
 
 def local(sizes, tokens, cotangent, w_qkv, w_out):
@@ -147,8 +202,7 @@
     w_head = w_qkv[:, 0, :]
     w_back = w_out[0]
     model, width = w_head.shape[0], w_back.shape[0]
-    t_pieces = gather_x(gather_z(tokens, n_z), n_x)
-    c_pieces = gather_x(gather_z(cotangent, n_z), n_x)
+    t_pieces, c_pieces = gather(tokens, cotangent, n_z, n_x)
     rows = tuple(p.shape[0] for p in t_pieces)
     total = sum(rows)
     small = jax.ShapeDtypeStruct((total, width), F32)
@@ -176,25 +230,60 @@
         compiler_params=PARAMS,
     )(*c_pieces, w_back, q, k, v, probs, sq, sk)
     blocks = (far, near, model // (far * near * cores))
-
-    def terms(core, *other):
+    one = jax.ShapeDtypeStruct((4 * width, blocks[2]), BF16)
+    two = jax.ShapeDtypeStruct((far, 4 * width, blocks[2]), BF16)
+    here = lax.axis_index("y").astype(jnp.int32)
+    core = lax.axis_index("c").astype(jnp.int32)
+
+    def terms(core, shapes, *other):
         return pl.pallas_call(
-            functools.partial(terms_kernel, count=len(rows), blocks=blocks, adds=len(other) > 0),
-            out_shape=jax.ShapeDtypeStruct((far * near, 4 * width, blocks[2]), BF16),
+            functools.partial(
+                terms_kernel, count=len(rows), blocks=blocks, slots=len(other) > 0
+            ),
+            out_shape=shapes,
             in_specs=[SMEM] + [VMEM] * (len(rows) + 3 + len(other)),
-            out_specs=VMEM,
+            out_specs=[VMEM] * len(shapes),
             compiler_params=PARAMS,
-        )(core.reshape(1), normed, *c_pieces, d_qkv, att, *other)
-
-    core = lax.axis_index("c").astype(jnp.int32)
-    theirs = lax.ppermute(terms(1 - core), "c", swap(cores, 1))
-    pair = terms(core, theirs)
-    summed = lax.psum_scatter(pair, "y", scatter_dimension=0, tiled=True)
-    zh = lax.axis_index("zh")
-    own = lax.dynamic_index_in_dim(summed, zh, 0, keepdims=False)
-    away = lax.dynamic_index_in_dim(summed, 1 - zh, 0, keepdims=False)
-    both = own.astype(F32) + lax.ppermute(away, "zh", swap(far, 1)).astype(F32)
-    return both[: 3 * width].T[:, None, :], both[3 * width :][None]
+        )(jnp.stack([core, here]), normed, *c_pieces, d_qkv, att, *other)
+
+    (mine,) = terms(1 - core, [jax.ShapeDtypeStruct((far * near, 4 * width, blocks[2]), BF16)])
+    theirs = lax.ppermute(mine, "c", swap(cores, 1))
+    first_up, first_down, *parts = terms(core, [one, one] + [two] * (near - 1), theirs)
+    ups, downs, own = parts[0:-1:2], parts[1:-1:2], parts[-1]
+    up, down = turn(near, 1), turn(near, -1)
+
+    def add(a, b):
+        return (a.astype(F32) + b.astype(F32)).astype(BF16)
+
+    goes_up = lax.ppermute(first_up, "y", up)
+    goes_down = lax.ppermute(first_down, "y", down)
+    for step, (a, b) in enumerate(zip(ups, downs)):
+        if step == 0:
+            a = jnp.stack([add(a[0], goes_up), a[1]])
+            b = jnp.stack([b[0], add(b[1], goes_down)])
+        else:
+            a, b = add(a, goes_up), add(b, goes_down)
+        goes_up = lax.ppermute(a, "y", up)
+        goes_down = lax.ppermute(b, "y", down)
+    away, kept = pl.pallas_call(
+        last_kernel,
+        out_shape=[one, jax.ShapeDtypeStruct(one.shape, F32)],
+        in_specs=[SMEM] + [VMEM] * 3,
+        out_specs=[VMEM] * 2,
+        compiler_params=PARAMS,
+    )(lax.axis_index("zh").astype(jnp.int32).reshape(1), own, goes_up, goes_down)
+    other = lax.ppermute(away, "zh", swap(far, 1))
+    grad_qkv, grad_out = pl.pallas_call(
+        finish_kernel,
+        out_shape=[
+            jax.ShapeDtypeStruct((blocks[2], 3 * width), F32),
+            jax.ShapeDtypeStruct((width, blocks[2]), F32),
+        ],
+        in_specs=[VMEM] * 2,
+        out_specs=[VMEM] * 2,
+        compiler_params=PARAMS,
+    )(kept, other)
+    return grad_qkv[:, None, :], grad_out[None]
 
 
 def solution(mesh):

time: 196 us -> 174 us (0.89)
  waiting for transfers between devices: 75.7 us -> 28.4 us
  starting transfers between devices: 77.1 us -> 123 us
  between operations: 14.3 us -> 1.15 us
  local copies, waits for them, and re-layouts: 9.93 us -> 4.44 us
  other arithmetic: 4.35 us -> 2.31 us
    reduce_scatter x1 -> x0, waiting for transfers between devices: 53.8 us -> none  [local(): summed = lax.psum_scatter(pair, 'y', scatter_dimension=0, tiled=True)]
    ppermute x16 -> x28, starting transfers between devices: 77 us -> 123 us  [the longest x4 26.6 us: join(): other = lax.ppermute(after(rows, *done), 'zl', swap(n_z, s))]
    ppermute x16 -> x28, waiting for transfers between devices: 21.8 us -> 28.4 us  [the longest x1 7.69 us: local(): other = lax.ppermute(away, 'zh', swap(far, 1))]
    slice x4 -> x2, local copies, waits for them, and re-layouts: 2.85 us -> 0.02 us  [the longest x1 0.01 us: local(): a = jnp.stack([add(a[0], goes_up), a[1]])]
    unnamed x15 -> x9, local copies, waits for them, and re-layouts: 5.47 us -> 4.41 us
  transfers between devices with their start and end apart: 17 -> 28, of which waited for: 7 -> 9; matrix products, arithmetic and copies ran while one was open for 4% -> 1% of each run, Pallas kernels for 4% -> 4%
where the time goes in v2:
time: 174 us; the launch traced here: 173 us
  starting transfers between devices  123 us (71%)
  waiting for transfers between devices  28.4 us (16%)
  Pallas kernels  14.4 us (8%)
  local copies, waits for them, and re-layouts  4.44 us (3%)
  other arithmetic  2.31 us (1%)
    ppermute x4, starting transfers between devices, join(): other = lax.ppermute(after(rows, *done), 'zl', swap(n_z, s))  26.6 us
    ppermute x3, starting transfers between devices, local(): goes_down = lax.ppermute(b, 'y', down)  16.8 us
    ppermute x1, starting transfers between devices, local(): other = lax.ppermute(away, 'zh', swap(far, 1))  14 us
    pallas_call x1, Pallas kernels, local(): pl.pallas_call(functools.partial(forward_kernel, rows=rows), out_shape=[j...  7.71 us
    ppermute x1, waiting for transfers between devices, local(): other = lax.ppermute(away, 'zh', swap(far, 1))  7.69 us
    ppermute x3, waiting for transfers between devices, local(): goes_down = lax.ppermute(b, 'y', down)  6.95 us
    ppermute x1, starting transfers between devices, gather(): tb = lax.ppermute(t, 'zl', swap(n_z, 1))  6.86 us
    ppermute x3, starting transfers between devices, local(): goes_up = lax.ppermute(a, 'y', up)  5.76 us
  transfers between devices with their start and end apart: 28, of which 9 were waited for; matrix products, arithmetic and copies ran while one was open for 1% of the time, Pallas kernels for 4%

profile of v2, /device:TPU:6, one launch (start us, length us, event | category | flops | bytes accessed | tf_op | source)
XLA Modules:
  0.0 173.2 jit_solution(1906753394415016852)
XLA Ops:
  0.6 10.9 %collective-permute-start = (bf16[8,4096]{1,0:T(8,128)(2,1)}, bf16[8,4096]{1,0:T(8,128)(2,1)S(1)}, u32[]{:S(2)}, u32[]{:S(2)}) collective-permute-start(bf16[8,4096]{1,0:T(8,128)(2,1)} %param.4), channel_id=1, source_target_pairs={{0,16},{4,20},{8,24},{12,28},{16,0},{20,4},{24,8},{28,12},{1,17},{... | collective-permute-start | bytes 196616 | tf_op jit(solution)/shard_map/ppermute | solution.py:169
  11.6 1.9 %collective-permute-start.9 = (bf16[8,4096]{1,0:T(8,128)(2,1)}, bf16[8,4096]{1,0:T(8,128)(2,1)S(1)}, u32[]{:S(2)}, u32[]{:S(2)}) collective-permute-start(bf16[8,4096]{1,0:T(8,128)(2,1)} %param.5), channel_id=1, source_target_pairs={{0,16},{4,20},{8,24},{12,28},{16,0},{20,4},{24,8},{28,12},{1,17},{... | collective-permute-start | bytes 196616 | tf_op jit(solution)/shard_map/ppermute | solution.py:169
  14.8 9.4 %collective-permute-start.1 = (bf16[16,4096]{1,0:T(8,128)(2,1)S(1)}, bf16[16,4096]{1,0:T(8,128)(2,1)S(1)}, u32[]{:S(2)}, u32[]{:S(2)}) collective-permute-start(bf16[16,4096]{1,0:T(8,128)(2,1)S(1)} %pad_maximum_fusion.4), channel_id=1, source_target_pairs={{0,8},{4,12},{8,0},{12,4},{16,24},{20,28},{24,16},{28,20},{1,9},{5... | collective-permute-start | bytes 393224 | tf_op jit(solution)/shard_map/ppermute | solution.py:169
  25.2 4.3 %collective-permute-start.10 = (bf16[16,4096]{1,0:T(8,128)(2,1)S(1)}, bf16[16,4096]{1,0:T(8,128)(2,1)S(1)}, u32[]{:S(2)}, u32[]{:S(2)}) collective-permute-start(bf16[16,4096]{1,0:T(8,128)(2,1)S(1)} %pad_maximum_fusion.5), channel_id=1, source_target_pairs={{0,8},{4,12},{8,0},{12,4},{16,24},{20,28},{24,16},{28,20},{1,9},{5... | collective-permute-start | bytes 393224 | tf_op jit(solution)/shard_map/ppermute | solution.py:169
  29.5 6.9 %collective-permute-start.4 = (bf16[32,4096]{1,0:T(8,128)(2,1)S(1)}, bf16[32,4096]{1,0:T(8,128)(2,1)S(1)}, u32[]{:S(2)}, u32[]{:S(2)}) collective-permute-start(bf16[32,4096]{1,0:T(8,128)(2,1)S(1)} %pad_maximum_fusion.refs_0_), channel_id=1, source_target_pairs={{0,4},{4,0},{8,12},{12,8},{16,20},{20,16},{24,28},{28,24},{1,5},{5... | collective-permute-start | bytes 786440 | tf_op jit(solution)/shard_map/ppermute | solution.py:180
  36.4 2.7 %collective-permute-start.3 = (bf16[32,4096]{1,0:T(8,128)(2,1)S(1)}, bf16[32,4096]{1,0:T(8,128)(2,1)S(1)}, u32[]{:S(2)}, u32[]{:S(2)}) collective-permute-start(bf16[32,4096]{1,0:T(8,128)(2,1)S(1)} %pad_maximum_fusion.refs_0_), channel_id=1, source_target_pairs={{0,3},{1,0},{2,1},{3,2},{4,7},{5,4},{6,5},{7,6},{8,11},{9,8},{10,9... | collective-permute-start | bytes 786440 | tf_op jit(solution)/shard_map/ppermute | solution.py:182
  39.1 4.7 %collective-permute-start.2 = (bf16[32,4096]{1,0:T(8,128)(2,1)S(1)}, bf16[32,4096]{1,0:T(8,128)(2,1)S(1)}, u32[]{:S(2)}, u32[]{:S(2)}) collective-permute-start(bf16[32,4096]{1,0:T(8,128)(2,1)S(1)} %pad_maximum_fusion.refs_0_), channel_id=1, source_target_pairs={{0,1},{1,2},{2,3},{3,0},{4,5},{5,6},{6,7},{7,4},{8,9},{9,10},{10,1... | collective-permute-start | bytes 786440 | tf_op jit(solution)/shard_map/ppermute | solution.py:181
  43.8 4.3 %collective-permute-start.5 = (bf16[32,4096]{1,0:T(8,128)(2,1)S(1)}, bf16[32,4096]{1,0:T(8,128)(2,1)S(1)}, u32[]{:S(2)}, u32[]{:S(2)}) collective-permute-start(bf16[32,4096]{1,0:T(8,128)(2,1)S(1)} %collective-permute-done.4.refs_3_), channel_id=1, source_target_pairs={{0,1},{1,2},{2,3},{3,0},{4,5},{5,6},{6,7},{7,4},{8,9},{9,10},{10,1... | collective-permute-start | bytes 786440 | tf_op jit(solution)/shard_map/ppermute | solution.py:184
  48.2 2.3 %collective-permute-done.2.refs_1_ = bf16[32,4096]{1,0:T(8,128)(2,1)S(1)} collective-permute-done((bf16[32,4096]{1,0:T(8,128)(2,1)S(1)}, bf16[32,4096]{1,0:T(8,128)(2,1)S(1)}, u32[]{:S(2)}, u32[]{:S(2)}) %collective-permute-start.2) | collective-permute-done | bytes 262176 | tf_op jit(solution)/shard_map/ppermute | solution.py:181
  50.5 3.4 %collective-permute-start.6 = (bf16[32,4096]{1,0:T(8,128)(2,1)S(1)}, bf16[32,4096]{1,0:T(8,128)(2,1)}, u32[]{:S(2)}, u32[]{:S(2)}) collective-permute-start(bf16[32,4096]{1,0:T(8,128)(2,1)S(1)} %collective-permute-done.4.refs_3_), channel_id=1, source_target_pairs={{0,3},{1,0},{2,1},{3,2},{4,7},{5,4},{6,5},{7,6},{8,11},{9,8},{10,9... | collective-permute-start | bytes 786440 | tf_op jit(solution)/shard_map/ppermute | solution.py:183
  53.9 3.4 %collective-permute-start.13 = (bf16[32,4096]{1,0:T(8,128)(2,1)S(1)}, bf16[32,4096]{1,0:T(8,128)(2,1)S(1)}, u32[]{:S(2)}, u32[]{:S(2)}) collective-permute-start(bf16[32,4096]{1,0:T(8,128)(2,1)S(1)} %pad_maximum_fusion.1.refs_0_.refs_2_), channel_id=1, source_target_pairs={{0,4},{4,0},{8,12},{12,8},{16,20},{20,16},{24,28},{28,24},{1,5},{5... | collective-permute-start | bytes 786440 | tf_op jit(solution)/shard_map/ppermute | solution.py:187
  57.3 3.3 %collective-permute-start.7 = (bf16[32,4096]{1,0:T(8,128)(2,1)S(1)}, bf16[32,4096]{1,0:T(8,128)(2,1)S(1)}, u32[]{:S(2)}, u32[]{:S(2)}) collective-permute-start(bf16[32,4096]{1,0:T(8,128)(2,1)S(1)} %collective-permute-done.2.refs_1_), channel_id=1, source_target_pairs={{0,1},{1,2},{2,3},{3,0},{4,5},{5,6},{6,7},{7,4},{8,9},{9,10},{10,1... | collective-permute-start | bytes 786440 | tf_op jit(solution)/shard_map/ppermute | solution.py:185
  60.6 3.9 %collective-permute-start.11 = (bf16[32,4096]{1,0:T(8,128)(2,1)S(1)}, bf16[32,4096]{1,0:T(8,128)(2,1)S(1)}, u32[]{:S(2)}, u32[]{:S(2)}) collective-permute-start(bf16[32,4096]{1,0:T(8,128)(2,1)S(1)} %pad_maximum_fusion.1.refs_0_.refs_2_), channel_id=1, source_target_pairs={{0,1},{1,2},{2,3},{3,0},{4,5},{5,6},{6,7},{7,4},{8,9},{9,10},{10,1... | collective-permute-start | bytes 786440 | tf_op jit(solution)/shard_map/ppermute | solution.py:188
  64.6 1.9 %collective-permute-start.15 = (bf16[32,4096]{1,0:T(8,128)(2,1)S(1)}, bf16[32,4096]{1,0:T(8,128)(2,1)S(1)}, u32[]{:S(2)}, u32[]{:S(2)}) collective-permute-start(bf16[32,4096]{1,0:T(8,128)(2,1)S(1)} %collective-permute-done.13.refs_3_.refs_5_), channel_id=1, source_target_pairs={{0,3},{1,0},{2,1},{3,2},{4,7},{5,4},{6,5},{7,6},{8,11},{9,8},{10,9... | collective-permute-start | bytes 786440 | tf_op jit(solution)/shard_map/ppermute | solution.py:189
  66.5 3.2 %collective-permute-start.8 = (bf16[32,4096]{1,0:T(8,128)(2,1)}, bf16[32,4096]{1,0:T(8,128)(2,1)}, u32[]{:S(2)}, u32[]{:S(2)}) collective-permute-start(bf16[32,4096]{1,0:T(8,128)(2,1)} %collective-permute-done.6.refs_5_), channel_id=1, source_target_pairs={{0,3},{1,0},{2,1},{3,2},{4,7},{5,4},{6,5},{7,6},{8,11},{9,8},{10,9... | collective-permute-start | bytes 786440 | tf_op jit(solution)/shard_map/ppermute | solution.py:186
  69.7 2.1 %collective-permute-start.12 = (bf16[32,4096]{1,0:T(8,128)(2,1)S(1)}, bf16[32,4096]{1,0:T(8,128)(2,1)S(1)}, u32[]{:S(2)}, u32[]{:S(2)}) collective-permute-start(bf16[32,4096]{1,0:T(8,128)(2,1)S(1)} %pad_maximum_fusion.1.refs_0_.refs_2_), channel_id=1, source_target_pairs={{0,3},{1,0},{2,1},{3,2},{4,7},{5,4},{6,5},{7,6},{8,11},{9,8},{10,9... | collective-permute-start | bytes 786440 | tf_op jit(solution)/shard_map/ppermute | solution.py:190
  72.4 5.0 %collective-permute-start.14 = (bf16[32,4096]{1,0:T(8,128)(2,1)S(1)}, bf16[32,4096]{1,0:T(8,128)(2,1)S(1)}, u32[]{:S(2)}, u32[]{:S(2)}) collective-permute-start(bf16[32,4096]{1,0:T(8,128)(2,1)S(1)} %collective-permute-done.13.refs_3_.refs_5_), channel_id=1, source_target_pairs={{0,1},{1,2},{2,3},{3,0},{4,5},{5,6},{6,7},{7,4},{8,9},{9,10},{10,1... | collective-permute-start | bytes 786440 | tf_op jit(solution)/shard_map/ppermute | solution.py:191
  77.4 2.7 %collective-permute-start.16 = (bf16[32,4096]{1,0:T(8,128)(2,1)S(1)}, bf16[32,4096]{1,0:T(8,128)(2,1)S(1)}, u32[]{:S(2)}, u32[]{:S(2)}) collective-permute-start(bf16[32,4096]{1,0:T(8,128)(2,1)S(1)} %collective-permute-done.11.refs_1_.refs_3_), channel_id=1, source_target_pairs={{0,1},{1,2},{2,3},{3,0},{4,5},{5,6},{6,7},{7,4},{8,9},{9,10},{10,1... | collective-permute-start | bytes 786440 | tf_op jit(solution)/shard_map/ppermute | solution.py:192
  80.1 3.2 %collective-permute-start.17 = (bf16[32,4096]{1,0:T(8,128)(2,1)S(1)}, bf16[32,4096]{1,0:T(8,128)(2,1)S(1)}, u32[]{:S(2)}, u32[]{:S(2)}) collective-permute-start(bf16[32,4096]{1,0:T(8,128)(2,1)S(1)} %collective-permute-done.15.refs_5_.refs_7_), channel_id=1, source_target_pairs={{0,3},{1,0},{2,1},{3,2},{4,7},{5,4},{6,5},{7,6},{8,11},{9,8},{10,9... | collective-permute-start | bytes 786440 | tf_op jit(solution)/shard_map/ppermute | solution.py:193
  86.2 7.7 %shard_map.59 = (bf16[256,4096]{1,0:T(8,128)(2,1)S(1)}, bf16[128,256]{1,0:T(8,128)(2,1)S(1)}, f32[256,128]{1,0:T(8,128)S(1)}, f32[256,128]{1,0:T(8,128)S(1)}, f3...) custom-call(bf16[32,4096]{1,0:T(8,128)(2,1)S(1)} %pad_maximum_fusion.refs_0_, ...), custom_call_target="tpu_custom_call" | custom-call | tf_op jit(solution)/shard_map/pallas_call | solution.py:209
  94.0 2.9 %shard_map.60.refs_10_ = bf16[384,256]{1,0:T(8,128)(2,1)S(1)} custom-call(bf16[32,4096]{1,0:T(8,128)(2,1)S(1)} %pad_maximum_fusion.1.refs_0_.refs_2_, bf16[32,4096]{1,0:T(8,128)(2,1)S(1)} %collective-permute-done.11.refs_1_.refs_3_, bf16[32,4096]{1,0:T(8,128)(2,1)S(1)} %collective-permute-done.12.refs_2_.refs_4_, ...), custom_call_target="tpu_custom_call" | custom-call | tf_op jit(solution)/shard_map/pallas_call | solution.py:225
  100.4 4.0 %collective-permute-done.18.refs_12_ = bf16[16,512,128]{2,1,0:T(8,128)(2,1)S(1)} collective-permute-done((bf16[16,512,128]{2,1,0:T(8,128)(2,1)S(1)}, bf16[16,512,128]{2,1,0:T(8,128)(2,1)S(1)}, u32[]{:S(2)}, u32[]{:S(2)}) %collective-permute-start.18) | collective-permute-done | bytes 2097184 | tf_op jit(solution)/shard_map/ppermute | solution.py:250
  106.0 5.0 %collective-permute-start.23 = (bf16[512,128]{1,0:T(8,128)(2,1)S(1)}, bf16[512,128]{1,0:T(8,128)(2,1)S(1)}, u32[]{:S(2)}, u32[]{:S(2)}) collective-permute-start(bf16[512,128]{1,0:T(8,128)(2,1)S(1)} %get-tuple-element.49), channel_id=1, source_target_pairs={{0,448},{64,0},{128,64},{192,128},{256,192},{320,256},{384,320},{4... | collective-permute-start | bytes 393224 | tf_op jit(solution)/shard_map/ppermute | solution.py:259
  114.1 5.6 %collective-permute-start.24 = (bf16[2,512,128]{2,1,0:T(8,128)(2,1)S(1)}, bf16[2,512,128]{2,1,0:T(8,128)(2,1)S(1)}, u32[]{:S(2)}, u32[]{:S(2)}) collective-permute-start(bf16[2,512,128]{2,1,0:T(8,128)(2,1)S(1)} %pad_maximum_fusion.3), channel_id=1, source_target_pairs={{0,448},{64,0},{128,64},{192,128},{256,192},{320,256},{384,320},{4... | collective-permute-start | bytes 786440 | tf_op jit(solution)/shard_map/ppermute | solution.py:267
  119.8 1.9 %collective-permute-start.20 = (bf16[2,512,128]{2,1,0:T(8,128)(2,1)S(1)}, bf16[2,512,128]{2,1,0:T(8,128)(2,1)S(1)}, u32[]{:S(2)}, u32[]{:S(2)}) collective-permute-start(bf16[2,512,128]{2,1,0:T(8,128)(2,1)S(1)} %pad_maximum_fusion.2), channel_id=1, source_target_pairs={{0,64},{64,128},{128,192},{192,256},{256,320},{320,384},{384,448},... | collective-permute-start | bytes 786440 | tf_op jit(solution)/shard_map/ppermute | solution.py:266
  121.8 3.0 %collective-permute-done.24 = bf16[2,512,128]{2,1,0:T(8,128)(2,1)S(1)} collective-permute-done((bf16[2,512,128]{2,1,0:T(8,128)(2,1)S(1)}, bf16[2,512,128]{2,1,0:T(8,128)(2,1)S(1)}, u32[]{:S(2)}, u32[]{:S(2)}) %collective-permute-start.24) | collective-permute-done | bytes 262176 | tf_op jit(solution)/shard_map/ppermute | solution.py:267
  124.9 5.6 %collective-permute-start.25 = (bf16[2,512,128]{2,1,0:T(8,128)(2,1)S(1)}, bf16[2,512,128]{2,1,0:T(8,128)(2,1)S(1)}, u32[]{:S(2)}, u32[]{:S(2)}) collective-permute-start(bf16[2,512,128]{2,1,0:T(8,128)(2,1)S(1)} %add_convert_fusion.1), channel_id=1, source_target_pairs={{0,448},{64,0},{128,64},{192,128},{256,192},{320,256},{384,320},{4... | collective-permute-start | bytes 786440 | tf_op jit(solution)/shard_map/ppermute | solution.py:267
  132.5 2.1 %collective-permute-done.25 = bf16[2,512,128]{2,1,0:T(8,128)(2,1)S(1)} collective-permute-done((bf16[2,512,128]{2,1,0:T(8,128)(2,1)S(1)}, bf16[2,512,128]{2,1,0:T(8,128)(2,1)S(1)}, u32[]{:S(2)}, u32[]{:S(2)}) %collective-permute-start.25) | collective-permute-done | bytes 262176 | tf_op jit(solution)/shard_map/ppermute | solution.py:267
  134.7 5.6 %collective-permute-start.26 = (bf16[2,512,128]{2,1,0:T(8,128)(2,1)S(1)}, bf16[2,512,128]{2,1,0:T(8,128)(2,1)S(1)}, u32[]{:S(2)}, u32[]{:S(2)}) collective-permute-start(bf16[2,512,128]{2,1,0:T(8,128)(2,1)S(1)} %add_convert_fusion), channel_id=1, source_target_pairs={{0,448},{64,0},{128,64},{192,128},{256,192},{320,256},{384,320},{4... | collective-permute-start | bytes 786440 | tf_op jit(solution)/shard_map/ppermute | solution.py:267
  144.1 5.7 %collective-permute-done.22.up_ref = bf16[2,512,128]{2,1,0:T(8,128)(2,1)S(1)} collective-permute-done((bf16[2,512,128]{2,1,0:T(8,128)(2,1)S(1)}, bf16[2,512,128]{2,1,0:T(8,128)(2,1)S(1)}, u32[]{:S(2)}, u32[]{:S(2)}) %collective-permute-start.22) | collective-permute-done | bytes 262176 | tf_op jit(solution)/shard_map/ppermute | solution.py:266
  149.9 14.0 %collective-permute-start.27 = (bf16[512,128]{1,0:T(8,128)(2,1)S(1)}, bf16[512,128]{1,0:T(8,128)(2,1)S(1)}, u32[]{:S(2)}, u32[]{:S(2)}) collective-permute-start(bf16[512,128]{1,0:T(8,128)(2,1)S(1)} %get-tuple-element.51), channel_id=1, source_target_pairs={{0,512},{512,0},{1,513},{513,1},{2,514},{514,2},{3,515},{515,3},{4... | collective-permute-start | bytes 393224 | tf_op jit(solution)/shard_map/ppermute | solution.py:275
  164.0 7.7 %collective-permute-done.27.other_ref = bf16[512,128]{1,0:T(8,128)(2,1)S(1)} collective-permute-done((bf16[512,128]{1,0:T(8,128)(2,1)S(1)}, bf16[512,128]{1,0:T(8,128)(2,1)S(1)}, u32[]{:S(2)}, u32[]{:S(2)}) %collective-permute-start.27) | collective-permute-done | bytes 131104 | tf_op jit(solution)/shard_map/ppermute | solution.py:275
  (55 shorter events, 21.7 us)
Async XLA Ops:
  0.6 13.4 %collective-permute-start = (bf16[8,4096]{1,0:T(8,128)(2,1)}, bf16[8,4096]{1,0:T(8,128)(2,1)S(1)}, u32[]{:S(2)}, u32[]{:S(2)}) collective-permute-start(bf16[8,4096]{1,0:T(8,128)(2,1)} %param.4), channel_id=1, source_target_pairs={{0,16},{4,20},{8,24},{12,28},{16,0},{20,4},{24,8},{28,12},{1,17},{... | collective-permute-start | bytes 196616 | tf_op jit(solution)/shard_map/ppermute | solution.py:169
  11.6 12.7 %collective-permute-start.9 = (bf16[8,4096]{1,0:T(8,128)(2,1)}, bf16[8,4096]{1,0:T(8,128)(2,1)S(1)}, u32[]{:S(2)}, u32[]{:S(2)}) collective-permute-start(bf16[8,4096]{1,0:T(8,128)(2,1)} %param.5), channel_id=1, source_target_pairs={{0,16},{4,20},{8,24},{12,28},{16,0},{20,4},{24,8},{28,12},{1,17},{... | collective-permute-start | bytes 196616 | tf_op jit(solution)/shard_map/ppermute | solution.py:169
  14.8 14.6 %collective-permute-start.1 = (bf16[16,4096]{1,0:T(8,128)(2,1)S(1)}, bf16[16,4096]{1,0:T(8,128)(2,1)S(1)}, u32[]{:S(2)}, u32[]{:S(2)}) collective-permute-start(bf16[16,4096]{1,0:T(8,128)(2,1)S(1)} %pad_maximum_fusion.4), channel_id=1, source_target_pairs={{0,8},{4,12},{8,0},{12,4},{16,24},{20,28},{24,16},{28,20},{1,9},{5... | collective-permute-start | bytes 393224 | tf_op jit(solution)/shard_map/ppermute | solution.py:169
  25.2 18.6 %collective-permute-start.10 = (bf16[16,4096]{1,0:T(8,128)(2,1)S(1)}, bf16[16,4096]{1,0:T(8,128)(2,1)S(1)}, u32[]{:S(2)}, u32[]{:S(2)}) collective-permute-start(bf16[16,4096]{1,0:T(8,128)(2,1)S(1)} %pad_maximum_fusion.5), channel_id=1, source_target_pairs={{0,8},{4,12},{8,0},{12,4},{16,24},{20,28},{24,16},{28,20},{1,9},{5... | collective-permute-start | bytes 393224 | tf_op jit(solution)/shard_map/ppermute | solution.py:169
  29.5 14.3 %collective-permute-start.4 = (bf16[32,4096]{1,0:T(8,128)(2,1)S(1)}, bf16[32,4096]{1,0:T(8,128)(2,1)S(1)}, u32[]{:S(2)}, u32[]{:S(2)}) collective-permute-start(bf16[32,4096]{1,0:T(8,128)(2,1)S(1)} %pad_maximum_fusion.refs_0_), channel_id=1, source_target_pairs={{0,4},{4,0},{8,12},{12,8},{16,20},{20,16},{24,28},{28,24},{1,5},{5... | collective-permute-start | bytes 786440 | tf_op jit(solution)/shard_map/ppermute | solution.py:180
  36.4 11.8 %collective-permute-start.3 = (bf16[32,4096]{1,0:T(8,128)(2,1)S(1)}, bf16[32,4096]{1,0:T(8,128)(2,1)S(1)}, u32[]{:S(2)}, u32[]{:S(2)}) collective-permute-start(bf16[32,4096]{1,0:T(8,128)(2,1)S(1)} %pad_maximum_fusion.refs_0_), channel_id=1, source_target_pairs={{0,3},{1,0},{2,1},{3,2},{4,7},{5,4},{6,5},{7,6},{8,11},{9,8},{10,9... | collective-permute-start | bytes 786440 | tf_op jit(solution)/shard_map/ppermute | solution.py:182
  39.1 11.4 %collective-permute-start.2 = (bf16[32,4096]{1,0:T(8,128)(2,1)S(1)}, bf16[32,4096]{1,0:T(8,128)(2,1)S(1)}, u32[]{:S(2)}, u32[]{:S(2)}) collective-permute-start(bf16[32,4096]{1,0:T(8,128)(2,1)S(1)} %pad_maximum_fusion.refs_0_), channel_id=1, source_target_pairs={{0,1},{1,2},{2,3},{3,0},{4,5},{5,6},{6,7},{7,4},{8,9},{9,10},{10,1... | collective-permute-start | bytes 786440 | tf_op jit(solution)/shard_map/ppermute | solution.py:181
  43.8 16.8 %collective-permute-start.5 = (bf16[32,4096]{1,0:T(8,128)(2,1)S(1)}, bf16[32,4096]{1,0:T(8,128)(2,1)S(1)}, u32[]{:S(2)}, u32[]{:S(2)}) collective-permute-start(bf16[32,4096]{1,0:T(8,128)(2,1)S(1)} %collective-permute-done.4.refs_3_), channel_id=1, source_target_pairs={{0,1},{1,2},{2,3},{3,0},{4,5},{5,6},{6,7},{7,4},{8,9},{9,10},{10,1... | collective-permute-start | bytes 786440 | tf_op jit(solution)/shard_map/ppermute | solution.py:184
  50.5 14.0 %collective-permute-start.6 = (bf16[32,4096]{1,0:T(8,128)(2,1)S(1)}, bf16[32,4096]{1,0:T(8,128)(2,1)}, u32[]{:S(2)}, u32[]{:S(2)}) collective-permute-start(bf16[32,4096]{1,0:T(8,128)(2,1)S(1)} %collective-permute-done.4.refs_3_), channel_id=1, source_target_pairs={{0,3},{1,0},{2,1},{3,2},{4,7},{5,4},{6,5},{7,6},{8,11},{9,8},{10,9... | collective-permute-start | bytes 786440 | tf_op jit(solution)/shard_map/ppermute | solution.py:183
  53.9 10.6 %collective-permute-start.13 = (bf16[32,4096]{1,0:T(8,128)(2,1)S(1)}, bf16[32,4096]{1,0:T(8,128)(2,1)S(1)}, u32[]{:S(2)}, u32[]{:S(2)}) collective-permute-start(bf16[32,4096]{1,0:T(8,128)(2,1)S(1)} %pad_maximum_fusion.1.refs_0_.refs_2_), channel_id=1, source_target_pairs={{0,4},{4,0},{8,12},{12,8},{16,20},{20,16},{24,28},{28,24},{1,5},{5... | collective-permute-start | bytes 786440 | tf_op jit(solution)/shard_map/ppermute | solution.py:187
  57.3 14.5 %collective-permute-start.7 = (bf16[32,4096]{1,0:T(8,128)(2,1)S(1)}, bf16[32,4096]{1,0:T(8,128)(2,1)S(1)}, u32[]{:S(2)}, u32[]{:S(2)}) collective-permute-start(bf16[32,4096]{1,0:T(8,128)(2,1)S(1)} %collective-permute-done.2.refs_1_), channel_id=1, source_target_pairs={{0,1},{1,2},{2,3},{3,0},{4,5},{5,6},{6,7},{7,4},{8,9},{9,10},{10,1... | collective-permute-start | bytes 786440 | tf_op jit(solution)/shard_map/ppermute | solution.py:185
  60.6 16.8 %collective-permute-start.11 = (bf16[32,4096]{1,0:T(8,128)(2,1)S(1)}, bf16[32,4096]{1,0:T(8,128)(2,1)S(1)}, u32[]{:S(2)}, u32[]{:S(2)}) collective-permute-start(bf16[32,4096]{1,0:T(8,128)(2,1)S(1)} %pad_maximum_fusion.1.refs_0_.refs_2_), channel_id=1, source_target_pairs={{0,1},{1,2},{2,3},{3,0},{4,5},{5,6},{6,7},{7,4},{8,9},{9,10},{10,1... | collective-permute-start | bytes 786440 | tf_op jit(solution)/shard_map/ppermute | solution.py:188
  64.6 15.6 %collective-permute-start.15 = (bf16[32,4096]{1,0:T(8,128)(2,1)S(1)}, bf16[32,4096]{1,0:T(8,128)(2,1)S(1)}, u32[]{:S(2)}, u32[]{:S(2)}) collective-permute-start(bf16[32,4096]{1,0:T(8,128)(2,1)S(1)} %collective-permute-done.13.refs_3_.refs_5_), channel_id=1, source_target_pairs={{0,3},{1,0},{2,1},{3,2},{4,7},{5,4},{6,5},{7,6},{8,11},{9,8},{10,9... | collective-permute-start | bytes 786440 | tf_op jit(solution)/shard_map/ppermute | solution.py:189
  66.5 16.9 %collective-permute-start.8 = (bf16[32,4096]{1,0:T(8,128)(2,1)}, bf16[32,4096]{1,0:T(8,128)(2,1)}, u32[]{:S(2)}, u32[]{:S(2)}) collective-permute-start(bf16[32,4096]{1,0:T(8,128)(2,1)} %collective-permute-done.6.refs_5_), channel_id=1, source_target_pairs={{0,3},{1,0},{2,1},{3,2},{4,7},{5,4},{6,5},{7,6},{8,11},{9,8},{10,9... | collective-permute-start | bytes 786440 | tf_op jit(solution)/shard_map/ppermute | solution.py:186
  69.7 24.3 %collective-permute-start.12 = (bf16[32,4096]{1,0:T(8,128)(2,1)S(1)}, bf16[32,4096]{1,0:T(8,128)(2,1)S(1)}, u32[]{:S(2)}, u32[]{:S(2)}) collective-permute-start(bf16[32,4096]{1,0:T(8,128)(2,1)S(1)} %pad_maximum_fusion.1.refs_0_.refs_2_), channel_id=1, source_target_pairs={{0,3},{1,0},{2,1},{3,2},{4,7},{5,4},{6,5},{7,6},{8,11},{9,8},{10,9... | collective-permute-start | bytes 786440 | tf_op jit(solution)/shard_map/ppermute | solution.py:190
  71.7 0.7 copy-start.2
  72.4 21.5 %collective-permute-start.14 = (bf16[32,4096]{1,0:T(8,128)(2,1)S(1)}, bf16[32,4096]{1,0:T(8,128)(2,1)S(1)}, u32[]{:S(2)}, u32[]{:S(2)}) collective-permute-start(bf16[32,4096]{1,0:T(8,128)(2,1)S(1)} %collective-permute-done.13.refs_3_.refs_5_), channel_id=1, source_target_pairs={{0,1},{1,2},{2,3},{3,0},{4,5},{5,6},{6,7},{7,4},{8,9},{9,10},{10,1... | collective-permute-start | bytes 786440 | tf_op jit(solution)/shard_map/ppermute | solution.py:191
  77.4 16.5 %collective-permute-start.16 = (bf16[32,4096]{1,0:T(8,128)(2,1)S(1)}, bf16[32,4096]{1,0:T(8,128)(2,1)S(1)}, u32[]{:S(2)}, u32[]{:S(2)}) collective-permute-start(bf16[32,4096]{1,0:T(8,128)(2,1)S(1)} %collective-permute-done.11.refs_1_.refs_3_), channel_id=1, source_target_pairs={{0,1},{1,2},{2,3},{3,0},{4,5},{5,6},{6,7},{7,4},{8,9},{9,10},{10,1... | collective-permute-start | bytes 786440 | tf_op jit(solution)/shard_map/ppermute | solution.py:192
  80.1 13.9 %collective-permute-start.17 = (bf16[32,4096]{1,0:T(8,128)(2,1)S(1)}, bf16[32,4096]{1,0:T(8,128)(2,1)S(1)}, u32[]{:S(2)}, u32[]{:S(2)}) collective-permute-start(bf16[32,4096]{1,0:T(8,128)(2,1)S(1)} %collective-permute-done.15.refs_5_.refs_7_), channel_id=1, source_target_pairs={{0,3},{1,0},{2,1},{3,2},{4,7},{5,4},{6,5},{7,6},{8,11},{9,8},{10,9... | collective-permute-start | bytes 786440 | tf_op jit(solution)/shard_map/ppermute | solution.py:193
  83.4 1.9 %copy-start = (bf16[4096,1,384]{2,0,1:T(8,128)(2,1)S(1)}, bf16[4096,1,384]{2,0,1:T(8,128)(2,1)}, u32[]{:S(2)}) copy-start(bf16[4096,1,384]{2,0,1:T(8,128)(2,1)} %param.6) | copy-start | bytes 9437188
  85.3 0.9 copy-start.3
  86.2 7.8 %copy-start.1 = (bf16[1,128,4096]{2,1,0:T(8,128)(2,1)S(1)}, bf16[1,128,4096]{2,1,0:T(8,128)(2,1)}, u32[]{:S(2)}) copy-start(bf16[1,128,4096]{2,1,0:T(8,128)(2,1)} %param.7) | copy-start | bytes 3145732
  98.4 6.1 %collective-permute-start.18 = (bf16[16,512,128]{2,1,0:T(8,128)(2,1)S(1)}, bf16[16,512,128]{2,1,0:T(8,128)(2,1)S(1)}, u32[]{:S(2)}, u32[]{:S(2)}) collective-permute-start(bf16[16,512,128]{2,1,0:T(8,128)(2,1)S(1)} %shard_map.61), channel_id=1, source_target_pairs={{0,32},{32,0},{1,33},{33,1},{2,34},{34,2},{3,35},{35,3},{4,36},{36... | collective-permute-start | bytes 6291464 | tf_op jit(solution)/shard_map/ppermute | solution.py:250
  106.0 8.1 %collective-permute-start.23 = (bf16[512,128]{1,0:T(8,128)(2,1)S(1)}, bf16[512,128]{1,0:T(8,128)(2,1)S(1)}, u32[]{:S(2)}, u32[]{:S(2)}) collective-permute-start(bf16[512,128]{1,0:T(8,128)(2,1)S(1)} %get-tuple-element.49), channel_id=1, source_target_pairs={{0,448},{64,0},{128,64},{192,128},{256,192},{320,256},{384,320},{4... | collective-permute-start | bytes 393224 | tf_op jit(solution)/shard_map/ppermute | solution.py:259
  111.0 8.7 %collective-permute-start.19 = (bf16[512,128]{1,0:T(8,128)(2,1)S(1)}, bf16[512,128]{1,0:T(8,128)(2,1)S(1)}, u32[]{:S(2)}, u32[]{:S(2)}) collective-permute-start(bf16[512,128]{1,0:T(8,128)(2,1)S(1)} %get-tuple-element.45), channel_id=1, source_target_pairs={{0,64},{64,128},{128,192},{192,256},{256,320},{320,384},{384,448},... | collective-permute-start | bytes 393224 | tf_op jit(solution)/shard_map/ppermute | solution.py:258
  114.1 10.6 %collective-permute-start.24 = (bf16[2,512,128]{2,1,0:T(8,128)(2,1)S(1)}, bf16[2,512,128]{2,1,0:T(8,128)(2,1)S(1)}, u32[]{:S(2)}, u32[]{:S(2)}) collective-permute-start(bf16[2,512,128]{2,1,0:T(8,128)(2,1)S(1)} %pad_maximum_fusion.3), channel_id=1, source_target_pairs={{0,448},{64,0},{128,64},{192,128},{256,192},{320,256},{384,320},{4... | collective-permute-start | bytes 786440 | tf_op jit(solution)/shard_map/ppermute | solution.py:267
  119.8 10.6 %collective-permute-start.20 = (bf16[2,512,128]{2,1,0:T(8,128)(2,1)S(1)}, bf16[2,512,128]{2,1,0:T(8,128)(2,1)S(1)}, u32[]{:S(2)}, u32[]{:S(2)}) collective-permute-start(bf16[2,512,128]{2,1,0:T(8,128)(2,1)S(1)} %pad_maximum_fusion.2), channel_id=1, source_target_pairs={{0,64},{64,128},{128,192},{192,256},{256,320},{320,384},{384,448},... | collective-permute-start | bytes 786440 | tf_op jit(solution)/shard_map/ppermute | solution.py:266
  124.9 9.7 %collective-permute-start.25 = (bf16[2,512,128]{2,1,0:T(8,128)(2,1)S(1)}, bf16[2,512,128]{2,1,0:T(8,128)(2,1)S(1)}, u32[]{:S(2)}, u32[]{:S(2)}) collective-permute-start(bf16[2,512,128]{2,1,0:T(8,128)(2,1)S(1)} %add_convert_fusion.1), channel_id=1, source_target_pairs={{0,448},{64,0},{128,64},{192,128},{256,192},{320,256},{384,320},{4... | collective-permute-start | bytes 786440 | tf_op jit(solution)/shard_map/ppermute | solution.py:267
  130.6 9.7 %collective-permute-start.21 = (bf16[2,512,128]{2,1,0:T(8,128)(2,1)S(1)}, bf16[2,512,128]{2,1,0:T(8,128)(2,1)S(1)}, u32[]{:S(2)}, u32[]{:S(2)}) collective-permute-start(bf16[2,512,128]{2,1,0:T(8,128)(2,1)S(1)} %add_convert_fusion.3), channel_id=1, source_target_pairs={{0,64},{64,128},{128,192},{192,256},{256,320},{320,384},{384,448},... | collective-permute-start | bytes 786440 | tf_op jit(solution)/shard_map/ppermute | solution.py:266
  134.7 9.5 %collective-permute-start.26 = (bf16[2,512,128]{2,1,0:T(8,128)(2,1)S(1)}, bf16[2,512,128]{2,1,0:T(8,128)(2,1)S(1)}, u32[]{:S(2)}, u32[]{:S(2)}) collective-permute-start(bf16[2,512,128]{2,1,0:T(8,128)(2,1)S(1)} %add_convert_fusion), channel_id=1, source_target_pairs={{0,448},{64,0},{128,64},{192,128},{256,192},{320,256},{384,320},{4... | collective-permute-start | bytes 786440 | tf_op jit(solution)/shard_map/ppermute | solution.py:267
  140.4 9.5 %collective-permute-start.22 = (bf16[2,512,128]{2,1,0:T(8,128)(2,1)S(1)}, bf16[2,512,128]{2,1,0:T(8,128)(2,1)S(1)}, u32[]{:S(2)}, u32[]{:S(2)}) collective-permute-start(bf16[2,512,128]{2,1,0:T(8,128)(2,1)S(1)} %add_convert_fusion.2), channel_id=1, source_target_pairs={{0,64},{64,128},{128,192},{192,256},{256,320},{320,384},{384,448},... | collective-permute-start | bytes 786440 | tf_op jit(solution)/shard_map/ppermute | solution.py:266
  149.9 21.7 %collective-permute-start.27 = (bf16[512,128]{1,0:T(8,128)(2,1)S(1)}, bf16[512,128]{1,0:T(8,128)(2,1)S(1)}, u32[]{:S(2)}, u32[]{:S(2)}) collective-permute-start(bf16[512,128]{1,0:T(8,128)(2,1)S(1)} %get-tuple-element.51), channel_id=1, source_target_pairs={{0,512},{512,0},{1,513},{513,1},{2,514},{514,2},{3,515},{515,3},{4... | collective-permute-start | bytes 393224 | tf_op jit(solution)/shard_map/ppermute | solution.py:275

commit v3 on v2

--- a/solution.py
+++ b/solution.py
@@ -17,6 +17,7 @@
 NN = (((1,), (0,)), ((), ()))
 VMEM = pl.BlockSpec(memory_space=pltpu.VMEM)
 SMEM = pl.BlockSpec(memory_space=pltpu.SMEM)
+ORDER = (4, 3, 1, -3, -1, 2, -2, 0)
 PARAMS = pltpu.CompilerParams(vmem_limit_bytes=16 * 1024 * 1024)
 
 
@@ -97,8 +98,7 @@
     core, here = place_ref[0], place_ref[1]
     d_all, att = d_ref[...], att_ref[...]
     split = d_all.shape[0]
-    order = distances(near)
-    for slot, distance in enumerate(order):
+    for slot, distance in enumerate(ORDER):
         y = lax.rem(here + distance + near, near)
         cols = [
             pl.ds(pl.multiple_of(((zh * near + y) * 2 + core) * width, width), width)
@@ -116,27 +116,36 @@
                 other = rest[0]
                 a = a + other[at, :split, :].astype(F32)
                 b = b + other[at, split:, :].astype(F32)
-                out = rest[1 + zh] if slot == 0 else rest[far + slot].at[zh]
+                first_up, first_down, near_up, near_down, mid_up, mid_down, own = rest[1:]
+                out = {
+                    4: (first_up, first_down)[zh],
+                    3: near_up.at[zh],
+                    1: near_up.at[far + zh],
+                    -3: near_down.at[zh],
+                    -1: near_down.at[far + zh],
+                    2: mid_up.at[zh],
+                    -2: mid_down.at[zh],
+                    0: own.at[zh],
+                }[distance]
             else:
                 out = rest[0].at[at]
             out[:split, :] = a.astype(BF16)
             out[split:, :] = b.astype(BF16)
 
 
-def distances(n):
-    order = [n // 2]
-    for d in range(n // 2 - 1, 0, -1):
-        order += [d, -d]
-    return order + [0]
-
-
-def last_kernel(zh_ref, own_ref, up_ref, down_ref, away_ref, kept_ref):
+def middle_kernel(own_ref, near_ref, first_ref, out_ref, *, half):
+    for zh in range(2):
+        total = own_ref[zh, :, :].astype(F32) + near_ref[zh, :, :].astype(F32)
+        if zh == half:
+            total = total + first_ref[...].astype(F32)
+        out_ref[zh, :, :] = total.astype(BF16)
+
+
+def last_kernel(zh_ref, own_ref, near_up_ref, near_down_ref, up_ref, down_ref, away_ref, kept_ref):
     def total(at):
-        return (
-            own_ref[at, :, :].astype(F32)
-            + up_ref[at, :, :].astype(F32)
-            + down_ref[at, :, :].astype(F32)
-        )
+        near = near_up_ref[2 + at, :, :].astype(F32) + near_down_ref[2 + at, :, :].astype(F32)
+        far = up_ref[at, :, :].astype(F32) + down_ref[at, :, :].astype(F32)
+        return own_ref[at, :, :].astype(F32) + near + far
 
     zh = zh_ref[0]
     away_ref[...] = total(1 - zh).astype(BF16)
@@ -165,36 +174,25 @@
 def gather(tokens, cotangent, n_z, n_x):
     up, down = turn(n_x, 1), turn(n_x, -1)
 
-    def join(rows, s, *done):
-        other = lax.ppermute(after(rows, *done), "zl", swap(n_z, s))
-        return lax.optimization_barrier(jnp.concatenate([rows, other], 0)), other
-
-    t, t_done = tokens, ()
-    c, c_done = cotangent, ()
-    s = n_z // 2
-    while s > 1:
-        t, other = join(t, s)
-        c, last = join(c, s, *t_done)
-        t_done = (other,)
-        s //= 2
-    tb = lax.ppermute(t, "zl", swap(n_z, 1))
-    ta_left = lax.ppermute(t, "x", up)
-    ta_right = lax.ppermute(t, "x", down)
-    tb_right = lax.ppermute(tb, "x", down)
-    tb_left = lax.ppermute(tb, "x", up)
-    ta_far = lax.ppermute(ta_left, "x", up)
-    tb_far = lax.ppermute(tb_right, "x", down)
-    cb = lax.ppermute(after(c, tb, ta_left, ta_right), "zl", swap(n_z, 1))
-    ca_left = lax.ppermute(after(c, ta_left, tb_left), "x", up)
-    cb_right = lax.ppermute(after(cb, tb_right, tb_left), "x", down)
-    ca_right = lax.ppermute(after(c, tb_right, tb_left), "x", down)
-    cb_left = lax.ppermute(cb, "x", up)
-    ca_far = lax.ppermute(ca_left, "x", up)
-    cb_far = lax.ppermute(cb_right, "x", down)
-    return (
-        [t, ta_left, ta_right, tb, tb_left, tb_right, ta_far, tb_far],
-        [c, ca_left, ca_right, cb, cb_left, cb_right, ca_far, cb_far],
-    )
+    def join(*rows):
+        return lax.optimization_barrier(jnp.concatenate(rows, 0))
+
+    def within(rows):
+        return [lax.ppermute(rows, "zl", swap(n_z, s)) for s in (2, 3, 1)]
+
+    t = join(tokens, lax.ppermute(tokens, "zl", swap(n_z, 4)))
+    c = join(cotangent, lax.ppermute(cotangent, "zl", swap(n_z, 4)))
+    t_near = within(t)
+    c_near = within(c)
+    t = join(t, *t_near)
+    c = join(c, *c_near)
+    t_left = lax.ppermute(t, "x", up)
+    t_right = lax.ppermute(t, "x", down)
+    t_far = lax.ppermute(t_left, "x", up)
+    c_right = lax.ppermute(after(c, t_left, t_right), "x", down)
+    c_left = lax.ppermute(after(c, t_left, t_right), "x", up)
+    c_far = lax.ppermute(c_right, "x", down)
+    return [t, t_left, t_right, t_far], [c, c_left, c_right, c_far]
 
 
 def local(sizes, tokens, cotangent, w_qkv, w_out):
@@ -232,6 +230,7 @@
     blocks = (far, near, model // (far * near * cores))
     one = jax.ShapeDtypeStruct((4 * width, blocks[2]), BF16)
     two = jax.ShapeDtypeStruct((far, 4 * width, blocks[2]), BF16)
+    four = jax.ShapeDtypeStruct((2 * far, 4 * width, blocks[2]), BF16)
     here = lax.axis_index("y").astype(jnp.int32)
     core = lax.axis_index("c").astype(jnp.int32)
 
@@ -248,30 +247,39 @@
 
     (mine,) = terms(1 - core, [jax.ShapeDtypeStruct((far * near, 4 * width, blocks[2]), BF16)])
     theirs = lax.ppermute(mine, "c", swap(cores, 1))
-    first_up, first_down, *parts = terms(core, [one, one] + [two] * (near - 1), theirs)
-    ups, downs, own = parts[0:-1:2], parts[1:-1:2], parts[-1]
-    up, down = turn(near, 1), turn(near, -1)
-
-    def add(a, b):
-        return (a.astype(F32) + b.astype(F32)).astype(BF16)
-
-    goes_up = lax.ppermute(first_up, "y", up)
-    goes_down = lax.ppermute(first_down, "y", down)
-    for step, (a, b) in enumerate(zip(ups, downs)):
-        if step == 0:
-            a = jnp.stack([add(a[0], goes_up), a[1]])
-            b = jnp.stack([b[0], add(b[1], goes_down)])
-        else:
-            a, b = add(a, goes_up), add(b, goes_down)
-        goes_up = lax.ppermute(a, "y", up)
-        goes_down = lax.ppermute(b, "y", down)
+    first_up, first_down, near_up, near_down, mid_up, mid_down, own = terms(
+        core, [one, one, four, four, two, two, two], theirs
+    )
+    first_up = lax.ppermute(first_up, "y", turn(near, 2))
+    near_up = lax.ppermute(near_up, "y", turn(near, 1))
+    first_down = lax.ppermute(first_down, "y", turn(near, -2))
+    near_down = lax.ppermute(near_down, "y", turn(near, -1))
+
+    def middle(half, *args):
+        return pl.pallas_call(
+            functools.partial(middle_kernel, half=half),
+            out_shape=two,
+            in_specs=[VMEM] * 3,
+            out_specs=VMEM,
+            compiler_params=PARAMS,
+        )(*args)
+
+    goes_up = lax.ppermute(middle(0, mid_up, near_up, first_up), "y", turn(near, 2))
+    goes_down = lax.ppermute(middle(1, mid_down, near_down, first_down), "y", turn(near, -2))
     away, kept = pl.pallas_call(
         last_kernel,
         out_shape=[one, jax.ShapeDtypeStruct(one.shape, F32)],
-        in_specs=[SMEM] + [VMEM] * 3,
+        in_specs=[SMEM] + [VMEM] * 5,
         out_specs=[VMEM] * 2,
         compiler_params=PARAMS,
-    )(lax.axis_index("zh").astype(jnp.int32).reshape(1), own, goes_up, goes_down)
+    )(
+        lax.axis_index("zh").astype(jnp.int32).reshape(1),
+        own,
+        near_up,
+        near_down,
+        goes_up,
+        goes_down,
+    )
     other = lax.ppermute(away, "zh", swap(far, 1))
     grad_qkv, grad_out = pl.pallas_call(
         finish_kernel,

time: 174 us -> 175 us (level)
  the two profiles are of different devices: /device:TPU:6 before, /device:TPU:56 now
where the time goes in v3:
time: 175 us; the launch traced here: 174 us
  starting transfers between devices  92.2 us (53%)
  waiting for transfers between devices  61.6 us (35%)
  Pallas kernels  14.8 us (8%)
  local copies, waits for them, and re-layouts  2.77 us (2%)
  other arithmetic  1.92 us (1%)
    ppermute x6, starting transfers between devices, within(): return [lax.ppermute(rows, 'zl', swap(n_z, s)) for s in (2, 3, 1)]  27.1 us
    ppermute x1, starting transfers between devices, local(): other = lax.ppermute(away, 'zh', swap(far, 1))  14.3 us
    ppermute x1, waiting for transfers between devices, local(): other = lax.ppermute(away, 'zh', swap(far, 1))  11 us
    ppermute x1, starting transfers between devices, gather(): t = join(tokens, lax.ppermute(tokens, 'zl', swap(n_z, 4)))  10.9 us
    ppermute x1, waiting for transfers between devices, local(): first_up = lax.ppermute(first_up, 'y', turn(near, 2))  9.67 us
    pallas_call x1, Pallas kernels, local(): pl.pallas_call(functools.partial(forward_kernel, rows=rows), out_shape=[j...  7.89 us
    ppermute x1, waiting for transfers between devices, local(): lax.ppermute(middle(0, mid_up, near_up, first_up), 'y', turn(near, 2))  6.78 us
    ppermute x1, waiting for transfers between devices, local(): lax.ppermute(middle(1, mid_down, near_down, first_down), 'y', turn(near,...  6.54 us
  transfers between devices with their start and end apart: 22, of which 11 were waited for; matrix products, arithmetic and copies ran while one was open for 1% of the time, Pallas kernels for 5%

profile of v3, /device:TPU:56, one launch (start us, length us, event | category | flops | bytes accessed | tf_op | source)
XLA Modules:
  0.0 174.2 jit_solution(12441564066420773181)
XLA Ops:
  0.6 10.9 %collective-permute-start = (bf16[8,4096]{1,0:T(8,128)(2,1)}, bf16[8,4096]{1,0:T(8,128)(2,1)S(1)}, u32[]{:S(2)}, u32[]{:S(2)}) collective-permute-start(bf16[8,4096]{1,0:T(8,128)(2,1)} %param.4), channel_id=1, source_target_pairs={{0,16},{4,20},{8,24},{12,28},{16,0},{20,4},{24,8},{28,12},{1,17},{... | collective-permute-start | bytes 196616 | tf_op jit(solution)/shard_map/ppermute | solution.py:183
  11.6 1.9 %collective-permute-start.7 = (bf16[8,4096]{1,0:T(8,128)(2,1)}, bf16[8,4096]{1,0:T(8,128)(2,1)S(1)}, u32[]{:S(2)}, u32[]{:S(2)}) collective-permute-start(bf16[8,4096]{1,0:T(8,128)(2,1)} %param.5), channel_id=1, source_target_pairs={{0,16},{4,20},{8,24},{12,28},{16,0},{20,4},{24,8},{28,12},{1,17},{... | collective-permute-start | bytes 196616 | tf_op jit(solution)/shard_map/ppermute | solution.py:184
  14.8 6.0 %collective-permute-start.3 = (bf16[16,4096]{1,0:T(8,128)(2,1)S(1)}, bf16[16,4096]{1,0:T(8,128)(2,1)S(1)}, u32[]{:S(2)}, u32[]{:S(2)}) collective-permute-start(bf16[16,4096]{1,0:T(8,128)(2,1)S(1)} %pad_maximum_fusion.2), channel_id=1, source_target_pairs={{0,4},{4,0},{8,12},{12,8},{16,20},{20,16},{24,28},{28,24},{1,5},{5... | collective-permute-start | bytes 393224 | tf_op jit(solution)/shard_map/ppermute | solution.py:181
  20.8 9.1 %collective-permute-start.2 = (bf16[16,4096]{1,0:T(8,128)(2,1)S(1)}, bf16[16,4096]{1,0:T(8,128)(2,1)S(1)}, u32[]{:S(2)}, u32[]{:S(2)}) collective-permute-start(bf16[16,4096]{1,0:T(8,128)(2,1)S(1)} %pad_maximum_fusion.2), channel_id=1, source_target_pairs={{0,12},{4,8},{8,4},{12,0},{16,28},{20,24},{24,20},{28,16},{1,13},{... | collective-permute-start | bytes 393224 | tf_op jit(solution)/shard_map/ppermute | solution.py:181
  29.9 2.5 %collective-permute-start.1 = (bf16[16,4096]{1,0:T(8,128)(2,1)S(1)}, bf16[16,4096]{1,0:T(8,128)(2,1)S(1)}, u32[]{:S(2)}, u32[]{:S(2)}) collective-permute-start(bf16[16,4096]{1,0:T(8,128)(2,1)S(1)} %pad_maximum_fusion.2), channel_id=1, source_target_pairs={{0,8},{4,12},{8,0},{12,4},{16,24},{20,28},{24,16},{28,20},{1,9},{5... | collective-permute-start | bytes 393224 | tf_op jit(solution)/shard_map/ppermute | solution.py:181
  33.2 2.5 %collective-permute-start.10 = (bf16[16,4096]{1,0:T(8,128)(2,1)S(1)}, bf16[16,4096]{1,0:T(8,128)(2,1)S(1)}, u32[]{:S(2)}, u32[]{:S(2)}) collective-permute-start(bf16[16,4096]{1,0:T(8,128)(2,1)S(1)} %pad_maximum_fusion.3), channel_id=1, source_target_pairs={{0,4},{4,0},{8,12},{12,8},{16,20},{20,16},{24,28},{28,24},{1,5},{5... | collective-permute-start | bytes 393224 | tf_op jit(solution)/shard_map/ppermute | solution.py:181
  35.7 5.2 %collective-permute-start.9 = (bf16[16,4096]{1,0:T(8,128)(2,1)S(1)}, bf16[16,4096]{1,0:T(8,128)(2,1)S(1)}, u32[]{:S(2)}, u32[]{:S(2)}) collective-permute-start(bf16[16,4096]{1,0:T(8,128)(2,1)S(1)} %pad_maximum_fusion.3), channel_id=1, source_target_pairs={{0,12},{4,8},{8,4},{12,0},{16,28},{20,24},{24,20},{28,16},{1,13},{... | collective-permute-start | bytes 393224 | tf_op jit(solution)/shard_map/ppermute | solution.py:181
  40.9 1.9 %collective-permute-start.8 = (bf16[16,4096]{1,0:T(8,128)(2,1)S(1)}, bf16[16,4096]{1,0:T(8,128)(2,1)S(1)}, u32[]{:S(2)}, u32[]{:S(2)}) collective-permute-start(bf16[16,4096]{1,0:T(8,128)(2,1)S(1)} %pad_maximum_fusion.3), channel_id=1, source_target_pairs={{0,8},{4,12},{8,0},{12,4},{16,24},{20,28},{24,16},{28,20},{1,9},{5... | collective-permute-start | bytes 393224 | tf_op jit(solution)/shard_map/ppermute | solution.py:181
  42.8 3.9 %collective-permute-done.1 = bf16[16,4096]{1,0:T(8,128)(2,1)S(1)} collective-permute-done((bf16[16,4096]{1,0:T(8,128)(2,1)S(1)}, bf16[16,4096]{1,0:T(8,128)(2,1)S(1)}, u32[]{:S(2)}, u32[]{:S(2)}) %collective-permute-start.1) | collective-permute-done | bytes 131104 | tf_op jit(solution)/shard_map/ppermute | solution.py:181
  46.8 4.7 %collective-permute-start.5 = (bf16[64,4096]{1,0:T(8,128)(2,1)S(1)}, bf16[64,4096]{1,0:T(8,128)(2,1)S(1)}, u32[]{:S(2)}, u32[]{:S(2)}) collective-permute-start(bf16[64,4096]{1,0:T(8,128)(2,1)S(1)} %pad_maximum_fusion.refs_0_), channel_id=1, source_target_pairs={{0,3},{1,0},{2,1},{3,2},{4,7},{5,4},{6,5},{7,6},{8,11},{9,8},{10,9... | collective-permute-start | bytes 1572872 | tf_op jit(solution)/shard_map/ppermute | solution.py:190
  51.5 1.9 %collective-permute-start.4 = (bf16[64,4096]{1,0:T(8,128)(2,1)S(1)}, bf16[64,4096]{1,0:T(8,128)(2,1)}, u32[]{:S(2)}, u32[]{:S(2)}) collective-permute-start(bf16[64,4096]{1,0:T(8,128)(2,1)S(1)} %pad_maximum_fusion.refs_0_), channel_id=1, source_target_pairs={{0,1},{1,2},{2,3},{3,0},{4,5},{5,6},{6,7},{7,4},{8,9},{9,10},{10,1... | collective-permute-start | bytes 1572872 | tf_op jit(solution)/shard_map/ppermute | solution.py:189
  53.5 4.7 %collective-permute-done.5.refs_2_ = bf16[64,4096]{1,0:T(8,128)(2,1)S(1)} collective-permute-done((bf16[64,4096]{1,0:T(8,128)(2,1)S(1)}, bf16[64,4096]{1,0:T(8,128)(2,1)S(1)}, u32[]{:S(2)}, u32[]{:S(2)}) %collective-permute-start.5) | collective-permute-done | bytes 524320 | tf_op jit(solution)/shard_map/ppermute | solution.py:190
  58.1 5.7 %collective-permute-done.4.refs_1_ = bf16[64,4096]{1,0:T(8,128)(2,1)} collective-permute-done((bf16[64,4096]{1,0:T(8,128)(2,1)S(1)}, bf16[64,4096]{1,0:T(8,128)(2,1)}, u32[]{:S(2)}, u32[]{:S(2)}) %collective-permute-start.4) | collective-permute-done | bytes 524320 | tf_op jit(solution)/shard_map/ppermute | solution.py:189
  65.8 3.9 %collective-permute-start.6 = (bf16[64,4096]{1,0:T(8,128)(2,1)}, bf16[64,4096]{1,0:T(8,128)(2,1)}, u32[]{:S(2)}, u32[]{:S(2)}) collective-permute-start(bf16[64,4096]{1,0:T(8,128)(2,1)} %collective-permute-done.4.refs_1_), channel_id=1, source_target_pairs={{0,1},{1,2},{2,3},{3,0},{4,5},{5,6},{6,7},{7,4},{8,9},{9,10},{10,1... | collective-permute-start | bytes 1572872 | tf_op jit(solution)/shard_map/ppermute | solution.py:191
  69.7 1.9 %collective-permute-start.11 = (bf16[64,4096]{1,0:T(8,128)(2,1)S(1)}, bf16[64,4096]{1,0:T(8,128)(2,1)S(1)}, u32[]{:S(2)}, u32[]{:S(2)}) collective-permute-start(bf16[64,4096]{1,0:T(8,128)(2,1)S(1)} %pad_maximum_fusion.1.refs_0_.refs_2_), channel_id=1, source_target_pairs={{0,1},{1,2},{2,3},{3,0},{4,5},{5,6},{6,7},{7,4},{8,9},{9,10},{10,1... | collective-permute-start | bytes 1572872 | tf_op jit(solution)/shard_map/ppermute | solution.py:193
  71.6 6.2 %collective-permute-done.12.refs_2_.refs_4_ = bf16[64,4096]{1,0:T(8,128)(2,1)S(1)} collective-permute-done((bf16[64,4096]{1,0:T(8,128)(2,1)S(1)}, bf16[64,4096]{1,0:T(8,128)(2,1)S(1)}, u32[]{:S(2)}, u32[]{:S(2)}) %collective-permute-start.12) | collective-permute-done | bytes 524320 | tf_op jit(solution)/shard_map/ppermute | solution.py:192
  79.8 2.5 %collective-permute-done.6.refs_3_ = bf16[64,4096]{1,0:T(8,128)(2,1)} collective-permute-done((bf16[64,4096]{1,0:T(8,128)(2,1)}, bf16[64,4096]{1,0:T(8,128)(2,1)}, u32[]{:S(2)}, u32[]{:S(2)}) %collective-permute-start.6) | collective-permute-done | bytes 524320 | tf_op jit(solution)/shard_map/ppermute | solution.py:191
  84.2 7.9 %shard_map.59 = (bf16[256,4096]{1,0:T(8,128)(2,1)S(1)}, bf16[128,256]{1,0:T(8,128)(2,1)S(1)}, f32[256,128]{1,0:T(8,128)S(1)}, f32[256,128]{1,0:T(8,128)S(1)}, f3...) custom-call(bf16[64,4096]{1,0:T(8,128)(2,1)S(1)} %pad_maximum_fusion.refs_0_, ...), custom_call_target="tpu_custom_call" | custom-call | tf_op jit(solution)/shard_map/pallas_call | solution.py:207
  92.1 2.9 %shard_map.60.refs_6_ = bf16[384,256]{1,0:T(8,128)(2,1)S(1)} custom-call(bf16[64,4096]{1,0:T(8,128)(2,1)S(1)} %pad_maximum_fusion.1.refs_0_.refs_2_, bf16[64,4096]{1,0:T(8,128)(2,1)S(1)} %collective-permute-done.11.refs_1_.refs_3_, bf16[64,4096]{1,0:T(8,128)(2,1)S(1)} %collective-permute-done.12.refs_2_.refs_4_, ...), custom_call_target="tpu_custom_call" | custom-call | tf_op jit(solution)/shard_map/pallas_call | solution.py:223
  96.5 1.9 %collective-permute-start.14 = (bf16[16,512,128]{2,1,0:T(8,128)(2,1)S(1)}, bf16[16,512,128]{2,1,0:T(8,128)(2,1)S(1)}, u32[]{:S(2)}, u32[]{:S(2)}) collective-permute-start(bf16[16,512,128]{2,1,0:T(8,128)(2,1)S(1)} %shard_map.61), channel_id=1, source_target_pairs={{0,32},{32,0},{1,33},{33,1},{2,34},{34,2},{3,35},{35,3},{4,36},{36... | collective-permute-start | bytes 6291464 | tf_op jit(solution)/shard_map/ppermute | solution.py:249
  98.5 4.0 %collective-permute-done.14.refs_8_ = bf16[16,512,128]{2,1,0:T(8,128)(2,1)S(1)} collective-permute-done((bf16[16,512,128]{2,1,0:T(8,128)(2,1)S(1)}, bf16[16,512,128]{2,1,0:T(8,128)(2,1)S(1)}, u32[]{:S(2)}, u32[]{:S(2)}) %collective-permute-start.14) | collective-permute-done | bytes 2097184 | tf_op jit(solution)/shard_map/ppermute | solution.py:249
  104.1 1.9 %collective-permute-start.15 = (bf16[4,512,128]{2,1,0:T(8,128)(2,1)S(1)}, bf16[4,512,128]{2,1,0:T(8,128)(2,1)S(1)}, u32[]{:S(2)}, u32[]{:S(2)}) collective-permute-start(bf16[4,512,128]{2,1,0:T(8,128)(2,1)S(1)} %get-tuple-element.32), channel_id=1, source_target_pairs={{0,64},{64,128},{128,192},{192,256},{256,320},{320,384},{384,448},... | collective-permute-start | bytes 1572872 | tf_op jit(solution)/shard_map/ppermute | solution.py:254
  106.0 3.9 %collective-permute-start.16 = (bf16[4,512,128]{2,1,0:T(8,128)(2,1)S(1)}, bf16[4,512,128]{2,1,0:T(8,128)(2,1)S(1)}, u32[]{:S(2)}, u32[]{:S(2)}) collective-permute-start(bf16[4,512,128]{2,1,0:T(8,128)(2,1)S(1)} %get-tuple-element.33), channel_id=1, source_target_pairs={{0,448},{64,0},{128,64},{192,128},{256,192},{320,256},{384,320},{4... | collective-permute-start | bytes 1572872 | tf_op jit(solution)/shard_map/ppermute | solution.py:256
  109.9 2.7 %collective-permute-start.17 = (bf16[512,128]{1,0:T(8,128)(2,1)S(1)}, bf16[512,128]{1,0:T(8,128)(2,1)S(1)}, u32[]{:S(2)}, u32[]{:S(2)}) collective-permute-start(bf16[512,128]{1,0:T(8,128)(2,1)S(1)} %get-tuple-element.35), channel_id=1, source_target_pairs={{0,128},{64,192},{128,256},{192,320},{256,384},{320,448},{384,0},{... | collective-permute-start | bytes 393224 | tf_op jit(solution)/shard_map/ppermute | solution.py:253
  112.6 4.0 %collective-permute-start.19 = (bf16[512,128]{1,0:T(8,128)(2,1)S(1)}, bf16[512,128]{1,0:T(8,128)(2,1)S(1)}, u32[]{:S(2)}, u32[]{:S(2)}) collective-permute-start(bf16[512,128]{1,0:T(8,128)(2,1)S(1)} %get-tuple-element.37), channel_id=1, source_target_pairs={{0,384},{64,448},{128,0},{192,64},{256,128},{320,192},{384,256},{4... | collective-permute-start | bytes 393224 | tf_op jit(solution)/shard_map/ppermute | solution.py:255
  116.7 9.7 %collective-permute-done.17.first_ref = bf16[512,128]{1,0:T(8,128)(2,1)S(1)} collective-permute-done((bf16[512,128]{1,0:T(8,128)(2,1)S(1)}, bf16[512,128]{1,0:T(8,128)(2,1)S(1)}, u32[]{:S(2)}, u32[]{:S(2)}) %collective-permute-start.17) | collective-permute-done | bytes 131104 | tf_op jit(solution)/shard_map/ppermute | solution.py:253
  126.5 3.5 %collective-permute-start.18 = (bf16[2,512,128]{2,1,0:T(8,128)(2,1)S(1)}, bf16[2,512,128]{2,1,0:T(8,128)(2,1)S(1)}, u32[]{:S(2)}, u32[]{:S(2)}) collective-permute-start(bf16[2,512,128]{2,1,0:T(8,128)(2,1)S(1)} %shard_map.63), channel_id=1, source_target_pairs={{0,128},{64,192},{128,256},{192,320},{256,384},{320,448},{384,0},{... | collective-permute-start | bytes 786440 | tf_op jit(solution)/shard_map/ppermute | solution.py:267
  130.1 3.6 %collective-permute-start.20 = (bf16[2,512,128]{2,1,0:T(8,128)(2,1)S(1)}, bf16[2,512,128]{2,1,0:T(8,128)(2,1)S(1)}, u32[]{:S(2)}, u32[]{:S(2)}) collective-permute-start(bf16[2,512,128]{2,1,0:T(8,128)(2,1)S(1)} %shard_map.64), channel_id=1, source_target_pairs={{0,384},{64,448},{128,0},{192,64},{256,128},{320,192},{384,256},{4... | collective-permute-start | bytes 786440 | tf_op jit(solution)/shard_map/ppermute | solution.py:268
  133.8 6.8 %collective-permute-done.18.up_ref = bf16[2,512,128]{2,1,0:T(8,128)(2,1)S(1)} collective-permute-done((bf16[2,512,128]{2,1,0:T(8,128)(2,1)S(1)}, bf16[2,512,128]{2,1,0:T(8,128)(2,1)S(1)}, u32[]{:S(2)}, u32[]{:S(2)}) %collective-permute-start.18) | collective-permute-done | bytes 262176 | tf_op jit(solution)/shard_map/ppermute | solution.py:267
  140.5 6.5 %collective-permute-done.20.down_ref = bf16[2,512,128]{2,1,0:T(8,128)(2,1)S(1)} collective-permute-done((bf16[2,512,128]{2,1,0:T(8,128)(2,1)S(1)}, bf16[2,512,128]{2,1,0:T(8,128)(2,1)S(1)}, u32[]{:S(2)}, u32[]{:S(2)}) %collective-permute-start.20) | collective-permute-done | bytes 262176 | tf_op jit(solution)/shard_map/ppermute | solution.py:268
  147.2 14.3 %collective-permute-start.21 = (bf16[512,128]{1,0:T(8,128)(2,1)S(1)}, bf16[512,128]{1,0:T(8,128)(2,1)S(1)}, u32[]{:S(2)}, u32[]{:S(2)}) collective-permute-start(bf16[512,128]{1,0:T(8,128)(2,1)S(1)} %get-tuple-element.39), channel_id=1, source_target_pairs={{0,512},{512,0},{1,513},{513,1},{2,514},{514,2},{3,515},{515,3},{4... | collective-permute-start | bytes 393224 | tf_op jit(solution)/shard_map/ppermute | solution.py:283
  161.6 11.0 %collective-permute-done.21.other_ref = bf16[512,128]{1,0:T(8,128)(2,1)S(1)} collective-permute-done((bf16[512,128]{1,0:T(8,128)(2,1)S(1)}, bf16[512,128]{1,0:T(8,128)(2,1)S(1)}, u32[]{:S(2)}, u32[]{:S(2)}) %collective-permute-start.21) | collective-permute-done | bytes 131104 | tf_op jit(solution)/shard_map/ppermute | solution.py:283
  (31 shorter events, 13.0 us)
Async XLA Ops:
  0.6 13.4 %collective-permute-start = (bf16[8,4096]{1,0:T(8,128)(2,1)}, bf16[8,4096]{1,0:T(8,128)(2,1)S(1)}, u32[]{:S(2)}, u32[]{:S(2)}) collective-permute-start(bf16[8,4096]{1,0:T(8,128)(2,1)} %param.4), channel_id=1, source_target_pairs={{0,16},{4,20},{8,24},{12,28},{16,0},{20,4},{24,8},{28,12},{1,17},{... | collective-permute-start | bytes 196616 | tf_op jit(solution)/shard_map/ppermute | solution.py:183
  11.6 20.8 %collective-permute-start.7 = (bf16[8,4096]{1,0:T(8,128)(2,1)}, bf16[8,4096]{1,0:T(8,128)(2,1)S(1)}, u32[]{:S(2)}, u32[]{:S(2)}) collective-permute-start(bf16[8,4096]{1,0:T(8,128)(2,1)} %param.5), channel_id=1, source_target_pairs={{0,16},{4,20},{8,24},{12,28},{16,0},{20,4},{24,8},{28,12},{1,17},{... | collective-permute-start | bytes 196616 | tf_op jit(solution)/shard_map/ppermute | solution.py:184
  14.8 26.0 %collective-permute-start.3 = (bf16[16,4096]{1,0:T(8,128)(2,1)S(1)}, bf16[16,4096]{1,0:T(8,128)(2,1)S(1)}, u32[]{:S(2)}, u32[]{:S(2)}) collective-permute-start(bf16[16,4096]{1,0:T(8,128)(2,1)S(1)} %pad_maximum_fusion.2), channel_id=1, source_target_pairs={{0,4},{4,0},{8,12},{12,8},{16,20},{20,16},{24,28},{28,24},{1,5},{5... | collective-permute-start | bytes 393224 | tf_op jit(solution)/shard_map/ppermute | solution.py:181
  20.8 22.0 %collective-permute-start.2 = (bf16[16,4096]{1,0:T(8,128)(2,1)S(1)}, bf16[16,4096]{1,0:T(8,128)(2,1)S(1)}, u32[]{:S(2)}, u32[]{:S(2)}) collective-permute-start(bf16[16,4096]{1,0:T(8,128)(2,1)S(1)} %pad_maximum_fusion.2), channel_id=1, source_target_pairs={{0,12},{4,8},{8,4},{12,0},{16,28},{20,24},{24,20},{28,16},{1,13},{... | collective-permute-start | bytes 393224 | tf_op jit(solution)/shard_map/ppermute | solution.py:181
  29.9 16.9 %collective-permute-start.1 = (bf16[16,4096]{1,0:T(8,128)(2,1)S(1)}, bf16[16,4096]{1,0:T(8,128)(2,1)S(1)}, u32[]{:S(2)}, u32[]{:S(2)}) collective-permute-start(bf16[16,4096]{1,0:T(8,128)(2,1)S(1)} %pad_maximum_fusion.2), channel_id=1, source_target_pairs={{0,8},{4,12},{8,0},{12,4},{16,24},{20,28},{24,16},{28,20},{1,9},{5... | collective-permute-start | bytes 393224 | tf_op jit(solution)/shard_map/ppermute | solution.py:181
  33.2 20.2 %collective-permute-start.10 = (bf16[16,4096]{1,0:T(8,128)(2,1)S(1)}, bf16[16,4096]{1,0:T(8,128)(2,1)S(1)}, u32[]{:S(2)}, u32[]{:S(2)}) collective-permute-start(bf16[16,4096]{1,0:T(8,128)(2,1)S(1)} %pad_maximum_fusion.3), channel_id=1, source_target_pairs={{0,4},{4,0},{8,12},{12,8},{16,20},{20,16},{24,28},{28,24},{1,5},{5... | collective-permute-start | bytes 393224 | tf_op jit(solution)/shard_map/ppermute | solution.py:181
  35.7 17.7 %collective-permute-start.9 = (bf16[16,4096]{1,0:T(8,128)(2,1)S(1)}, bf16[16,4096]{1,0:T(8,128)(2,1)S(1)}, u32[]{:S(2)}, u32[]{:S(2)}) collective-permute-start(bf16[16,4096]{1,0:T(8,128)(2,1)S(1)} %pad_maximum_fusion.3), channel_id=1, source_target_pairs={{0,12},{4,8},{8,4},{12,0},{16,28},{20,24},{24,20},{28,16},{1,13},{... | collective-permute-start | bytes 393224 | tf_op jit(solution)/shard_map/ppermute | solution.py:181
  40.9 12.5 %collective-permute-start.8 = (bf16[16,4096]{1,0:T(8,128)(2,1)S(1)}, bf16[16,4096]{1,0:T(8,128)(2,1)S(1)}, u32[]{:S(2)}, u32[]{:S(2)}) collective-permute-start(bf16[16,4096]{1,0:T(8,128)(2,1)S(1)} %pad_maximum_fusion.3), channel_id=1, source_target_pairs={{0,8},{4,12},{8,0},{12,4},{16,24},{20,28},{24,16},{28,20},{1,9},{5... | collective-permute-start | bytes 393224 | tf_op jit(solution)/shard_map/ppermute | solution.py:181
  46.8 11.4 %collective-permute-start.5 = (bf16[64,4096]{1,0:T(8,128)(2,1)S(1)}, bf16[64,4096]{1,0:T(8,128)(2,1)S(1)}, u32[]{:S(2)}, u32[]{:S(2)}) collective-permute-start(bf16[64,4096]{1,0:T(8,128)(2,1)S(1)} %pad_maximum_fusion.refs_0_), channel_id=1, source_target_pairs={{0,3},{1,0},{2,1},{3,2},{4,7},{5,4},{6,5},{7,6},{8,11},{9,8},{10,9... | collective-permute-start | bytes 1572872 | tf_op jit(solution)/shard_map/ppermute | solution.py:190
  51.5 12.4 %collective-permute-start.4 = (bf16[64,4096]{1,0:T(8,128)(2,1)S(1)}, bf16[64,4096]{1,0:T(8,128)(2,1)}, u32[]{:S(2)}, u32[]{:S(2)}) collective-permute-start(bf16[64,4096]{1,0:T(8,128)(2,1)S(1)} %pad_maximum_fusion.refs_0_), channel_id=1, source_target_pairs={{0,1},{1,2},{2,3},{3,0},{4,5},{5,6},{6,7},{7,4},{8,9},{9,10},{10,1... | collective-permute-start | bytes 1572872 | tf_op jit(solution)/shard_map/ppermute | solution.py:189
  63.8 14.0 %collective-permute-start.12 = (bf16[64,4096]{1,0:T(8,128)(2,1)S(1)}, bf16[64,4096]{1,0:T(8,128)(2,1)S(1)}, u32[]{:S(2)}, u32[]{:S(2)}) collective-permute-start(bf16[64,4096]{1,0:T(8,128)(2,1)S(1)} %pad_maximum_fusion.1.refs_0_.refs_2_), channel_id=1, source_target_pairs={{0,3},{1,0},{2,1},{3,2},{4,7},{5,4},{6,5},{7,6},{8,11},{9,8},{10,9... | collective-permute-start | bytes 1572872 | tf_op jit(solution)/shard_map/ppermute | solution.py:192
  65.8 16.5 %collective-permute-start.6 = (bf16[64,4096]{1,0:T(8,128)(2,1)}, bf16[64,4096]{1,0:T(8,128)(2,1)}, u32[]{:S(2)}, u32[]{:S(2)}) collective-permute-start(bf16[64,4096]{1,0:T(8,128)(2,1)} %collective-permute-done.4.refs_1_), channel_id=1, source_target_pairs={{0,1},{1,2},{2,3},{3,0},{4,5},{5,6},{6,7},{7,4},{8,9},{9,10},{10,1... | collective-permute-start | bytes 1572872 | tf_op jit(solution)/shard_map/ppermute | solution.py:191
  69.7 22.4 %collective-permute-start.11 = (bf16[64,4096]{1,0:T(8,128)(2,1)S(1)}, bf16[64,4096]{1,0:T(8,128)(2,1)S(1)}, u32[]{:S(2)}, u32[]{:S(2)}) collective-permute-start(bf16[64,4096]{1,0:T(8,128)(2,1)S(1)} %pad_maximum_fusion.1.refs_0_.refs_2_), channel_id=1, source_target_pairs={{0,1},{1,2},{2,3},{3,0},{4,5},{5,6},{6,7},{7,4},{8,9},{9,10},{10,1... | collective-permute-start | bytes 1572872 | tf_op jit(solution)/shard_map/ppermute | solution.py:193
  77.8 14.3 %collective-permute-start.13 = (bf16[64,4096]{1,0:T(8,128)(2,1)S(1)}, bf16[64,4096]{1,0:T(8,128)(2,1)S(1)}, u32[]{:S(2)}, u32[]{:S(2)}) collective-permute-start(bf16[64,4096]{1,0:T(8,128)(2,1)S(1)} %collective-permute-done.12.refs_2_.refs_4_), channel_id=1, source_target_pairs={{0,3},{1,0},{2,1},{3,2},{4,7},{5,4},{6,5},{7,6},{8,11},{9,8},{10,9... | collective-permute-start | bytes 1572872 | tf_op jit(solution)/shard_map/ppermute | solution.py:194
  82.3 1.9 %copy-start = (bf16[4096,1,384]{2,0,1:T(8,128)(2,1)S(1)}, bf16[4096,1,384]{2,0,1:T(8,128)(2,1)}, u32[]{:S(2)}) copy-start(bf16[4096,1,384]{2,0,1:T(8,128)(2,1)} %param.6) | copy-start | bytes 9437188
  84.2 7.9 %copy-start.1 = (bf16[1,128,4096]{2,1,0:T(8,128)(2,1)S(1)}, bf16[1,128,4096]{2,1,0:T(8,128)(2,1)}, u32[]{:S(2)}) copy-start(bf16[1,128,4096]{2,1,0:T(8,128)(2,1)} %param.7) | copy-start | bytes 3145732
  96.5 6.1 %collective-permute-start.14 = (bf16[16,512,128]{2,1,0:T(8,128)(2,1)S(1)}, bf16[16,512,128]{2,1,0:T(8,128)(2,1)S(1)}, u32[]{:S(2)}, u32[]{:S(2)}) collective-permute-start(bf16[16,512,128]{2,1,0:T(8,128)(2,1)S(1)} %shard_map.61), channel_id=1, source_target_pairs={{0,32},{32,0},{1,33},{33,1},{2,34},{34,2},{3,35},{35,3},{4,36},{36... | collective-permute-start | bytes 6291464 | tf_op jit(solution)/shard_map/ppermute | solution.py:249
  104.1 22.3 %collective-permute-start.15 = (bf16[4,512,128]{2,1,0:T(8,128)(2,1)S(1)}, bf16[4,512,128]{2,1,0:T(8,128)(2,1)S(1)}, u32[]{:S(2)}, u32[]{:S(2)}) collective-permute-start(bf16[4,512,128]{2,1,0:T(8,128)(2,1)S(1)} %get-tuple-element.32), channel_id=1, source_target_pairs={{0,64},{64,128},{128,192},{192,256},{256,320},{320,384},{384,448},... | collective-permute-start | bytes 1572872 | tf_op jit(solution)/shard_map/ppermute | solution.py:254
  106.0 24.0 %collective-permute-start.16 = (bf16[4,512,128]{2,1,0:T(8,128)(2,1)S(1)}, bf16[4,512,128]{2,1,0:T(8,128)(2,1)S(1)}, u32[]{:S(2)}, u32[]{:S(2)}) collective-permute-start(bf16[4,512,128]{2,1,0:T(8,128)(2,1)S(1)} %get-tuple-element.33), channel_id=1, source_target_pairs={{0,448},{64,0},{128,64},{192,128},{256,192},{320,256},{384,320},{4... | collective-permute-start | bytes 1572872 | tf_op jit(solution)/shard_map/ppermute | solution.py:256
  109.9 16.4 %collective-permute-start.17 = (bf16[512,128]{1,0:T(8,128)(2,1)S(1)}, bf16[512,128]{1,0:T(8,128)(2,1)S(1)}, u32[]{:S(2)}, u32[]{:S(2)}) collective-permute-start(bf16[512,128]{1,0:T(8,128)(2,1)S(1)} %get-tuple-element.35), channel_id=1, source_target_pairs={{0,128},{64,192},{128,256},{192,320},{256,384},{320,448},{384,0},{... | collective-permute-start | bytes 393224 | tf_op jit(solution)/shard_map/ppermute | solution.py:253
  112.6 17.3 %collective-permute-start.19 = (bf16[512,128]{1,0:T(8,128)(2,1)S(1)}, bf16[512,128]{1,0:T(8,128)(2,1)S(1)}, u32[]{:S(2)}, u32[]{:S(2)}) collective-permute-start(bf16[512,128]{1,0:T(8,128)(2,1)S(1)} %get-tuple-element.37), channel_id=1, source_target_pairs={{0,384},{64,448},{128,0},{192,64},{256,128},{320,192},{384,256},{4... | collective-permute-start | bytes 393224 | tf_op jit(solution)/shard_map/ppermute | solution.py:255
  126.5 14.1 %collective-permute-start.18 = (bf16[2,512,128]{2,1,0:T(8,128)(2,1)S(1)}, bf16[2,512,128]{2,1,0:T(8,128)(2,1)S(1)}, u32[]{:S(2)}, u32[]{:S(2)}) collective-permute-start(bf16[2,512,128]{2,1,0:T(8,128)(2,1)S(1)} %shard_map.63), channel_id=1, source_target_pairs={{0,128},{64,192},{128,256},{192,320},{256,384},{320,448},{384,0},{... | collective-permute-start | bytes 786440 | tf_op jit(solution)/shard_map/ppermute | solution.py:267
  130.1 17.0 %collective-permute-start.20 = (bf16[2,512,128]{2,1,0:T(8,128)(2,1)S(1)}, bf16[2,512,128]{2,1,0:T(8,128)(2,1)S(1)}, u32[]{:S(2)}, u32[]{:S(2)}) collective-permute-start(bf16[2,512,128]{2,1,0:T(8,128)(2,1)S(1)} %shard_map.64), channel_id=1, source_target_pairs={{0,384},{64,448},{128,0},{192,64},{256,128},{320,192},{384,256},{4... | collective-permute-start | bytes 786440 | tf_op jit(solution)/shard_map/ppermute | solution.py:268
  147.2 25.4 %collective-permute-start.21 = (bf16[512,128]{1,0:T(8,128)(2,1)S(1)}, bf16[512,128]{1,0:T(8,128)(2,1)S(1)}, u32[]{:S(2)}, u32[]{:S(2)}) collective-permute-start(bf16[512,128]{1,0:T(8,128)(2,1)S(1)} %get-tuple-element.39), channel_id=1, source_target_pairs={{0,512},{512,0},{1,513},{513,1},{2,514},{514,2},{3,515},{515,3},{4... | collective-permute-start | bytes 393224 | tf_op jit(solution)/shard_map/ppermute | solution.py:283

commit v4 on v3

--- a/solution.py
+++ b/solution.py
@@ -17,7 +17,7 @@
 NN = (((1,), (0,)), ((), ()))
 VMEM = pl.BlockSpec(memory_space=pltpu.VMEM)
 SMEM = pl.BlockSpec(memory_space=pltpu.SMEM)
-ORDER = (4, 3, 1, -3, -1, 2, -2, 0)
+FIRST, SECOND = (4, 3, -3), (2, -2, 1, -1, 0)
 PARAMS = pltpu.CompilerParams(vmem_limit_bytes=16 * 1024 * 1024)
 
 
@@ -36,24 +36,31 @@
     return lax.dot_general(a, b, dims, precision=HIGHEST, preferred_element_type=F32)
 
 
+def normalize_rows(piece, normed_ref, at, count):
+    step = 16
+
+    def body(i, carry):
+        x = piece[pl.ds(pl.multiple_of(i * step, step), step), :].astype(F32)
+        centred = x - jnp.mean(x, -1, keepdims=True)
+        spread = lax.rsqrt(jnp.mean(centred * centred, -1, keepdims=True) + EPS)
+        rows = pl.ds(pl.multiple_of(at + i * step, step), step)
+        normed_ref[rows, :] = (centred * spread).astype(BF16)
+        return carry
+
+    lax.fori_loop(0, count // step, body, 0)
+
+
+def own_kernel(rows_ref, normed_ref):
+    normalize_rows(rows_ref, normed_ref, 0, rows_ref.shape[0])
+
+
 def forward_kernel(*refs, rows):
-    pieces = refs[: len(rows)]
+    own_ref, *pieces = refs[: len(rows)]
     w_ref, normed_ref, att_ref, q_ref, k_ref, v_ref, prob_ref, sq_ref, sk_ref = refs[len(rows) :]
-    step = 16
-    at = 0
-    for piece, count in zip(pieces, rows):
-
-        def body(i, carry, piece=piece, at=at):
-            part = pl.ds(pl.multiple_of(i * step, step), step)
-            x = piece[part, :].astype(F32)
-            centred = x - jnp.mean(x, -1, keepdims=True)
-            spread = lax.rsqrt(jnp.mean(centred * centred, -1, keepdims=True) + EPS)
-            normed_ref[pl.ds(pl.multiple_of(at + i * step, step), step), :] = (
-                centred * spread
-            ).astype(BF16)
-            return carry
-
-        lax.fori_loop(0, count // step, body, 0)
+    at = rows[0]
+    normed_ref[:at, :] = own_ref[...]
+    for piece, count in zip(pieces, rows[1:]):
+        normalize_rows(piece, normed_ref, at, count)
         at += count
     width = w_ref.shape[1] // 3
     qkv = jnp.dot(normed_ref[...], w_ref[...], preferred_element_type=F32)
@@ -89,7 +96,7 @@
     out_ref[2 * width :, :] = d_value.T.astype(BF16)
 
 
-def terms_kernel(*refs, count, blocks, slots):
+def terms_kernel(*refs, count, blocks, order, adds):
     place_ref, normed_ref = refs[:2]
     pieces = refs[2 : 2 + count]
     d_ref, att_ref = refs[2 + count : 4 + count]
@@ -98,7 +105,18 @@
     core, here = place_ref[0], place_ref[1]
     d_all, att = d_ref[...], att_ref[...]
     split = d_all.shape[0]
-    for slot, distance in enumerate(ORDER):
+    if adds:
+        other, outs = rest[0], []
+        rest = list(rest[1:])
+        for distance in order:
+            if distance == near // 2:
+                outs.append([rest.pop(0), rest.pop(0)])
+            else:
+                block = rest.pop(0)
+                outs.append([block.at[zh] for zh in range(far)])
+    else:
+        outs = [[rest[0].at[slot * far + zh] for zh in range(far)] for slot in range(len(order))]
+    for slot, distance in enumerate(order):
         y = lax.rem(here + distance + near, near)
         cols = [
             pl.ds(pl.multiple_of(((zh * near + y) * 2 + core) * width, width), width)
@@ -111,41 +129,27 @@
         for zh in range(far):
             a = top[:, zh * width : (zh + 1) * width]
             b = low[:, zh * width : (zh + 1) * width]
-            at = slot * far + zh
-            if slots:
-                other = rest[0]
-                a = a + other[at, :split, :].astype(F32)
-                b = b + other[at, split:, :].astype(F32)
-                first_up, first_down, near_up, near_down, mid_up, mid_down, own = rest[1:]
-                out = {
-                    4: (first_up, first_down)[zh],
-                    3: near_up.at[zh],
-                    1: near_up.at[far + zh],
-                    -3: near_down.at[zh],
-                    -1: near_down.at[far + zh],
-                    2: mid_up.at[zh],
-                    -2: mid_down.at[zh],
-                    0: own.at[zh],
-                }[distance]
-            else:
-                out = rest[0].at[at]
-            out[:split, :] = a.astype(BF16)
-            out[split:, :] = b.astype(BF16)
-
-
-def middle_kernel(own_ref, near_ref, first_ref, out_ref, *, half):
+            if adds:
+                a = a + other[slot * far + zh, :split, :].astype(F32)
+                b = b + other[slot * far + zh, split:, :].astype(F32)
+            outs[slot][zh][:split, :] = a.astype(BF16)
+            outs[slot][zh][split:, :] = b.astype(BF16)
+
+
+def hop_kernel(own_ref, came_ref, out_ref, *, half):
     for zh in range(2):
-        total = own_ref[zh, :, :].astype(F32) + near_ref[zh, :, :].astype(F32)
-        if zh == half:
-            total = total + first_ref[...].astype(F32)
+        total = own_ref[zh, :, :].astype(F32)
+        if half is None:
+            total = total + came_ref[zh, :, :].astype(F32)
+        elif zh == half:
+            total = total + came_ref[...].astype(F32)
         out_ref[zh, :, :] = total.astype(BF16)
 
 
-def last_kernel(zh_ref, own_ref, near_up_ref, near_down_ref, up_ref, down_ref, away_ref, kept_ref):
+def last_kernel(zh_ref, own_ref, up_ref, down_ref, away_ref, kept_ref):
     def total(at):
-        near = near_up_ref[2 + at, :, :].astype(F32) + near_down_ref[2 + at, :, :].astype(F32)
-        far = up_ref[at, :, :].astype(F32) + down_ref[at, :, :].astype(F32)
-        return own_ref[at, :, :].astype(F32) + near + far
+        came = up_ref[at, :, :].astype(F32) + down_ref[at, :, :].astype(F32)
+        return own_ref[at, :, :].astype(F32) + came
 
     zh = zh_ref[0]
     away_ref[...] = total(1 - zh).astype(BF16)
@@ -180,19 +184,27 @@
     def within(rows):
         return [lax.ppermute(rows, "zl", swap(n_z, s)) for s in (2, 3, 1)]
 
-    t = join(tokens, lax.ppermute(tokens, "zl", swap(n_z, 4)))
-    c = join(cotangent, lax.ppermute(cotangent, "zl", swap(n_z, 4)))
+    t_other = lax.ppermute(tokens, "zl", swap(n_z, 4))
+    t = join(tokens, t_other)
     t_near = within(t)
-    c_near = within(c)
+    c = join(cotangent, lax.ppermute(after(cotangent, t), "zl", swap(n_z, 4)))
     t = join(t, *t_near)
-    c = join(c, *c_near)
     t_left = lax.ppermute(t, "x", up)
     t_right = lax.ppermute(t, "x", down)
+    normed = pl.pallas_call(
+        own_kernel,
+        out_shape=jax.ShapeDtypeStruct(t.shape, BF16),
+        in_specs=[VMEM],
+        out_specs=VMEM,
+        compiler_params=PARAMS,
+    )(t)
+    c_near = within(after(c, normed))
+    c = join(after(c, t_left, t_right), *c_near)
     t_far = lax.ppermute(t_left, "x", up)
     c_right = lax.ppermute(after(c, t_left, t_right), "x", down)
     c_left = lax.ppermute(after(c, t_left, t_right), "x", up)
     c_far = lax.ppermute(c_right, "x", down)
-    return [t, t_left, t_right, t_far], [c, c_left, c_right, c_far]
+    return [normed, t_left, t_right, t_far], [c, c_left, c_right, c_far]
 
 
 def local(sizes, tokens, cotangent, w_qkv, w_out):
@@ -230,14 +242,20 @@
     blocks = (far, near, model // (far * near * cores))
     one = jax.ShapeDtypeStruct((4 * width, blocks[2]), BF16)
     two = jax.ShapeDtypeStruct((far, 4 * width, blocks[2]), BF16)
-    four = jax.ShapeDtypeStruct((2 * far, 4 * width, blocks[2]), BF16)
     here = lax.axis_index("y").astype(jnp.int32)
     core = lax.axis_index("c").astype(jnp.int32)
 
-    def terms(core, shapes, *other):
+    def terms(core, order, *other):
+        adds = len(other) > 0
+        if adds:
+            shapes = []
+            for distance in order:
+                shapes += [one, one] if distance == near // 2 else [two]
+        else:
+            shapes = [jax.ShapeDtypeStruct((far * len(order), 4 * width, blocks[2]), BF16)]
         return pl.pallas_call(
             functools.partial(
-                terms_kernel, count=len(rows), blocks=blocks, slots=len(other) > 0
+                terms_kernel, count=len(rows), blocks=blocks, order=order, adds=adds
             ),
             out_shape=shapes,
             in_specs=[SMEM] + [VMEM] * (len(rows) + 3 + len(other)),
@@ -245,41 +263,35 @@
             compiler_params=PARAMS,
         )(jnp.stack([core, here]), normed, *c_pieces, d_qkv, att, *other)
 
-    (mine,) = terms(1 - core, [jax.ShapeDtypeStruct((far * near, 4 * width, blocks[2]), BF16)])
-    theirs = lax.ppermute(mine, "c", swap(cores, 1))
-    first_up, first_down, near_up, near_down, mid_up, mid_down, own = terms(
-        core, [one, one, four, four, two, two, two], theirs
-    )
-    first_up = lax.ppermute(first_up, "y", turn(near, 2))
-    near_up = lax.ppermute(near_up, "y", turn(near, 1))
-    first_down = lax.ppermute(first_down, "y", turn(near, -2))
-    near_down = lax.ppermute(near_down, "y", turn(near, -1))
-
-    def middle(half, *args):
+    (sent_first,) = terms(1 - core, FIRST)
+    theirs_first = lax.ppermute(sent_first, "c", swap(cores, 1))
+    (sent,) = terms(1 - core, SECOND)
+    theirs = lax.ppermute(after(sent, theirs_first), "c", swap(cores, 1))
+    up, down = turn(near, 1), turn(near, -1)
+    goes_up, goes_down, up_3, down_3 = terms(core, FIRST, theirs_first)
+    goes_up = lax.ppermute(goes_up, "y", up)
+    goes_down = lax.ppermute(goes_down, "y", down)
+    up_2, down_2, up_1, down_1, own = terms(core, SECOND, theirs)
+
+    def hop(half, *args):
         return pl.pallas_call(
-            functools.partial(middle_kernel, half=half),
+            functools.partial(hop_kernel, half=half),
             out_shape=two,
-            in_specs=[VMEM] * 3,
+            in_specs=[VMEM] * 2,
             out_specs=VMEM,
             compiler_params=PARAMS,
         )(*args)
 
-    goes_up = lax.ppermute(middle(0, mid_up, near_up, first_up), "y", turn(near, 2))
-    goes_down = lax.ppermute(middle(1, mid_down, near_down, first_down), "y", turn(near, -2))
+    for a, b, halves in ((up_3, down_3, (0, 1)), (up_2, down_2, (None, None)), (up_1, down_1, (None, None))):
+        goes_up = lax.ppermute(hop(halves[0], a, goes_up), "y", up)
+        goes_down = lax.ppermute(hop(halves[1], b, goes_down), "y", down)
     away, kept = pl.pallas_call(
         last_kernel,
         out_shape=[one, jax.ShapeDtypeStruct(one.shape, F32)],
-        in_specs=[SMEM] + [VMEM] * 5,
+        in_specs=[SMEM] + [VMEM] * 3,
         out_specs=[VMEM] * 2,
         compiler_params=PARAMS,
-    )(
-        lax.axis_index("zh").astype(jnp.int32).reshape(1),
-        own,
-        near_up,
-        near_down,
-        goes_up,
-        goes_down,
-    )
+    )(lax.axis_index("zh").astype(jnp.int32).reshape(1), own, goes_up, goes_down)
     other = lax.ppermute(away, "zh", swap(far, 1))
     grad_qkv, grad_out = pl.pallas_call(
         finish_kernel,

time: 175 us -> 176 us (level)
  the two profiles are of different devices: /device:TPU:56 before, /device:TPU:24 now
where the time goes in v4:
time: 176 us; the launch traced here: 175 us
  starting transfers between devices  109 us (62%)
  waiting for transfers between devices  43.7 us (25%)
  Pallas kernels  16.4 us (9%)
  local copies, waits for them, and re-layouts  2.77 us (2%)
  other arithmetic  1.92 us (1%)
    ppermute x6, starting transfers between devices, within(): return [lax.ppermute(rows, 'zl', swap(n_z, s)) for s in (2, 3, 1)]  22.4 us
    ppermute x3, starting transfers between devices, local(): goes_up = lax.ppermute(hop(halves[0], a, goes_up), 'y', up)  16.8 us
    ppermute x1, starting transfers between devices, local(): other = lax.ppermute(away, 'zh', swap(far, 1))  13.3 us
    ppermute x1, starting transfers between devices, gather(): t_other = lax.ppermute(tokens, 'zl', swap(n_z, 4))  10.9 us
    ppermute x6, waiting for transfers between devices, within(): return [lax.ppermute(rows, 'zl', swap(n_z, s)) for s in (2, 3, 1)]  9.83 us
    ppermute x1, starting transfers between devices, gather(): c = join(cotangent, lax.ppermute(after(cotangent, t), 'zl', swap(n_z, 4)))  8.19 us
    pallas_call x1, Pallas kernels, local(): pl.pallas_call(functools.partial(forward_kernel, rows=rows), out_shape=[j...  6.91 us
    ppermute x1, waiting for transfers between devices, gather(): c_right = lax.ppermute(after(c, t_left, t_right), 'x', down)  6.31 us
  transfers between devices with their start and end apart: 25, of which 13 were waited for; matrix products, arithmetic and copies ran while one was open for 1% of the time, Pallas kernels for 7%

profile of v4, /device:TPU:24, one launch (start us, length us, event | category | flops | bytes accessed | tf_op | source)
XLA Modules:
  0.0 174.7 jit_solution(12835945134964439934)
XLA Ops:
  0.6 10.9 %collective-permute-start = (bf16[8,4096]{1,0:T(8,128)(2,1)}, bf16[8,4096]{1,0:T(8,128)(2,1)S(1)}, u32[]{:S(2)}, u32[]{:S(2)}) collective-permute-start(bf16[8,4096]{1,0:T(8,128)(2,1)} %param.4), channel_id=1, source_target_pairs={{0,16},{4,20},{8,24},{12,28},{16,0},{20,4},{24,8},{28,12},{1,17},{... | collective-permute-start | bytes 196616 | tf_op jit(solution)/shard_map/ppermute | solution.py:187
  11.6 2.4 %collective-permute-done = bf16[8,4096]{1,0:T(8,128)(2,1)S(1)} collective-permute-done((bf16[8,4096]{1,0:T(8,128)(2,1)}, bf16[8,4096]{1,0:T(8,128)(2,1)S(1)}, u32[]{:S(2)}, u32[]{:S(2)}) %collective-permute-start) | collective-permute-done | bytes 65568 | tf_op jit(solution)/shard_map/ppermute | solution.py:187
  14.8 4.3 %collective-permute-start.3 = (bf16[16,4096]{1,0:T(8,128)(2,1)S(1)}, bf16[16,4096]{1,0:T(8,128)(2,1)S(1)}, u32[]{:S(2)}, u32[]{:S(2)}) collective-permute-start(bf16[16,4096]{1,0:T(8,128)(2,1)S(1)} %pad_maximum_fusion.2), channel_id=1, source_target_pairs={{0,4},{4,0},{8,12},{12,8},{16,20},{20,16},{24,28},{28,24},{1,5},{5... | collective-permute-start | bytes 393224 | tf_op jit(solution)/shard_map/ppermute | solution.py:185
  19.1 6.4 %collective-permute-start.2 = (bf16[16,4096]{1,0:T(8,128)(2,1)S(1)}, bf16[16,4096]{1,0:T(8,128)(2,1)S(1)}, u32[]{:S(2)}, u32[]{:S(2)}) collective-permute-start(bf16[16,4096]{1,0:T(8,128)(2,1)S(1)} %pad_maximum_fusion.2), channel_id=1, source_target_pairs={{0,12},{4,8},{8,4},{12,0},{16,28},{20,24},{24,20},{28,16},{1,13},{... | collective-permute-start | bytes 393224 | tf_op jit(solution)/shard_map/ppermute | solution.py:185
  25.6 2.5 %collective-permute-start.1 = (bf16[16,4096]{1,0:T(8,128)(2,1)S(1)}, bf16[16,4096]{1,0:T(8,128)(2,1)S(1)}, u32[]{:S(2)}, u32[]{:S(2)}) collective-permute-start(bf16[16,4096]{1,0:T(8,128)(2,1)S(1)} %pad_maximum_fusion.2), channel_id=1, source_target_pairs={{0,8},{4,12},{8,0},{12,4},{16,24},{20,28},{24,16},{28,20},{1,9},{5... | collective-permute-start | bytes 393224 | tf_op jit(solution)/shard_map/ppermute | solution.py:185
  28.1 8.2 %collective-permute-start.7 = (bf16[8,4096]{1,0:T(8,128)(2,1)}, bf16[8,4096]{1,0:T(8,128)(2,1)S(1)}, u32[]{:S(2)}, u32[]{:S(2)}) collective-permute-start(bf16[8,4096]{1,0:T(8,128)(2,1)} %param.5), channel_id=1, source_target_pairs={{0,16},{4,20},{8,24},{12,28},{16,0},{20,4},{24,8},{28,12},{1,17},{... | collective-permute-start | bytes 196616 | tf_op jit(solution)/shard_map/ppermute | solution.py:190
  36.3 4.2 %collective-permute-done.1 = bf16[16,4096]{1,0:T(8,128)(2,1)S(1)} collective-permute-done((bf16[16,4096]{1,0:T(8,128)(2,1)S(1)}, bf16[16,4096]{1,0:T(8,128)(2,1)S(1)}, u32[]{:S(2)}, u32[]{:S(2)}) %collective-permute-start.1) | collective-permute-done | bytes 131104 | tf_op jit(solution)/shard_map/ppermute | solution.py:185
  40.6 4.7 %collective-permute-start.5 = (bf16[64,4096]{1,0:T(8,128)(2,1)S(1)}, bf16[64,4096]{1,0:T(8,128)(2,1)S(1)}, u32[]{:S(2)}, u32[]{:S(2)}) collective-permute-start(bf16[64,4096]{1,0:T(8,128)(2,1)S(1)} %pad_maximum_fusion.rows_ref), channel_id=1, source_target_pairs={{0,3},{1,0},{2,1},{3,2},{4,7},{5,4},{6,5},{7,6},{8,11},{9,8},{10,9... | collective-permute-start | bytes 1572872 | tf_op jit(solution)/shard_map/ppermute | solution.py:193
  45.2 1.9 %collective-permute-start.4 = (bf16[64,4096]{1,0:T(8,128)(2,1)S(1)}, bf16[64,4096]{1,0:T(8,128)(2,1)}, u32[]{:S(2)}, u32[]{:S(2)}) collective-permute-start(bf16[64,4096]{1,0:T(8,128)(2,1)S(1)} %pad_maximum_fusion.rows_ref), channel_id=1, source_target_pairs={{0,1},{1,2},{2,3},{3,0},{4,5},{5,6},{6,7},{7,4},{8,9},{9,10},{10,1... | collective-permute-start | bytes 1572872 | tf_op jit(solution)/shard_map/ppermute | solution.py:192
  51.0 3.3 %collective-permute-start.9 = (bf16[16,4096]{1,0:T(8,128)(2,1)S(1)}, bf16[16,4096]{1,0:T(8,128)(2,1)S(1)}, u32[]{:S(2)}, u32[]{:S(2)}) collective-permute-start(bf16[16,4096]{1,0:T(8,128)(2,1)S(1)} %pad_maximum_fusion.3), channel_id=1, source_target_pairs={{0,12},{4,8},{8,4},{12,0},{16,28},{20,24},{24,20},{28,16},{1,13},{... | collective-permute-start | bytes 393224 | tf_op jit(solution)/shard_map/ppermute | solution.py:185
  54.3 4.0 %collective-permute-start.8 = (bf16[16,4096]{1,0:T(8,128)(2,1)S(1)}, bf16[16,4096]{1,0:T(8,128)(2,1)S(1)}, u32[]{:S(2)}, u32[]{:S(2)}) collective-permute-start(bf16[16,4096]{1,0:T(8,128)(2,1)S(1)} %pad_maximum_fusion.3), channel_id=1, source_target_pairs={{0,8},{4,12},{8,0},{12,4},{16,24},{20,28},{24,16},{28,20},{1,9},{5... | collective-permute-start | bytes 393224 | tf_op jit(solution)/shard_map/ppermute | solution.py:185
  58.3 2.9 %collective-permute-done.4.refs_1_ = bf16[64,4096]{1,0:T(8,128)(2,1)} collective-permute-done((bf16[64,4096]{1,0:T(8,128)(2,1)S(1)}, bf16[64,4096]{1,0:T(8,128)(2,1)}, u32[]{:S(2)}, u32[]{:S(2)}) %collective-permute-start.4) | collective-permute-done | bytes 524320 | tf_op jit(solution)/shard_map/ppermute | solution.py:192
  61.2 5.6 %collective-permute-done.8 = bf16[16,4096]{1,0:T(8,128)(2,1)S(1)} collective-permute-done((bf16[16,4096]{1,0:T(8,128)(2,1)S(1)}, bf16[16,4096]{1,0:T(8,128)(2,1)S(1)}, u32[]{:S(2)}, u32[]{:S(2)}) %collective-permute-start.8) | collective-permute-done | bytes 131104 | tf_op jit(solution)/shard_map/ppermute | solution.py:185
  66.8 4.9 %collective-permute-start.12 = (bf16[64,4096]{1,0:T(8,128)(2,1)S(1)}, bf16[64,4096]{1,0:T(8,128)(2,1)S(1)}, u32[]{:S(2)}, u32[]{:S(2)}) collective-permute-start(bf16[64,4096]{1,0:T(8,128)(2,1)S(1)} %pad_maximum_fusion.1.refs_0_.refs_2_), channel_id=1, source_target_pairs={{0,3},{1,0},{2,1},{3,2},{4,7},{5,4},{6,5},{7,6},{8,11},{9,8},{10,9... | collective-permute-start | bytes 1572872 | tf_op jit(solution)/shard_map/ppermute | solution.py:204
  71.7 1.9 %collective-permute-start.6 = (bf16[64,4096]{1,0:T(8,128)(2,1)}, bf16[64,4096]{1,0:T(8,128)(2,1)}, u32[]{:S(2)}, u32[]{:S(2)}) collective-permute-start(bf16[64,4096]{1,0:T(8,128)(2,1)} %collective-permute-done.4.refs_1_), channel_id=1, source_target_pairs={{0,1},{1,2},{2,3},{3,0},{4,5},{5,6},{6,7},{7,4},{8,9},{9,10},{10,1... | collective-permute-start | bytes 1572872 | tf_op jit(solution)/shard_map/ppermute | solution.py:203
  73.6 1.9 %collective-permute-start.11 = (bf16[64,4096]{1,0:T(8,128)(2,1)S(1)}, bf16[64,4096]{1,0:T(8,128)(2,1)S(1)}, u32[]{:S(2)}, u32[]{:S(2)}) collective-permute-start(bf16[64,4096]{1,0:T(8,128)(2,1)S(1)} %pad_maximum_fusion.1.refs_0_.refs_2_), channel_id=1, source_target_pairs={{0,1},{1,2},{2,3},{3,0},{4,5},{5,6},{6,7},{7,4},{8,9},{9,10},{10,1... | collective-permute-start | bytes 1572872 | tf_op jit(solution)/shard_map/ppermute | solution.py:205
  75.5 6.3 %collective-permute-done.12.refs_2_.refs_4_ = bf16[64,4096]{1,0:T(8,128)(2,1)S(1)} collective-permute-done((bf16[64,4096]{1,0:T(8,128)(2,1)S(1)}, bf16[64,4096]{1,0:T(8,128)(2,1)S(1)}, u32[]{:S(2)}, u32[]{:S(2)}) %collective-permute-start.12) | collective-permute-done | bytes 524320 | tf_op jit(solution)/shard_map/ppermute | solution.py:204
  81.8 5.6 %collective-permute-start.13 = (bf16[64,4096]{1,0:T(8,128)(2,1)S(1)}, bf16[64,4096]{1,0:T(8,128)(2,1)S(1)}, u32[]{:S(2)}, u32[]{:S(2)}) collective-permute-start(bf16[64,4096]{1,0:T(8,128)(2,1)S(1)} %collective-permute-done.12.refs_2_.refs_4_), channel_id=1, source_target_pairs={{0,3},{1,0},{2,1},{3,2},{4,7},{5,4},{6,5},{7,6},{8,11},{9,8},{10,9... | collective-permute-start | bytes 1572872 | tf_op jit(solution)/shard_map/ppermute | solution.py:206
  87.5 2.4 %collective-permute-done.6.refs_3_ = bf16[64,4096]{1,0:T(8,128)(2,1)} collective-permute-done((bf16[64,4096]{1,0:T(8,128)(2,1)}, bf16[64,4096]{1,0:T(8,128)(2,1)}, u32[]{:S(2)}, u32[]{:S(2)}) %collective-permute-start.6) | collective-permute-done | bytes 524320 | tf_op jit(solution)/shard_map/ppermute | solution.py:203
  91.8 6.9 %shard_map.60 = (bf16[256,4096]{1,0:T(8,128)(2,1)S(1)}, bf16[128,256]{1,0:T(8,128)(2,1)S(1)}, f32[256,128]{1,0:T(8,128)S(1)}, f32[256,128]{1,0:T(8,128)S(1)}, f3...) custom-call(bf16[64,4096]{1,0:T(8,128)(2,1)S(1)} %shard_map.59.refs_0_, ...), custom_call_target="tpu_custom_call" | custom-call | tf_op jit(solution)/shard_map/pallas_call | solution.py:219
  98.8 2.9 %shard_map.61.refs_6_ = bf16[384,256]{1,0:T(8,128)(2,1)S(1)} custom-call(bf16[64,4096]{1,0:T(8,128)(2,1)S(1)} %pad_maximum_fusion.1.refs_0_.refs_2_, bf16[64,4096]{1,0:T(8,128)(2,1)S(1)} %collective-permute-done.11.refs_1_.refs_3_, bf16[64,4096]{1,0:T(8,128)(2,1)S(1)} %collective-permute-done.12.refs_2_.refs_4_, ...), custom_call_target="tpu_custom_call" | custom-call | tf_op jit(solution)/shard_map/pallas_call | solution.py:235
  102.7 1.9 %collective-permute-start.14 = (bf16[6,512,128]{2,1,0:T(8,128)(2,1)S(1)}, bf16[6,512,128]{2,1,0:T(8,128)(2,1)S(1)}, u32[]{:S(2)}, u32[]{:S(2)}) collective-permute-start(bf16[6,512,128]{2,1,0:T(8,128)(2,1)S(1)} %shard_map.63), channel_id=1, source_target_pairs={{0,32},{32,0},{1,33},{33,1},{2,34},{34,2},{3,35},{35,3},{4,36},{36... | collective-permute-start | bytes 2359304 | tf_op jit(solution)/shard_map/ppermute | solution.py:267
  106.9 2.0 %collective-permute-start.15 = (bf16[10,512,128]{2,1,0:T(8,128)(2,1)S(1)}, bf16[10,512,128]{2,1,0:T(8,128)(2,1)S(1)}, u32[]{:S(2)}, u32[]{:S(2)}) collective-permute-start(bf16[10,512,128]{2,1,0:T(8,128)(2,1)S(1)} %shard_map.62), channel_id=1, source_target_pairs={{0,32},{32,0},{1,33},{33,1},{2,34},{34,2},{3,35},{35,3},{4,36},{36... | collective-permute-start | bytes 3932168 | tf_op jit(solution)/shard_map/ppermute | solution.py:269
  110.1 4.7 %collective-permute-start.16 = (bf16[512,128]{1,0:T(8,128)(2,1)S(1)}, bf16[512,128]{1,0:T(8,128)(2,1)S(1)}, u32[]{:S(2)}, u32[]{:S(2)}) collective-permute-start(bf16[512,128]{1,0:T(8,128)(2,1)S(1)} %get-tuple-element.45), channel_id=1, source_target_pairs={{0,64},{64,128},{128,192},{192,256},{256,320},{320,384},{384,448},... | collective-permute-start | bytes 393224 | tf_op jit(solution)/shard_map/ppermute | solution.py:272
  118.1 5.6 %collective-permute-start.17 = (bf16[2,512,128]{2,1,0:T(8,128)(2,1)S(1)}, bf16[2,512,128]{2,1,0:T(8,128)(2,1)S(1)}, u32[]{:S(2)}, u32[]{:S(2)}) collective-permute-start(bf16[2,512,128]{2,1,0:T(8,128)(2,1)S(1)} %shard_map.66), channel_id=1, source_target_pairs={{0,64},{64,128},{128,192},{192,256},{256,320},{320,384},{384,448},... | collective-permute-start | bytes 786440 | tf_op jit(solution)/shard_map/ppermute | solution.py:286
  126.9 2.0 %collective-permute-done.17.came_ref = bf16[2,512,128]{2,1,0:T(8,128)(2,1)S(1)} collective-permute-done((bf16[2,512,128]{2,1,0:T(8,128)(2,1)S(1)}, bf16[2,512,128]{2,1,0:T(8,128)(2,1)S(1)}, u32[]{:S(2)}, u32[]{:S(2)}) %collective-permute-start.17) | collective-permute-done | bytes 262176 | tf_op jit(solution)/shard_map/ppermute | solution.py:286
  129.0 5.6 %collective-permute-start.18 = (bf16[2,512,128]{2,1,0:T(8,128)(2,1)S(1)}, bf16[2,512,128]{2,1,0:T(8,128)(2,1)S(1)}, u32[]{:S(2)}, u32[]{:S(2)}) collective-permute-start(bf16[2,512,128]{2,1,0:T(8,128)(2,1)S(1)} %shard_map.67), channel_id=1, source_target_pairs={{0,64},{64,128},{128,192},{192,256},{256,320},{320,384},{384,448},... | collective-permute-start | bytes 786440 | tf_op jit(solution)/shard_map/ppermute | solution.py:286
  136.6 2.3 %collective-permute-done.18.came_ref = bf16[2,512,128]{2,1,0:T(8,128)(2,1)S(1)} collective-permute-done((bf16[2,512,128]{2,1,0:T(8,128)(2,1)S(1)}, bf16[2,512,128]{2,1,0:T(8,128)(2,1)S(1)}, u32[]{:S(2)}, u32[]{:S(2)}) %collective-permute-start.18) | collective-permute-done | bytes 262176 | tf_op jit(solution)/shard_map/ppermute | solution.py:286
  139.0 5.6 %collective-permute-start.19 = (bf16[2,512,128]{2,1,0:T(8,128)(2,1)S(1)}, bf16[2,512,128]{2,1,0:T(8,128)(2,1)S(1)}, u32[]{:S(2)}, u32[]{:S(2)}) collective-permute-start(bf16[2,512,128]{2,1,0:T(8,128)(2,1)S(1)} %shard_map.68), channel_id=1, source_target_pairs={{0,64},{64,128},{128,192},{192,256},{256,320},{320,384},{384,448},... | collective-permute-start | bytes 786440 | tf_op jit(solution)/shard_map/ppermute | solution.py:286
  148.5 5.7 %collective-permute-done.23.down_ref = bf16[2,512,128]{2,1,0:T(8,128)(2,1)S(1)} collective-permute-done((bf16[2,512,128]{2,1,0:T(8,128)(2,1)S(1)}, bf16[2,512,128]{2,1,0:T(8,128)(2,1)S(1)}, u32[]{:S(2)}, u32[]{:S(2)}) %collective-permute-start.23) | collective-permute-done | bytes 262176 | tf_op jit(solution)/shard_map/ppermute | solution.py:287
  154.3 13.3 %collective-permute-start.24 = (bf16[512,128]{1,0:T(8,128)(2,1)S(1)}, bf16[512,128]{1,0:T(8,128)(2,1)S(1)}, u32[]{:S(2)}, u32[]{:S(2)}) collective-permute-start(bf16[512,128]{1,0:T(8,128)(2,1)S(1)} %get-tuple-element.51), channel_id=1, source_target_pairs={{0,512},{512,0},{1,513},{513,1},{2,514},{514,2},{3,515},{515,3},{4... | collective-permute-start | bytes 393224 | tf_op jit(solution)/shard_map/ppermute | solution.py:295
  167.6 5.5 %collective-permute-done.24.other_ref = bf16[512,128]{1,0:T(8,128)(2,1)S(1)} collective-permute-done((bf16[512,128]{1,0:T(8,128)(2,1)S(1)}, bf16[512,128]{1,0:T(8,128)(2,1)S(1)}, u32[]{:S(2)}, u32[]{:S(2)}) %collective-permute-start.24) | collective-permute-done | bytes 131104 | tf_op jit(solution)/shard_map/ppermute | solution.py:295
  (44 shorter events, 25.1 us)
Async XLA Ops:
  0.6 13.4 %collective-permute-start = (bf16[8,4096]{1,0:T(8,128)(2,1)}, bf16[8,4096]{1,0:T(8,128)(2,1)S(1)}, u32[]{:S(2)}, u32[]{:S(2)}) collective-permute-start(bf16[8,4096]{1,0:T(8,128)(2,1)} %param.4), channel_id=1, source_target_pairs={{0,16},{4,20},{8,24},{12,28},{16,0},{20,4},{24,8},{28,12},{1,17},{... | collective-permute-start | bytes 196616 | tf_op jit(solution)/shard_map/ppermute | solution.py:187
  14.8 21.4 %collective-permute-start.3 = (bf16[16,4096]{1,0:T(8,128)(2,1)S(1)}, bf16[16,4096]{1,0:T(8,128)(2,1)S(1)}, u32[]{:S(2)}, u32[]{:S(2)}) collective-permute-start(bf16[16,4096]{1,0:T(8,128)(2,1)S(1)} %pad_maximum_fusion.2), channel_id=1, source_target_pairs={{0,4},{4,0},{8,12},{12,8},{16,20},{20,16},{24,28},{28,24},{1,5},{5... | collective-permute-start | bytes 393224 | tf_op jit(solution)/shard_map/ppermute | solution.py:185
  19.1 17.1 %collective-permute-start.2 = (bf16[16,4096]{1,0:T(8,128)(2,1)S(1)}, bf16[16,4096]{1,0:T(8,128)(2,1)S(1)}, u32[]{:S(2)}, u32[]{:S(2)}) collective-permute-start(bf16[16,4096]{1,0:T(8,128)(2,1)S(1)} %pad_maximum_fusion.2), channel_id=1, source_target_pairs={{0,12},{4,8},{8,4},{12,0},{16,28},{20,24},{24,20},{28,16},{1,13},{... | collective-permute-start | bytes 393224 | tf_op jit(solution)/shard_map/ppermute | solution.py:185
  25.6 14.9 %collective-permute-start.1 = (bf16[16,4096]{1,0:T(8,128)(2,1)S(1)}, bf16[16,4096]{1,0:T(8,128)(2,1)S(1)}, u32[]{:S(2)}, u32[]{:S(2)}) collective-permute-start(bf16[16,4096]{1,0:T(8,128)(2,1)S(1)} %pad_maximum_fusion.2), channel_id=1, source_target_pairs={{0,8},{4,12},{8,0},{12,4},{16,24},{20,28},{24,16},{28,20},{1,9},{5... | collective-permute-start | bytes 393224 | tf_op jit(solution)/shard_map/ppermute | solution.py:185
  28.1 19.1 %collective-permute-start.7 = (bf16[8,4096]{1,0:T(8,128)(2,1)}, bf16[8,4096]{1,0:T(8,128)(2,1)S(1)}, u32[]{:S(2)}, u32[]{:S(2)}) collective-permute-start(bf16[8,4096]{1,0:T(8,128)(2,1)} %param.5), channel_id=1, source_target_pairs={{0,16},{4,20},{8,24},{12,28},{16,0},{20,4},{24,8},{28,12},{1,17},{... | collective-permute-start | bytes 196616 | tf_op jit(solution)/shard_map/ppermute | solution.py:190
  40.6 17.7 %collective-permute-start.5 = (bf16[64,4096]{1,0:T(8,128)(2,1)S(1)}, bf16[64,4096]{1,0:T(8,128)(2,1)S(1)}, u32[]{:S(2)}, u32[]{:S(2)}) collective-permute-start(bf16[64,4096]{1,0:T(8,128)(2,1)S(1)} %pad_maximum_fusion.rows_ref), channel_id=1, source_target_pairs={{0,3},{1,0},{2,1},{3,2},{4,7},{5,4},{6,5},{7,6},{8,11},{9,8},{10,9... | collective-permute-start | bytes 1572872 | tf_op jit(solution)/shard_map/ppermute | solution.py:193
  45.2 16.0 %collective-permute-start.4 = (bf16[64,4096]{1,0:T(8,128)(2,1)S(1)}, bf16[64,4096]{1,0:T(8,128)(2,1)}, u32[]{:S(2)}, u32[]{:S(2)}) collective-permute-start(bf16[64,4096]{1,0:T(8,128)(2,1)S(1)} %pad_maximum_fusion.rows_ref), channel_id=1, source_target_pairs={{0,1},{1,2},{2,3},{3,0},{4,5},{5,6},{6,7},{7,4},{8,9},{9,10},{10,1... | collective-permute-start | bytes 1572872 | tf_op jit(solution)/shard_map/ppermute | solution.py:192
  49.0 12.2 %collective-permute-start.10 = (bf16[16,4096]{1,0:T(8,128)(2,1)S(1)}, bf16[16,4096]{1,0:T(8,128)(2,1)S(1)}, u32[]{:S(2)}, u32[]{:S(2)}) collective-permute-start(bf16[16,4096]{1,0:T(8,128)(2,1)S(1)} %pad_maximum_fusion.3), channel_id=1, source_target_pairs={{0,4},{4,0},{8,12},{12,8},{16,20},{20,16},{24,28},{28,24},{1,5},{5... | collective-permute-start | bytes 393224 | tf_op jit(solution)/shard_map/ppermute | solution.py:185
  51.0 10.2 %collective-permute-start.9 = (bf16[16,4096]{1,0:T(8,128)(2,1)S(1)}, bf16[16,4096]{1,0:T(8,128)(2,1)S(1)}, u32[]{:S(2)}, u32[]{:S(2)}) collective-permute-start(bf16[16,4096]{1,0:T(8,128)(2,1)S(1)} %pad_maximum_fusion.3), channel_id=1, source_target_pairs={{0,12},{4,8},{8,4},{12,0},{16,28},{20,24},{24,20},{28,16},{1,13},{... | collective-permute-start | bytes 393224 | tf_op jit(solution)/shard_map/ppermute | solution.py:185
  54.3 12.5 %collective-permute-start.8 = (bf16[16,4096]{1,0:T(8,128)(2,1)S(1)}, bf16[16,4096]{1,0:T(8,128)(2,1)S(1)}, u32[]{:S(2)}, u32[]{:S(2)}) collective-permute-start(bf16[16,4096]{1,0:T(8,128)(2,1)S(1)} %pad_maximum_fusion.3), channel_id=1, source_target_pairs={{0,8},{4,12},{8,0},{12,4},{16,24},{20,28},{24,16},{28,20},{1,9},{5... | collective-permute-start | bytes 393224 | tf_op jit(solution)/shard_map/ppermute | solution.py:185
  66.8 15.0 %collective-permute-start.12 = (bf16[64,4096]{1,0:T(8,128)(2,1)S(1)}, bf16[64,4096]{1,0:T(8,128)(2,1)S(1)}, u32[]{:S(2)}, u32[]{:S(2)}) collective-permute-start(bf16[64,4096]{1,0:T(8,128)(2,1)S(1)} %pad_maximum_fusion.1.refs_0_.refs_2_), channel_id=1, source_target_pairs={{0,3},{1,0},{2,1},{3,2},{4,7},{5,4},{6,5},{7,6},{8,11},{9,8},{10,9... | collective-permute-start | bytes 1572872 | tf_op jit(solution)/shard_map/ppermute | solution.py:204
  71.7 18.3 %collective-permute-start.6 = (bf16[64,4096]{1,0:T(8,128)(2,1)}, bf16[64,4096]{1,0:T(8,128)(2,1)}, u32[]{:S(2)}, u32[]{:S(2)}) collective-permute-start(bf16[64,4096]{1,0:T(8,128)(2,1)} %collective-permute-done.4.refs_1_), channel_id=1, source_target_pairs={{0,1},{1,2},{2,3},{3,0},{4,5},{5,6},{6,7},{7,4},{8,9},{9,10},{10,1... | collective-permute-start | bytes 1572872 | tf_op jit(solution)/shard_map/ppermute | solution.py:203
  73.6 25.2 %collective-permute-start.11 = (bf16[64,4096]{1,0:T(8,128)(2,1)S(1)}, bf16[64,4096]{1,0:T(8,128)(2,1)S(1)}, u32[]{:S(2)}, u32[]{:S(2)}) collective-permute-start(bf16[64,4096]{1,0:T(8,128)(2,1)S(1)} %pad_maximum_fusion.1.refs_0_.refs_2_), channel_id=1, source_target_pairs={{0,1},{1,2},{2,3},{3,0},{4,5},{5,6},{6,7},{7,4},{8,9},{9,10},{10,1... | collective-permute-start | bytes 1572872 | tf_op jit(solution)/shard_map/ppermute | solution.py:205
  81.8 16.9 %collective-permute-start.13 = (bf16[64,4096]{1,0:T(8,128)(2,1)S(1)}, bf16[64,4096]{1,0:T(8,128)(2,1)S(1)}, u32[]{:S(2)}, u32[]{:S(2)}) collective-permute-start(bf16[64,4096]{1,0:T(8,128)(2,1)S(1)} %collective-permute-done.12.refs_2_.refs_4_), channel_id=1, source_target_pairs={{0,3},{1,0},{2,1},{3,2},{4,7},{5,4},{6,5},{7,6},{8,11},{9,8},{10,9... | collective-permute-start | bytes 1572872 | tf_op jit(solution)/shard_map/ppermute | solution.py:206
  90.0 1.9 %copy-start = (bf16[4096,1,384]{2,0,1:T(8,128)(2,1)S(1)}, bf16[4096,1,384]{2,0,1:T(8,128)(2,1)}, u32[]{:S(2)}) copy-start(bf16[4096,1,384]{2,0,1:T(8,128)(2,1)} %param.6) | copy-start | bytes 9437188
  91.8 6.9 %copy-start.1 = (bf16[1,128,4096]{2,1,0:T(8,128)(2,1)S(1)}, bf16[1,128,4096]{2,1,0:T(8,128)(2,1)}, u32[]{:S(2)}) copy-start(bf16[1,128,4096]{2,1,0:T(8,128)(2,1)} %param.7) | copy-start | bytes 3145732
  102.7 4.2 %collective-permute-start.14 = (bf16[6,512,128]{2,1,0:T(8,128)(2,1)S(1)}, bf16[6,512,128]{2,1,0:T(8,128)(2,1)S(1)}, u32[]{:S(2)}, u32[]{:S(2)}) collective-permute-start(bf16[6,512,128]{2,1,0:T(8,128)(2,1)S(1)} %shard_map.63), channel_id=1, source_target_pairs={{0,32},{32,0},{1,33},{33,1},{2,34},{34,2},{3,35},{35,3},{4,36},{36... | collective-permute-start | bytes 2359304 | tf_op jit(solution)/shard_map/ppermute | solution.py:267
  106.9 18.8 %collective-permute-start.15 = (bf16[10,512,128]{2,1,0:T(8,128)(2,1)S(1)}, bf16[10,512,128]{2,1,0:T(8,128)(2,1)S(1)}, u32[]{:S(2)}, u32[]{:S(2)}) collective-permute-start(bf16[10,512,128]{2,1,0:T(8,128)(2,1)S(1)} %shard_map.62), channel_id=1, source_target_pairs={{0,32},{32,0},{1,33},{33,1},{2,34},{34,2},{3,35},{35,3},{4,36},{36... | collective-permute-start | bytes 3932168 | tf_op jit(solution)/shard_map/ppermute | solution.py:269
  110.1 8.0 %collective-permute-start.16 = (bf16[512,128]{1,0:T(8,128)(2,1)S(1)}, bf16[512,128]{1,0:T(8,128)(2,1)S(1)}, u32[]{:S(2)}, u32[]{:S(2)}) collective-permute-start(bf16[512,128]{1,0:T(8,128)(2,1)S(1)} %get-tuple-element.45), channel_id=1, source_target_pairs={{0,64},{64,128},{128,192},{192,256},{256,320},{320,384},{384,448},... | collective-permute-start | bytes 393224 | tf_op jit(solution)/shard_map/ppermute | solution.py:272
  114.8 8.9 %collective-permute-start.20 = (bf16[512,128]{1,0:T(8,128)(2,1)S(1)}, bf16[512,128]{1,0:T(8,128)(2,1)S(1)}, u32[]{:S(2)}, u32[]{:S(2)}) collective-permute-start(bf16[512,128]{1,0:T(8,128)(2,1)S(1)} %get-tuple-element.49), channel_id=1, source_target_pairs={{0,448},{64,0},{128,64},{192,128},{256,192},{320,256},{384,320},{4... | collective-permute-start | bytes 393224 | tf_op jit(solution)/shard_map/ppermute | solution.py:273
  118.1 10.9 %collective-permute-start.17 = (bf16[2,512,128]{2,1,0:T(8,128)(2,1)S(1)}, bf16[2,512,128]{2,1,0:T(8,128)(2,1)S(1)}, u32[]{:S(2)}, u32[]{:S(2)}) collective-permute-start(bf16[2,512,128]{2,1,0:T(8,128)(2,1)S(1)} %shard_map.66), channel_id=1, source_target_pairs={{0,64},{64,128},{128,192},{192,256},{256,320},{320,384},{384,448},... | collective-permute-start | bytes 786440 | tf_op jit(solution)/shard_map/ppermute | solution.py:286
  123.8 10.9 %collective-permute-start.21 = (bf16[2,512,128]{2,1,0:T(8,128)(2,1)S(1)}, bf16[2,512,128]{2,1,0:T(8,128)(2,1)S(1)}, u32[]{:S(2)}, u32[]{:S(2)}) collective-permute-start(bf16[2,512,128]{2,1,0:T(8,128)(2,1)S(1)} %shard_map.69), channel_id=1, source_target_pairs={{0,448},{64,0},{128,64},{192,128},{256,192},{320,256},{384,320},{4... | collective-permute-start | bytes 786440 | tf_op jit(solution)/shard_map/ppermute | solution.py:287
  129.0 10.0 %collective-permute-start.18 = (bf16[2,512,128]{2,1,0:T(8,128)(2,1)S(1)}, bf16[2,512,128]{2,1,0:T(8,128)(2,1)S(1)}, u32[]{:S(2)}, u32[]{:S(2)}) collective-permute-start(bf16[2,512,128]{2,1,0:T(8,128)(2,1)S(1)} %shard_map.67), channel_id=1, source_target_pairs={{0,64},{64,128},{128,192},{192,256},{256,320},{320,384},{384,448},... | collective-permute-start | bytes 786440 | tf_op jit(solution)/shard_map/ppermute | solution.py:286
  134.7 9.9 %collective-permute-start.22 = (bf16[2,512,128]{2,1,0:T(8,128)(2,1)S(1)}, bf16[2,512,128]{2,1,0:T(8,128)(2,1)S(1)}, u32[]{:S(2)}, u32[]{:S(2)}) collective-permute-start(bf16[2,512,128]{2,1,0:T(8,128)(2,1)S(1)} %shard_map.70), channel_id=1, source_target_pairs={{0,448},{64,0},{128,64},{192,128},{256,192},{320,256},{384,320},{4... | collective-permute-start | bytes 786440 | tf_op jit(solution)/shard_map/ppermute | solution.py:287
  139.0 9.5 %collective-permute-start.19 = (bf16[2,512,128]{2,1,0:T(8,128)(2,1)S(1)}, bf16[2,512,128]{2,1,0:T(8,128)(2,1)S(1)}, u32[]{:S(2)}, u32[]{:S(2)}) collective-permute-start(bf16[2,512,128]{2,1,0:T(8,128)(2,1)S(1)} %shard_map.68), channel_id=1, source_target_pairs={{0,64},{64,128},{128,192},{192,256},{256,320},{320,384},{384,448},... | collective-permute-start | bytes 786440 | tf_op jit(solution)/shard_map/ppermute | solution.py:286
  144.7 9.5 %collective-permute-start.23 = (bf16[2,512,128]{2,1,0:T(8,128)(2,1)S(1)}, bf16[2,512,128]{2,1,0:T(8,128)(2,1)S(1)}, u32[]{:S(2)}, u32[]{:S(2)}) collective-permute-start(bf16[2,512,128]{2,1,0:T(8,128)(2,1)S(1)} %shard_map.71), channel_id=1, source_target_pairs={{0,448},{64,0},{128,64},{192,128},{256,192},{320,256},{384,320},{4... | collective-permute-start | bytes 786440 | tf_op jit(solution)/shard_map/ppermute | solution.py:287
  154.3 18.8 %collective-permute-start.24 = (bf16[512,128]{1,0:T(8,128)(2,1)S(1)}, bf16[512,128]{1,0:T(8,128)(2,1)S(1)}, u32[]{:S(2)}, u32[]{:S(2)}) collective-permute-start(bf16[512,128]{1,0:T(8,128)(2,1)S(1)} %get-tuple-element.51), channel_id=1, source_target_pairs={{0,512},{512,0},{1,513},{513,1},{2,514},{514,2},{3,515},{515,3},{4... | collective-permute-start | bytes 393224 | tf_op jit(solution)/shard_map/ppermute | solution.py:295

commit v5 on v1

v5 whole, which is shorter than its diff:
```python
import functools

import jax
import jax.numpy as jnp
from jax import lax
from jax.experimental import pallas as pl
from jax.experimental.pallas import tpu as pltpu
from jax.sharding import Mesh
from jax.sharding import PartitionSpec as P

HIGHEST = lax.Precision.HIGHEST
BF16 = jnp.bfloat16
F32 = jnp.float32
EPS = 1e-6
TM = (((0,), (0,)), ((), ()))
NT = (((1,), (1,)), ((), ()))
NN = (((1,), (0,)), ((), ()))
VMEM = pl.BlockSpec(memory_space=pltpu.VMEM)
SMEM = pl.BlockSpec(memory_space=pltpu.SMEM)
ORDER = (4, 3, -3, 2, -2, 1, -1, 0)
PARAMS = pltpu.CompilerParams(vmem_limit_bytes=16 * 1024 * 1024)


def normalize(values):
    centred = values - jnp.mean(values, -1, keepdims=True)
    spread = lax.rsqrt(jnp.mean(centred * centred, -1, keepdims=True) + EPS)
    return centred * spread, spread


def normalize_back(grad, normed, spread):
    inner = jnp.mean(grad * normed, -1, keepdims=True)
    return spread * (grad - jnp.mean(grad, -1, keepdims=True) - normed * inner)


def exact(a, b, dims):
    return lax.dot_general(a, b, dims, precision=HIGHEST, preferred_element_type=F32)


def normalize_rows(piece, normed_ref, at, count):
    step = 16

    def body(i, carry):
        x = piece[pl.ds(pl.multiple_of(i * step, step), step), :].astype(F32)
        centred = x - jnp.mean(x, -1, keepdims=True)
        spread = lax.rsqrt(jnp.mean(centred * centred, -1, keepdims=True) + EPS)
        rows = pl.ds(pl.multiple_of(at + i * step, step), step)
        normed_ref[rows, :] = (centred * spread).astype(BF16)
        return carry

    lax.fori_loop(0, count // step, body, 0)


def normalize_kernel(*refs):
    normed_ref, at = refs[-1], 0
    for piece in refs[:-1]:
        normalize_rows(piece, normed_ref, at, piece.shape[0])
        at += piece.shape[0]


def forward_kernel(*refs, count):
    pieces = refs[:count]
    w_ref, att_ref, q_ref, k_ref, v_ref, prob_ref, sq_ref, sk_ref = refs[count:]
    width = w_ref.shape[1] // 3
    qkv = jnp.concatenate(
        [jnp.dot(p[...], w_ref[...], preferred_element_type=F32) for p in pieces], 0
    )
    q, sq = normalize(qkv[:, :width])
    k, sk = normalize(qkv[:, width : 2 * width])
    v = qkv[:, 2 * width :]
    weights = jnp.exp(exact(q, k, NT) * width ** (-0.5))
    probs = weights / jnp.sum(weights, -1, keepdims=True)
    att_ref[...] = exact(probs, v, NN).T.astype(BF16)
    q_ref[...] = q
    k_ref[...] = k
    v_ref[...] = v
    prob_ref[...] = probs
    sq_ref[...] = jnp.broadcast_to(sq, q.shape)
    sk_ref[...] = jnp.broadcast_to(sk, k.shape)


def backward_kernel(*refs, count):
    pieces = refs[:count]
    w_ref, q_ref, k_ref, v_ref, prob_ref, sq_ref, sk_ref, out_ref = refs[count:]
    width = w_ref.shape[0]
    cot = jnp.concatenate([piece[...] for piece in pieces], 0)
    d_att = lax.dot_general(cot, w_ref[...], NT, preferred_element_type=F32)
    q, k, v, probs = q_ref[...], k_ref[...], v_ref[...], prob_ref[...]
    d_value = exact(probs, d_att, TM)
    d_probs = exact(d_att, v, NT)
    inner = jnp.sum(d_probs * probs, -1, keepdims=True)
    d_scores = probs * (d_probs - inner) * width ** (-0.5)
    d_q = normalize_back(exact(d_scores, k, NN), q, sq_ref[...])
    d_k = normalize_back(exact(d_scores, q, TM), k, sk_ref[...])
    out_ref[:width, :] = d_q.T.astype(BF16)
    out_ref[width : 2 * width, :] = d_k.T.astype(BF16)
    out_ref[2 * width :, :] = d_value.T.astype(BF16)


def terms_kernel(*refs, counts, blocks):
    place_ref, refs = refs[0], refs[1:]
    normed, pieces = refs[: counts[0]], refs[counts[0] : sum(counts)]
    d_ref, att_ref, out_ref = refs[sum(counts) :]
    far, near, width = blocks
    core, here, zh = place_ref[0], place_ref[1], place_ref[2]
    d_all, att = d_ref[...], att_ref[...]
    split = d_all.shape[0]
    for slot, distance in enumerate(ORDER):
        y = lax.rem(here + distance + near, near)
        cols = [
            pl.ds(pl.multiple_of(((z * near + y) * 2 + core) * width, width), width)
            for z in (1 - zh, zh)
        ]
        rhs = jnp.concatenate([jnp.concatenate([p[:, c] for p in normed], 0) for c in cols], 1)
        cot = jnp.concatenate([jnp.concatenate([p[:, c] for p in pieces], 0) for c in cols], 1)
        top = jnp.dot(d_all, rhs, preferred_element_type=F32)
        low = jnp.dot(att, cot, preferred_element_type=F32)
        for i in range(far):
            out_ref[slot * far + i, :split, :] = top[:, i * width : (i + 1) * width].astype(BF16)
            out_ref[slot * far + i, split:, :] = low[:, i * width : (i + 1) * width].astype(BF16)


def sum_kernel(*refs, ats):
    own_ref, theirs_ref, *came = refs[: len(refs) - len(ats)]
    for out_ref, at in zip(refs[len(refs) - len(ats) :], ats):
        total = own_ref[at, :, :].astype(F32) + theirs_ref[at, :, :].astype(F32)
        for ref in came:
            total = total + ref[...].astype(F32)
        out_ref[...] = total.astype(BF16)


def finish_kernel(own_ref, theirs_ref, up_ref, down_ref, other_ref, qkv_ref, out_ref, *, at):
    both = own_ref[at, :, :].astype(F32) + theirs_ref[at, :, :].astype(F32)
    for ref in (up_ref, down_ref, other_ref):
        both = both + ref[...].astype(F32)
    split = qkv_ref.shape[-1]
    qkv_ref[:, 0, :] = both[:split].T
    out_ref[0, :, :] = both[split:]


def swap(n, s):
    return [(i, i ^ s) for i in range(n)]


def turn(n, s):
    return [(i, (i + s) % n) for i in range(n)]


def after(value, *done):
    return lax.optimization_barrier((value, *done))[0]


def normalized(*pieces):
    rows = sum(p.shape[0] for p in pieces)
    return pl.pallas_call(
        normalize_kernel,
        out_shape=jax.ShapeDtypeStruct((rows, pieces[0].shape[1]), BF16),
        in_specs=[VMEM] * len(pieces),
        out_specs=VMEM,
        compiler_params=PARAMS,
    )(*pieces)


def gather(tokens, cotangent, n_z, n_x):
    up, down = turn(n_x, 1), turn(n_x, -1)

    def join(*rows):
        return lax.optimization_barrier(jnp.concatenate(rows, 0))

    def within(rows):
        return [lax.ppermute(rows, "zl", swap(n_z, s)) for s in (2, 3, 1)]

    t_other = lax.ppermute(tokens, "zl", swap(n_z, 4))
    t = join(tokens, t_other)
    t_near = within(t)
    c = join(cotangent, lax.ppermute(after(cotangent, t), "zl", swap(n_z, 4)))
    t = join(t, *t_near)
    t_left = lax.ppermute(t, "x", up)
    t_right = lax.ppermute(t, "x", down)
    normed = normalized(t)
    c_near = within(after(c, normed))
    half = t.shape[0] // 2
    t_top, t_low = lax.optimization_barrier((t_left[:half], t_right[half:]))
    c = join(after(c, t_top, t_low), *c_near)
    t_top = lax.ppermute(t_top, "x", up)
    t_low = lax.ppermute(t_low, "x", down)
    c = after(c, t_top, t_low)
    c_right = lax.ppermute(c, "x", down)
    c_left = lax.ppermute(c, "x", up)
    return [normed, normalized(t_left, t_right, t_top, t_low)], [c, c_left, c_right]


def far_halves(pieces, n_x, *done):
    rows, left, right = pieces
    half = rows.shape[0] // 2
    top = lax.ppermute(after(left, *done)[:half], "x", turn(n_x, 1))
    low = lax.ppermute(after(right, *done)[half:], "x", turn(n_x, -1))
    return [rows, left, right, top, low]


def local(sizes, tokens, cotangent, w_qkv, w_out):
    far, near, cores, n_z, n_x = sizes
    w_head = w_qkv[:, 0, :]
    w_back = w_out[0]
    model, width = w_head.shape[0], w_back.shape[0]
    normed, c_pieces = gather(tokens, cotangent, n_z, n_x)
    c_pieces = far_halves(c_pieces, n_x, normed[-1])
    total = sum(p.shape[0] for p in normed)
    small = jax.ShapeDtypeStruct((total, width), F32)
    att, *saved = pl.pallas_call(
        functools.partial(forward_kernel, count=len(normed)),
        out_shape=[
            jax.ShapeDtypeStruct((width, total), BF16),
            small,
            small,
            small,
            jax.ShapeDtypeStruct((total, total), F32),
            small,
            small,
        ],
        in_specs=[VMEM] * (len(normed) + 1),
        out_specs=[VMEM] * 7,
        compiler_params=PARAMS,
    )(*normed, w_head)
    d_qkv = pl.pallas_call(
        functools.partial(backward_kernel, count=len(c_pieces)),
        out_shape=jax.ShapeDtypeStruct((3 * width, total), BF16),
        in_specs=[VMEM] * (len(c_pieces) + 7),
        out_specs=VMEM,
        compiler_params=PARAMS,
    )(*c_pieces, w_back, *saved)
    blocks = (far, near, model // (far * near * cores))
    one = jax.ShapeDtypeStruct((4 * width, blocks[2]), BF16)
    here = lax.axis_index("y").astype(jnp.int32)
    core = lax.axis_index("c").astype(jnp.int32)
    zh = lax.axis_index("zh").astype(jnp.int32)

    def terms(core):
        return pl.pallas_call(
            functools.partial(
                terms_kernel, counts=(len(normed), len(c_pieces)), blocks=blocks
            ),
            out_shape=jax.ShapeDtypeStruct((far * near, *one.shape), BF16),
            in_specs=[SMEM] + [VMEM] * (len(normed) + len(c_pieces) + 2),
            out_specs=VMEM,
            compiler_params=PARAMS,
        )(jnp.stack([core, here, zh]), *normed, *c_pieces, d_qkv, att)

    theirs = lax.ppermute(terms(1 - core), "c", swap(cores, 1))
    mine = terms(core)

    def place(distance, kept):
        return ORDER.index(distance) * far + kept

    def added(ats, *came):
        return pl.pallas_call(
            functools.partial(sum_kernel, ats=ats),
            out_shape=[one] * len(ats),
            in_specs=[VMEM] * (2 + len(came)),
            out_specs=[VMEM] * len(ats),
            compiler_params=PARAMS,
        )(mine, theirs, *came)

    chains = [(4, 1, 0), (3, -1, 0), (4, -1, 1), (3, 1, 1)]
    first = added([place(n if n == 4 else n * way, kept) for n, way, kept in chains])
    came = {}
    for step in range(4):
        for at, (n, way, kept) in enumerate(chains):
            left = n - step
            if left < 1:
                continue
            if step == 0:
                message = first[at]
            else:
                (message,) = added([place(left * way, kept)], came[way, kept])
            came[way, kept] = lax.ppermute(message, "y", turn(near, way))
    (away,) = added([place(0, 0)], came[1, 0], came[-1, 0])
    other = lax.ppermute(away, "zh", swap(far, 1))
    return pl.pallas_call(
        functools.partial(finish_kernel, at=place(0, 1)),
        out_shape=[
            jax.ShapeDtypeStruct((blocks[2], 1, 3 * width), F32),
            jax.ShapeDtypeStruct((1, width, blocks[2]), F32),
        ],
        in_specs=[VMEM] * 5,
        out_specs=[VMEM] * 2,
        compiler_params=PARAMS,
    )(mine, theirs, came[1, 1], came[-1, 1], other)


def solution(mesh):
    sizes = (2, mesh.shape["dp"] // 4, 2, mesh.shape["mp"] // 4, 4)
    fine = Mesh(mesh.devices.reshape(sizes), ("zh", "y", "c", "zl", "x"))
    dp, mp = ("zh", "y", "c"), ("zl", "x")
    in_specs = (P(dp + mp, None), P(dp + mp, None), P(None, mp, None), P(mp, None, None))
    out_specs = (P(dp, mp, None), P(mp, None, dp))
    return jax.shard_map(
        functools.partial(local, sizes),
        mesh=fine,
        in_specs=in_specs,
        out_specs=out_specs,
        check_vma=False,
    )
```

time: 196 us -> 183 us (0.934); the launches traced: 195 us -> 179 us
  starting transfers between devices: 77.1 us -> 130 us
  waiting for transfers between devices: 75.7 us -> 25.8 us
  between operations: 14.3 us -> 1.26 us
  local copies, waits for them, and re-layouts: 9.93 us -> 4.16 us
  other arithmetic: 4.35 us -> 1.93 us
  Pallas kernels: 13.7 us -> 15.8 us
    reduce_scatter x1 -> x0, waiting for transfers between devices: 53.8 us -> none  [local(): summed = lax.psum_scatter(pair, 'y', scatter_dimension=0, tiled=True)]
    ppermute x15 -> x31, starting transfers between devices: 75.1 us -> 128 us  [the longest x14 46 us: local(): came[way, kept] = lax.ppermute(message, 'y', turn(near, way))]
    ppermute x15 -> x31, waiting for transfers between devices: 17.7 us -> 23.6 us  [the longest x1 5.98 us: local(): other = lax.ppermute(away, 'zh', swap(far, 1))]
    unnamed x15 -> x8, local copies, waits for them, and re-layouts: 5.47 us -> 2.69 us
    pallas_call x4 -> x19, Pallas kernels: 13.7 us -> 15.8 us  [the longest x2 4.02 us: normalized(): pl.pallas_call(normalize_kernel, out_shape=jax.ShapeDtypeStruct((rows, pi...]
  transfers between devices with their start and end apart: 17 -> 32, of which waited for: 7 -> 8; matrix products, arithmetic and copies ran while one was open for 4% -> 1% of each run, Pallas kernels for 4% -> 5%
where the time goes in v5:
time: 183 us; the launch traced here: 179 us
  starting transfers between devices  130 us (71%)
  waiting for transfers between devices  25.8 us (14%)
  Pallas kernels  15.8 us (9%)
  local copies, waits for them, and re-layouts  4.16 us (2%)
  other arithmetic  1.93 us (1%)
    ppermute x14, starting transfers between devices, local(): came[way, kept] = lax.ppermute(message, 'y', turn(near, way))  46 us
    ppermute x6, starting transfers between devices, within(): return [lax.ppermute(rows, 'zl', swap(n_z, s)) for s in (2, 3, 1)]  22.4 us
    ppermute x1, starting transfers between devices, local(): other = lax.ppermute(away, 'zh', swap(far, 1))  13.3 us
    ppermute x1, starting transfers between devices, gather(): t_other = lax.ppermute(tokens, 'zl', swap(n_z, 4))  10.9 us
    ppermute x1, starting transfers between devices, gather(): c = join(cotangent, lax.ppermute(after(cotangent, t), 'zl', swap(n_z, 4)))  8.19 us
    ppermute x1, waiting for transfers between devices, local(): other = lax.ppermute(away, 'zh', swap(far, 1))  5.98 us
    ppermute x6, waiting for transfers between devices, within(): return [lax.ppermute(rows, 'zl', swap(n_z, s)) for s in (2, 3, 1)]  5.76 us
    ppermute x1, waiting for transfers between devices, gather(): t_low = lax.ppermute(t_low, 'x', down)  5.61 us
  transfers between devices with their start and end apart: 32, of which 8 were waited for; matrix products, arithmetic and copies ran while one was open for 1% of the time, Pallas kernels for 5%

profile of v5, /device:TPU:6, one launch (start us, length us, event | category | flops | bytes accessed | tf_op | source)
XLA Modules:
  0.0 179.4 jit_solution(16684357612637443037)
XLA Ops:
  0.6 10.9 %collective-permute-start = (bf16[8,4096]{1,0:T(8,128)(2,1)}, bf16[8,4096]{1,0:T(8,128)(2,1)S(1)}, u32[]{:S(2)}, u32[]{:S(2)}) collective-permute-start(bf16[8,4096]{1,0:T(8,128)(2,1)} %param.4), channel_id=1, source_target_pairs={{0,16},{4,20},{8,24},{12,28},{16,0},{20,4},{24,8},{28,12},{1,17},{... | collective-permute-start | bytes 196616 | tf_op jit(solution)/shard_map/ppermute | solution.py:172
  11.6 2.4 %collective-permute-done = bf16[8,4096]{1,0:T(8,128)(2,1)S(1)} collective-permute-done((bf16[8,4096]{1,0:T(8,128)(2,1)}, bf16[8,4096]{1,0:T(8,128)(2,1)S(1)}, u32[]{:S(2)}, u32[]{:S(2)}) %collective-permute-start) | collective-permute-done | bytes 65568 | tf_op jit(solution)/shard_map/ppermute | solution.py:172
  14.8 4.3 %collective-permute-start.3 = (bf16[16,4096]{1,0:T(8,128)(2,1)S(1)}, bf16[16,4096]{1,0:T(8,128)(2,1)S(1)}, u32[]{:S(2)}, u32[]{:S(2)}) collective-permute-start(bf16[16,4096]{1,0:T(8,128)(2,1)S(1)} %pad_maximum_fusion.2), channel_id=1, source_target_pairs={{0,4},{4,0},{8,12},{12,8},{16,20},{20,16},{24,28},{28,24},{1,5},{5... | collective-permute-start | bytes 393224 | tf_op jit(solution)/shard_map/ppermute | solution.py:170
  19.1 6.4 %collective-permute-start.2 = (bf16[16,4096]{1,0:T(8,128)(2,1)S(1)}, bf16[16,4096]{1,0:T(8,128)(2,1)S(1)}, u32[]{:S(2)}, u32[]{:S(2)}) collective-permute-start(bf16[16,4096]{1,0:T(8,128)(2,1)S(1)} %pad_maximum_fusion.2), channel_id=1, source_target_pairs={{0,12},{4,8},{8,4},{12,0},{16,28},{20,24},{24,20},{28,16},{1,13},{... | collective-permute-start | bytes 393224 | tf_op jit(solution)/shard_map/ppermute | solution.py:170
  25.6 2.5 %collective-permute-start.1 = (bf16[16,4096]{1,0:T(8,128)(2,1)S(1)}, bf16[16,4096]{1,0:T(8,128)(2,1)S(1)}, u32[]{:S(2)}, u32[]{:S(2)}) collective-permute-start(bf16[16,4096]{1,0:T(8,128)(2,1)S(1)} %pad_maximum_fusion.2), channel_id=1, source_target_pairs={{0,8},{4,12},{8,0},{12,4},{16,24},{20,28},{24,16},{28,20},{1,9},{5... | collective-permute-start | bytes 393224 | tf_op jit(solution)/shard_map/ppermute | solution.py:170
  28.1 8.2 %collective-permute-start.8 = (bf16[8,4096]{1,0:T(8,128)(2,1)}, bf16[8,4096]{1,0:T(8,128)(2,1)S(1)}, u32[]{:S(2)}, u32[]{:S(2)}) collective-permute-start(bf16[8,4096]{1,0:T(8,128)(2,1)} %param.5), channel_id=1, source_target_pairs={{0,16},{4,20},{8,24},{12,28},{16,0},{20,4},{24,8},{28,12},{1,17},{... | collective-permute-start | bytes 196616 | tf_op jit(solution)/shard_map/ppermute | solution.py:175
  36.3 4.2 %collective-permute-done.1 = bf16[16,4096]{1,0:T(8,128)(2,1)S(1)} collective-permute-done((bf16[16,4096]{1,0:T(8,128)(2,1)S(1)}, bf16[16,4096]{1,0:T(8,128)(2,1)S(1)}, u32[]{:S(2)}, u32[]{:S(2)}) %collective-permute-start.1) | collective-permute-done | bytes 131104 | tf_op jit(solution)/shard_map/ppermute | solution.py:170
  40.6 2.7 %collective-permute-start.5 = (bf16[64,4096]{1,0:T(8,128)(2,1)S(1)}, bf16[64,4096]{1,0:T(8,128)(2,1)S(1)}, u32[]{:S(2)}, u32[]{:S(2)}) collective-permute-start(bf16[64,4096]{1,0:T(8,128)(2,1)S(1)} %pad_maximum_fusion.refs_0_), channel_id=1, source_target_pairs={{0,3},{1,0},{2,1},{3,2},{4,7},{5,4},{6,5},{7,6},{8,11},{9,8},{10,9... | collective-permute-start | bytes 1572872 | tf_op jit(solution)/shard_map/ppermute | solution.py:178
  43.3 4.3 %collective-permute-start.4 = (bf16[64,4096]{1,0:T(8,128)(2,1)S(1)}, bf16[64,4096]{1,0:T(8,128)(2,1)S(1)}, u32[]{:S(2)}, u32[]{:S(2)}) collective-permute-start(bf16[64,4096]{1,0:T(8,128)(2,1)S(1)} %pad_maximum_fusion.refs_0_), channel_id=1, source_target_pairs={{0,1},{1,2},{2,3},{3,0},{4,5},{5,6},{6,7},{7,4},{8,9},{9,10},{10,1... | collective-permute-start | bytes 1572872 | tf_op jit(solution)/shard_map/ppermute | solution.py:177
  51.4 3.3 %collective-permute-start.10 = (bf16[16,4096]{1,0:T(8,128)(2,1)S(1)}, bf16[16,4096]{1,0:T(8,128)(2,1)S(1)}, u32[]{:S(2)}, u32[]{:S(2)}) collective-permute-start(bf16[16,4096]{1,0:T(8,128)(2,1)S(1)} %pad_maximum_fusion.3), channel_id=1, source_target_pairs={{0,12},{4,8},{8,4},{12,0},{16,28},{20,24},{24,20},{28,16},{1,13},{... | collective-permute-start | bytes 393224 | tf_op jit(solution)/shard_map/ppermute | solution.py:170
  54.8 4.0 %collective-permute-start.9 = (bf16[16,4096]{1,0:T(8,128)(2,1)S(1)}, bf16[16,4096]{1,0:T(8,128)(2,1)S(1)}, u32[]{:S(2)}, u32[]{:S(2)}) collective-permute-start(bf16[16,4096]{1,0:T(8,128)(2,1)S(1)} %pad_maximum_fusion.3), channel_id=1, source_target_pairs={{0,8},{4,12},{8,0},{12,4},{16,24},{20,28},{24,16},{28,20},{1,9},{5... | collective-permute-start | bytes 393224 | tf_op jit(solution)/shard_map/ppermute | solution.py:170
  58.8 4.7 %collective-permute-start.6 = (bf16[32,4096]{1,0:T(8,128)(2,1)S(1)}, bf16[32,4096]{1,0:T(8,128)(2,1)S(1)}, u32[]{:S(2)}, u32[]{:S(2)}) collective-permute-start(bf16[32,4096]{1,0:T(8,128)(2,1)S(1)} %slice.16), channel_id=1, source_target_pairs={{0,1},{1,2},{2,3},{3,0},{4,5},{5,6},{6,7},{7,4},{8,9},{9,10},{10,1... | collective-permute-start | bytes 786440 | tf_op jit(solution)/shard_map/ppermute | solution.py:184
  67.4 5.6 %collective-permute-done.7.refs_3_ = bf16[32,4096]{1,0:T(8,128)(2,1)S(1)} collective-permute-done((bf16[32,4096]{1,0:T(8,128)(2,1)S(1)}, bf16[32,4096]{1,0:T(8,128)(2,1)S(1)}, u32[]{:S(2)}, u32[]{:S(2)}) %collective-permute-start.7) | collective-permute-done | bytes 262176 | tf_op jit(solution)/shard_map/ppermute | solution.py:185
  74.9 5.1 %collective-permute-start.12 = (bf16[64,4096]{1,0:T(8,128)(2,1)S(1)}, bf16[64,4096]{1,0:T(8,128)(2,1)S(1)}, u32[]{:S(2)}, u32[]{:S(2)}) collective-permute-start(bf16[64,4096]{1,0:T(8,128)(2,1)S(1)} %pad_maximum_fusion.1.refs_0_.refs_3_), channel_id=1, source_target_pairs={{0,1},{1,2},{2,3},{3,0},{4,5},{5,6},{6,7},{7,4},{8,9},{9,10},{10,1... | collective-permute-start | bytes 1572872 | tf_op jit(solution)/shard_map/ppermute | solution.py:188
  80.0 3.0 %shard_map.60.refs_1_.refs_2_ = bf16[192,4096]{1,0:T(8,128)(2,1)S(1)} custom-call(bf16[64,4096]{1,0:T(8,128)(2,1)S(1)} %collective-permute-done.4.refs_0_, bf16[64,4096]{1,0:T(8,128)(2,1)S(1)} %collective-permute-done.5.refs_1_, bf16[32,4096]{1,0:T(8,128)(2,1)S(1)} %collective-permute-done.6.refs_2_, bf16[32,4096]{1,0:T(8,128)(2,1)S(1)} %collective-permute-done.7.refs_3_), custom_call_target="tpu_custom_call" | custom-call | tf_op jit(solution)/shard_map/pallas_call | solution.py:154
  83.1 3.4 %collective-permute-done.13.refs_2_.refs_5_ = bf16[64,4096]{1,0:T(8,128)(2,1)S(1)} collective-permute-done((bf16[64,4096]{1,0:T(8,128)(2,1)S(1)}, bf16[64,4096]{1,0:T(8,128)(2,1)S(1)}, u32[]{:S(2)}, u32[]{:S(2)}) %collective-permute-start.13) | collective-permute-done | bytes 524320 | tf_op jit(solution)/shard_map/ppermute | solution.py:187
  90.6 5.1 %collective-permute-start.14 = (bf16[32,4096]{1,0:T(8,128)(2,1)}, bf16[32,4096]{1,0:T(8,128)(2,1)}, u32[]{:S(2)}, u32[]{:S(2)}) collective-permute-start(bf16[32,4096]{1,0:T(8,128)(2,1)} %slice.14), channel_id=1, source_target_pairs={{0,1},{1,2},{2,3},{3,0},{4,5},{5,6},{6,7},{7,4},{8,9},{9,10},{10,1... | collective-permute-start | bytes 786440 | tf_op jit(solution)/shard_map/ppermute | solution.py:195
  97.7 2.7 %shard_map.61 = (bf16[128,256]{1,0:T(8,128)(2,1)S(1)}, f32[256,128]{1,0:T(8,128)S(1)}, f32[256,128]{1,0:T(8,128)S(1)}, f32[256,128]{1,0:T(8,128)S(1)}, f32[256,2...) custom-call(bf16[64,4096]{1,0:T(8,128)(2,1)S(1)} %shard_map.59.refs_0_.refs_1_, ...), custom_call_target="tpu_custom_call" | custom-call | tf_op jit(solution)/shard_map/pallas_call | solution.py:209
  100.5 3.9 %shard_map.62.refs_8_ = bf16[384,256]{1,0:T(8,128)(2,1)S(1)} custom-call(bf16[64,4096]{1,0:T(8,128)(2,1)S(1)} %pad_maximum_fusion.1.refs_0_.refs_3_, bf16[64,4096]{1,0:T(8,128)(2,1)S(1)} %copy-done.1, bf16[64,4096]{1,0:T(8,128)(2,1)S(1)} %collective-permute-done.13.refs_2_.refs_5_, bf16[32,4096]{1,0:T(8,128)(2,1)} %collective-permute-done.14.refs_3_.refs_6_, ...), custom_call_target="tpu_custom_call" | custom-call | tf_op jit(solution)/shard_map/pallas_call | solution.py:224
  110.1 2.2 %collective-permute-done.16.refs_1_.theirs_ref = bf16[16,512,128]{2,1,0:T(8,128)(2,1)S(1)} collective-permute-done((bf16[16,512,128]{2,1,0:T(8,128)(2,1)S(1)}, bf16[16,512,128]{2,1,0:T(8,128)(2,1)S(1)}, u32[]{:S(2)}, u32[]{:S(2)}) %collective-permute-start.16) | collective-permute-done | bytes 2097184 | tf_op jit(solution)/shard_map/ppermute | solution.py:248
  112.4 3.5 %collective-permute-start.24 = (bf16[512,128]{1,0:T(8,128)(2,1)S(1)}, bf16[512,128]{1,0:T(8,128)(2,1)S(1)}, u32[]{:S(2)}, u32[]{:S(2)}) collective-permute-start(bf16[512,128]{1,0:T(8,128)(2,1)S(1)} %get-tuple-element.38), channel_id=1, source_target_pairs={{0,64},{64,128},{128,192},{192,256},{256,320},{320,384},{384,448},... | collective-permute-start | bytes 393224 | tf_op jit(solution)/shard_map/ppermute | solution.py:275
  115.9 3.8 %collective-permute-start.20 = (bf16[512,128]{1,0:T(8,128)(2,1)S(1)}, bf16[512,128]{1,0:T(8,128)(2,1)S(1)}, u32[]{:S(2)}, u32[]{:S(2)}) collective-permute-start(bf16[512,128]{1,0:T(8,128)(2,1)S(1)} %get-tuple-element.37), channel_id=1, source_target_pairs={{0,448},{64,0},{128,64},{192,128},{256,192},{320,256},{384,320},{4... | collective-permute-start | bytes 393224 | tf_op jit(solution)/shard_map/ppermute | solution.py:275
  119.7 3.9 %collective-permute-start.28 = (bf16[512,128]{1,0:T(8,128)(2,1)S(1)}, bf16[512,128]{1,0:T(8,128)(2,1)S(1)}, u32[]{:S(2)}, u32[]{:S(2)}) collective-permute-start(bf16[512,128]{1,0:T(8,128)(2,1)S(1)} %get-tuple-element.39), channel_id=1, source_target_pairs={{0,448},{64,0},{128,64},{192,128},{256,192},{320,256},{384,320},{4... | collective-permute-start | bytes 393224 | tf_op jit(solution)/shard_map/ppermute | solution.py:275
  125.6 2.0 %collective-permute-start.17 = (bf16[512,128]{1,0:T(8,128)(2,1)S(1)}, bf16[512,128]{1,0:T(8,128)(2,1)S(1)}, u32[]{:S(2)}, u32[]{:S(2)}) collective-permute-start(bf16[512,128]{1,0:T(8,128)(2,1)S(1)} %get-tuple-element.36), channel_id=1, source_target_pairs={{0,64},{64,128},{128,192},{192,256},{256,320},{320,384},{384,448},... | collective-permute-start | bytes 393224 | tf_op jit(solution)/shard_map/ppermute | solution.py:275
  127.7 5.0 %collective-permute-start.21 = (bf16[512,128]{1,0:T(8,128)(2,1)S(1)}, bf16[512,128]{1,0:T(8,128)(2,1)S(1)}, u32[]{:S(2)}, u32[]{:S(2)}) collective-permute-start(bf16[512,128]{1,0:T(8,128)(2,1)S(1)} %shard_map.68), channel_id=1, source_target_pairs={{0,448},{64,0},{128,64},{192,128},{256,192},{320,256},{384,320},{4... | collective-permute-start | bytes 393224 | tf_op jit(solution)/shard_map/ppermute | solution.py:275
  132.8 3.9 %collective-permute-start.29 = (bf16[512,128]{1,0:T(8,128)(2,1)S(1)}, bf16[512,128]{1,0:T(8,128)(2,1)S(1)}, u32[]{:S(2)}, u32[]{:S(2)}) collective-permute-start(bf16[512,128]{1,0:T(8,128)(2,1)S(1)} %shard_map.74), channel_id=1, source_target_pairs={{0,448},{64,0},{128,64},{192,128},{256,192},{320,256},{384,320},{4... | collective-permute-start | bytes 393224 | tf_op jit(solution)/shard_map/ppermute | solution.py:275
  138.8 1.9 %collective-permute-start.18 = (bf16[512,128]{1,0:T(8,128)(2,1)S(1)}, bf16[512,128]{1,0:T(8,128)(2,1)S(1)}, u32[]{:S(2)}, u32[]{:S(2)}) collective-permute-start(bf16[512,128]{1,0:T(8,128)(2,1)S(1)} %shard_map.66), channel_id=1, source_target_pairs={{0,64},{64,128},{128,192},{192,256},{256,320},{320,384},{384,448},... | collective-permute-start | bytes 393224 | tf_op jit(solution)/shard_map/ppermute | solution.py:275
  140.8 5.1 %collective-permute-start.22 = (bf16[512,128]{1,0:T(8,128)(2,1)S(1)}, bf16[512,128]{1,0:T(8,128)(2,1)S(1)}, u32[]{:S(2)}, u32[]{:S(2)}) collective-permute-start(bf16[512,128]{1,0:T(8,128)(2,1)S(1)} %shard_map.69), channel_id=1, source_target_pairs={{0,448},{64,0},{128,64},{192,128},{256,192},{320,256},{384,320},{4... | collective-permute-start | bytes 393224 | tf_op jit(solution)/shard_map/ppermute | solution.py:275
  146.0 3.9 %collective-permute-start.30 = (bf16[512,128]{1,0:T(8,128)(2,1)S(1)}, bf16[512,128]{1,0:T(8,128)(2,1)S(1)}, u32[]{:S(2)}, u32[]{:S(2)}) collective-permute-start(bf16[512,128]{1,0:T(8,128)(2,1)S(1)} %shard_map.75), channel_id=1, source_target_pairs={{0,448},{64,0},{128,64},{192,128},{256,192},{320,256},{384,320},{4... | collective-permute-start | bytes 393224 | tf_op jit(solution)/shard_map/ppermute | solution.py:275
  154.0 5.1 %collective-permute-start.23 = (bf16[512,128]{1,0:T(8,128)(2,1)S(1)}, bf16[512,128]{1,0:T(8,128)(2,1)S(1)}, u32[]{:S(2)}, u32[]{:S(2)}) collective-permute-start(bf16[512,128]{1,0:T(8,128)(2,1)S(1)} %shard_map.70), channel_id=1, source_target_pairs={{0,448},{64,0},{128,64},{192,128},{256,192},{320,256},{384,320},{4... | collective-permute-start | bytes 393224 | tf_op jit(solution)/shard_map/ppermute | solution.py:275
  159.2 13.3 %collective-permute-start.31 = (bf16[512,128]{1,0:T(8,128)(2,1)S(1)}, bf16[512,128]{1,0:T(8,128)(2,1)S(1)}, u32[]{:S(2)}, u32[]{:S(2)}) collective-permute-start(bf16[512,128]{1,0:T(8,128)(2,1)S(1)} %shard_map.76), channel_id=1, source_target_pairs={{0,512},{512,0},{1,513},{513,1},{2,514},{514,2},{3,515},{515,3},{4... | collective-permute-start | bytes 393224 | tf_op jit(solution)/shard_map/ppermute | solution.py:277
  172.6 6.0 %collective-permute-done.31.other_ref = bf16[512,128]{1,0:T(8,128)(2,1)S(1)} collective-permute-done((bf16[512,128]{1,0:T(8,128)(2,1)S(1)}, bf16[512,128]{1,0:T(8,128)(2,1)S(1)}, u32[]{:S(2)}, u32[]{:S(2)}) %collective-permute-start.31) | collective-permute-done | bytes 131104 | tf_op jit(solution)/shard_map/ppermute | solution.py:277
  (69 shorter events, 31.6 us)
Async XLA Ops:
  0.6 13.4 %collective-permute-start = (bf16[8,4096]{1,0:T(8,128)(2,1)}, bf16[8,4096]{1,0:T(8,128)(2,1)S(1)}, u32[]{:S(2)}, u32[]{:S(2)}) collective-permute-start(bf16[8,4096]{1,0:T(8,128)(2,1)} %param.4), channel_id=1, source_target_pairs={{0,16},{4,20},{8,24},{12,28},{16,0},{20,4},{24,8},{28,12},{1,17},{... | collective-permute-start | bytes 196616 | tf_op jit(solution)/shard_map/ppermute | solution.py:172
  14.8 21.4 %collective-permute-start.3 = (bf16[16,4096]{1,0:T(8,128)(2,1)S(1)}, bf16[16,4096]{1,0:T(8,128)(2,1)S(1)}, u32[]{:S(2)}, u32[]{:S(2)}) collective-permute-start(bf16[16,4096]{1,0:T(8,128)(2,1)S(1)} %pad_maximum_fusion.2), channel_id=1, source_target_pairs={{0,4},{4,0},{8,12},{12,8},{16,20},{20,16},{24,28},{28,24},{1,5},{5... | collective-permute-start | bytes 393224 | tf_op jit(solution)/shard_map/ppermute | solution.py:170
  19.1 17.1 %collective-permute-start.2 = (bf16[16,4096]{1,0:T(8,128)(2,1)S(1)}, bf16[16,4096]{1,0:T(8,128)(2,1)S(1)}, u32[]{:S(2)}, u32[]{:S(2)}) collective-permute-start(bf16[16,4096]{1,0:T(8,128)(2,1)S(1)} %pad_maximum_fusion.2), channel_id=1, source_target_pairs={{0,12},{4,8},{8,4},{12,0},{16,28},{20,24},{24,20},{28,16},{1,13},{... | collective-permute-start | bytes 393224 | tf_op jit(solution)/shard_map/ppermute | solution.py:170
  25.6 14.9 %collective-permute-start.1 = (bf16[16,4096]{1,0:T(8,128)(2,1)S(1)}, bf16[16,4096]{1,0:T(8,128)(2,1)S(1)}, u32[]{:S(2)}, u32[]{:S(2)}) collective-permute-start(bf16[16,4096]{1,0:T(8,128)(2,1)S(1)} %pad_maximum_fusion.2), channel_id=1, source_target_pairs={{0,8},{4,12},{8,0},{12,4},{16,24},{20,28},{24,16},{28,20},{1,9},{5... | collective-permute-start | bytes 393224 | tf_op jit(solution)/shard_map/ppermute | solution.py:170
  28.1 19.6 %collective-permute-start.8 = (bf16[8,4096]{1,0:T(8,128)(2,1)}, bf16[8,4096]{1,0:T(8,128)(2,1)S(1)}, u32[]{:S(2)}, u32[]{:S(2)}) collective-permute-start(bf16[8,4096]{1,0:T(8,128)(2,1)} %param.5), channel_id=1, source_target_pairs={{0,16},{4,20},{8,24},{12,28},{16,0},{20,4},{24,8},{28,12},{1,17},{... | collective-permute-start | bytes 196616 | tf_op jit(solution)/shard_map/ppermute | solution.py:175
  40.6 18.2 %collective-permute-start.5 = (bf16[64,4096]{1,0:T(8,128)(2,1)S(1)}, bf16[64,4096]{1,0:T(8,128)(2,1)S(1)}, u32[]{:S(2)}, u32[]{:S(2)}) collective-permute-start(bf16[64,4096]{1,0:T(8,128)(2,1)S(1)} %pad_maximum_fusion.refs_0_), channel_id=1, source_target_pairs={{0,3},{1,0},{2,1},{3,2},{4,7},{5,4},{6,5},{7,6},{8,11},{9,8},{10,9... | collective-permute-start | bytes 1572872 | tf_op jit(solution)/shard_map/ppermute | solution.py:178
  43.3 15.5 %collective-permute-start.4 = (bf16[64,4096]{1,0:T(8,128)(2,1)S(1)}, bf16[64,4096]{1,0:T(8,128)(2,1)S(1)}, u32[]{:S(2)}, u32[]{:S(2)}) collective-permute-start(bf16[64,4096]{1,0:T(8,128)(2,1)S(1)} %pad_maximum_fusion.refs_0_), channel_id=1, source_target_pairs={{0,1},{1,2},{2,3},{3,0},{4,5},{5,6},{6,7},{7,4},{8,9},{9,10},{10,1... | collective-permute-start | bytes 1572872 | tf_op jit(solution)/shard_map/ppermute | solution.py:177
  49.5 15.9 %collective-permute-start.11 = (bf16[16,4096]{1,0:T(8,128)(2,1)S(1)}, bf16[16,4096]{1,0:T(8,128)(2,1)S(1)}, u32[]{:S(2)}, u32[]{:S(2)}) collective-permute-start(bf16[16,4096]{1,0:T(8,128)(2,1)S(1)} %pad_maximum_fusion.3), channel_id=1, source_target_pairs={{0,4},{4,0},{8,12},{12,8},{16,20},{20,16},{24,28},{28,24},{1,5},{5... | collective-permute-start | bytes 393224 | tf_op jit(solution)/shard_map/ppermute | solution.py:170
  51.4 14.0 %collective-permute-start.10 = (bf16[16,4096]{1,0:T(8,128)(2,1)S(1)}, bf16[16,4096]{1,0:T(8,128)(2,1)S(1)}, u32[]{:S(2)}, u32[]{:S(2)}) collective-permute-start(bf16[16,4096]{1,0:T(8,128)(2,1)S(1)} %pad_maximum_fusion.3), channel_id=1, source_target_pairs={{0,12},{4,8},{8,4},{12,0},{16,28},{20,24},{24,20},{28,16},{1,13},{... | collective-permute-start | bytes 393224 | tf_op jit(solution)/shard_map/ppermute | solution.py:170
  54.8 12.2 %collective-permute-start.9 = (bf16[16,4096]{1,0:T(8,128)(2,1)S(1)}, bf16[16,4096]{1,0:T(8,128)(2,1)S(1)}, u32[]{:S(2)}, u32[]{:S(2)}) collective-permute-start(bf16[16,4096]{1,0:T(8,128)(2,1)S(1)} %pad_maximum_fusion.3), channel_id=1, source_target_pairs={{0,8},{4,12},{8,0},{12,4},{16,24},{20,28},{24,16},{28,20},{1,9},{5... | collective-permute-start | bytes 393224 | tf_op jit(solution)/shard_map/ppermute | solution.py:170
  58.8 8.6 %collective-permute-start.6 = (bf16[32,4096]{1,0:T(8,128)(2,1)S(1)}, bf16[32,4096]{1,0:T(8,128)(2,1)S(1)}, u32[]{:S(2)}, u32[]{:S(2)}) collective-permute-start(bf16[32,4096]{1,0:T(8,128)(2,1)S(1)} %slice.16), channel_id=1, source_target_pairs={{0,1},{1,2},{2,3},{3,0},{4,5},{5,6},{6,7},{7,4},{8,9},{9,10},{10,1... | collective-permute-start | bytes 786440 | tf_op jit(solution)/shard_map/ppermute | solution.py:184
  63.5 9.5 %collective-permute-start.7 = (bf16[32,4096]{1,0:T(8,128)(2,1)S(1)}, bf16[32,4096]{1,0:T(8,128)(2,1)S(1)}, u32[]{:S(2)}, u32[]{:S(2)}) collective-permute-start(bf16[32,4096]{1,0:T(8,128)(2,1)S(1)} %slice.17), channel_id=1, source_target_pairs={{0,3},{1,0},{2,1},{3,2},{4,7},{5,4},{6,5},{7,6},{8,11},{9,8},{10,9... | collective-permute-start | bytes 786440 | tf_op jit(solution)/shard_map/ppermute | solution.py:185
  73.0 13.5 %collective-permute-start.13 = (bf16[64,4096]{1,0:T(8,128)(2,1)S(1)}, bf16[64,4096]{1,0:T(8,128)(2,1)S(1)}, u32[]{:S(2)}, u32[]{:S(2)}) collective-permute-start(bf16[64,4096]{1,0:T(8,128)(2,1)S(1)} %pad_maximum_fusion.1.refs_0_.refs_3_), channel_id=1, source_target_pairs={{0,3},{1,0},{2,1},{3,2},{4,7},{5,4},{6,5},{7,6},{8,11},{9,8},{10,9... | collective-permute-start | bytes 1572872 | tf_op jit(solution)/shard_map/ppermute | solution.py:187
  74.9 14.2 %collective-permute-start.12 = (bf16[64,4096]{1,0:T(8,128)(2,1)S(1)}, bf16[64,4096]{1,0:T(8,128)(2,1)S(1)}, u32[]{:S(2)}, u32[]{:S(2)}) collective-permute-start(bf16[64,4096]{1,0:T(8,128)(2,1)S(1)} %pad_maximum_fusion.1.refs_0_.refs_3_), channel_id=1, source_target_pairs={{0,1},{1,2},{2,3},{3,0},{4,5},{5,6},{6,7},{7,4},{8,9},{9,10},{10,1... | collective-permute-start | bytes 1572872 | tf_op jit(solution)/shard_map/ppermute | solution.py:188
  87.2 13.2 %collective-permute-start.15 = (bf16[32,4096]{1,0:T(8,128)(2,1)}, bf16[32,4096]{1,0:T(8,128)(2,1)S(1)}, u32[]{:S(2)}, u32[]{:S(2)}) collective-permute-start(bf16[32,4096]{1,0:T(8,128)(2,1)} %slice.15), channel_id=1, source_target_pairs={{0,3},{1,0},{2,1},{3,2},{4,7},{5,4},{6,5},{7,6},{8,11},{9,8},{10,9... | collective-permute-start | bytes 786440 | tf_op jit(solution)/shard_map/ppermute | solution.py:196
  90.6 9.8 %collective-permute-start.14 = (bf16[32,4096]{1,0:T(8,128)(2,1)}, bf16[32,4096]{1,0:T(8,128)(2,1)}, u32[]{:S(2)}, u32[]{:S(2)}) collective-permute-start(bf16[32,4096]{1,0:T(8,128)(2,1)} %slice.14), channel_id=1, source_target_pairs={{0,1},{1,2},{2,3},{3,0},{4,5},{5,6},{6,7},{7,4},{8,9},{9,10},{10,1... | collective-permute-start | bytes 786440 | tf_op jit(solution)/shard_map/ppermute | solution.py:195
  106.2 6.1 %collective-permute-start.16 = (bf16[16,512,128]{2,1,0:T(8,128)(2,1)S(1)}, bf16[16,512,128]{2,1,0:T(8,128)(2,1)S(1)}, u32[]{:S(2)}, u32[]{:S(2)}) collective-permute-start(bf16[16,512,128]{2,1,0:T(8,128)(2,1)S(1)} %shard_map.64), channel_id=1, source_target_pairs={{0,32},{32,0},{1,33},{33,1},{2,34},{34,2},{3,35},{35,3},{4,36},{36... | collective-permute-start | bytes 6291464 | tf_op jit(solution)/shard_map/ppermute | solution.py:248
  112.4 11.2 %collective-permute-start.24 = (bf16[512,128]{1,0:T(8,128)(2,1)S(1)}, bf16[512,128]{1,0:T(8,128)(2,1)S(1)}, u32[]{:S(2)}, u32[]{:S(2)}) collective-permute-start(bf16[512,128]{1,0:T(8,128)(2,1)S(1)} %get-tuple-element.38), channel_id=1, source_target_pairs={{0,64},{64,128},{128,192},{192,256},{256,320},{320,384},{384,448},... | collective-permute-start | bytes 393224 | tf_op jit(solution)/shard_map/ppermute | solution.py:275
  115.9 11.8 %collective-permute-start.20 = (bf16[512,128]{1,0:T(8,128)(2,1)S(1)}, bf16[512,128]{1,0:T(8,128)(2,1)S(1)}, u32[]{:S(2)}, u32[]{:S(2)}) collective-permute-start(bf16[512,128]{1,0:T(8,128)(2,1)S(1)} %get-tuple-element.37), channel_id=1, source_target_pairs={{0,448},{64,0},{128,64},{192,128},{256,192},{320,256},{384,320},{4... | collective-permute-start | bytes 393224 | tf_op jit(solution)/shard_map/ppermute | solution.py:275
  119.7 13.1 %collective-permute-start.28 = (bf16[512,128]{1,0:T(8,128)(2,1)S(1)}, bf16[512,128]{1,0:T(8,128)(2,1)S(1)}, u32[]{:S(2)}, u32[]{:S(2)}) collective-permute-start(bf16[512,128]{1,0:T(8,128)(2,1)S(1)} %get-tuple-element.39), channel_id=1, source_target_pairs={{0,448},{64,0},{128,64},{192,128},{256,192},{320,256},{384,320},{4... | collective-permute-start | bytes 393224 | tf_op jit(solution)/shard_map/ppermute | solution.py:275
  123.7 13.1 %collective-permute-start.25 = (bf16[512,128]{1,0:T(8,128)(2,1)S(1)}, bf16[512,128]{1,0:T(8,128)(2,1)S(1)}, u32[]{:S(2)}, u32[]{:S(2)}) collective-permute-start(bf16[512,128]{1,0:T(8,128)(2,1)S(1)} %shard_map.71), channel_id=1, source_target_pairs={{0,64},{64,128},{128,192},{192,256},{256,320},{320,384},{384,448},... | collective-permute-start | bytes 393224 | tf_op jit(solution)/shard_map/ppermute | solution.py:275
  125.6 13.1 %collective-permute-start.17 = (bf16[512,128]{1,0:T(8,128)(2,1)S(1)}, bf16[512,128]{1,0:T(8,128)(2,1)S(1)}, u32[]{:S(2)}, u32[]{:S(2)}) collective-permute-start(bf16[512,128]{1,0:T(8,128)(2,1)S(1)} %get-tuple-element.36), channel_id=1, source_target_pairs={{0,64},{64,128},{128,192},{192,256},{256,320},{320,384},{384,448},... | collective-permute-start | bytes 393224 | tf_op jit(solution)/shard_map/ppermute | solution.py:275
  127.7 13.0 %collective-permute-start.21 = (bf16[512,128]{1,0:T(8,128)(2,1)S(1)}, bf16[512,128]{1,0:T(8,128)(2,1)S(1)}, u32[]{:S(2)}, u32[]{:S(2)}) collective-permute-start(bf16[512,128]{1,0:T(8,128)(2,1)S(1)} %shard_map.68), channel_id=1, source_target_pairs={{0,448},{64,0},{128,64},{192,128},{256,192},{320,256},{384,320},{4... | collective-permute-start | bytes 393224 | tf_op jit(solution)/shard_map/ppermute | solution.py:275
  132.8 13.1 %collective-permute-start.29 = (bf16[512,128]{1,0:T(8,128)(2,1)S(1)}, bf16[512,128]{1,0:T(8,128)(2,1)S(1)}, u32[]{:S(2)}, u32[]{:S(2)}) collective-permute-start(bf16[512,128]{1,0:T(8,128)(2,1)S(1)} %shard_map.74), channel_id=1, source_target_pairs={{0,448},{64,0},{128,64},{192,128},{256,192},{320,256},{384,320},{4... | collective-permute-start | bytes 393224 | tf_op jit(solution)/shard_map/ppermute | solution.py:275
  136.8 13.1 %collective-permute-start.26 = (bf16[512,128]{1,0:T(8,128)(2,1)S(1)}, bf16[512,128]{1,0:T(8,128)(2,1)S(1)}, u32[]{:S(2)}, u32[]{:S(2)}) collective-permute-start(bf16[512,128]{1,0:T(8,128)(2,1)S(1)} %shard_map.72), channel_id=1, source_target_pairs={{0,64},{64,128},{128,192},{192,256},{256,320},{320,384},{384,448},... | collective-permute-start | bytes 393224 | tf_op jit(solution)/shard_map/ppermute | solution.py:275
  138.8 13.1 %collective-permute-start.18 = (bf16[512,128]{1,0:T(8,128)(2,1)S(1)}, bf16[512,128]{1,0:T(8,128)(2,1)S(1)}, u32[]{:S(2)}, u32[]{:S(2)}) collective-permute-start(bf16[512,128]{1,0:T(8,128)(2,1)S(1)} %shard_map.66), channel_id=1, source_target_pairs={{0,64},{64,128},{128,192},{192,256},{256,320},{320,384},{384,448},... | collective-permute-start | bytes 393224 | tf_op jit(solution)/shard_map/ppermute | solution.py:275
  140.8 13.1 %collective-permute-start.22 = (bf16[512,128]{1,0:T(8,128)(2,1)S(1)}, bf16[512,128]{1,0:T(8,128)(2,1)S(1)}, u32[]{:S(2)}, u32[]{:S(2)}) collective-permute-start(bf16[512,128]{1,0:T(8,128)(2,1)S(1)} %shard_map.69), channel_id=1, source_target_pairs={{0,448},{64,0},{128,64},{192,128},{256,192},{320,256},{384,320},{4... | collective-permute-start | bytes 393224 | tf_op jit(solution)/shard_map/ppermute | solution.py:275
  146.0 13.1 %collective-permute-start.30 = (bf16[512,128]{1,0:T(8,128)(2,1)S(1)}, bf16[512,128]{1,0:T(8,128)(2,1)S(1)}, u32[]{:S(2)}, u32[]{:S(2)}) collective-permute-start(bf16[512,128]{1,0:T(8,128)(2,1)S(1)} %shard_map.75), channel_id=1, source_target_pairs={{0,448},{64,0},{128,64},{192,128},{256,192},{320,256},{384,320},{4... | collective-permute-start | bytes 393224 | tf_op jit(solution)/shard_map/ppermute | solution.py:275
  150.0 9.2 %collective-permute-start.27 = (bf16[512,128]{1,0:T(8,128)(2,1)S(1)}, bf16[512,128]{1,0:T(8,128)(2,1)S(1)}, u32[]{:S(2)}, u32[]{:S(2)}) collective-permute-start(bf16[512,128]{1,0:T(8,128)(2,1)S(1)} %shard_map.73), channel_id=1, source_target_pairs={{0,64},{64,128},{128,192},{192,256},{256,320},{320,384},{384,448},... | collective-permute-start | bytes 393224 | tf_op jit(solution)/shard_map/ppermute | solution.py:275
  152.0 20.5 %collective-permute-start.19 = (bf16[512,128]{1,0:T(8,128)(2,1)S(1)}, bf16[512,128]{1,0:T(8,128)(2,1)S(1)}, u32[]{:S(2)}, u32[]{:S(2)}) collective-permute-start(bf16[512,128]{1,0:T(8,128)(2,1)S(1)} %shard_map.67), channel_id=1, source_target_pairs={{0,64},{64,128},{128,192},{192,256},{256,320},{320,384},{384,448},... | collective-permute-start | bytes 393224 | tf_op jit(solution)/shard_map/ppermute | solution.py:275
  154.0 18.5 %collective-permute-start.23 = (bf16[512,128]{1,0:T(8,128)(2,1)S(1)}, bf16[512,128]{1,0:T(8,128)(2,1)S(1)}, u32[]{:S(2)}, u32[]{:S(2)}) collective-permute-start(bf16[512,128]{1,0:T(8,128)(2,1)S(1)} %shard_map.70), channel_id=1, source_target_pairs={{0,448},{64,0},{128,64},{192,128},{256,192},{320,256},{384,320},{4... | collective-permute-start | bytes 393224 | tf_op jit(solution)/shard_map/ppermute | solution.py:275
  159.2 19.3 %collective-permute-start.31 = (bf16[512,128]{1,0:T(8,128)(2,1)S(1)}, bf16[512,128]{1,0:T(8,128)(2,1)S(1)}, u32[]{:S(2)}, u32[]{:S(2)}) collective-permute-start(bf16[512,128]{1,0:T(8,128)(2,1)S(1)} %shard_map.76), channel_id=1, source_target_pairs={{0,512},{512,0},{1,513},{513,1},{2,514},{514,2},{3,515},{515,3},{4... | collective-permute-start | bytes 393224 | tf_op jit(solution)/shard_map/ppermute | solution.py:277
  (4 other events, 8.1 us)

commit v6 on v5

--- a/solution.py
+++ b/solution.py
@@ -119,19 +119,33 @@
             out_ref[slot * far + i, split:, :] = low[:, i * width : (i + 1) * width].astype(BF16)
 
 
-def sum_kernel(*refs, ats):
-    own_ref, theirs_ref, *came = refs[: len(refs) - len(ats)]
-    for out_ref, at in zip(refs[len(refs) - len(ats) :], ats):
-        total = own_ref[at, :, :].astype(F32) + theirs_ref[at, :, :].astype(F32)
-        for ref in came:
-            total = total + ref[...].astype(F32)
-        out_ref[...] = total.astype(BF16)
+def first_kernel(own_ref, theirs_ref, up_ref, down_ref):
+    for at, out_ref in enumerate((up_ref, down_ref)):
+        out_ref[...] = (own_ref[at, :, :].astype(F32) + theirs_ref[at, :, :].astype(F32)).astype(BF16)
+
+
+def sum_kernel(own_ref, theirs_ref, came_ref, out_ref, *, at, half):
+    for i in range(2):
+        total = own_ref[at + i, :, :].astype(F32) + theirs_ref[at + i, :, :].astype(F32)
+        if half is None:
+            total = total + came_ref[i, :, :].astype(F32)
+        elif half == i:
+            total = total + came_ref[...].astype(F32)
+        out_ref[i, :, :] = total.astype(BF16)
+
+
+def away_kernel(own_ref, theirs_ref, up_ref, down_ref, out_ref, *, at):
+    total = own_ref[at, :, :].astype(F32) + theirs_ref[at, :, :].astype(F32)
+    for ref in (up_ref, down_ref):
+        total = total + ref[0, :, :].astype(F32)
+    out_ref[...] = total.astype(BF16)
 
 
 def finish_kernel(own_ref, theirs_ref, up_ref, down_ref, other_ref, qkv_ref, out_ref, *, at):
     both = own_ref[at, :, :].astype(F32) + theirs_ref[at, :, :].astype(F32)
-    for ref in (up_ref, down_ref, other_ref):
-        both = both + ref[...].astype(F32)
+    for ref in (up_ref, down_ref):
+        both = both + ref[1, :, :].astype(F32)
+    both = both + other_ref[...].astype(F32)
     split = qkv_ref.shape[-1]
     qkv_ref[:, 0, :] = both[:split].T
     out_ref[0, :, :] = both[split:]
@@ -178,23 +192,13 @@
     t_right = lax.ppermute(t, "x", down)
     normed = normalized(t)
     c_near = within(after(c, normed))
-    half = t.shape[0] // 2
-    t_top, t_low = lax.optimization_barrier((t_left[:half], t_right[half:]))
-    c = join(after(c, t_top, t_low), *c_near)
-    t_top = lax.ppermute(t_top, "x", up)
-    t_low = lax.ppermute(t_low, "x", down)
-    c = after(c, t_top, t_low)
+    c = join(after(c, t_left, t_right), *c_near)
+    t_far = lax.ppermute(t_left, "x", up)
     c_right = lax.ppermute(c, "x", down)
     c_left = lax.ppermute(c, "x", up)
-    return [normed, normalized(t_left, t_right, t_top, t_low)], [c, c_left, c_right]
-
-
-def far_halves(pieces, n_x, *done):
-    rows, left, right = pieces
-    half = rows.shape[0] // 2
-    top = lax.ppermute(after(left, *done)[:half], "x", turn(n_x, 1))
-    low = lax.ppermute(after(right, *done)[half:], "x", turn(n_x, -1))
-    return [rows, left, right, top, low]
+    rest = normalized(t_left, t_right, t_far)
+    c_far = lax.ppermute(after(c_right, rest), "x", down)
+    return [normed, rest], [c, c_left, c_right, c_far]
 
 
 def local(sizes, tokens, cotangent, w_qkv, w_out):
@@ -203,7 +207,6 @@
     w_back = w_out[0]
     model, width = w_head.shape[0], w_back.shape[0]
     normed, c_pieces = gather(tokens, cotangent, n_z, n_x)
-    c_pieces = far_halves(c_pieces, n_x, normed[-1])
     total = sum(p.shape[0] for p in normed)
     small = jax.ShapeDtypeStruct((total, width), F32)
     att, *saved = pl.pallas_call(
@@ -248,35 +251,31 @@
     theirs = lax.ppermute(terms(1 - core), "c", swap(cores, 1))
     mine = terms(core)
 
-    def place(distance, kept):
-        return ORDER.index(distance) * far + kept
-
-    def added(ats, *came):
+    two = jax.ShapeDtypeStruct((far, *one.shape), BF16)
+
+    def call(kernel, shapes, *came):
         return pl.pallas_call(
-            functools.partial(sum_kernel, ats=ats),
-            out_shape=[one] * len(ats),
+            kernel,
+            out_shape=shapes,
             in_specs=[VMEM] * (2 + len(came)),
-            out_specs=[VMEM] * len(ats),
+            out_specs=[VMEM] * len(shapes),
             compiler_params=PARAMS,
         )(mine, theirs, *came)
 
-    chains = [(4, 1, 0), (3, -1, 0), (4, -1, 1), (3, 1, 1)]
-    first = added([place(n if n == 4 else n * way, kept) for n, way, kept in chains])
-    came = {}
-    for step in range(4):
-        for at, (n, way, kept) in enumerate(chains):
-            left = n - step
-            if left < 1:
-                continue
-            if step == 0:
-                message = first[at]
-            else:
-                (message,) = added([place(left * way, kept)], came[way, kept])
-            came[way, kept] = lax.ppermute(message, "y", turn(near, way))
-    (away,) = added([place(0, 0)], came[1, 0], came[-1, 0])
+    goes = list(call(first_kernel, [one, one]))
+    for distance in (3, 2, 1, 0):
+        goes = [lax.ppermute(m, "y", turn(near, way)) for m, way in zip(goes, (1, -1))]
+        if distance == 0:
+            break
+        for i, way in enumerate((1, -1)):
+            at = ORDER.index(distance * way) * far
+            half = i if distance == 3 else None
+            (goes[i],) = call(functools.partial(sum_kernel, at=at, half=half), [two], goes[i])
+    at = ORDER.index(0) * far
+    (away,) = call(functools.partial(away_kernel, at=at), [one], *goes)
     other = lax.ppermute(away, "zh", swap(far, 1))
     return pl.pallas_call(
-        functools.partial(finish_kernel, at=place(0, 1)),
+        functools.partial(finish_kernel, at=at + 1),
         out_shape=[
             jax.ShapeDtypeStruct((blocks[2], 1, 3 * width), F32),
             jax.ShapeDtypeStruct((1, width, blocks[2]), F32),
@@ -284,7 +283,7 @@
         in_specs=[VMEM] * 5,
         out_specs=[VMEM] * 2,
         compiler_params=PARAMS,
-    )(mine, theirs, came[1, 1], came[-1, 1], other)
+    )(mine, theirs, *goes, other)
 
 
 def solution(mesh):

time: 183 us -> 174 us (0.951); the launches traced: 179 us -> 173 us
  starting transfers between devices: 130 us -> 107 us
  waiting for transfers between devices: 25.8 us -> 44.7 us
  local copies, waits for them, and re-layouts: 4.16 us -> 1.89 us
    ppermute x18 -> x10, starting transfers between devices: 59.6 us -> 36.5 us  [the longest x8 29.9 us: local(): lax.ppermute(m, 'y', turn(near, way))]
    ppermute x18 -> x10, waiting for transfers between devices: 6.02 us -> 22.1 us  [the longest x8 13.7 us: local(): lax.ppermute(m, 'y', turn(near, way))]
    ppermute x1, waiting for transfers between devices: 3.41 us -> 5.67 us  [gather(): c_right = lax.ppermute(c, 'x', down)]
    ppermute x6, waiting for transfers between devices: 5.76 us -> 7.72 us  [within(): return [lax.ppermute(rows, 'zl', swap(n_z, s)) for s in (2, 3, 1)]]
  transfers between devices with their start and end apart: 32 -> 24, of which waited for: 8 -> 12; matrix products, arithmetic and copies ran while one was open for 1% -> 1% of each run, Pallas kernels for 5% -> 5%
where the time goes in v6:
time: 174 us; the launch traced here: 173 us
  starting transfers between devices  107 us (61%)
  waiting for transfers between devices  44.7 us (26%)
  Pallas kernels  16.5 us (9%)
  other arithmetic  1.93 us (1%)
  local copies, waits for them, and re-layouts  1.89 us (1%)
    ppermute x8, starting transfers between devices, local(): lax.ppermute(m, 'y', turn(near, way))  29.9 us
    ppermute x6, starting transfers between devices, within(): return [lax.ppermute(rows, 'zl', swap(n_z, s)) for s in (2, 3, 1)]  22.4 us
    ppermute x8, waiting for transfers between devices, local(): lax.ppermute(m, 'y', turn(near, way))  13.7 us
    ppermute x1, starting transfers between devices, local(): other = lax.ppermute(away, 'zh', swap(far, 1))  13.3 us
    ppermute x1, starting transfers between devices, gather(): t_other = lax.ppermute(tokens, 'zl', swap(n_z, 4))  10.9 us
    ppermute x1, waiting for transfers between devices, gather(): c_far = lax.ppermute(after(c_right, rest), 'x', down)  8.36 us
    ppermute x1, starting transfers between devices, gather(): c = join(cotangent, lax.ppermute(after(cotangent, t), 'zl', swap(n_z, 4)))  8.19 us
    ppermute x6, waiting for transfers between devices, within(): return [lax.ppermute(rows, 'zl', swap(n_z, s)) for s in (2, 3, 1)]  7.72 us
  transfers between devices with their start and end apart: 24, of which 12 were waited for; matrix products, arithmetic and copies ran while one was open for 1% of the time, Pallas kernels for 5%

profile of v6, /device:TPU:6, one launch (start us, length us, event | category | flops | bytes accessed | tf_op | source)
XLA Modules:
  0.0 173.4 jit_solution(9130623338568290276)
XLA Ops:
  0.6 10.9 %collective-permute-start = (bf16[8,4096]{1,0:T(8,128)(2,1)}, bf16[8,4096]{1,0:T(8,128)(2,1)S(1)}, u32[]{:S(2)}, u32[]{:S(2)}) collective-permute-start(bf16[8,4096]{1,0:T(8,128)(2,1)} %param.4), channel_id=1, source_target_pairs={{0,16},{4,20},{8,24},{12,28},{16,0},{20,4},{24,8},{28,12},{1,17},{... | collective-permute-start | bytes 196616 | tf_op jit(solution)/shard_map/ppermute | solution.py:186
  11.6 2.4 %collective-permute-done = bf16[8,4096]{1,0:T(8,128)(2,1)S(1)} collective-permute-done((bf16[8,4096]{1,0:T(8,128)(2,1)}, bf16[8,4096]{1,0:T(8,128)(2,1)S(1)}, u32[]{:S(2)}, u32[]{:S(2)}) %collective-permute-start) | collective-permute-done | bytes 65568 | tf_op jit(solution)/shard_map/ppermute | solution.py:186
  14.8 4.3 %collective-permute-start.3 = (bf16[16,4096]{1,0:T(8,128)(2,1)S(1)}, bf16[16,4096]{1,0:T(8,128)(2,1)S(1)}, u32[]{:S(2)}, u32[]{:S(2)}) collective-permute-start(bf16[16,4096]{1,0:T(8,128)(2,1)S(1)} %pad_maximum_fusion.2), channel_id=1, source_target_pairs={{0,4},{4,0},{8,12},{12,8},{16,20},{20,16},{24,28},{28,24},{1,5},{5... | collective-permute-start | bytes 393224 | tf_op jit(solution)/shard_map/ppermute | solution.py:184
  19.1 6.4 %collective-permute-start.2 = (bf16[16,4096]{1,0:T(8,128)(2,1)S(1)}, bf16[16,4096]{1,0:T(8,128)(2,1)S(1)}, u32[]{:S(2)}, u32[]{:S(2)}) collective-permute-start(bf16[16,4096]{1,0:T(8,128)(2,1)S(1)} %pad_maximum_fusion.2), channel_id=1, source_target_pairs={{0,12},{4,8},{8,4},{12,0},{16,28},{20,24},{24,20},{28,16},{1,13},{... | collective-permute-start | bytes 393224 | tf_op jit(solution)/shard_map/ppermute | solution.py:184
  25.6 2.5 %collective-permute-start.1 = (bf16[16,4096]{1,0:T(8,128)(2,1)S(1)}, bf16[16,4096]{1,0:T(8,128)(2,1)S(1)}, u32[]{:S(2)}, u32[]{:S(2)}) collective-permute-start(bf16[16,4096]{1,0:T(8,128)(2,1)S(1)} %pad_maximum_fusion.2), channel_id=1, source_target_pairs={{0,8},{4,12},{8,0},{12,4},{16,24},{20,28},{24,16},{28,20},{1,9},{5... | collective-permute-start | bytes 393224 | tf_op jit(solution)/shard_map/ppermute | solution.py:184
  28.1 8.2 %collective-permute-start.7 = (bf16[8,4096]{1,0:T(8,128)(2,1)}, bf16[8,4096]{1,0:T(8,128)(2,1)S(1)}, u32[]{:S(2)}, u32[]{:S(2)}) collective-permute-start(bf16[8,4096]{1,0:T(8,128)(2,1)} %param.5), channel_id=1, source_target_pairs={{0,16},{4,20},{8,24},{12,28},{16,0},{20,4},{24,8},{28,12},{1,17},{... | collective-permute-start | bytes 196616 | tf_op jit(solution)/shard_map/ppermute | solution.py:189
  36.3 4.2 %collective-permute-done.1 = bf16[16,4096]{1,0:T(8,128)(2,1)S(1)} collective-permute-done((bf16[16,4096]{1,0:T(8,128)(2,1)S(1)}, bf16[16,4096]{1,0:T(8,128)(2,1)S(1)}, u32[]{:S(2)}, u32[]{:S(2)}) %collective-permute-start.1) | collective-permute-done | bytes 131104 | tf_op jit(solution)/shard_map/ppermute | solution.py:184
  40.6 2.7 %collective-permute-start.5 = (bf16[64,4096]{1,0:T(8,128)(2,1)S(1)}, bf16[64,4096]{1,0:T(8,128)(2,1)S(1)}, u32[]{:S(2)}, u32[]{:S(2)}) collective-permute-start(bf16[64,4096]{1,0:T(8,128)(2,1)S(1)} %pad_maximum_fusion.refs_0_), channel_id=1, source_target_pairs={{0,3},{1,0},{2,1},{3,2},{4,7},{5,4},{6,5},{7,6},{8,11},{9,8},{10,9... | collective-permute-start | bytes 1572872 | tf_op jit(solution)/shard_map/ppermute | solution.py:192
  43.3 4.3 %collective-permute-start.4 = (bf16[64,4096]{1,0:T(8,128)(2,1)S(1)}, bf16[64,4096]{1,0:T(8,128)(2,1)S(1)}, u32[]{:S(2)}, u32[]{:S(2)}) collective-permute-start(bf16[64,4096]{1,0:T(8,128)(2,1)S(1)} %pad_maximum_fusion.refs_0_), channel_id=1, source_target_pairs={{0,1},{1,2},{2,3},{3,0},{4,5},{5,6},{6,7},{7,4},{8,9},{9,10},{10,1... | collective-permute-start | bytes 1572872 | tf_op jit(solution)/shard_map/ppermute | solution.py:191
  51.4 3.3 %collective-permute-start.9 = (bf16[16,4096]{1,0:T(8,128)(2,1)S(1)}, bf16[16,4096]{1,0:T(8,128)(2,1)S(1)}, u32[]{:S(2)}, u32[]{:S(2)}) collective-permute-start(bf16[16,4096]{1,0:T(8,128)(2,1)S(1)} %pad_maximum_fusion.3), channel_id=1, source_target_pairs={{0,12},{4,8},{8,4},{12,0},{16,28},{20,24},{24,20},{28,16},{1,13},{... | collective-permute-start | bytes 393224 | tf_op jit(solution)/shard_map/ppermute | solution.py:184
  54.8 4.0 %collective-permute-start.8 = (bf16[16,4096]{1,0:T(8,128)(2,1)S(1)}, bf16[16,4096]{1,0:T(8,128)(2,1)S(1)}, u32[]{:S(2)}, u32[]{:S(2)}) collective-permute-start(bf16[16,4096]{1,0:T(8,128)(2,1)S(1)} %pad_maximum_fusion.3), channel_id=1, source_target_pairs={{0,8},{4,12},{8,0},{12,4},{16,24},{20,28},{24,16},{28,20},{1,9},{5... | collective-permute-start | bytes 393224 | tf_op jit(solution)/shard_map/ppermute | solution.py:184
  58.8 4.7 %collective-permute-start.6 = (bf16[64,4096]{1,0:T(8,128)(2,1)S(1)}, bf16[64,4096]{1,0:T(8,128)(2,1)S(1)}, u32[]{:S(2)}, u32[]{:S(2)}) collective-permute-start(bf16[64,4096]{1,0:T(8,128)(2,1)S(1)} %collective-permute-done.4.refs_0_), channel_id=1, source_target_pairs={{0,1},{1,2},{2,3},{3,0},{4,5},{5,6},{6,7},{7,4},{8,9},{9,10},{10,1... | collective-permute-start | bytes 1572872 | tf_op jit(solution)/shard_map/ppermute | solution.py:196
  63.5 3.5 %collective-permute-done.8 = bf16[16,4096]{1,0:T(8,128)(2,1)S(1)} collective-permute-done((bf16[16,4096]{1,0:T(8,128)(2,1)S(1)}, bf16[16,4096]{1,0:T(8,128)(2,1)S(1)}, u32[]{:S(2)}, u32[]{:S(2)}) %collective-permute-start.8) | collective-permute-done | bytes 131104 | tf_op jit(solution)/shard_map/ppermute | solution.py:184
  67.0 1.9 %collective-permute-start.12 = (bf16[64,4096]{1,0:T(8,128)(2,1)S(1)}, bf16[64,4096]{1,0:T(8,128)(2,1)S(1)}, u32[]{:S(2)}, u32[]{:S(2)}) collective-permute-start(bf16[64,4096]{1,0:T(8,128)(2,1)S(1)} %pad_maximum_fusion.1.refs_0_.refs_3_), channel_id=1, source_target_pairs={{0,3},{1,0},{2,1},{3,2},{4,7},{5,4},{6,5},{7,6},{8,11},{9,8},{10,9... | collective-permute-start | bytes 1572872 | tf_op jit(solution)/shard_map/ppermute | solution.py:197
  68.9 5.1 %collective-permute-start.11 = (bf16[64,4096]{1,0:T(8,128)(2,1)S(1)}, bf16[64,4096]{1,0:T(8,128)(2,1)}, u32[]{:S(2)}, u32[]{:S(2)}) collective-permute-start(bf16[64,4096]{1,0:T(8,128)(2,1)S(1)} %pad_maximum_fusion.1.refs_0_.refs_3_), channel_id=1, source_target_pairs={{0,1},{1,2},{2,3},{3,0},{4,5},{5,6},{6,7},{7,4},{8,9},{9,10},{10,1... | collective-permute-start | bytes 1572872 | tf_op jit(solution)/shard_map/ppermute | solution.py:198
  74.1 3.0 %shard_map.60.refs_1_.refs_2_ = bf16[192,4096]{1,0:T(8,128)(2,1)S(1)} custom-call(bf16[64,4096]{1,0:T(8,128)(2,1)S(1)} %collective-permute-done.4.refs_0_, bf16[64,4096]{1,0:T(8,128)(2,1)S(1)} %collective-permute-done.5.refs_1_, bf16[64,4096]{1,0:T(8,128)(2,1)S(1)} %collective-permute-done.6.refs_2_), custom_call_target="tpu_custom_call" | custom-call | tf_op jit(solution)/shard_map/pallas_call | solution.py:168
  77.1 5.7 %collective-permute-done.12.refs_2_.refs_5_ = bf16[64,4096]{1,0:T(8,128)(2,1)S(1)} collective-permute-done((bf16[64,4096]{1,0:T(8,128)(2,1)S(1)}, bf16[64,4096]{1,0:T(8,128)(2,1)S(1)}, u32[]{:S(2)}, u32[]{:S(2)}) %collective-permute-start.12) | collective-permute-done | bytes 524320 | tf_op jit(solution)/shard_map/ppermute | solution.py:197
  86.7 2.7 %shard_map.61 = (bf16[128,256]{1,0:T(8,128)(2,1)S(1)}, f32[256,128]{1,0:T(8,128)S(1)}, f32[256,128]{1,0:T(8,128)S(1)}, f32[256,128]{1,0:T(8,128)S(1)}, f32[256,2...) custom-call(bf16[64,4096]{1,0:T(8,128)(2,1)S(1)} %shard_map.59.refs_0_.refs_1_, ...), custom_call_target="tpu_custom_call" | custom-call | tf_op jit(solution)/shard_map/pallas_call | solution.py:212
  89.4 8.4 %collective-permute-done.13.refs_3_.refs_6_ = bf16[64,4096]{1,0:T(8,128)(2,1)} collective-permute-done((bf16[64,4096]{1,0:T(8,128)(2,1)S(1)}, bf16[64,4096]{1,0:T(8,128)(2,1)}, u32[]{:S(2)}, u32[]{:S(2)}) %collective-permute-start.13) | collective-permute-done | bytes 524320 | tf_op jit(solution)/shard_map/ppermute | solution.py:200
  97.7 4.1 %shard_map.62.refs_7_ = bf16[384,256]{1,0:T(8,128)(2,1)S(1)} custom-call(bf16[64,4096]{1,0:T(8,128)(2,1)S(1)} %pad_maximum_fusion.1.refs_0_.refs_3_, bf16[64,4096]{1,0:T(8,128)(2,1)} %collective-permute-done.11.refs_1_.refs_4_, bf16[64,4096]{1,0:T(8,128)(2,1)S(1)} %collective-permute-done.12.refs_2_.refs_5_, ...), custom_call_target="tpu_custom_call" | custom-call | tf_op jit(solution)/shard_map/pallas_call | solution.py:227
  101.8 2.1 %shard_map.64 = bf16[16,512,128]{2,1,0:T(8,128)(2,1)S(1)} custom-call(s32[3]{0:T(128)S(1)} %add_add_fusion.1.refs_0_, bf16[64,4096]{1,0:T(8,128)(2,1)S(1)} %shard_map.59.refs_0_.refs_1_, bf16[192,4096]{1,0:T(8,128)(2,1)S(1)} %shard_map.60.refs_1_.refs_2_, bf16[64,4096]{1,0:T(8,128)(2,1)S(1)} %pad_maximum_fusion.1.refs_0_.refs_3_, ...), custom_call_target="tpu_custom_call" | custom-call | tf_op jit(solution)/shard_map/pallas_call | solution.py:241
  106.0 2.1 %shard_map.63.own_ref = bf16[16,512,128]{2,1,0:T(8,128)(2,1)S(1)} custom-call(s32[3]{0:T(128)S(1)} %add_add_fusion.refs_0_, bf16[64,4096]{1,0:T(8,128)(2,1)S(1)} %shard_map.59.refs_0_.refs_1_, bf16[192,4096]{1,0:T(8,128)(2,1)S(1)} %shard_map.60.refs_1_.refs_2_, bf16[64,4096]{1,0:T(8,128)(2,1)S(1)} %pad_maximum_fusion.1.refs_0_.refs_3_, ...), custom_call_target="tpu_custom_call" | custom-call | tf_op jit(solution)/shard_map/pallas_call | solution.py:241
  108.1 1.9 %collective-permute-done.14.theirs_ref = bf16[16,512,128]{2,1,0:T(8,128)(2,1)S(1)} collective-permute-done((bf16[16,512,128]{2,1,0:T(8,128)(2,1)S(1)}, bf16[16,512,128]{2,1,0:T(8,128)(2,1)S(1)}, u32[]{:S(2)}, u32[]{:S(2)}) %collective-permute-start.14) | collective-permute-done | bytes 2097184 | tf_op jit(solution)/shard_map/ppermute | solution.py:251
  110.1 5.4 %collective-permute-start.19 = (bf16[512,128]{1,0:T(8,128)(2,1)S(1)}, bf16[512,128]{1,0:T(8,128)(2,1)S(1)}, u32[]{:S(2)}, u32[]{:S(2)}) collective-permute-start(bf16[512,128]{1,0:T(8,128)(2,1)S(1)} %get-tuple-element.27), channel_id=1, source_target_pairs={{0,448},{64,0},{128,64},{192,128},{256,192},{320,256},{384,320},{4... | collective-permute-start | bytes 393224 | tf_op jit(solution)/shard_map/ppermute | solution.py:267
  118.6 5.6 %collective-permute-start.20 = (bf16[2,512,128]{2,1,0:T(8,128)(2,1)S(1)}, bf16[2,512,128]{2,1,0:T(8,128)(2,1)S(1)}, u32[]{:S(2)}, u32[]{:S(2)}) collective-permute-start(bf16[2,512,128]{2,1,0:T(8,128)(2,1)S(1)} %shard_map.69), channel_id=1, source_target_pairs={{0,448},{64,0},{128,64},{192,128},{256,192},{320,256},{384,320},{4... | collective-permute-start | bytes 786440 | tf_op jit(solution)/shard_map/ppermute | solution.py:267
  126.2 3.0 %collective-permute-done.20.came_ref = bf16[2,512,128]{2,1,0:T(8,128)(2,1)S(1)} collective-permute-done((bf16[2,512,128]{2,1,0:T(8,128)(2,1)S(1)}, bf16[2,512,128]{2,1,0:T(8,128)(2,1)S(1)}, u32[]{:S(2)}, u32[]{:S(2)}) %collective-permute-start.20) | collective-permute-done | bytes 262176 | tf_op jit(solution)/shard_map/ppermute | solution.py:267
  129.3 5.6 %collective-permute-start.21 = (bf16[2,512,128]{2,1,0:T(8,128)(2,1)S(1)}, bf16[2,512,128]{2,1,0:T(8,128)(2,1)S(1)}, u32[]{:S(2)}, u32[]{:S(2)}) collective-permute-start(bf16[2,512,128]{2,1,0:T(8,128)(2,1)S(1)} %shard_map.70), channel_id=1, source_target_pairs={{0,448},{64,0},{128,64},{192,128},{256,192},{320,256},{384,320},{4... | collective-permute-start | bytes 786440 | tf_op jit(solution)/shard_map/ppermute | solution.py:267
  136.9 2.0 %collective-permute-done.21.came_ref = bf16[2,512,128]{2,1,0:T(8,128)(2,1)S(1)} collective-permute-done((bf16[2,512,128]{2,1,0:T(8,128)(2,1)S(1)}, bf16[2,512,128]{2,1,0:T(8,128)(2,1)S(1)}, u32[]{:S(2)}, u32[]{:S(2)}) %collective-permute-start.21) | collective-permute-done | bytes 262176 | tf_op jit(solution)/shard_map/ppermute | solution.py:267
  139.1 5.6 %collective-permute-start.22 = (bf16[2,512,128]{2,1,0:T(8,128)(2,1)S(1)}, bf16[2,512,128]{2,1,0:T(8,128)(2,1)S(1)}, u32[]{:S(2)}, u32[]{:S(2)}) collective-permute-start(bf16[2,512,128]{2,1,0:T(8,128)(2,1)S(1)} %shard_map.71), channel_id=1, source_target_pairs={{0,448},{64,0},{128,64},{192,128},{256,192},{320,256},{384,320},{4... | collective-permute-start | bytes 786440 | tf_op jit(solution)/shard_map/ppermute | solution.py:267
  148.6 5.7 %collective-permute-done.18.up_ref = bf16[2,512,128]{2,1,0:T(8,128)(2,1)S(1)} collective-permute-done((bf16[2,512,128]{2,1,0:T(8,128)(2,1)S(1)}, bf16[2,512,128]{2,1,0:T(8,128)(2,1)S(1)}, u32[]{:S(2)}, u32[]{:S(2)}) %collective-permute-start.18) | collective-permute-done | bytes 262176 | tf_op jit(solution)/shard_map/ppermute | solution.py:267
  154.4 13.3 %collective-permute-start.23 = (bf16[512,128]{1,0:T(8,128)(2,1)S(1)}, bf16[512,128]{1,0:T(8,128)(2,1)S(1)}, u32[]{:S(2)}, u32[]{:S(2)}) collective-permute-start(bf16[512,128]{1,0:T(8,128)(2,1)S(1)} %shard_map.72), channel_id=1, source_target_pairs={{0,512},{512,0},{1,513},{513,1},{2,514},{514,2},{3,515},{515,3},{4... | collective-permute-start | bytes 393224 | tf_op jit(solution)/shard_map/ppermute | solution.py:276
  167.7 4.9 %collective-permute-done.23.other_ref = bf16[512,128]{1,0:T(8,128)(2,1)S(1)} collective-permute-done((bf16[512,128]{1,0:T(8,128)(2,1)S(1)}, bf16[512,128]{1,0:T(8,128)(2,1)S(1)}, u32[]{:S(2)}, u32[]{:S(2)}) %collective-permute-start.23) | collective-permute-done | bytes 131104 | tf_op jit(solution)/shard_map/ppermute | solution.py:276
  (41 shorter events, 22.7 us)
Async XLA Ops:
  0.6 13.4 %collective-permute-start = (bf16[8,4096]{1,0:T(8,128)(2,1)}, bf16[8,4096]{1,0:T(8,128)(2,1)S(1)}, u32[]{:S(2)}, u32[]{:S(2)}) collective-permute-start(bf16[8,4096]{1,0:T(8,128)(2,1)} %param.4), channel_id=1, source_target_pairs={{0,16},{4,20},{8,24},{12,28},{16,0},{20,4},{24,8},{28,12},{1,17},{... | collective-permute-start | bytes 196616 | tf_op jit(solution)/shard_map/ppermute | solution.py:186
  14.8 21.4 %collective-permute-start.3 = (bf16[16,4096]{1,0:T(8,128)(2,1)S(1)}, bf16[16,4096]{1,0:T(8,128)(2,1)S(1)}, u32[]{:S(2)}, u32[]{:S(2)}) collective-permute-start(bf16[16,4096]{1,0:T(8,128)(2,1)S(1)} %pad_maximum_fusion.2), channel_id=1, source_target_pairs={{0,4},{4,0},{8,12},{12,8},{16,20},{20,16},{24,28},{28,24},{1,5},{5... | collective-permute-start | bytes 393224 | tf_op jit(solution)/shard_map/ppermute | solution.py:184
  19.1 17.1 %collective-permute-start.2 = (bf16[16,4096]{1,0:T(8,128)(2,1)S(1)}, bf16[16,4096]{1,0:T(8,128)(2,1)S(1)}, u32[]{:S(2)}, u32[]{:S(2)}) collective-permute-start(bf16[16,4096]{1,0:T(8,128)(2,1)S(1)} %pad_maximum_fusion.2), channel_id=1, source_target_pairs={{0,12},{4,8},{8,4},{12,0},{16,28},{20,24},{24,20},{28,16},{1,13},{... | collective-permute-start | bytes 393224 | tf_op jit(solution)/shard_map/ppermute | solution.py:184
  25.6 14.9 %collective-permute-start.1 = (bf16[16,4096]{1,0:T(8,128)(2,1)S(1)}, bf16[16,4096]{1,0:T(8,128)(2,1)S(1)}, u32[]{:S(2)}, u32[]{:S(2)}) collective-permute-start(bf16[16,4096]{1,0:T(8,128)(2,1)S(1)} %pad_maximum_fusion.2), channel_id=1, source_target_pairs={{0,8},{4,12},{8,0},{12,4},{16,24},{20,28},{24,16},{28,20},{1,9},{5... | collective-permute-start | bytes 393224 | tf_op jit(solution)/shard_map/ppermute | solution.py:184
  28.1 19.6 %collective-permute-start.7 = (bf16[8,4096]{1,0:T(8,128)(2,1)}, bf16[8,4096]{1,0:T(8,128)(2,1)S(1)}, u32[]{:S(2)}, u32[]{:S(2)}) collective-permute-start(bf16[8,4096]{1,0:T(8,128)(2,1)} %param.5), channel_id=1, source_target_pairs={{0,16},{4,20},{8,24},{12,28},{16,0},{20,4},{24,8},{28,12},{1,17},{... | collective-permute-start | bytes 196616 | tf_op jit(solution)/shard_map/ppermute | solution.py:189
  40.6 18.2 %collective-permute-start.5 = (bf16[64,4096]{1,0:T(8,128)(2,1)S(1)}, bf16[64,4096]{1,0:T(8,128)(2,1)S(1)}, u32[]{:S(2)}, u32[]{:S(2)}) collective-permute-start(bf16[64,4096]{1,0:T(8,128)(2,1)S(1)} %pad_maximum_fusion.refs_0_), channel_id=1, source_target_pairs={{0,3},{1,0},{2,1},{3,2},{4,7},{5,4},{6,5},{7,6},{8,11},{9,8},{10,9... | collective-permute-start | bytes 1572872 | tf_op jit(solution)/shard_map/ppermute | solution.py:192
  43.3 15.5 %collective-permute-start.4 = (bf16[64,4096]{1,0:T(8,128)(2,1)S(1)}, bf16[64,4096]{1,0:T(8,128)(2,1)S(1)}, u32[]{:S(2)}, u32[]{:S(2)}) collective-permute-start(bf16[64,4096]{1,0:T(8,128)(2,1)S(1)} %pad_maximum_fusion.refs_0_), channel_id=1, source_target_pairs={{0,1},{1,2},{2,3},{3,0},{4,5},{5,6},{6,7},{7,4},{8,9},{9,10},{10,1... | collective-permute-start | bytes 1572872 | tf_op jit(solution)/shard_map/ppermute | solution.py:191
  49.5 14.0 %collective-permute-start.10 = (bf16[16,4096]{1,0:T(8,128)(2,1)S(1)}, bf16[16,4096]{1,0:T(8,128)(2,1)S(1)}, u32[]{:S(2)}, u32[]{:S(2)}) collective-permute-start(bf16[16,4096]{1,0:T(8,128)(2,1)S(1)} %pad_maximum_fusion.3), channel_id=1, source_target_pairs={{0,4},{4,0},{8,12},{12,8},{16,20},{20,16},{24,28},{28,24},{1,5},{5... | collective-permute-start | bytes 393224 | tf_op jit(solution)/shard_map/ppermute | solution.py:184
  51.4 12.0 %collective-permute-start.9 = (bf16[16,4096]{1,0:T(8,128)(2,1)S(1)}, bf16[16,4096]{1,0:T(8,128)(2,1)S(1)}, u32[]{:S(2)}, u32[]{:S(2)}) collective-permute-start(bf16[16,4096]{1,0:T(8,128)(2,1)S(1)} %pad_maximum_fusion.3), channel_id=1, source_target_pairs={{0,12},{4,8},{8,4},{12,0},{16,28},{20,24},{24,20},{28,16},{1,13},{... | collective-permute-start | bytes 393224 | tf_op jit(solution)/shard_map/ppermute | solution.py:184
  54.8 12.2 %collective-permute-start.8 = (bf16[16,4096]{1,0:T(8,128)(2,1)S(1)}, bf16[16,4096]{1,0:T(8,128)(2,1)S(1)}, u32[]{:S(2)}, u32[]{:S(2)}) collective-permute-start(bf16[16,4096]{1,0:T(8,128)(2,1)S(1)} %pad_maximum_fusion.3), channel_id=1, source_target_pairs={{0,8},{4,12},{8,0},{12,4},{16,24},{20,28},{24,16},{28,20},{1,9},{5... | collective-permute-start | bytes 393224 | tf_op jit(solution)/shard_map/ppermute | solution.py:184
  58.8 15.3 %collective-permute-start.6 = (bf16[64,4096]{1,0:T(8,128)(2,1)S(1)}, bf16[64,4096]{1,0:T(8,128)(2,1)S(1)}, u32[]{:S(2)}, u32[]{:S(2)}) collective-permute-start(bf16[64,4096]{1,0:T(8,128)(2,1)S(1)} %collective-permute-done.4.refs_0_), channel_id=1, source_target_pairs={{0,1},{1,2},{2,3},{3,0},{4,5},{5,6},{6,7},{7,4},{8,9},{9,10},{10,1... | collective-permute-start | bytes 1572872 | tf_op jit(solution)/shard_map/ppermute | solution.py:196
  67.0 15.8 %collective-permute-start.12 = (bf16[64,4096]{1,0:T(8,128)(2,1)S(1)}, bf16[64,4096]{1,0:T(8,128)(2,1)S(1)}, u32[]{:S(2)}, u32[]{:S(2)}) collective-permute-start(bf16[64,4096]{1,0:T(8,128)(2,1)S(1)} %pad_maximum_fusion.1.refs_0_.refs_3_), channel_id=1, source_target_pairs={{0,3},{1,0},{2,1},{3,2},{4,7},{5,4},{6,5},{7,6},{8,11},{9,8},{10,9... | collective-permute-start | bytes 1572872 | tf_op jit(solution)/shard_map/ppermute | solution.py:197
  68.9 20.4 %collective-permute-start.11 = (bf16[64,4096]{1,0:T(8,128)(2,1)S(1)}, bf16[64,4096]{1,0:T(8,128)(2,1)}, u32[]{:S(2)}, u32[]{:S(2)}) collective-permute-start(bf16[64,4096]{1,0:T(8,128)(2,1)S(1)} %pad_maximum_fusion.1.refs_0_.refs_3_), channel_id=1, source_target_pairs={{0,1},{1,2},{2,3},{3,0},{4,5},{5,6},{6,7},{7,4},{8,9},{9,10},{10,1... | collective-permute-start | bytes 1572872 | tf_op jit(solution)/shard_map/ppermute | solution.py:198
  82.8 14.9 %collective-permute-start.13 = (bf16[64,4096]{1,0:T(8,128)(2,1)S(1)}, bf16[64,4096]{1,0:T(8,128)(2,1)}, u32[]{:S(2)}, u32[]{:S(2)}) collective-permute-start(bf16[64,4096]{1,0:T(8,128)(2,1)S(1)} %collective-permute-done.12.refs_2_.refs_5_), channel_id=1, source_target_pairs={{0,3},{1,0},{2,1},{3,2},{4,7},{5,4},{6,5},{7,6},{8,11},{9,8},{10,9... | collective-permute-start | bytes 1572872 | tf_op jit(solution)/shard_map/ppermute | solution.py:200
  84.8 1.9 %copy-start = (bf16[4096,1,384]{2,0,1:T(8,128)(2,1)S(1)}, bf16[4096,1,384]{2,0,1:T(8,128)(2,1)}, u32[]{:S(2)}) copy-start(bf16[4096,1,384]{2,0,1:T(8,128)(2,1)} %param.6) | copy-start | bytes 9437188
  86.7 11.1 %copy-start.1 = (bf16[1,128,4096]{2,1,0:T(8,128)(2,1)S(1)}, bf16[1,128,4096]{2,1,0:T(8,128)(2,1)}, u32[]{:S(2)}) copy-start(bf16[1,128,4096]{2,1,0:T(8,128)(2,1)} %param.7) | copy-start | bytes 3145732
  104.0 6.1 %collective-permute-start.14 = (bf16[16,512,128]{2,1,0:T(8,128)(2,1)S(1)}, bf16[16,512,128]{2,1,0:T(8,128)(2,1)S(1)}, u32[]{:S(2)}, u32[]{:S(2)}) collective-permute-start(bf16[16,512,128]{2,1,0:T(8,128)(2,1)S(1)} %shard_map.64), channel_id=1, source_target_pairs={{0,32},{32,0},{1,33},{33,1},{2,34},{34,2},{3,35},{35,3},{4,36},{36... | collective-permute-start | bytes 6291464 | tf_op jit(solution)/shard_map/ppermute | solution.py:251
  110.1 8.4 %collective-permute-start.19 = (bf16[512,128]{1,0:T(8,128)(2,1)S(1)}, bf16[512,128]{1,0:T(8,128)(2,1)S(1)}, u32[]{:S(2)}, u32[]{:S(2)}) collective-permute-start(bf16[512,128]{1,0:T(8,128)(2,1)S(1)} %get-tuple-element.27), channel_id=1, source_target_pairs={{0,448},{64,0},{128,64},{192,128},{256,192},{320,256},{384,320},{4... | collective-permute-start | bytes 393224 | tf_op jit(solution)/shard_map/ppermute | solution.py:267
  115.4 8.7 %collective-permute-start.15 = (bf16[512,128]{1,0:T(8,128)(2,1)S(1)}, bf16[512,128]{1,0:T(8,128)(2,1)S(1)}, u32[]{:S(2)}, u32[]{:S(2)}) collective-permute-start(bf16[512,128]{1,0:T(8,128)(2,1)S(1)} %get-tuple-element.26), channel_id=1, source_target_pairs={{0,64},{64,128},{128,192},{192,256},{256,320},{320,384},{384,448},... | collective-permute-start | bytes 393224 | tf_op jit(solution)/shard_map/ppermute | solution.py:267
  118.6 10.6 %collective-permute-start.20 = (bf16[2,512,128]{2,1,0:T(8,128)(2,1)S(1)}, bf16[2,512,128]{2,1,0:T(8,128)(2,1)S(1)}, u32[]{:S(2)}, u32[]{:S(2)}) collective-permute-start(bf16[2,512,128]{2,1,0:T(8,128)(2,1)S(1)} %shard_map.69), channel_id=1, source_target_pairs={{0,448},{64,0},{128,64},{192,128},{256,192},{320,256},{384,320},{4... | collective-permute-start | bytes 786440 | tf_op jit(solution)/shard_map/ppermute | solution.py:267
  124.3 10.6 %collective-permute-start.16 = (bf16[2,512,128]{2,1,0:T(8,128)(2,1)S(1)}, bf16[2,512,128]{2,1,0:T(8,128)(2,1)S(1)}, u32[]{:S(2)}, u32[]{:S(2)}) collective-permute-start(bf16[2,512,128]{2,1,0:T(8,128)(2,1)S(1)} %shard_map.66), channel_id=1, source_target_pairs={{0,64},{64,128},{128,192},{192,256},{256,320},{320,384},{384,448},... | collective-permute-start | bytes 786440 | tf_op jit(solution)/shard_map/ppermute | solution.py:267
  129.3 9.7 %collective-permute-start.21 = (bf16[2,512,128]{2,1,0:T(8,128)(2,1)S(1)}, bf16[2,512,128]{2,1,0:T(8,128)(2,1)S(1)}, u32[]{:S(2)}, u32[]{:S(2)}) collective-permute-start(bf16[2,512,128]{2,1,0:T(8,128)(2,1)S(1)} %shard_map.70), channel_id=1, source_target_pairs={{0,448},{64,0},{128,64},{192,128},{256,192},{320,256},{384,320},{4... | collective-permute-start | bytes 786440 | tf_op jit(solution)/shard_map/ppermute | solution.py:267
  135.0 9.7 %collective-permute-start.17 = (bf16[2,512,128]{2,1,0:T(8,128)(2,1)S(1)}, bf16[2,512,128]{2,1,0:T(8,128)(2,1)S(1)}, u32[]{:S(2)}, u32[]{:S(2)}) collective-permute-start(bf16[2,512,128]{2,1,0:T(8,128)(2,1)S(1)} %shard_map.67), channel_id=1, source_target_pairs={{0,64},{64,128},{128,192},{192,256},{256,320},{320,384},{384,448},... | collective-permute-start | bytes 786440 | tf_op jit(solution)/shard_map/ppermute | solution.py:267
  139.1 9.5 %collective-permute-start.22 = (bf16[2,512,128]{2,1,0:T(8,128)(2,1)S(1)}, bf16[2,512,128]{2,1,0:T(8,128)(2,1)S(1)}, u32[]{:S(2)}, u32[]{:S(2)}) collective-permute-start(bf16[2,512,128]{2,1,0:T(8,128)(2,1)S(1)} %shard_map.71), channel_id=1, source_target_pairs={{0,448},{64,0},{128,64},{192,128},{256,192},{320,256},{384,320},{4... | collective-permute-start | bytes 786440 | tf_op jit(solution)/shard_map/ppermute | solution.py:267
  144.8 9.5 %collective-permute-start.18 = (bf16[2,512,128]{2,1,0:T(8,128)(2,1)S(1)}, bf16[2,512,128]{2,1,0:T(8,128)(2,1)S(1)}, u32[]{:S(2)}, u32[]{:S(2)}) collective-permute-start(bf16[2,512,128]{2,1,0:T(8,128)(2,1)S(1)} %shard_map.68), channel_id=1, source_target_pairs={{0,64},{64,128},{128,192},{192,256},{256,320},{320,384},{384,448},... | collective-permute-start | bytes 786440 | tf_op jit(solution)/shard_map/ppermute | solution.py:267
  154.4 18.1 %collective-permute-start.23 = (bf16[512,128]{1,0:T(8,128)(2,1)S(1)}, bf16[512,128]{1,0:T(8,128)(2,1)S(1)}, u32[]{:S(2)}, u32[]{:S(2)}) collective-permute-start(bf16[512,128]{1,0:T(8,128)(2,1)S(1)} %shard_map.72), channel_id=1, source_target_pairs={{0,512},{512,0},{1,513},{513,1},{2,514},{514,2},{3,515},{515,3},{4... | collective-permute-start | bytes 393224 | tf_op jit(solution)/shard_map/ppermute | solution.py:276

commit v7 on v6

--- a/solution.py
+++ b/solution.py
@@ -105,7 +105,7 @@
     d_all, att = d_ref[...], att_ref[...]
     split = d_all.shape[0]
     for slot, distance in enumerate(ORDER):
-        y = lax.rem(here + distance + near, near)
+        y = lax.rem(here + distance * (1 - 2 * core) + near, near)
         cols = [
             pl.ds(pl.multiple_of(((z * near + y) * 2 + core) * width, width), width)
             for z in (1 - zh, zh)
@@ -155,10 +155,6 @@
     return [(i, i ^ s) for i in range(n)]
 
 
-def turn(n, s):
-    return [(i, (i + s) % n) for i in range(n)]
-
-
 def after(value, *done):
     return lax.optimization_barrier((value, *done))[0]
 
@@ -175,10 +171,14 @@
 
 
 def gather(tokens, cotangent, n_z, n_x):
-    up, down = turn(n_x, 1), turn(n_x, -1)
-
     def join(*rows):
         return lax.optimization_barrier(jnp.concatenate(rows, 0))
+
+    def round_x(rows, way):
+        pairs = [
+            (c * n_x + x, c * n_x + (x + way * (1 - 2 * c)) % n_x) for c in range(2) for x in range(n_x)
+        ]
+        return lax.ppermute(rows, ("c", "x"), pairs)
 
     def within(rows):
         return [lax.ppermute(rows, "zl", swap(n_z, s)) for s in (2, 3, 1)]
@@ -188,17 +188,17 @@
     t_near = within(t)
     c = join(cotangent, lax.ppermute(after(cotangent, t), "zl", swap(n_z, 4)))
     t = join(t, *t_near)
-    t_left = lax.ppermute(t, "x", up)
-    t_right = lax.ppermute(t, "x", down)
+    t_one = round_x(t, 1)
+    t_two = round_x(t, -1)
     normed = normalized(t)
     c_near = within(after(c, normed))
-    c = join(after(c, t_left, t_right), *c_near)
-    t_far = lax.ppermute(t_left, "x", up)
-    c_right = lax.ppermute(c, "x", down)
-    c_left = lax.ppermute(c, "x", up)
-    rest = normalized(t_left, t_right, t_far)
-    c_far = lax.ppermute(after(c_right, rest), "x", down)
-    return [normed, rest], [c, c_left, c_right, c_far]
+    c = join(after(c, t_one, t_two), *c_near)
+    t_far = round_x(t_two, -1)
+    c_one = round_x(c, 1)
+    c_two = round_x(c, -1)
+    rest = normalized(t_one, t_two, t_far)
+    c_far = round_x(after(c_one, rest), 1)
+    return [normed, rest], [c, c_one, c_two, c_far]
 
 
 def local(sizes, tokens, cotangent, w_qkv, w_out):
@@ -262,9 +262,15 @@
             compiler_params=PARAMS,
         )(mine, theirs, *came)
 
+    def round_y(block, way):
+        pairs = [
+            (y * 2 + c, (y + way * (1 - 2 * c)) % near * 2 + c) for y in range(near) for c in range(2)
+        ]
+        return lax.ppermute(block, ("y", "c"), pairs)
+
     goes = list(call(first_kernel, [one, one]))
     for distance in (3, 2, 1, 0):
-        goes = [lax.ppermute(m, "y", turn(near, way)) for m, way in zip(goes, (1, -1))]
+        goes = [round_y(m, way) for m, way in zip(goes, (1, -1))]
         if distance == 0:
             break
         for i, way in enumerate((1, -1)):

time: 174 us -> 177 us (1.017)
  waiting for transfers between devices: 44.7 us -> 48.3 us
    ppermute x14, starting transfers between devices: 50.6 us -> 48 us  [the longest x8 29.8 us: round_y(): return lax.ppermute(block, ('y', 'c'), pairs)]
    ppermute x1, waiting for transfers between devices: 4.86 us -> 7.13 us  [local(): other = lax.ppermute(away, 'zh', swap(far, 1))]
where the time goes in v7:
time: 177 us; the launch traced here: 176 us
  starting transfers between devices  106 us (60%)
  waiting for transfers between devices  48.3 us (27%)
  Pallas kernels  16.5 us (9%)
  other arithmetic  1.93 us (1%)
  local copies, waits for them, and re-layouts  1.89 us (1%)
    ppermute x8, starting transfers between devices, round_y(): return lax.ppermute(block, ('y', 'c'), pairs)  29.8 us
    ppermute x6, starting transfers between devices, within(): return [lax.ppermute(rows, 'zl', swap(n_z, s)) for s in (2, 3, 1)]  22.4 us
    ppermute x6, starting transfers between devices, round_x(): return lax.ppermute(rows, ('c', 'x'), pairs)  18.2 us
    ppermute x8, waiting for transfers between devices, round_y(): return lax.ppermute(block, ('y', 'c'), pairs)  16.8 us
    ppermute x1, starting transfers between devices, local(): other = lax.ppermute(away, 'zh', swap(far, 1))  14.4 us
    ppermute x1, starting transfers between devices, gather(): t_other = lax.ppermute(tokens, 'zl', swap(n_z, 4))  10.9 us
    ppermute x6, waiting for transfers between devices, round_x(): return lax.ppermute(rows, ('c', 'x'), pairs)  10.6 us
    ppermute x6, waiting for transfers between devices, within(): return [lax.ppermute(rows, 'zl', swap(n_z, s)) for s in (2, 3, 1)]  9.45 us
  transfers between devices with their start and end apart: 24, of which 12 were waited for; matrix products, arithmetic and copies ran while one was open for 1% of the time, Pallas kernels for 5%

profile of v7, /device:TPU:6, one launch (start us, length us, event | category | flops | bytes accessed | tf_op | source)
XLA Modules:
  0.0 175.6 jit_solution(2730193810322287275)
XLA Ops:
  0.6 10.9 %collective-permute-start = (bf16[8,4096]{1,0:T(8,128)(2,1)}, bf16[8,4096]{1,0:T(8,128)(2,1)S(1)}, u32[]{:S(2)}, u32[]{:S(2)}) collective-permute-start(bf16[8,4096]{1,0:T(8,128)(2,1)} %param.4), channel_id=1, source_target_pairs={{0,16},{4,20},{8,24},{12,28},{16,0},{20,4},{24,8},{28,12},{1,17},{... | collective-permute-start | bytes 196616 | tf_op jit(solution)/shard_map/ppermute | solution.py:186
  11.6 2.4 %collective-permute-done = bf16[8,4096]{1,0:T(8,128)(2,1)S(1)} collective-permute-done((bf16[8,4096]{1,0:T(8,128)(2,1)}, bf16[8,4096]{1,0:T(8,128)(2,1)S(1)}, u32[]{:S(2)}, u32[]{:S(2)}) %collective-permute-start) | collective-permute-done | bytes 65568 | tf_op jit(solution)/shard_map/ppermute | solution.py:186
  14.8 4.3 %collective-permute-start.3 = (bf16[16,4096]{1,0:T(8,128)(2,1)S(1)}, bf16[16,4096]{1,0:T(8,128)(2,1)S(1)}, u32[]{:S(2)}, u32[]{:S(2)}) collective-permute-start(bf16[16,4096]{1,0:T(8,128)(2,1)S(1)} %pad_maximum_fusion.2), channel_id=1, source_target_pairs={{0,4},{4,0},{8,12},{12,8},{16,20},{20,16},{24,28},{28,24},{1,5},{5... | collective-permute-start | bytes 393224 | tf_op jit(solution)/shard_map/ppermute | solution.py:184
  19.1 6.4 %collective-permute-start.2 = (bf16[16,4096]{1,0:T(8,128)(2,1)S(1)}, bf16[16,4096]{1,0:T(8,128)(2,1)S(1)}, u32[]{:S(2)}, u32[]{:S(2)}) collective-permute-start(bf16[16,4096]{1,0:T(8,128)(2,1)S(1)} %pad_maximum_fusion.2), channel_id=1, source_target_pairs={{0,12},{4,8},{8,4},{12,0},{16,28},{20,24},{24,20},{28,16},{1,13},{... | collective-permute-start | bytes 393224 | tf_op jit(solution)/shard_map/ppermute | solution.py:184
  25.6 2.5 %collective-permute-start.1 = (bf16[16,4096]{1,0:T(8,128)(2,1)S(1)}, bf16[16,4096]{1,0:T(8,128)(2,1)S(1)}, u32[]{:S(2)}, u32[]{:S(2)}) collective-permute-start(bf16[16,4096]{1,0:T(8,128)(2,1)S(1)} %pad_maximum_fusion.2), channel_id=1, source_target_pairs={{0,8},{4,12},{8,0},{12,4},{16,24},{20,28},{24,16},{28,20},{1,9},{5... | collective-permute-start | bytes 393224 | tf_op jit(solution)/shard_map/ppermute | solution.py:184
  28.1 8.2 %collective-permute-start.7 = (bf16[8,4096]{1,0:T(8,128)(2,1)}, bf16[8,4096]{1,0:T(8,128)(2,1)S(1)}, u32[]{:S(2)}, u32[]{:S(2)}) collective-permute-start(bf16[8,4096]{1,0:T(8,128)(2,1)} %param.5), channel_id=1, source_target_pairs={{0,16},{4,20},{8,24},{12,28},{16,0},{20,4},{24,8},{28,12},{1,17},{... | collective-permute-start | bytes 196616 | tf_op jit(solution)/shard_map/ppermute | solution.py:189
  36.3 4.2 %collective-permute-done.1 = bf16[16,4096]{1,0:T(8,128)(2,1)S(1)} collective-permute-done((bf16[16,4096]{1,0:T(8,128)(2,1)S(1)}, bf16[16,4096]{1,0:T(8,128)(2,1)S(1)}, u32[]{:S(2)}, u32[]{:S(2)}) %collective-permute-start.1) | collective-permute-done | bytes 131104 | tf_op jit(solution)/shard_map/ppermute | solution.py:184
  40.6 2.7 %collective-permute-start.5 = (bf16[64,4096]{1,0:T(8,128)(2,1)S(1)}, bf16[64,4096]{1,0:T(8,128)(2,1)S(1)}, u32[]{:S(2)}, u32[]{:S(2)}) collective-permute-start(bf16[64,4096]{1,0:T(8,128)(2,1)S(1)} %pad_maximum_fusion.refs_0_), channel_id=1, source_target_pairs={{0,3},{1,0},{2,1},{3,2},{32,33},{33,34},{34,35},{35,32},{4,7},{5,4... | collective-permute-start | bytes 1572872 | tf_op jit(solution)/shard_map/ppermute | solution.py:181
  43.3 4.3 %collective-permute-start.4 = (bf16[64,4096]{1,0:T(8,128)(2,1)S(1)}, bf16[64,4096]{1,0:T(8,128)(2,1)S(1)}, u32[]{:S(2)}, u32[]{:S(2)}) collective-permute-start(bf16[64,4096]{1,0:T(8,128)(2,1)S(1)} %pad_maximum_fusion.refs_0_), channel_id=1, source_target_pairs={{0,1},{1,2},{2,3},{3,0},{32,35},{33,32},{34,33},{35,34},{4,5},{5,6... | collective-permute-start | bytes 1572872 | tf_op jit(solution)/shard_map/ppermute | solution.py:181
  51.4 3.3 %collective-permute-start.9 = (bf16[16,4096]{1,0:T(8,128)(2,1)S(1)}, bf16[16,4096]{1,0:T(8,128)(2,1)S(1)}, u32[]{:S(2)}, u32[]{:S(2)}) collective-permute-start(bf16[16,4096]{1,0:T(8,128)(2,1)S(1)} %pad_maximum_fusion.3), channel_id=1, source_target_pairs={{0,12},{4,8},{8,4},{12,0},{16,28},{20,24},{24,20},{28,16},{1,13},{... | collective-permute-start | bytes 393224 | tf_op jit(solution)/shard_map/ppermute | solution.py:184
  54.8 4.0 %collective-permute-start.8 = (bf16[16,4096]{1,0:T(8,128)(2,1)S(1)}, bf16[16,4096]{1,0:T(8,128)(2,1)S(1)}, u32[]{:S(2)}, u32[]{:S(2)}) collective-permute-start(bf16[16,4096]{1,0:T(8,128)(2,1)S(1)} %pad_maximum_fusion.3), channel_id=1, source_target_pairs={{0,8},{4,12},{8,0},{12,4},{16,24},{20,28},{24,16},{28,20},{1,9},{5... | collective-permute-start | bytes 393224 | tf_op jit(solution)/shard_map/ppermute | solution.py:184
  60.7 5.2 %collective-permute-done.8 = bf16[16,4096]{1,0:T(8,128)(2,1)S(1)} collective-permute-done((bf16[16,4096]{1,0:T(8,128)(2,1)S(1)}, bf16[16,4096]{1,0:T(8,128)(2,1)S(1)}, u32[]{:S(2)}, u32[]{:S(2)}) %collective-permute-start.8) | collective-permute-done | bytes 131104 | tf_op jit(solution)/shard_map/ppermute | solution.py:184
  66.0 3.2 %collective-permute-start.11 = (bf16[64,4096]{1,0:T(8,128)(2,1)S(1)}, bf16[64,4096]{1,0:T(8,128)(2,1)S(1)}, u32[]{:S(2)}, u32[]{:S(2)}) collective-permute-start(bf16[64,4096]{1,0:T(8,128)(2,1)S(1)} %pad_maximum_fusion.1.refs_0_.refs_3_), channel_id=1, source_target_pairs={{0,1},{1,2},{2,3},{3,0},{32,35},{33,32},{34,33},{35,34},{4,5},{5,6... | collective-permute-start | bytes 1572872 | tf_op jit(solution)/shard_map/ppermute | solution.py:181
  69.2 2.6 %collective-permute-start.12 = (bf16[64,4096]{1,0:T(8,128)(2,1)S(1)}, bf16[64,4096]{1,0:T(8,128)(2,1)}, u32[]{:S(2)}, u32[]{:S(2)}) collective-permute-start(bf16[64,4096]{1,0:T(8,128)(2,1)S(1)} %pad_maximum_fusion.1.refs_0_.refs_3_), channel_id=1, source_target_pairs={{0,3},{1,0},{2,1},{3,2},{32,33},{33,34},{34,35},{35,32},{4,7},{5,4... | collective-permute-start | bytes 1572872 | tf_op jit(solution)/shard_map/ppermute | solution.py:181
  71.8 3.0 %shard_map.60.refs_1_.refs_2_ = bf16[192,4096]{1,0:T(8,128)(2,1)S(1)} custom-call(bf16[64,4096]{1,0:T(8,128)(2,1)S(1)} %collective-permute-done.4.refs_0_, bf16[64,4096]{1,0:T(8,128)(2,1)S(1)} %collective-permute-done.5.refs_1_, bf16[64,4096]{1,0:T(8,128)(2,1)S(1)} %collective-permute-done.6.refs_2_), custom_call_target="tpu_custom_call" | custom-call | tf_op jit(solution)/shard_map/pallas_call | solution.py:164
  74.8 7.5 %collective-permute-done.11.refs_1_.refs_4_ = bf16[64,4096]{1,0:T(8,128)(2,1)S(1)} collective-permute-done((bf16[64,4096]{1,0:T(8,128)(2,1)S(1)}, bf16[64,4096]{1,0:T(8,128)(2,1)S(1)}, u32[]{:S(2)}, u32[]{:S(2)}) %collective-permute-start.11) | collective-permute-done | bytes 524320 | tf_op jit(solution)/shard_map/ppermute | solution.py:181
  82.4 3.4 %collective-permute-start.13 = (bf16[64,4096]{1,0:T(8,128)(2,1)S(1)}, bf16[64,4096]{1,0:T(8,128)(2,1)}, u32[]{:S(2)}, u32[]{:S(2)}) collective-permute-start(bf16[64,4096]{1,0:T(8,128)(2,1)S(1)} %collective-permute-done.11.refs_1_.refs_4_), channel_id=1, source_target_pairs={{0,1},{1,2},{2,3},{3,0},{32,35},{33,32},{34,33},{35,34},{4,5},{5,6... | collective-permute-start | bytes 1572872 | tf_op jit(solution)/shard_map/ppermute | solution.py:181
  87.7 2.7 %shard_map.61 = (bf16[128,256]{1,0:T(8,128)(2,1)S(1)}, f32[256,128]{1,0:T(8,128)S(1)}, f32[256,128]{1,0:T(8,128)S(1)}, f32[256,128]{1,0:T(8,128)S(1)}, f32[256,2...) custom-call(bf16[64,4096]{1,0:T(8,128)(2,1)S(1)} %shard_map.59.refs_0_.refs_1_, ...), custom_call_target="tpu_custom_call" | custom-call | tf_op jit(solution)/shard_map/pallas_call | solution.py:212
  90.4 3.1 %collective-permute-done.13.refs_3_.refs_6_ = bf16[64,4096]{1,0:T(8,128)(2,1)} collective-permute-done((bf16[64,4096]{1,0:T(8,128)(2,1)S(1)}, bf16[64,4096]{1,0:T(8,128)(2,1)}, u32[]{:S(2)}, u32[]{:S(2)}) %collective-permute-start.13) | collective-permute-done | bytes 524320 | tf_op jit(solution)/shard_map/ppermute | solution.py:181
  93.5 4.1 %shard_map.62.refs_7_ = bf16[384,256]{1,0:T(8,128)(2,1)S(1)} custom-call(bf16[64,4096]{1,0:T(8,128)(2,1)S(1)} %pad_maximum_fusion.1.refs_0_.refs_3_, bf16[64,4096]{1,0:T(8,128)(2,1)S(1)} %collective-permute-done.11.refs_1_.refs_4_, bf16[64,4096]{1,0:T(8,128)(2,1)} %collective-permute-done.12.refs_2_.refs_5_, ...), custom_call_target="tpu_custom_call" | custom-call | tf_op jit(solution)/shard_map/pallas_call | solution.py:227
  97.6 2.1 %shard_map.64 = bf16[16,512,128]{2,1,0:T(8,128)(2,1)S(1)} custom-call(s32[3]{0:T(128)S(1)} %add_add_fusion.1.refs_0_, bf16[64,4096]{1,0:T(8,128)(2,1)S(1)} %shard_map.59.refs_0_.refs_1_, bf16[192,4096]{1,0:T(8,128)(2,1)S(1)} %shard_map.60.refs_1_.refs_2_, bf16[64,4096]{1,0:T(8,128)(2,1)S(1)} %pad_maximum_fusion.1.refs_0_.refs_3_, ...), custom_call_target="tpu_custom_call" | custom-call | tf_op jit(solution)/shard_map/pallas_call | solution.py:241
  101.8 2.1 %shard_map.63.own_ref = bf16[16,512,128]{2,1,0:T(8,128)(2,1)S(1)} custom-call(s32[3]{0:T(128)S(1)} %add_add_fusion.refs_0_, bf16[64,4096]{1,0:T(8,128)(2,1)S(1)} %shard_map.59.refs_0_.refs_1_, bf16[192,4096]{1,0:T(8,128)(2,1)S(1)} %shard_map.60.refs_1_.refs_2_, bf16[64,4096]{1,0:T(8,128)(2,1)S(1)} %pad_maximum_fusion.1.refs_0_.refs_3_, ...), custom_call_target="tpu_custom_call" | custom-call | tf_op jit(solution)/shard_map/pallas_call | solution.py:241
  105.9 5.4 %collective-permute-start.19 = (bf16[512,128]{1,0:T(8,128)(2,1)S(1)}, bf16[512,128]{1,0:T(8,128)(2,1)S(1)}, u32[]{:S(2)}, u32[]{:S(2)}) collective-permute-start(bf16[512,128]{1,0:T(8,128)(2,1)S(1)} %get-tuple-element.27), channel_id=1, source_target_pairs={{0,448},{32,96},{64,0},{96,160},{128,64},{160,224},{192,128},{224,... | collective-permute-start | bytes 393224 | tf_op jit(solution)/shard_map/ppermute | solution.py:269
  114.1 5.6 %collective-permute-start.20 = (bf16[2,512,128]{2,1,0:T(8,128)(2,1)S(1)}, bf16[2,512,128]{2,1,0:T(8,128)(2,1)S(1)}, u32[]{:S(2)}, u32[]{:S(2)}) collective-permute-start(bf16[2,512,128]{2,1,0:T(8,128)(2,1)S(1)} %shard_map.69), channel_id=1, source_target_pairs={{0,448},{32,96},{64,0},{96,160},{128,64},{160,224},{192,128},{224,... | collective-permute-start | bytes 786440 | tf_op jit(solution)/shard_map/ppermute | solution.py:269
  121.7 4.6 %collective-permute-done.20.came_ref = bf16[2,512,128]{2,1,0:T(8,128)(2,1)S(1)} collective-permute-done((bf16[2,512,128]{2,1,0:T(8,128)(2,1)S(1)}, bf16[2,512,128]{2,1,0:T(8,128)(2,1)S(1)}, u32[]{:S(2)}, u32[]{:S(2)}) %collective-permute-start.20) | collective-permute-done | bytes 262176 | tf_op jit(solution)/shard_map/ppermute | solution.py:269
  126.5 5.6 %collective-permute-start.21 = (bf16[2,512,128]{2,1,0:T(8,128)(2,1)S(1)}, bf16[2,512,128]{2,1,0:T(8,128)(2,1)S(1)}, u32[]{:S(2)}, u32[]{:S(2)}) collective-permute-start(bf16[2,512,128]{2,1,0:T(8,128)(2,1)S(1)} %shard_map.70), channel_id=1, source_target_pairs={{0,448},{32,96},{64,0},{96,160},{128,64},{160,224},{192,128},{224,... | collective-permute-start | bytes 786440 | tf_op jit(solution)/shard_map/ppermute | solution.py:269
  134.1 3.7 %collective-permute-done.21.came_ref = bf16[2,512,128]{2,1,0:T(8,128)(2,1)S(1)} collective-permute-done((bf16[2,512,128]{2,1,0:T(8,128)(2,1)S(1)}, bf16[2,512,128]{2,1,0:T(8,128)(2,1)S(1)}, u32[]{:S(2)}, u32[]{:S(2)}) %collective-permute-start.21) | collective-permute-done | bytes 262176 | tf_op jit(solution)/shard_map/ppermute | solution.py:269
  137.9 5.6 %collective-permute-start.22 = (bf16[2,512,128]{2,1,0:T(8,128)(2,1)S(1)}, bf16[2,512,128]{2,1,0:T(8,128)(2,1)S(1)}, u32[]{:S(2)}, u32[]{:S(2)}) collective-permute-start(bf16[2,512,128]{2,1,0:T(8,128)(2,1)S(1)} %shard_map.71), channel_id=1, source_target_pairs={{0,448},{32,96},{64,0},{96,160},{128,64},{160,224},{192,128},{224,... | collective-permute-start | bytes 786440 | tf_op jit(solution)/shard_map/ppermute | solution.py:269
  145.6 2.9 %collective-permute-done.22.down_ref = bf16[2,512,128]{2,1,0:T(8,128)(2,1)S(1)} collective-permute-done((bf16[2,512,128]{2,1,0:T(8,128)(2,1)S(1)}, bf16[2,512,128]{2,1,0:T(8,128)(2,1)S(1)}, u32[]{:S(2)}, u32[]{:S(2)}) %collective-permute-start.22) | collective-permute-done | bytes 262176 | tf_op jit(solution)/shard_map/ppermute | solution.py:269
  148.5 4.7 %collective-permute-done.18.up_ref = bf16[2,512,128]{2,1,0:T(8,128)(2,1)S(1)} collective-permute-done((bf16[2,512,128]{2,1,0:T(8,128)(2,1)S(1)}, bf16[2,512,128]{2,1,0:T(8,128)(2,1)S(1)}, u32[]{:S(2)}, u32[]{:S(2)}) %collective-permute-start.18) | collective-permute-done | bytes 262176 | tf_op jit(solution)/shard_map/ppermute | solution.py:269
  153.2 14.4 %collective-permute-start.23 = (bf16[512,128]{1,0:T(8,128)(2,1)S(1)}, bf16[512,128]{1,0:T(8,128)(2,1)S(1)}, u32[]{:S(2)}, u32[]{:S(2)}) collective-permute-start(bf16[512,128]{1,0:T(8,128)(2,1)S(1)} %shard_map.72), channel_id=1, source_target_pairs={{0,512},{512,0},{1,513},{513,1},{2,514},{514,2},{3,515},{515,3},{4... | collective-permute-start | bytes 393224 | tf_op jit(solution)/shard_map/ppermute | solution.py:282
  167.6 7.1 %collective-permute-done.23.other_ref = bf16[512,128]{1,0:T(8,128)(2,1)S(1)} collective-permute-done((bf16[512,128]{1,0:T(8,128)(2,1)S(1)}, bf16[512,128]{1,0:T(8,128)(2,1)S(1)}, u32[]{:S(2)}, u32[]{:S(2)}) %collective-permute-start.23) | collective-permute-done | bytes 131104 | tf_op jit(solution)/shard_map/ppermute | solution.py:282
  (41 shorter events, 22.6 us)
Async XLA Ops:
  0.6 13.4 %collective-permute-start = (bf16[8,4096]{1,0:T(8,128)(2,1)}, bf16[8,4096]{1,0:T(8,128)(2,1)S(1)}, u32[]{:S(2)}, u32[]{:S(2)}) collective-permute-start(bf16[8,4096]{1,0:T(8,128)(2,1)} %param.4), channel_id=1, source_target_pairs={{0,16},{4,20},{8,24},{12,28},{16,0},{20,4},{24,8},{28,12},{1,17},{... | collective-permute-start | bytes 196616 | tf_op jit(solution)/shard_map/ppermute | solution.py:186
  14.8 21.4 %collective-permute-start.3 = (bf16[16,4096]{1,0:T(8,128)(2,1)S(1)}, bf16[16,4096]{1,0:T(8,128)(2,1)S(1)}, u32[]{:S(2)}, u32[]{:S(2)}) collective-permute-start(bf16[16,4096]{1,0:T(8,128)(2,1)S(1)} %pad_maximum_fusion.2), channel_id=1, source_target_pairs={{0,4},{4,0},{8,12},{12,8},{16,20},{20,16},{24,28},{28,24},{1,5},{5... | collective-permute-start | bytes 393224 | tf_op jit(solution)/shard_map/ppermute | solution.py:184
  19.1 17.1 %collective-permute-start.2 = (bf16[16,4096]{1,0:T(8,128)(2,1)S(1)}, bf16[16,4096]{1,0:T(8,128)(2,1)S(1)}, u32[]{:S(2)}, u32[]{:S(2)}) collective-permute-start(bf16[16,4096]{1,0:T(8,128)(2,1)S(1)} %pad_maximum_fusion.2), channel_id=1, source_target_pairs={{0,12},{4,8},{8,4},{12,0},{16,28},{20,24},{24,20},{28,16},{1,13},{... | collective-permute-start | bytes 393224 | tf_op jit(solution)/shard_map/ppermute | solution.py:184
  25.6 14.9 %collective-permute-start.1 = (bf16[16,4096]{1,0:T(8,128)(2,1)S(1)}, bf16[16,4096]{1,0:T(8,128)(2,1)S(1)}, u32[]{:S(2)}, u32[]{:S(2)}) collective-permute-start(bf16[16,4096]{1,0:T(8,128)(2,1)S(1)} %pad_maximum_fusion.2), channel_id=1, source_target_pairs={{0,8},{4,12},{8,0},{12,4},{16,24},{20,28},{24,16},{28,20},{1,9},{5... | collective-permute-start | bytes 393224 | tf_op jit(solution)/shard_map/ppermute | solution.py:184
  28.1 19.6 %collective-permute-start.7 = (bf16[8,4096]{1,0:T(8,128)(2,1)}, bf16[8,4096]{1,0:T(8,128)(2,1)S(1)}, u32[]{:S(2)}, u32[]{:S(2)}) collective-permute-start(bf16[8,4096]{1,0:T(8,128)(2,1)} %param.5), channel_id=1, source_target_pairs={{0,16},{4,20},{8,24},{12,28},{16,0},{20,4},{24,8},{28,12},{1,17},{... | collective-permute-start | bytes 196616 | tf_op jit(solution)/shard_map/ppermute | solution.py:189
  40.6 18.2 %collective-permute-start.5 = (bf16[64,4096]{1,0:T(8,128)(2,1)S(1)}, bf16[64,4096]{1,0:T(8,128)(2,1)S(1)}, u32[]{:S(2)}, u32[]{:S(2)}) collective-permute-start(bf16[64,4096]{1,0:T(8,128)(2,1)S(1)} %pad_maximum_fusion.refs_0_), channel_id=1, source_target_pairs={{0,3},{1,0},{2,1},{3,2},{32,33},{33,34},{34,35},{35,32},{4,7},{5,4... | collective-permute-start | bytes 1572872 | tf_op jit(solution)/shard_map/ppermute | solution.py:181
  43.3 15.5 %collective-permute-start.4 = (bf16[64,4096]{1,0:T(8,128)(2,1)S(1)}, bf16[64,4096]{1,0:T(8,128)(2,1)S(1)}, u32[]{:S(2)}, u32[]{:S(2)}) collective-permute-start(bf16[64,4096]{1,0:T(8,128)(2,1)S(1)} %pad_maximum_fusion.refs_0_), channel_id=1, source_target_pairs={{0,1},{1,2},{2,3},{3,0},{32,35},{33,32},{34,33},{35,34},{4,5},{5,6... | collective-permute-start | bytes 1572872 | tf_op jit(solution)/shard_map/ppermute | solution.py:181
  49.5 11.2 %collective-permute-start.10 = (bf16[16,4096]{1,0:T(8,128)(2,1)S(1)}, bf16[16,4096]{1,0:T(8,128)(2,1)S(1)}, u32[]{:S(2)}, u32[]{:S(2)}) collective-permute-start(bf16[16,4096]{1,0:T(8,128)(2,1)S(1)} %pad_maximum_fusion.3), channel_id=1, source_target_pairs={{0,4},{4,0},{8,12},{12,8},{16,20},{20,16},{24,28},{28,24},{1,5},{5... | collective-permute-start | bytes 393224 | tf_op jit(solution)/shard_map/ppermute | solution.py:184
  51.4 9.3 %collective-permute-start.9 = (bf16[16,4096]{1,0:T(8,128)(2,1)S(1)}, bf16[16,4096]{1,0:T(8,128)(2,1)S(1)}, u32[]{:S(2)}, u32[]{:S(2)}) collective-permute-start(bf16[16,4096]{1,0:T(8,128)(2,1)S(1)} %pad_maximum_fusion.3), channel_id=1, source_target_pairs={{0,12},{4,8},{8,4},{12,0},{16,28},{20,24},{24,20},{28,16},{1,13},{... | collective-permute-start | bytes 393224 | tf_op jit(solution)/shard_map/ppermute | solution.py:184
  54.8 11.1 %collective-permute-start.8 = (bf16[16,4096]{1,0:T(8,128)(2,1)S(1)}, bf16[16,4096]{1,0:T(8,128)(2,1)S(1)}, u32[]{:S(2)}, u32[]{:S(2)}) collective-permute-start(bf16[16,4096]{1,0:T(8,128)(2,1)S(1)} %pad_maximum_fusion.3), channel_id=1, source_target_pairs={{0,8},{4,12},{8,0},{12,4},{16,24},{20,28},{24,16},{28,20},{1,9},{5... | collective-permute-start | bytes 393224 | tf_op jit(solution)/shard_map/ppermute | solution.py:184
  58.8 13.1 %collective-permute-start.6 = (bf16[64,4096]{1,0:T(8,128)(2,1)S(1)}, bf16[64,4096]{1,0:T(8,128)(2,1)S(1)}, u32[]{:S(2)}, u32[]{:S(2)}) collective-permute-start(bf16[64,4096]{1,0:T(8,128)(2,1)S(1)} %collective-permute-done.5.refs_1_), channel_id=1, source_target_pairs={{0,3},{1,0},{2,1},{3,2},{32,33},{33,34},{34,35},{35,32},{4,7},{5,4... | collective-permute-start | bytes 1572872 | tf_op jit(solution)/shard_map/ppermute | solution.py:181
  66.0 16.4 %collective-permute-start.11 = (bf16[64,4096]{1,0:T(8,128)(2,1)S(1)}, bf16[64,4096]{1,0:T(8,128)(2,1)S(1)}, u32[]{:S(2)}, u32[]{:S(2)}) collective-permute-start(bf16[64,4096]{1,0:T(8,128)(2,1)S(1)} %pad_maximum_fusion.1.refs_0_.refs_3_), channel_id=1, source_target_pairs={{0,1},{1,2},{2,3},{3,0},{32,35},{33,32},{34,33},{35,34},{4,5},{5,6... | collective-permute-start | bytes 1572872 | tf_op jit(solution)/shard_map/ppermute | solution.py:181
  69.2 21.2 %collective-permute-start.12 = (bf16[64,4096]{1,0:T(8,128)(2,1)S(1)}, bf16[64,4096]{1,0:T(8,128)(2,1)}, u32[]{:S(2)}, u32[]{:S(2)}) collective-permute-start(bf16[64,4096]{1,0:T(8,128)(2,1)S(1)} %pad_maximum_fusion.1.refs_0_.refs_3_), channel_id=1, source_target_pairs={{0,3},{1,0},{2,1},{3,2},{32,33},{33,34},{34,35},{35,32},{4,7},{5,4... | collective-permute-start | bytes 1572872 | tf_op jit(solution)/shard_map/ppermute | solution.py:181
  82.4 11.2 %collective-permute-start.13 = (bf16[64,4096]{1,0:T(8,128)(2,1)S(1)}, bf16[64,4096]{1,0:T(8,128)(2,1)}, u32[]{:S(2)}, u32[]{:S(2)}) collective-permute-start(bf16[64,4096]{1,0:T(8,128)(2,1)S(1)} %collective-permute-done.11.refs_1_.refs_4_), channel_id=1, source_target_pairs={{0,1},{1,2},{2,3},{3,0},{32,35},{33,32},{34,33},{35,34},{4,5},{5,6... | collective-permute-start | bytes 1572872 | tf_op jit(solution)/shard_map/ppermute | solution.py:181
  85.8 1.9 %copy-start = (bf16[4096,1,384]{2,0,1:T(8,128)(2,1)S(1)}, bf16[4096,1,384]{2,0,1:T(8,128)(2,1)}, u32[]{:S(2)}) copy-start(bf16[4096,1,384]{2,0,1:T(8,128)(2,1)} %param.6) | copy-start | bytes 9437188
  87.7 5.8 %copy-start.1 = (bf16[1,128,4096]{2,1,0:T(8,128)(2,1)S(1)}, bf16[1,128,4096]{2,1,0:T(8,128)(2,1)}, u32[]{:S(2)}) copy-start(bf16[1,128,4096]{2,1,0:T(8,128)(2,1)} %param.7) | copy-start | bytes 3145732
  99.8 6.1 %collective-permute-start.14 = (bf16[16,512,128]{2,1,0:T(8,128)(2,1)S(1)}, bf16[16,512,128]{2,1,0:T(8,128)(2,1)S(1)}, u32[]{:S(2)}, u32[]{:S(2)}) collective-permute-start(bf16[16,512,128]{2,1,0:T(8,128)(2,1)S(1)} %shard_map.64), channel_id=1, source_target_pairs={{0,32},{32,0},{1,33},{33,1},{2,34},{34,2},{3,35},{35,3},{4,36},{36... | collective-permute-start | bytes 6291464 | tf_op jit(solution)/shard_map/ppermute | solution.py:251
  105.9 8.1 %collective-permute-start.19 = (bf16[512,128]{1,0:T(8,128)(2,1)S(1)}, bf16[512,128]{1,0:T(8,128)(2,1)S(1)}, u32[]{:S(2)}, u32[]{:S(2)}) collective-permute-start(bf16[512,128]{1,0:T(8,128)(2,1)S(1)} %get-tuple-element.27), channel_id=1, source_target_pairs={{0,448},{32,96},{64,0},{96,160},{128,64},{160,224},{192,128},{224,... | collective-permute-start | bytes 393224 | tf_op jit(solution)/shard_map/ppermute | solution.py:269
  111.3 8.5 %collective-permute-start.15 = (bf16[512,128]{1,0:T(8,128)(2,1)S(1)}, bf16[512,128]{1,0:T(8,128)(2,1)S(1)}, u32[]{:S(2)}, u32[]{:S(2)}) collective-permute-start(bf16[512,128]{1,0:T(8,128)(2,1)S(1)} %get-tuple-element.26), channel_id=1, source_target_pairs={{0,64},{32,480},{64,128},{96,32},{128,192},{160,96},{192,256},{224... | collective-permute-start | bytes 393224 | tf_op jit(solution)/shard_map/ppermute | solution.py:269
  114.1 12.3 %collective-permute-start.20 = (bf16[2,512,128]{2,1,0:T(8,128)(2,1)S(1)}, bf16[2,512,128]{2,1,0:T(8,128)(2,1)S(1)}, u32[]{:S(2)}, u32[]{:S(2)}) collective-permute-start(bf16[2,512,128]{2,1,0:T(8,128)(2,1)S(1)} %shard_map.69), channel_id=1, source_target_pairs={{0,448},{32,96},{64,0},{96,160},{128,64},{160,224},{192,128},{224,... | collective-permute-start | bytes 786440 | tf_op jit(solution)/shard_map/ppermute | solution.py:269
  119.8 12.2 %collective-permute-start.16 = (bf16[2,512,128]{2,1,0:T(8,128)(2,1)S(1)}, bf16[2,512,128]{2,1,0:T(8,128)(2,1)S(1)}, u32[]{:S(2)}, u32[]{:S(2)}) collective-permute-start(bf16[2,512,128]{2,1,0:T(8,128)(2,1)S(1)} %shard_map.66), channel_id=1, source_target_pairs={{0,64},{32,480},{64,128},{96,32},{128,192},{160,96},{192,256},{224... | collective-permute-start | bytes 786440 | tf_op jit(solution)/shard_map/ppermute | solution.py:269
  126.5 11.4 %collective-permute-start.21 = (bf16[2,512,128]{2,1,0:T(8,128)(2,1)S(1)}, bf16[2,512,128]{2,1,0:T(8,128)(2,1)S(1)}, u32[]{:S(2)}, u32[]{:S(2)}) collective-permute-start(bf16[2,512,128]{2,1,0:T(8,128)(2,1)S(1)} %shard_map.70), channel_id=1, source_target_pairs={{0,448},{32,96},{64,0},{96,160},{128,64},{160,224},{192,128},{224,... | collective-permute-start | bytes 786440 | tf_op jit(solution)/shard_map/ppermute | solution.py:269
  132.2 11.4 %collective-permute-start.17 = (bf16[2,512,128]{2,1,0:T(8,128)(2,1)S(1)}, bf16[2,512,128]{2,1,0:T(8,128)(2,1)S(1)}, u32[]{:S(2)}, u32[]{:S(2)}) collective-permute-start(bf16[2,512,128]{2,1,0:T(8,128)(2,1)S(1)} %shard_map.67), channel_id=1, source_target_pairs={{0,64},{32,480},{64,128},{96,32},{128,192},{160,96},{192,256},{224... | collective-permute-start | bytes 786440 | tf_op jit(solution)/shard_map/ppermute | solution.py:269
  137.9 10.5 %collective-permute-start.22 = (bf16[2,512,128]{2,1,0:T(8,128)(2,1)S(1)}, bf16[2,512,128]{2,1,0:T(8,128)(2,1)S(1)}, u32[]{:S(2)}, u32[]{:S(2)}) collective-permute-start(bf16[2,512,128]{2,1,0:T(8,128)(2,1)S(1)} %shard_map.71), channel_id=1, source_target_pairs={{0,448},{32,96},{64,0},{96,160},{128,64},{160,224},{192,128},{224,... | collective-permute-start | bytes 786440 | tf_op jit(solution)/shard_map/ppermute | solution.py:269
  143.7 9.5 %collective-permute-start.18 = (bf16[2,512,128]{2,1,0:T(8,128)(2,1)S(1)}, bf16[2,512,128]{2,1,0:T(8,128)(2,1)S(1)}, u32[]{:S(2)}, u32[]{:S(2)}) collective-permute-start(bf16[2,512,128]{2,1,0:T(8,128)(2,1)S(1)} %shard_map.68), channel_id=1, source_target_pairs={{0,64},{32,480},{64,128},{96,32},{128,192},{160,96},{192,256},{224... | collective-permute-start | bytes 786440 | tf_op jit(solution)/shard_map/ppermute | solution.py:269
  153.2 21.5 %collective-permute-start.23 = (bf16[512,128]{1,0:T(8,128)(2,1)S(1)}, bf16[512,128]{1,0:T(8,128)(2,1)S(1)}, u32[]{:S(2)}, u32[]{:S(2)}) collective-permute-start(bf16[512,128]{1,0:T(8,128)(2,1)S(1)} %shard_map.72), channel_id=1, source_target_pairs={{0,512},{512,0},{1,513},{513,1},{2,514},{514,2},{3,515},{515,3},{4... | collective-permute-start | bytes 393224 | tf_op jit(solution)/shard_map/ppermute | solution.py:282

commit v8 on v6

--- a/solution.py
+++ b/solution.py
@@ -186,18 +186,18 @@
     t_other = lax.ppermute(tokens, "zl", swap(n_z, 4))
     t = join(tokens, t_other)
     t_near = within(t)
-    c = join(cotangent, lax.ppermute(after(cotangent, t), "zl", swap(n_z, 4)))
+    c = join(cotangent, lax.ppermute(cotangent, "zl", swap(n_z, 4)))
     t = join(t, *t_near)
     t_left = lax.ppermute(t, "x", up)
     t_right = lax.ppermute(t, "x", down)
     normed = normalized(t)
-    c_near = within(after(c, normed))
-    c = join(after(c, t_left, t_right), *c_near)
+    c_near = within(c)
+    c = join(c, *c_near)
     t_far = lax.ppermute(t_left, "x", up)
     c_right = lax.ppermute(c, "x", down)
-    c_left = lax.ppermute(c, "x", up)
+    c_left = lax.ppermute(after(c, t_left), "x", up)
     rest = normalized(t_left, t_right, t_far)
-    c_far = lax.ppermute(after(c_right, rest), "x", down)
+    c_far = lax.ppermute(c_right, "x", down)
     return [normed, rest], [c, c_left, c_right, c_far]
 
 

time: 174 us -> 168 us (0.966)
  starting transfers between devices: 107 us -> 104 us
  local copies, waits for them, and re-layouts: 1.89 us -> 0.01 us
    ppermute x1, waiting for transfers between devices: 0.01 us -> 8.33 us  [gather(): t_right = lax.ppermute(t, 'x', down)]
    ppermute x3, starting transfers between devices: 15.2 us -> 6.94 us  [the longest x1 3.11 us: gather(): c_left = lax.ppermute(after(c, t_left), 'x', up)]
    ppermute x3, waiting for transfers between devices: 8.36 us -> 2.65 us  [the longest x1 2.65 us: gather(): c_far = lax.ppermute(c_right, 'x', down)]
    ppermute x6, starting transfers between devices: 22.4 us -> 27.1 us  [within(): return [lax.ppermute(rows, 'zl', swap(n_z, s)) for s in (2, 3, 1)]]
    ppermute x1, waiting for transfers between devices: 2.44 us -> 0.51 us  [gather(): t_other = lax.ppermute(tokens, 'zl', swap(n_z, 4))]
    unnamed x4, local copies, waits for them, and re-layouts: 1.89 us -> 0.01 us
  transfers between devices with their start and end apart: 24 -> 24, of which waited for: 12 -> 13; matrix products, arithmetic and copies ran while one was open for 1% -> 1% of each run, Pallas kernels for 5% -> 6%
where the time goes in v8:
time: 168 us; the launch traced here: 167 us
  starting transfers between devices  104 us (62%)
  waiting for transfers between devices  44.9 us (27%)
  Pallas kernels  15.2 us (9%)
  other arithmetic  1.93 us (1%)
    ppermute x8, starting transfers between devices, local(): lax.ppermute(m, 'y', turn(near, way))  29.9 us
    ppermute x6, starting transfers between devices, within(): return [lax.ppermute(rows, 'zl', swap(n_z, s)) for s in (2, 3, 1)]  27.1 us
    ppermute x1, starting transfers between devices, local(): other = lax.ppermute(away, 'zh', swap(far, 1))  14.3 us
    ppermute x8, waiting for transfers between devices, local(): lax.ppermute(m, 'y', turn(near, way))  13.7 us
    ppermute x1, starting transfers between devices, gather(): t_other = lax.ppermute(tokens, 'zl', swap(n_z, 4))  10.9 us
    ppermute x1, waiting for transfers between devices, gather(): t_right = lax.ppermute(t, 'x', down)  8.33 us
    ppermute x6, waiting for transfers between devices, within(): return [lax.ppermute(rows, 'zl', swap(n_z, s)) for s in (2, 3, 1)]  7.26 us
    pallas_call x2, Pallas kernels, normalized(): pl.pallas_call(normalize_kernel, out_shape=jax.ShapeDtypeStruct((rows, pi...  5.21 us
  transfers between devices with their start and end apart: 24, of which 13 were waited for; matrix products, arithmetic and copies ran while one was open for 1% of the time, Pallas kernels for 6%

profile of v8, /device:TPU:6, one launch (start us, length us, event | category | flops | bytes accessed | tf_op | source)
XLA Modules:
  0.0 166.9 jit_solution(4832178666370564733)
XLA Ops:
  0.6 10.9 %collective-permute-start = (bf16[8,4096]{1,0:T(8,128)(2,1)}, bf16[8,4096]{1,0:T(8,128)(2,1)S(1)}, u32[]{:S(2)}, u32[]{:S(2)}) collective-permute-start(bf16[8,4096]{1,0:T(8,128)(2,1)} %param.4), channel_id=1, source_target_pairs={{0,16},{4,20},{8,24},{12,28},{16,0},{20,4},{24,8},{28,12},{1,17},{... | collective-permute-start | bytes 196616 | tf_op jit(solution)/shard_map/ppermute | solution.py:186
  11.6 1.9 %collective-permute-start.7 = (bf16[8,4096]{1,0:T(8,128)(2,1)}, bf16[8,4096]{1,0:T(8,128)(2,1)S(1)}, u32[]{:S(2)}, u32[]{:S(2)}) collective-permute-start(bf16[8,4096]{1,0:T(8,128)(2,1)} %param.5), channel_id=1, source_target_pairs={{0,16},{4,20},{8,24},{12,28},{16,0},{20,4},{24,8},{28,12},{1,17},{... | collective-permute-start | bytes 196616 | tf_op jit(solution)/shard_map/ppermute | solution.py:189
  14.8 6.0 %collective-permute-start.3 = (bf16[16,4096]{1,0:T(8,128)(2,1)S(1)}, bf16[16,4096]{1,0:T(8,128)(2,1)S(1)}, u32[]{:S(2)}, u32[]{:S(2)}) collective-permute-start(bf16[16,4096]{1,0:T(8,128)(2,1)S(1)} %pad_maximum_fusion.2), channel_id=1, source_target_pairs={{0,4},{4,0},{8,12},{12,8},{16,20},{20,16},{24,28},{28,24},{1,5},{5... | collective-permute-start | bytes 393224 | tf_op jit(solution)/shard_map/ppermute | solution.py:184
  20.8 9.1 %collective-permute-start.2 = (bf16[16,4096]{1,0:T(8,128)(2,1)S(1)}, bf16[16,4096]{1,0:T(8,128)(2,1)S(1)}, u32[]{:S(2)}, u32[]{:S(2)}) collective-permute-start(bf16[16,4096]{1,0:T(8,128)(2,1)S(1)} %pad_maximum_fusion.2), channel_id=1, source_target_pairs={{0,12},{4,8},{8,4},{12,0},{16,28},{20,24},{24,20},{28,16},{1,13},{... | collective-permute-start | bytes 393224 | tf_op jit(solution)/shard_map/ppermute | solution.py:184
  29.9 2.5 %collective-permute-start.1 = (bf16[16,4096]{1,0:T(8,128)(2,1)S(1)}, bf16[16,4096]{1,0:T(8,128)(2,1)S(1)}, u32[]{:S(2)}, u32[]{:S(2)}) collective-permute-start(bf16[16,4096]{1,0:T(8,128)(2,1)S(1)} %pad_maximum_fusion.2), channel_id=1, source_target_pairs={{0,8},{4,12},{8,0},{12,4},{16,24},{20,28},{24,16},{28,20},{1,9},{5... | collective-permute-start | bytes 393224 | tf_op jit(solution)/shard_map/ppermute | solution.py:184
  33.2 2.5 %collective-permute-start.10 = (bf16[16,4096]{1,0:T(8,128)(2,1)S(1)}, bf16[16,4096]{1,0:T(8,128)(2,1)S(1)}, u32[]{:S(2)}, u32[]{:S(2)}) collective-permute-start(bf16[16,4096]{1,0:T(8,128)(2,1)S(1)} %pad_maximum_fusion.3), channel_id=1, source_target_pairs={{0,4},{4,0},{8,12},{12,8},{16,20},{20,16},{24,28},{28,24},{1,5},{5... | collective-permute-start | bytes 393224 | tf_op jit(solution)/shard_map/ppermute | solution.py:184
  35.7 5.2 %collective-permute-start.9 = (bf16[16,4096]{1,0:T(8,128)(2,1)S(1)}, bf16[16,4096]{1,0:T(8,128)(2,1)S(1)}, u32[]{:S(2)}, u32[]{:S(2)}) collective-permute-start(bf16[16,4096]{1,0:T(8,128)(2,1)S(1)} %pad_maximum_fusion.3), channel_id=1, source_target_pairs={{0,12},{4,8},{8,4},{12,0},{16,28},{20,24},{24,20},{28,16},{1,13},{... | collective-permute-start | bytes 393224 | tf_op jit(solution)/shard_map/ppermute | solution.py:184
  40.9 1.9 %collective-permute-start.8 = (bf16[16,4096]{1,0:T(8,128)(2,1)S(1)}, bf16[16,4096]{1,0:T(8,128)(2,1)S(1)}, u32[]{:S(2)}, u32[]{:S(2)}) collective-permute-start(bf16[16,4096]{1,0:T(8,128)(2,1)S(1)} %pad_maximum_fusion.3), channel_id=1, source_target_pairs={{0,8},{4,12},{8,0},{12,4},{16,24},{20,28},{24,16},{28,20},{1,9},{5... | collective-permute-start | bytes 393224 | tf_op jit(solution)/shard_map/ppermute | solution.py:184
  42.8 3.9 %collective-permute-done.1 = bf16[16,4096]{1,0:T(8,128)(2,1)S(1)} collective-permute-done((bf16[16,4096]{1,0:T(8,128)(2,1)S(1)}, bf16[16,4096]{1,0:T(8,128)(2,1)S(1)}, u32[]{:S(2)}, u32[]{:S(2)}) %collective-permute-start.1) | collective-permute-done | bytes 131104 | tf_op jit(solution)/shard_map/ppermute | solution.py:184
  46.8 3.0 %collective-permute-start.4 = (bf16[64,4096]{1,0:T(8,128)(2,1)S(1)}, bf16[64,4096]{1,0:T(8,128)(2,1)S(1)}, u32[]{:S(2)}, u32[]{:S(2)}) collective-permute-start(bf16[64,4096]{1,0:T(8,128)(2,1)S(1)} %pad_maximum_fusion.refs_0_), channel_id=1, source_target_pairs={{0,1},{1,2},{2,3},{3,0},{4,5},{5,6},{6,7},{7,4},{8,9},{9,10},{10,1... | collective-permute-start | bytes 1572872 | tf_op jit(solution)/shard_map/ppermute | solution.py:191
  49.8 3.3 %collective-permute-done.8 = bf16[16,4096]{1,0:T(8,128)(2,1)S(1)} collective-permute-done((bf16[16,4096]{1,0:T(8,128)(2,1)S(1)}, bf16[16,4096]{1,0:T(8,128)(2,1)S(1)}, u32[]{:S(2)}, u32[]{:S(2)}) %collective-permute-start.8) | collective-permute-done | bytes 131104 | tf_op jit(solution)/shard_map/ppermute | solution.py:184
  53.2 2.7 %collective-permute-start.12 = (bf16[64,4096]{1,0:T(8,128)(2,1)S(1)}, bf16[64,4096]{1,0:T(8,128)(2,1)S(1)}, u32[]{:S(2)}, u32[]{:S(2)}) collective-permute-start(bf16[64,4096]{1,0:T(8,128)(2,1)S(1)} %pad_maximum_fusion.1.refs_0_.refs_3_), channel_id=1, source_target_pairs={{0,3},{1,0},{2,1},{3,2},{4,7},{5,4},{6,5},{7,6},{8,11},{9,8},{10,9... | collective-permute-start | bytes 1572872 | tf_op jit(solution)/shard_map/ppermute | solution.py:197
  55.9 2.4 %collective-permute-start.5 = (bf16[64,4096]{1,0:T(8,128)(2,1)S(1)}, bf16[64,4096]{1,0:T(8,128)(2,1)}, u32[]{:S(2)}, u32[]{:S(2)}) collective-permute-start(bf16[64,4096]{1,0:T(8,128)(2,1)S(1)} %pad_maximum_fusion.refs_0_), channel_id=1, source_target_pairs={{0,3},{1,0},{2,1},{3,2},{4,7},{5,4},{6,5},{7,6},{8,11},{9,8},{10,9... | collective-permute-start | bytes 1572872 | tf_op jit(solution)/shard_map/ppermute | solution.py:192
  58.4 4.6 %collective-permute-start.6 = (bf16[64,4096]{1,0:T(8,128)(2,1)S(1)}, bf16[64,4096]{1,0:T(8,128)(2,1)}, u32[]{:S(2)}, u32[]{:S(2)}) collective-permute-start(bf16[64,4096]{1,0:T(8,128)(2,1)S(1)} %collective-permute-done.4.refs_0_), channel_id=1, source_target_pairs={{0,1},{1,2},{2,3},{3,0},{4,5},{5,6},{6,7},{7,4},{8,9},{9,10},{10,1... | collective-permute-start | bytes 1572872 | tf_op jit(solution)/shard_map/ppermute | solution.py:196
  63.0 3.1 %collective-permute-start.11 = (bf16[64,4096]{1,0:T(8,128)(2,1)S(1)}, bf16[64,4096]{1,0:T(8,128)(2,1)S(1)}, u32[]{:S(2)}, u32[]{:S(2)}) collective-permute-start(bf16[64,4096]{1,0:T(8,128)(2,1)S(1)} %pad_maximum_fusion.1.refs_0_.refs_3_), channel_id=1, source_target_pairs={{0,1},{1,2},{2,3},{3,0},{4,5},{5,6},{6,7},{7,4},{8,9},{9,10},{10,1... | collective-permute-start | bytes 1572872 | tf_op jit(solution)/shard_map/ppermute | solution.py:198
  66.1 5.0 %collective-permute-done.12.refs_2_.refs_5_ = bf16[64,4096]{1,0:T(8,128)(2,1)S(1)} collective-permute-done((bf16[64,4096]{1,0:T(8,128)(2,1)S(1)}, bf16[64,4096]{1,0:T(8,128)(2,1)S(1)}, u32[]{:S(2)}, u32[]{:S(2)}) %collective-permute-start.12) | collective-permute-done | bytes 524320 | tf_op jit(solution)/shard_map/ppermute | solution.py:197
  74.2 8.3 %collective-permute-done.5.refs_1_ = bf16[64,4096]{1,0:T(8,128)(2,1)} collective-permute-done((bf16[64,4096]{1,0:T(8,128)(2,1)S(1)}, bf16[64,4096]{1,0:T(8,128)(2,1)}, u32[]{:S(2)}, u32[]{:S(2)}) %collective-permute-start.5) | collective-permute-done | bytes 524320 | tf_op jit(solution)/shard_map/ppermute | solution.py:192
  82.5 4.2 %shard_map.60.refs_1_.refs_2_ = bf16[192,4096]{1,0:T(8,128)(2,1)S(1)} custom-call(bf16[64,4096]{1,0:T(8,128)(2,1)S(1)} %collective-permute-done.4.refs_0_, bf16[64,4096]{1,0:T(8,128)(2,1)} %collective-permute-done.5.refs_1_, bf16[64,4096]{1,0:T(8,128)(2,1)} %collective-permute-done.6.refs_2_), custom_call_target="tpu_custom_call" | custom-call | tf_op jit(solution)/shard_map/pallas_call | solution.py:168
  86.7 2.7 %shard_map.61 = (bf16[128,256]{1,0:T(8,128)(2,1)S(1)}, f32[256,128]{1,0:T(8,128)S(1)}, f32[256,128]{1,0:T(8,128)S(1)}, f32[256,128]{1,0:T(8,128)S(1)}, f32[256,2...) custom-call(bf16[64,4096]{1,0:T(8,128)(2,1)S(1)} %shard_map.59.refs_0_.refs_1_, ...), custom_call_target="tpu_custom_call" | custom-call | tf_op jit(solution)/shard_map/pallas_call | solution.py:212
  89.4 2.6 %collective-permute-done.13.refs_3_.refs_6_ = bf16[64,4096]{1,0:T(8,128)(2,1)S(1)} collective-permute-done((bf16[64,4096]{1,0:T(8,128)(2,1)S(1)}, bf16[64,4096]{1,0:T(8,128)(2,1)S(1)}, u32[]{:S(2)}, u32[]{:S(2)}) %collective-permute-start.13) | collective-permute-done | bytes 524320 | tf_op jit(solution)/shard_map/ppermute | solution.py:200
  92.1 2.9 %shard_map.62.refs_7_ = bf16[384,256]{1,0:T(8,128)(2,1)S(1)} custom-call(bf16[64,4096]{1,0:T(8,128)(2,1)S(1)} %pad_maximum_fusion.1.refs_0_.refs_3_, bf16[64,4096]{1,0:T(8,128)(2,1)S(1)} %collective-permute-done.11.refs_1_.refs_4_, bf16[64,4096]{1,0:T(8,128)(2,1)S(1)} %collective-permute-done.12.refs_2_.refs_5_, ...), custom_call_target="tpu_custom_call" | custom-call | tf_op jit(solution)/shard_map/pallas_call | solution.py:227
  99.9 2.6 %collective-permute-done.14.theirs_ref = bf16[16,512,128]{2,1,0:T(8,128)(2,1)S(1)} collective-permute-done((bf16[16,512,128]{2,1,0:T(8,128)(2,1)S(1)}, bf16[16,512,128]{2,1,0:T(8,128)(2,1)S(1)}, u32[]{:S(2)}, u32[]{:S(2)}) %collective-permute-start.14) | collective-permute-done | bytes 2097184 | tf_op jit(solution)/shard_map/ppermute | solution.py:251
  102.6 5.4 %collective-permute-start.19 = (bf16[512,128]{1,0:T(8,128)(2,1)S(1)}, bf16[512,128]{1,0:T(8,128)(2,1)S(1)}, u32[]{:S(2)}, u32[]{:S(2)}) collective-permute-start(bf16[512,128]{1,0:T(8,128)(2,1)S(1)} %get-tuple-element.21), channel_id=1, source_target_pairs={{0,448},{64,0},{128,64},{192,128},{256,192},{320,256},{384,320},{4... | collective-permute-start | bytes 393224 | tf_op jit(solution)/shard_map/ppermute | solution.py:267
  111.1 5.6 %collective-permute-start.20 = (bf16[2,512,128]{2,1,0:T(8,128)(2,1)S(1)}, bf16[2,512,128]{2,1,0:T(8,128)(2,1)S(1)}, u32[]{:S(2)}, u32[]{:S(2)}) collective-permute-start(bf16[2,512,128]{2,1,0:T(8,128)(2,1)S(1)} %shard_map.69), channel_id=1, source_target_pairs={{0,448},{64,0},{128,64},{192,128},{256,192},{320,256},{384,320},{4... | collective-permute-start | bytes 786440 | tf_op jit(solution)/shard_map/ppermute | solution.py:267
  118.7 3.0 %collective-permute-done.20.came_ref = bf16[2,512,128]{2,1,0:T(8,128)(2,1)S(1)} collective-permute-done((bf16[2,512,128]{2,1,0:T(8,128)(2,1)S(1)}, bf16[2,512,128]{2,1,0:T(8,128)(2,1)S(1)}, u32[]{:S(2)}, u32[]{:S(2)}) %collective-permute-start.20) | collective-permute-done | bytes 262176 | tf_op jit(solution)/shard_map/ppermute | solution.py:267
  121.8 5.6 %collective-permute-start.21 = (bf16[2,512,128]{2,1,0:T(8,128)(2,1)S(1)}, bf16[2,512,128]{2,1,0:T(8,128)(2,1)S(1)}, u32[]{:S(2)}, u32[]{:S(2)}) collective-permute-start(bf16[2,512,128]{2,1,0:T(8,128)(2,1)S(1)} %shard_map.70), channel_id=1, source_target_pairs={{0,448},{64,0},{128,64},{192,128},{256,192},{320,256},{384,320},{4... | collective-permute-start | bytes 786440 | tf_op jit(solution)/shard_map/ppermute | solution.py:267
  127.5 1.9 %collective-permute-start.17 = (bf16[2,512,128]{2,1,0:T(8,128)(2,1)S(1)}, bf16[2,512,128]{2,1,0:T(8,128)(2,1)S(1)}, u32[]{:S(2)}, u32[]{:S(2)}) collective-permute-start(bf16[2,512,128]{2,1,0:T(8,128)(2,1)S(1)} %shard_map.67), channel_id=1, source_target_pairs={{0,64},{64,128},{128,192},{192,256},{256,320},{320,384},{384,448},... | collective-permute-start | bytes 786440 | tf_op jit(solution)/shard_map/ppermute | solution.py:267
  129.4 2.0 %collective-permute-done.21.came_ref = bf16[2,512,128]{2,1,0:T(8,128)(2,1)S(1)} collective-permute-done((bf16[2,512,128]{2,1,0:T(8,128)(2,1)S(1)}, bf16[2,512,128]{2,1,0:T(8,128)(2,1)S(1)}, u32[]{:S(2)}, u32[]{:S(2)}) %collective-permute-start.21) | collective-permute-done | bytes 262176 | tf_op jit(solution)/shard_map/ppermute | solution.py:267
  131.6 5.6 %collective-permute-start.22 = (bf16[2,512,128]{2,1,0:T(8,128)(2,1)S(1)}, bf16[2,512,128]{2,1,0:T(8,128)(2,1)S(1)}, u32[]{:S(2)}, u32[]{:S(2)}) collective-permute-start(bf16[2,512,128]{2,1,0:T(8,128)(2,1)S(1)} %shard_map.71), channel_id=1, source_target_pairs={{0,448},{64,0},{128,64},{192,128},{256,192},{320,256},{384,320},{4... | collective-permute-start | bytes 786440 | tf_op jit(solution)/shard_map/ppermute | solution.py:267
  141.1 5.7 %collective-permute-done.18.up_ref = bf16[2,512,128]{2,1,0:T(8,128)(2,1)S(1)} collective-permute-done((bf16[2,512,128]{2,1,0:T(8,128)(2,1)S(1)}, bf16[2,512,128]{2,1,0:T(8,128)(2,1)S(1)}, u32[]{:S(2)}, u32[]{:S(2)}) %collective-permute-start.18) | collective-permute-done | bytes 262176 | tf_op jit(solution)/shard_map/ppermute | solution.py:267
  146.9 14.3 %collective-permute-start.23 = (bf16[512,128]{1,0:T(8,128)(2,1)S(1)}, bf16[512,128]{1,0:T(8,128)(2,1)S(1)}, u32[]{:S(2)}, u32[]{:S(2)}) collective-permute-start(bf16[512,128]{1,0:T(8,128)(2,1)S(1)} %shard_map.72), channel_id=1, source_target_pairs={{0,512},{512,0},{1,513},{513,1},{2,514},{514,2},{3,515},{515,3},{4... | collective-permute-start | bytes 393224 | tf_op jit(solution)/shard_map/ppermute | solution.py:276
  161.2 4.9 %collective-permute-done.23.other_ref = bf16[512,128]{1,0:T(8,128)(2,1)S(1)} collective-permute-done((bf16[512,128]{1,0:T(8,128)(2,1)S(1)}, bf16[512,128]{1,0:T(8,128)(2,1)S(1)}, u32[]{:S(2)}, u32[]{:S(2)}) %collective-permute-start.23) | collective-permute-done | bytes 131104 | tf_op jit(solution)/shard_map/ppermute | solution.py:276
  (41 shorter events, 20.4 us)
Async XLA Ops:
  0.6 13.4 %collective-permute-start = (bf16[8,4096]{1,0:T(8,128)(2,1)}, bf16[8,4096]{1,0:T(8,128)(2,1)S(1)}, u32[]{:S(2)}, u32[]{:S(2)}) collective-permute-start(bf16[8,4096]{1,0:T(8,128)(2,1)} %param.4), channel_id=1, source_target_pairs={{0,16},{4,20},{8,24},{12,28},{16,0},{20,4},{24,8},{28,12},{1,17},{... | collective-permute-start | bytes 196616 | tf_op jit(solution)/shard_map/ppermute | solution.py:186
  11.6 20.8 %collective-permute-start.7 = (bf16[8,4096]{1,0:T(8,128)(2,1)}, bf16[8,4096]{1,0:T(8,128)(2,1)S(1)}, u32[]{:S(2)}, u32[]{:S(2)}) collective-permute-start(bf16[8,4096]{1,0:T(8,128)(2,1)} %param.5), channel_id=1, source_target_pairs={{0,16},{4,20},{8,24},{12,28},{16,0},{20,4},{24,8},{28,12},{1,17},{... | collective-permute-start | bytes 196616 | tf_op jit(solution)/shard_map/ppermute | solution.py:189
  14.8 26.0 %collective-permute-start.3 = (bf16[16,4096]{1,0:T(8,128)(2,1)S(1)}, bf16[16,4096]{1,0:T(8,128)(2,1)S(1)}, u32[]{:S(2)}, u32[]{:S(2)}) collective-permute-start(bf16[16,4096]{1,0:T(8,128)(2,1)S(1)} %pad_maximum_fusion.2), channel_id=1, source_target_pairs={{0,4},{4,0},{8,12},{12,8},{16,20},{20,16},{24,28},{28,24},{1,5},{5... | collective-permute-start | bytes 393224 | tf_op jit(solution)/shard_map/ppermute | solution.py:184
  20.8 22.0 %collective-permute-start.2 = (bf16[16,4096]{1,0:T(8,128)(2,1)S(1)}, bf16[16,4096]{1,0:T(8,128)(2,1)S(1)}, u32[]{:S(2)}, u32[]{:S(2)}) collective-permute-start(bf16[16,4096]{1,0:T(8,128)(2,1)S(1)} %pad_maximum_fusion.2), channel_id=1, source_target_pairs={{0,12},{4,8},{8,4},{12,0},{16,28},{20,24},{24,20},{28,16},{1,13},{... | collective-permute-start | bytes 393224 | tf_op jit(solution)/shard_map/ppermute | solution.py:184
  29.9 16.9 %collective-permute-start.1 = (bf16[16,4096]{1,0:T(8,128)(2,1)S(1)}, bf16[16,4096]{1,0:T(8,128)(2,1)S(1)}, u32[]{:S(2)}, u32[]{:S(2)}) collective-permute-start(bf16[16,4096]{1,0:T(8,128)(2,1)S(1)} %pad_maximum_fusion.2), channel_id=1, source_target_pairs={{0,8},{4,12},{8,0},{12,4},{16,24},{20,28},{24,16},{28,20},{1,9},{5... | collective-permute-start | bytes 393224 | tf_op jit(solution)/shard_map/ppermute | solution.py:184
  33.2 16.6 %collective-permute-start.10 = (bf16[16,4096]{1,0:T(8,128)(2,1)S(1)}, bf16[16,4096]{1,0:T(8,128)(2,1)S(1)}, u32[]{:S(2)}, u32[]{:S(2)}) collective-permute-start(bf16[16,4096]{1,0:T(8,128)(2,1)S(1)} %pad_maximum_fusion.3), channel_id=1, source_target_pairs={{0,4},{4,0},{8,12},{12,8},{16,20},{20,16},{24,28},{28,24},{1,5},{5... | collective-permute-start | bytes 393224 | tf_op jit(solution)/shard_map/ppermute | solution.py:184
  35.7 14.1 %collective-permute-start.9 = (bf16[16,4096]{1,0:T(8,128)(2,1)S(1)}, bf16[16,4096]{1,0:T(8,128)(2,1)S(1)}, u32[]{:S(2)}, u32[]{:S(2)}) collective-permute-start(bf16[16,4096]{1,0:T(8,128)(2,1)S(1)} %pad_maximum_fusion.3), channel_id=1, source_target_pairs={{0,12},{4,8},{8,4},{12,0},{16,28},{20,24},{24,20},{28,16},{1,13},{... | collective-permute-start | bytes 393224 | tf_op jit(solution)/shard_map/ppermute | solution.py:184
  40.9 12.3 %collective-permute-start.8 = (bf16[16,4096]{1,0:T(8,128)(2,1)S(1)}, bf16[16,4096]{1,0:T(8,128)(2,1)S(1)}, u32[]{:S(2)}, u32[]{:S(2)}) collective-permute-start(bf16[16,4096]{1,0:T(8,128)(2,1)S(1)} %pad_maximum_fusion.3), channel_id=1, source_target_pairs={{0,8},{4,12},{8,0},{12,4},{16,24},{20,28},{24,16},{28,20},{1,9},{5... | collective-permute-start | bytes 393224 | tf_op jit(solution)/shard_map/ppermute | solution.py:184
  46.8 11.6 %collective-permute-start.4 = (bf16[64,4096]{1,0:T(8,128)(2,1)S(1)}, bf16[64,4096]{1,0:T(8,128)(2,1)S(1)}, u32[]{:S(2)}, u32[]{:S(2)}) collective-permute-start(bf16[64,4096]{1,0:T(8,128)(2,1)S(1)} %pad_maximum_fusion.refs_0_), channel_id=1, source_target_pairs={{0,1},{1,2},{2,3},{3,0},{4,5},{5,6},{6,7},{7,4},{8,9},{9,10},{10,1... | collective-permute-start | bytes 1572872 | tf_op jit(solution)/shard_map/ppermute | solution.py:191
  53.2 18.0 %collective-permute-start.12 = (bf16[64,4096]{1,0:T(8,128)(2,1)S(1)}, bf16[64,4096]{1,0:T(8,128)(2,1)S(1)}, u32[]{:S(2)}, u32[]{:S(2)}) collective-permute-start(bf16[64,4096]{1,0:T(8,128)(2,1)S(1)} %pad_maximum_fusion.1.refs_0_.refs_3_), channel_id=1, source_target_pairs={{0,3},{1,0},{2,1},{3,2},{4,7},{5,4},{6,5},{7,6},{8,11},{9,8},{10,9... | collective-permute-start | bytes 1572872 | tf_op jit(solution)/shard_map/ppermute | solution.py:197
  55.9 26.6 %collective-permute-start.5 = (bf16[64,4096]{1,0:T(8,128)(2,1)S(1)}, bf16[64,4096]{1,0:T(8,128)(2,1)}, u32[]{:S(2)}, u32[]{:S(2)}) collective-permute-start(bf16[64,4096]{1,0:T(8,128)(2,1)S(1)} %pad_maximum_fusion.refs_0_), channel_id=1, source_target_pairs={{0,3},{1,0},{2,1},{3,2},{4,7},{5,4},{6,5},{7,6},{8,11},{9,8},{10,9... | collective-permute-start | bytes 1572872 | tf_op jit(solution)/shard_map/ppermute | solution.py:192
  58.4 24.1 %collective-permute-start.6 = (bf16[64,4096]{1,0:T(8,128)(2,1)S(1)}, bf16[64,4096]{1,0:T(8,128)(2,1)}, u32[]{:S(2)}, u32[]{:S(2)}) collective-permute-start(bf16[64,4096]{1,0:T(8,128)(2,1)S(1)} %collective-permute-done.4.refs_0_), channel_id=1, source_target_pairs={{0,1},{1,2},{2,3},{3,0},{4,5},{5,6},{6,7},{7,4},{8,9},{9,10},{10,1... | collective-permute-start | bytes 1572872 | tf_op jit(solution)/shard_map/ppermute | solution.py:196
  63.0 26.4 %collective-permute-start.11 = (bf16[64,4096]{1,0:T(8,128)(2,1)S(1)}, bf16[64,4096]{1,0:T(8,128)(2,1)S(1)}, u32[]{:S(2)}, u32[]{:S(2)}) collective-permute-start(bf16[64,4096]{1,0:T(8,128)(2,1)S(1)} %pad_maximum_fusion.1.refs_0_.refs_3_), channel_id=1, source_target_pairs={{0,1},{1,2},{2,3},{3,0},{4,5},{5,6},{6,7},{7,4},{8,9},{9,10},{10,1... | collective-permute-start | bytes 1572872 | tf_op jit(solution)/shard_map/ppermute | solution.py:198
  71.2 20.9 %collective-permute-start.13 = (bf16[64,4096]{1,0:T(8,128)(2,1)S(1)}, bf16[64,4096]{1,0:T(8,128)(2,1)S(1)}, u32[]{:S(2)}, u32[]{:S(2)}) collective-permute-start(bf16[64,4096]{1,0:T(8,128)(2,1)S(1)} %collective-permute-done.12.refs_2_.refs_5_), channel_id=1, source_target_pairs={{0,3},{1,0},{2,1},{3,2},{4,7},{5,4},{6,5},{7,6},{8,11},{9,8},{10,9... | collective-permute-start | bytes 1572872 | tf_op jit(solution)/shard_map/ppermute | solution.py:200
  73.2 13.6 %copy-start = (bf16[4096,1,384]{2,0,1:T(8,128)(2,1)S(1)}, bf16[4096,1,384]{2,0,1:T(8,128)(2,1)}, u32[]{:S(2)}) copy-start(bf16[4096,1,384]{2,0,1:T(8,128)(2,1)} %param.6) | copy-start | bytes 9437188
  86.7 5.4 %copy-start.1 = (bf16[1,128,4096]{2,1,0:T(8,128)(2,1)S(1)}, bf16[1,128,4096]{2,1,0:T(8,128)(2,1)}, u32[]{:S(2)}) copy-start(bf16[1,128,4096]{2,1,0:T(8,128)(2,1)} %param.7) | copy-start | bytes 3145732
  96.4 6.1 %collective-permute-start.14 = (bf16[16,512,128]{2,1,0:T(8,128)(2,1)S(1)}, bf16[16,512,128]{2,1,0:T(8,128)(2,1)S(1)}, u32[]{:S(2)}, u32[]{:S(2)}) collective-permute-start(bf16[16,512,128]{2,1,0:T(8,128)(2,1)S(1)} %shard_map.64), channel_id=1, source_target_pairs={{0,32},{32,0},{1,33},{33,1},{2,34},{34,2},{3,35},{35,3},{4,36},{36... | collective-permute-start | bytes 6291464 | tf_op jit(solution)/shard_map/ppermute | solution.py:251
  102.6 8.4 %collective-permute-start.19 = (bf16[512,128]{1,0:T(8,128)(2,1)S(1)}, bf16[512,128]{1,0:T(8,128)(2,1)S(1)}, u32[]{:S(2)}, u32[]{:S(2)}) collective-permute-start(bf16[512,128]{1,0:T(8,128)(2,1)S(1)} %get-tuple-element.21), channel_id=1, source_target_pairs={{0,448},{64,0},{128,64},{192,128},{256,192},{320,256},{384,320},{4... | collective-permute-start | bytes 393224 | tf_op jit(solution)/shard_map/ppermute | solution.py:267
  107.9 8.7 %collective-permute-start.15 = (bf16[512,128]{1,0:T(8,128)(2,1)S(1)}, bf16[512,128]{1,0:T(8,128)(2,1)S(1)}, u32[]{:S(2)}, u32[]{:S(2)}) collective-permute-start(bf16[512,128]{1,0:T(8,128)(2,1)S(1)} %get-tuple-element.20), channel_id=1, source_target_pairs={{0,64},{64,128},{128,192},{192,256},{256,320},{320,384},{384,448},... | collective-permute-start | bytes 393224 | tf_op jit(solution)/shard_map/ppermute | solution.py:267
  111.1 10.6 %collective-permute-start.20 = (bf16[2,512,128]{2,1,0:T(8,128)(2,1)S(1)}, bf16[2,512,128]{2,1,0:T(8,128)(2,1)S(1)}, u32[]{:S(2)}, u32[]{:S(2)}) collective-permute-start(bf16[2,512,128]{2,1,0:T(8,128)(2,1)S(1)} %shard_map.69), channel_id=1, source_target_pairs={{0,448},{64,0},{128,64},{192,128},{256,192},{320,256},{384,320},{4... | collective-permute-start | bytes 786440 | tf_op jit(solution)/shard_map/ppermute | solution.py:267
  116.8 10.6 %collective-permute-start.16 = (bf16[2,512,128]{2,1,0:T(8,128)(2,1)S(1)}, bf16[2,512,128]{2,1,0:T(8,128)(2,1)S(1)}, u32[]{:S(2)}, u32[]{:S(2)}) collective-permute-start(bf16[2,512,128]{2,1,0:T(8,128)(2,1)S(1)} %shard_map.66), channel_id=1, source_target_pairs={{0,64},{64,128},{128,192},{192,256},{256,320},{320,384},{384,448},... | collective-permute-start | bytes 786440 | tf_op jit(solution)/shard_map/ppermute | solution.py:267
  121.8 9.7 %collective-permute-start.21 = (bf16[2,512,128]{2,1,0:T(8,128)(2,1)S(1)}, bf16[2,512,128]{2,1,0:T(8,128)(2,1)S(1)}, u32[]{:S(2)}, u32[]{:S(2)}) collective-permute-start(bf16[2,512,128]{2,1,0:T(8,128)(2,1)S(1)} %shard_map.70), channel_id=1, source_target_pairs={{0,448},{64,0},{128,64},{192,128},{256,192},{320,256},{384,320},{4... | collective-permute-start | bytes 786440 | tf_op jit(solution)/shard_map/ppermute | solution.py:267
  127.5 9.7 %collective-permute-start.17 = (bf16[2,512,128]{2,1,0:T(8,128)(2,1)S(1)}, bf16[2,512,128]{2,1,0:T(8,128)(2,1)S(1)}, u32[]{:S(2)}, u32[]{:S(2)}) collective-permute-start(bf16[2,512,128]{2,1,0:T(8,128)(2,1)S(1)} %shard_map.67), channel_id=1, source_target_pairs={{0,64},{64,128},{128,192},{192,256},{256,320},{320,384},{384,448},... | collective-permute-start | bytes 786440 | tf_op jit(solution)/shard_map/ppermute | solution.py:267
  131.6 9.5 %collective-permute-start.22 = (bf16[2,512,128]{2,1,0:T(8,128)(2,1)S(1)}, bf16[2,512,128]{2,1,0:T(8,128)(2,1)S(1)}, u32[]{:S(2)}, u32[]{:S(2)}) collective-permute-start(bf16[2,512,128]{2,1,0:T(8,128)(2,1)S(1)} %shard_map.71), channel_id=1, source_target_pairs={{0,448},{64,0},{128,64},{192,128},{256,192},{320,256},{384,320},{4... | collective-permute-start | bytes 786440 | tf_op jit(solution)/shard_map/ppermute | solution.py:267
  137.3 9.5 %collective-permute-start.18 = (bf16[2,512,128]{2,1,0:T(8,128)(2,1)S(1)}, bf16[2,512,128]{2,1,0:T(8,128)(2,1)S(1)}, u32[]{:S(2)}, u32[]{:S(2)}) collective-permute-start(bf16[2,512,128]{2,1,0:T(8,128)(2,1)S(1)} %shard_map.68), channel_id=1, source_target_pairs={{0,64},{64,128},{128,192},{192,256},{256,320},{320,384},{384,448},... | collective-permute-start | bytes 786440 | tf_op jit(solution)/shard_map/ppermute | solution.py:267
  146.9 19.2 %collective-permute-start.23 = (bf16[512,128]{1,0:T(8,128)(2,1)S(1)}, bf16[512,128]{1,0:T(8,128)(2,1)S(1)}, u32[]{:S(2)}, u32[]{:S(2)}) collective-permute-start(bf16[512,128]{1,0:T(8,128)(2,1)S(1)} %shard_map.72), channel_id=1, source_target_pairs={{0,512},{512,0},{1,513},{513,1},{2,514},{514,2},{3,515},{515,3},{4... | collective-permute-start | bytes 393224 | tf_op jit(solution)/shard_map/ppermute | solution.py:276

commit v9 on v8

--- a/solution.py
+++ b/solution.py
@@ -186,7 +186,7 @@
     t_other = lax.ppermute(tokens, "zl", swap(n_z, 4))
     t = join(tokens, t_other)
     t_near = within(t)
-    c = join(cotangent, lax.ppermute(cotangent, "zl", swap(n_z, 4)))
+    c = join(cotangent, lax.ppermute(after(cotangent, t), "zl", swap(n_z, 4)))
     t = join(t, *t_near)
     t_left = lax.ppermute(t, "x", up)
     t_right = lax.ppermute(t, "x", down)
@@ -196,9 +196,10 @@
     t_far = lax.ppermute(t_left, "x", up)
     c_right = lax.ppermute(c, "x", down)
     c_left = lax.ppermute(after(c, t_left), "x", up)
-    rest = normalized(t_left, t_right, t_far)
+    left = normalized(t_left)
+    rest = normalized(t_right, t_far)
     c_far = lax.ppermute(c_right, "x", down)
-    return [normed, rest], [c, c_left, c_right, c_far]
+    return [normed, left, rest], [c, c_left, c_right, c_far]
 
 
 def local(sizes, tokens, cotangent, w_qkv, w_out):

time: 168 us -> 174 us (1.036)
  starting transfers between devices: 104 us -> 107 us
  waiting for transfers between devices: 44.9 us -> 47.5 us
    ppermute x1, starting transfers between devices: 1.92 us -> 7.95 us  [gather(): c = join(cotangent, lax.ppermute(after(cotangent, t), 'zl', swap(n_z, 4)))]
    ppermute x6, starting transfers between devices: 27.1 us -> 23 us  [within(): return [lax.ppermute(rows, 'zl', swap(n_z, s)) for s in (2, 3, 1)]]
    ppermute x1, waiting for transfers between devices: 4.86 us -> 7.28 us  [local(): other = lax.ppermute(away, 'zh', swap(far, 1))]
    ppermute x1, waiting for transfers between devices: 0.51 us -> 2.44 us  [gather(): t_other = lax.ppermute(tokens, 'zl', swap(n_z, 4))]
    pallas_call x2 -> x3, Pallas kernels: 5.21 us -> 5.21 us  [normalized(): pl.pallas_call(normalize_kernel, out_shape=jax.ShapeDtypeStruct((rows, pi...]
where the time goes in v9:
time: 174 us; the launch traced here: 173 us
  starting transfers between devices  107 us (61%)
  waiting for transfers between devices  47.5 us (27%)
  Pallas kernels  15.5 us (9%)
  other arithmetic  1.93 us (1%)
    ppermute x8, starting transfers between devices, local(): lax.ppermute(m, 'y', turn(near, way))  29.9 us
    ppermute x6, starting transfers between devices, within(): return [lax.ppermute(rows, 'zl', swap(n_z, s)) for s in (2, 3, 1)]  23 us
    ppermute x1, starting transfers between devices, local(): other = lax.ppermute(away, 'zh', swap(far, 1))  14.2 us
    ppermute x8, waiting for transfers between devices, local(): lax.ppermute(m, 'y', turn(near, way))  13.7 us
    ppermute x1, starting transfers between devices, gather(): t_other = lax.ppermute(tokens, 'zl', swap(n_z, 4))  10.9 us
    ppermute x1, starting transfers between devices, gather(): c = join(cotangent, lax.ppermute(after(cotangent, t), 'zl', swap(n_z, 4)))  7.95 us
    ppermute x1, waiting for transfers between devices, gather(): t_right = lax.ppermute(t, 'x', down)  7.31 us
    ppermute x1, waiting for transfers between devices, local(): other = lax.ppermute(away, 'zh', swap(far, 1))  7.28 us
  transfers between devices with their start and end apart: 24, of which 13 were waited for; matrix products, arithmetic and copies ran while one was open for 1% of the time, Pallas kernels for 6%

profile of v9, /device:TPU:6, one launch (start us, length us, event | category | flops | bytes accessed | tf_op | source)
XLA Modules:
  0.0 173.0 jit_solution(8443241377607590858)
XLA Ops:
  0.6 10.9 %collective-permute-start = (bf16[8,4096]{1,0:T(8,128)(2,1)}, bf16[8,4096]{1,0:T(8,128)(2,1)S(1)}, u32[]{:S(2)}, u32[]{:S(2)}) collective-permute-start(bf16[8,4096]{1,0:T(8,128)(2,1)} %param.4), channel_id=1, source_target_pairs={{0,16},{4,20},{8,24},{12,28},{16,0},{20,4},{24,8},{28,12},{1,17},{... | collective-permute-start | bytes 196616 | tf_op jit(solution)/shard_map/ppermute | solution.py:186
  11.6 2.4 %collective-permute-done = bf16[8,4096]{1,0:T(8,128)(2,1)S(1)} collective-permute-done((bf16[8,4096]{1,0:T(8,128)(2,1)}, bf16[8,4096]{1,0:T(8,128)(2,1)S(1)}, u32[]{:S(2)}, u32[]{:S(2)}) %collective-permute-start) | collective-permute-done | bytes 65568 | tf_op jit(solution)/shard_map/ppermute | solution.py:186
  14.8 7.9 %collective-permute-start.7 = (bf16[8,4096]{1,0:T(8,128)(2,1)}, bf16[8,4096]{1,0:T(8,128)(2,1)S(1)}, u32[]{:S(2)}, u32[]{:S(2)}) collective-permute-start(bf16[8,4096]{1,0:T(8,128)(2,1)} %param.5), channel_id=1, source_target_pairs={{0,16},{4,20},{8,24},{12,28},{16,0},{20,4},{24,8},{28,12},{1,17},{... | collective-permute-start | bytes 196616 | tf_op jit(solution)/shard_map/ppermute | solution.py:189
  22.8 4.6 %collective-permute-start.3 = (bf16[16,4096]{1,0:T(8,128)(2,1)S(1)}, bf16[16,4096]{1,0:T(8,128)(2,1)S(1)}, u32[]{:S(2)}, u32[]{:S(2)}) collective-permute-start(bf16[16,4096]{1,0:T(8,128)(2,1)S(1)} %pad_maximum_fusion.2), channel_id=1, source_target_pairs={{0,4},{4,0},{8,12},{12,8},{16,20},{20,16},{24,28},{28,24},{1,5},{5... | collective-permute-start | bytes 393224 | tf_op jit(solution)/shard_map/ppermute | solution.py:184
  27.4 6.4 %collective-permute-start.2 = (bf16[16,4096]{1,0:T(8,128)(2,1)S(1)}, bf16[16,4096]{1,0:T(8,128)(2,1)S(1)}, u32[]{:S(2)}, u32[]{:S(2)}) collective-permute-start(bf16[16,4096]{1,0:T(8,128)(2,1)S(1)} %pad_maximum_fusion.2), channel_id=1, source_target_pairs={{0,12},{4,8},{8,4},{12,0},{16,28},{20,24},{24,20},{28,16},{1,13},{... | collective-permute-start | bytes 393224 | tf_op jit(solution)/shard_map/ppermute | solution.py:184
  33.8 2.5 %collective-permute-start.1 = (bf16[16,4096]{1,0:T(8,128)(2,1)S(1)}, bf16[16,4096]{1,0:T(8,128)(2,1)S(1)}, u32[]{:S(2)}, u32[]{:S(2)}) collective-permute-start(bf16[16,4096]{1,0:T(8,128)(2,1)S(1)} %pad_maximum_fusion.2), channel_id=1, source_target_pairs={{0,8},{4,12},{8,0},{12,4},{16,24},{20,28},{24,16},{28,20},{1,9},{5... | collective-permute-start | bytes 393224 | tf_op jit(solution)/shard_map/ppermute | solution.py:184
  37.1 2.5 %collective-permute-start.10 = (bf16[16,4096]{1,0:T(8,128)(2,1)S(1)}, bf16[16,4096]{1,0:T(8,128)(2,1)S(1)}, u32[]{:S(2)}, u32[]{:S(2)}) collective-permute-start(bf16[16,4096]{1,0:T(8,128)(2,1)S(1)} %pad_maximum_fusion.3), channel_id=1, source_target_pairs={{0,4},{4,0},{8,12},{12,8},{16,20},{20,16},{24,28},{28,24},{1,5},{5... | collective-permute-start | bytes 393224 | tf_op jit(solution)/shard_map/ppermute | solution.py:184
  39.6 5.2 %collective-permute-start.9 = (bf16[16,4096]{1,0:T(8,128)(2,1)S(1)}, bf16[16,4096]{1,0:T(8,128)(2,1)S(1)}, u32[]{:S(2)}, u32[]{:S(2)}) collective-permute-start(bf16[16,4096]{1,0:T(8,128)(2,1)S(1)} %pad_maximum_fusion.3), channel_id=1, source_target_pairs={{0,12},{4,8},{8,4},{12,0},{16,28},{20,24},{24,20},{28,16},{1,13},{... | collective-permute-start | bytes 393224 | tf_op jit(solution)/shard_map/ppermute | solution.py:184
  46.7 3.9 %collective-permute-done.1 = bf16[16,4096]{1,0:T(8,128)(2,1)S(1)} collective-permute-done((bf16[16,4096]{1,0:T(8,128)(2,1)S(1)}, bf16[16,4096]{1,0:T(8,128)(2,1)S(1)}, u32[]{:S(2)}, u32[]{:S(2)}) %collective-permute-start.1) | collective-permute-done | bytes 131104 | tf_op jit(solution)/shard_map/ppermute | solution.py:184
  50.7 4.3 %collective-permute-start.4 = (bf16[64,4096]{1,0:T(8,128)(2,1)S(1)}, bf16[64,4096]{1,0:T(8,128)(2,1)S(1)}, u32[]{:S(2)}, u32[]{:S(2)}) collective-permute-start(bf16[64,4096]{1,0:T(8,128)(2,1)S(1)} %pad_maximum_fusion.refs_0_), channel_id=1, source_target_pairs={{0,1},{1,2},{2,3},{3,0},{4,5},{5,6},{6,7},{7,4},{8,9},{9,10},{10,1... | collective-permute-start | bytes 1572872 | tf_op jit(solution)/shard_map/ppermute | solution.py:191
  55.0 2.0 %collective-permute-done.8 = bf16[16,4096]{1,0:T(8,128)(2,1)S(1)} collective-permute-done((bf16[16,4096]{1,0:T(8,128)(2,1)S(1)}, bf16[16,4096]{1,0:T(8,128)(2,1)S(1)}, u32[]{:S(2)}, u32[]{:S(2)}) %collective-permute-start.8) | collective-permute-done | bytes 131104 | tf_op jit(solution)/shard_map/ppermute | solution.py:184
  57.0 2.7 %collective-permute-start.12 = (bf16[64,4096]{1,0:T(8,128)(2,1)S(1)}, bf16[64,4096]{1,0:T(8,128)(2,1)S(1)}, u32[]{:S(2)}, u32[]{:S(2)}) collective-permute-start(bf16[64,4096]{1,0:T(8,128)(2,1)S(1)} %pad_maximum_fusion.1.refs_0_.refs_4_), channel_id=1, source_target_pairs={{0,3},{1,0},{2,1},{3,2},{4,7},{5,4},{6,5},{7,6},{8,11},{9,8},{10,9... | collective-permute-start | bytes 1572872 | tf_op jit(solution)/shard_map/ppermute | solution.py:197
  59.8 2.4 %collective-permute-start.5 = (bf16[64,4096]{1,0:T(8,128)(2,1)S(1)}, bf16[64,4096]{1,0:T(8,128)(2,1)}, u32[]{:S(2)}, u32[]{:S(2)}) collective-permute-start(bf16[64,4096]{1,0:T(8,128)(2,1)S(1)} %pad_maximum_fusion.refs_0_), channel_id=1, source_target_pairs={{0,3},{1,0},{2,1},{3,2},{4,7},{5,4},{6,5},{7,6},{8,11},{9,8},{10,9... | collective-permute-start | bytes 1572872 | tf_op jit(solution)/shard_map/ppermute | solution.py:192
  62.2 5.0 %collective-permute-start.6 = (bf16[64,4096]{1,0:T(8,128)(2,1)S(1)}, bf16[64,4096]{1,0:T(8,128)(2,1)}, u32[]{:S(2)}, u32[]{:S(2)}) collective-permute-start(bf16[64,4096]{1,0:T(8,128)(2,1)S(1)} %collective-permute-done.4.refs_0_), channel_id=1, source_target_pairs={{0,1},{1,2},{2,3},{3,0},{4,5},{5,6},{6,7},{7,4},{8,9},{9,10},{10,1... | collective-permute-start | bytes 1572872 | tf_op jit(solution)/shard_map/ppermute | solution.py:196
  67.3 2.7 %collective-permute-start.11 = (bf16[64,4096]{1,0:T(8,128)(2,1)S(1)}, bf16[64,4096]{1,0:T(8,128)(2,1)S(1)}, u32[]{:S(2)}, u32[]{:S(2)}) collective-permute-start(bf16[64,4096]{1,0:T(8,128)(2,1)S(1)} %pad_maximum_fusion.1.refs_0_.refs_4_), channel_id=1, source_target_pairs={{0,1},{1,2},{2,3},{3,0},{4,5},{5,6},{6,7},{7,4},{8,9},{9,10},{10,1... | collective-permute-start | bytes 1572872 | tf_op jit(solution)/shard_map/ppermute | solution.py:198
  70.0 5.0 %collective-permute-done.12.refs_2_.refs_6_ = bf16[64,4096]{1,0:T(8,128)(2,1)S(1)} collective-permute-done((bf16[64,4096]{1,0:T(8,128)(2,1)S(1)}, bf16[64,4096]{1,0:T(8,128)(2,1)S(1)}, u32[]{:S(2)}, u32[]{:S(2)}) %collective-permute-start.12) | collective-permute-done | bytes 524320 | tf_op jit(solution)/shard_map/ppermute | solution.py:197
  79.0 7.3 %collective-permute-done.5.refs_0_ = bf16[64,4096]{1,0:T(8,128)(2,1)} collective-permute-done((bf16[64,4096]{1,0:T(8,128)(2,1)S(1)}, bf16[64,4096]{1,0:T(8,128)(2,1)}, u32[]{:S(2)}, u32[]{:S(2)}) %collective-permute-start.5) | collective-permute-done | bytes 524320 | tf_op jit(solution)/shard_map/ppermute | solution.py:192
  86.3 3.2 %shard_map.61.refs_2_.refs_3_ = bf16[128,4096]{1,0:T(8,128)(2,1)S(1)} custom-call(bf16[64,4096]{1,0:T(8,128)(2,1)} %collective-permute-done.5.refs_0_, bf16[64,4096]{1,0:T(8,128)(2,1)} %collective-permute-done.6.refs_1_), custom_call_target="tpu_custom_call" | custom-call | tf_op jit(solution)/shard_map/pallas_call | solution.py:168
  89.6 3.0 %shard_map.62 = (bf16[128,256]{1,0:T(8,128)(2,1)S(1)}, f32[256,128]{1,0:T(8,128)S(1)}, f32[256,128]{1,0:T(8,128)S(1)}, f32[256,128]{1,0:T(8,128)S(1)}, f32[256,2...) custom-call(bf16[64,4096]{1,0:T(8,128)(2,1)S(1)} %shard_map.59.refs_0_.refs_1_, ...), custom_call_target="tpu_custom_call" | custom-call | tf_op jit(solution)/shard_map/pallas_call | solution.py:213
  92.6 3.3 %collective-permute-done.13.refs_3_.refs_7_ = bf16[64,4096]{1,0:T(8,128)(2,1)S(1)} collective-permute-done((bf16[64,4096]{1,0:T(8,128)(2,1)S(1)}, bf16[64,4096]{1,0:T(8,128)(2,1)S(1)}, u32[]{:S(2)}, u32[]{:S(2)}) %collective-permute-start.13) | collective-permute-done | bytes 524320 | tf_op jit(solution)/shard_map/ppermute | solution.py:201
  95.9 2.9 %shard_map.63.refs_8_ = bf16[384,256]{1,0:T(8,128)(2,1)S(1)} custom-call(bf16[64,4096]{1,0:T(8,128)(2,1)S(1)} %pad_maximum_fusion.1.refs_0_.refs_4_, bf16[64,4096]{1,0:T(8,128)(2,1)S(1)} %collective-permute-done.11.refs_1_.refs_5_, bf16[64,4096]{1,0:T(8,128)(2,1)S(1)} %collective-permute-done.12.refs_2_.refs_6_, ...), custom_call_target="tpu_custom_call" | custom-call | tf_op jit(solution)/shard_map/pallas_call | solution.py:228
  103.7 2.6 %collective-permute-done.14.theirs_ref = bf16[16,512,128]{2,1,0:T(8,128)(2,1)S(1)} collective-permute-done((bf16[16,512,128]{2,1,0:T(8,128)(2,1)S(1)}, bf16[16,512,128]{2,1,0:T(8,128)(2,1)S(1)}, u32[]{:S(2)}, u32[]{:S(2)}) %collective-permute-start.14) | collective-permute-done | bytes 2097184 | tf_op jit(solution)/shard_map/ppermute | solution.py:252
  106.4 5.4 %collective-permute-start.19 = (bf16[512,128]{1,0:T(8,128)(2,1)S(1)}, bf16[512,128]{1,0:T(8,128)(2,1)S(1)}, u32[]{:S(2)}, u32[]{:S(2)}) collective-permute-start(bf16[512,128]{1,0:T(8,128)(2,1)S(1)} %get-tuple-element.23), channel_id=1, source_target_pairs={{0,448},{64,0},{128,64},{192,128},{256,192},{320,256},{384,320},{4... | collective-permute-start | bytes 393224 | tf_op jit(solution)/shard_map/ppermute | solution.py:268
  111.8 1.9 %collective-permute-start.15 = (bf16[512,128]{1,0:T(8,128)(2,1)S(1)}, bf16[512,128]{1,0:T(8,128)(2,1)S(1)}, u32[]{:S(2)}, u32[]{:S(2)}) collective-permute-start(bf16[512,128]{1,0:T(8,128)(2,1)S(1)} %get-tuple-element.22), channel_id=1, source_target_pairs={{0,64},{64,128},{128,192},{192,256},{256,320},{320,384},{384,448},... | collective-permute-start | bytes 393224 | tf_op jit(solution)/shard_map/ppermute | solution.py:268
  114.9 5.6 %collective-permute-start.20 = (bf16[2,512,128]{2,1,0:T(8,128)(2,1)S(1)}, bf16[2,512,128]{2,1,0:T(8,128)(2,1)S(1)}, u32[]{:S(2)}, u32[]{:S(2)}) collective-permute-start(bf16[2,512,128]{2,1,0:T(8,128)(2,1)S(1)} %shard_map.70), channel_id=1, source_target_pairs={{0,448},{64,0},{128,64},{192,128},{256,192},{320,256},{384,320},{4... | collective-permute-start | bytes 786440 | tf_op jit(solution)/shard_map/ppermute | solution.py:268
  122.5 3.0 %collective-permute-done.20.came_ref = bf16[2,512,128]{2,1,0:T(8,128)(2,1)S(1)} collective-permute-done((bf16[2,512,128]{2,1,0:T(8,128)(2,1)S(1)}, bf16[2,512,128]{2,1,0:T(8,128)(2,1)S(1)}, u32[]{:S(2)}, u32[]{:S(2)}) %collective-permute-start.20) | collective-permute-done | bytes 262176 | tf_op jit(solution)/shard_map/ppermute | solution.py:268
  125.6 5.6 %collective-permute-start.21 = (bf16[2,512,128]{2,1,0:T(8,128)(2,1)S(1)}, bf16[2,512,128]{2,1,0:T(8,128)(2,1)S(1)}, u32[]{:S(2)}, u32[]{:S(2)}) collective-permute-start(bf16[2,512,128]{2,1,0:T(8,128)(2,1)S(1)} %shard_map.71), channel_id=1, source_target_pairs={{0,448},{64,0},{128,64},{192,128},{256,192},{320,256},{384,320},{4... | collective-permute-start | bytes 786440 | tf_op jit(solution)/shard_map/ppermute | solution.py:268
  133.3 2.0 %collective-permute-done.21.came_ref = bf16[2,512,128]{2,1,0:T(8,128)(2,1)S(1)} collective-permute-done((bf16[2,512,128]{2,1,0:T(8,128)(2,1)S(1)}, bf16[2,512,128]{2,1,0:T(8,128)(2,1)S(1)}, u32[]{:S(2)}, u32[]{:S(2)}) %collective-permute-start.21) | collective-permute-done | bytes 262176 | tf_op jit(solution)/shard_map/ppermute | solution.py:268
  135.4 5.6 %collective-permute-start.22 = (bf16[2,512,128]{2,1,0:T(8,128)(2,1)S(1)}, bf16[2,512,128]{2,1,0:T(8,128)(2,1)S(1)}, u32[]{:S(2)}, u32[]{:S(2)}) collective-permute-start(bf16[2,512,128]{2,1,0:T(8,128)(2,1)S(1)} %shard_map.72), channel_id=1, source_target_pairs={{0,448},{64,0},{128,64},{192,128},{256,192},{320,256},{384,320},{4... | collective-permute-start | bytes 786440 | tf_op jit(solution)/shard_map/ppermute | solution.py:268
  144.9 5.7 %collective-permute-done.18.up_ref = bf16[2,512,128]{2,1,0:T(8,128)(2,1)S(1)} collective-permute-done((bf16[2,512,128]{2,1,0:T(8,128)(2,1)S(1)}, bf16[2,512,128]{2,1,0:T(8,128)(2,1)S(1)}, u32[]{:S(2)}, u32[]{:S(2)}) %collective-permute-start.18) | collective-permute-done | bytes 262176 | tf_op jit(solution)/shard_map/ppermute | solution.py:268
  150.7 14.2 %collective-permute-start.23 = (bf16[512,128]{1,0:T(8,128)(2,1)S(1)}, bf16[512,128]{1,0:T(8,128)(2,1)S(1)}, u32[]{:S(2)}, u32[]{:S(2)}) collective-permute-start(bf16[512,128]{1,0:T(8,128)(2,1)S(1)} %shard_map.73), channel_id=1, source_target_pairs={{0,512},{512,0},{1,513},{513,1},{2,514},{514,2},{3,515},{515,3},{4... | collective-permute-start | bytes 393224 | tf_op jit(solution)/shard_map/ppermute | solution.py:277
  164.9 7.3 %collective-permute-done.23.other_ref = bf16[512,128]{1,0:T(8,128)(2,1)S(1)} collective-permute-done((bf16[512,128]{1,0:T(8,128)(2,1)S(1)}, bf16[512,128]{1,0:T(8,128)(2,1)S(1)}, u32[]{:S(2)}, u32[]{:S(2)}) %collective-permute-start.23) | collective-permute-done | bytes 131104 | tf_op jit(solution)/shard_map/ppermute | solution.py:277
  (42 shorter events, 22.8 us)
Async XLA Ops:
  0.6 13.4 %collective-permute-start = (bf16[8,4096]{1,0:T(8,128)(2,1)}, bf16[8,4096]{1,0:T(8,128)(2,1)S(1)}, u32[]{:S(2)}, u32[]{:S(2)}) collective-permute-start(bf16[8,4096]{1,0:T(8,128)(2,1)} %param.4), channel_id=1, source_target_pairs={{0,16},{4,20},{8,24},{12,28},{16,0},{20,4},{24,8},{28,12},{1,17},{... | collective-permute-start | bytes 196616 | tf_op jit(solution)/shard_map/ppermute | solution.py:186
  14.8 21.4 %collective-permute-start.7 = (bf16[8,4096]{1,0:T(8,128)(2,1)}, bf16[8,4096]{1,0:T(8,128)(2,1)S(1)}, u32[]{:S(2)}, u32[]{:S(2)}) collective-permute-start(bf16[8,4096]{1,0:T(8,128)(2,1)} %param.5), channel_id=1, source_target_pairs={{0,16},{4,20},{8,24},{12,28},{16,0},{20,4},{24,8},{28,12},{1,17},{... | collective-permute-start | bytes 196616 | tf_op jit(solution)/shard_map/ppermute | solution.py:189
  22.8 22.0 %collective-permute-start.3 = (bf16[16,4096]{1,0:T(8,128)(2,1)S(1)}, bf16[16,4096]{1,0:T(8,128)(2,1)S(1)}, u32[]{:S(2)}, u32[]{:S(2)}) collective-permute-start(bf16[16,4096]{1,0:T(8,128)(2,1)S(1)} %pad_maximum_fusion.2), channel_id=1, source_target_pairs={{0,4},{4,0},{8,12},{12,8},{16,20},{20,16},{24,28},{28,24},{1,5},{5... | collective-permute-start | bytes 393224 | tf_op jit(solution)/shard_map/ppermute | solution.py:184
  27.4 19.3 %collective-permute-start.2 = (bf16[16,4096]{1,0:T(8,128)(2,1)S(1)}, bf16[16,4096]{1,0:T(8,128)(2,1)S(1)}, u32[]{:S(2)}, u32[]{:S(2)}) collective-permute-start(bf16[16,4096]{1,0:T(8,128)(2,1)S(1)} %pad_maximum_fusion.2), channel_id=1, source_target_pairs={{0,12},{4,8},{8,4},{12,0},{16,28},{20,24},{24,20},{28,16},{1,13},{... | collective-permute-start | bytes 393224 | tf_op jit(solution)/shard_map/ppermute | solution.py:184
  33.8 16.8 %collective-permute-start.1 = (bf16[16,4096]{1,0:T(8,128)(2,1)S(1)}, bf16[16,4096]{1,0:T(8,128)(2,1)S(1)}, u32[]{:S(2)}, u32[]{:S(2)}) collective-permute-start(bf16[16,4096]{1,0:T(8,128)(2,1)S(1)} %pad_maximum_fusion.2), channel_id=1, source_target_pairs={{0,8},{4,12},{8,0},{12,4},{16,24},{20,28},{24,16},{28,20},{1,9},{5... | collective-permute-start | bytes 393224 | tf_op jit(solution)/shard_map/ppermute | solution.py:184
  37.1 17.9 %collective-permute-start.10 = (bf16[16,4096]{1,0:T(8,128)(2,1)S(1)}, bf16[16,4096]{1,0:T(8,128)(2,1)S(1)}, u32[]{:S(2)}, u32[]{:S(2)}) collective-permute-start(bf16[16,4096]{1,0:T(8,128)(2,1)S(1)} %pad_maximum_fusion.3), channel_id=1, source_target_pairs={{0,4},{4,0},{8,12},{12,8},{16,20},{20,16},{24,28},{28,24},{1,5},{5... | collective-permute-start | bytes 393224 | tf_op jit(solution)/shard_map/ppermute | solution.py:184
  39.6 15.4 %collective-permute-start.9 = (bf16[16,4096]{1,0:T(8,128)(2,1)S(1)}, bf16[16,4096]{1,0:T(8,128)(2,1)S(1)}, u32[]{:S(2)}, u32[]{:S(2)}) collective-permute-start(bf16[16,4096]{1,0:T(8,128)(2,1)S(1)} %pad_maximum_fusion.3), channel_id=1, source_target_pairs={{0,12},{4,8},{8,4},{12,0},{16,28},{20,24},{24,20},{28,16},{1,13},{... | collective-permute-start | bytes 393224 | tf_op jit(solution)/shard_map/ppermute | solution.py:184
  44.8 12.2 %collective-permute-start.8 = (bf16[16,4096]{1,0:T(8,128)(2,1)S(1)}, bf16[16,4096]{1,0:T(8,128)(2,1)S(1)}, u32[]{:S(2)}, u32[]{:S(2)}) collective-permute-start(bf16[16,4096]{1,0:T(8,128)(2,1)S(1)} %pad_maximum_fusion.3), channel_id=1, source_target_pairs={{0,8},{4,12},{8,0},{12,4},{16,24},{20,28},{24,16},{28,20},{1,9},{5... | collective-permute-start | bytes 393224 | tf_op jit(solution)/shard_map/ppermute | solution.py:184
  50.7 11.6 %collective-permute-start.4 = (bf16[64,4096]{1,0:T(8,128)(2,1)S(1)}, bf16[64,4096]{1,0:T(8,128)(2,1)S(1)}, u32[]{:S(2)}, u32[]{:S(2)}) collective-permute-start(bf16[64,4096]{1,0:T(8,128)(2,1)S(1)} %pad_maximum_fusion.refs_0_), channel_id=1, source_target_pairs={{0,1},{1,2},{2,3},{3,0},{4,5},{5,6},{6,7},{7,4},{8,9},{9,10},{10,1... | collective-permute-start | bytes 1572872 | tf_op jit(solution)/shard_map/ppermute | solution.py:191
  57.0 18.0 %collective-permute-start.12 = (bf16[64,4096]{1,0:T(8,128)(2,1)S(1)}, bf16[64,4096]{1,0:T(8,128)(2,1)S(1)}, u32[]{:S(2)}, u32[]{:S(2)}) collective-permute-start(bf16[64,4096]{1,0:T(8,128)(2,1)S(1)} %pad_maximum_fusion.1.refs_0_.refs_4_), channel_id=1, source_target_pairs={{0,3},{1,0},{2,1},{3,2},{4,7},{5,4},{6,5},{7,6},{8,11},{9,8},{10,9... | collective-permute-start | bytes 1572872 | tf_op jit(solution)/shard_map/ppermute | solution.py:197
  59.8 26.6 %collective-permute-start.5 = (bf16[64,4096]{1,0:T(8,128)(2,1)S(1)}, bf16[64,4096]{1,0:T(8,128)(2,1)}, u32[]{:S(2)}, u32[]{:S(2)}) collective-permute-start(bf16[64,4096]{1,0:T(8,128)(2,1)S(1)} %pad_maximum_fusion.refs_0_), channel_id=1, source_target_pairs={{0,3},{1,0},{2,1},{3,2},{4,7},{5,4},{6,5},{7,6},{8,11},{9,8},{10,9... | collective-permute-start | bytes 1572872 | tf_op jit(solution)/shard_map/ppermute | solution.py:192
  62.2 24.1 %collective-permute-start.6 = (bf16[64,4096]{1,0:T(8,128)(2,1)S(1)}, bf16[64,4096]{1,0:T(8,128)(2,1)}, u32[]{:S(2)}, u32[]{:S(2)}) collective-permute-start(bf16[64,4096]{1,0:T(8,128)(2,1)S(1)} %collective-permute-done.4.refs_0_), channel_id=1, source_target_pairs={{0,1},{1,2},{2,3},{3,0},{4,5},{5,6},{6,7},{7,4},{8,9},{9,10},{10,1... | collective-permute-start | bytes 1572872 | tf_op jit(solution)/shard_map/ppermute | solution.py:196
  67.3 25.4 %collective-permute-start.11 = (bf16[64,4096]{1,0:T(8,128)(2,1)S(1)}, bf16[64,4096]{1,0:T(8,128)(2,1)S(1)}, u32[]{:S(2)}, u32[]{:S(2)}) collective-permute-start(bf16[64,4096]{1,0:T(8,128)(2,1)S(1)} %pad_maximum_fusion.1.refs_0_.refs_4_), channel_id=1, source_target_pairs={{0,1},{1,2},{2,3},{3,0},{4,5},{5,6},{6,7},{7,4},{8,9},{9,10},{10,1... | collective-permute-start | bytes 1572872 | tf_op jit(solution)/shard_map/ppermute | solution.py:198
  75.0 20.9 %collective-permute-start.13 = (bf16[64,4096]{1,0:T(8,128)(2,1)S(1)}, bf16[64,4096]{1,0:T(8,128)(2,1)S(1)}, u32[]{:S(2)}, u32[]{:S(2)}) collective-permute-start(bf16[64,4096]{1,0:T(8,128)(2,1)S(1)} %collective-permute-done.12.refs_2_.refs_6_), channel_id=1, source_target_pairs={{0,3},{1,0},{2,1},{3,2},{4,7},{5,4},{6,5},{7,6},{8,11},{9,8},{10,9... | collective-permute-start | bytes 1572872 | tf_op jit(solution)/shard_map/ppermute | solution.py:201
  77.0 12.6 %copy-start = (bf16[4096,1,384]{2,0,1:T(8,128)(2,1)S(1)}, bf16[4096,1,384]{2,0,1:T(8,128)(2,1)}, u32[]{:S(2)}) copy-start(bf16[4096,1,384]{2,0,1:T(8,128)(2,1)} %param.6) | copy-start | bytes 9437188
  89.6 6.3 %copy-start.1 = (bf16[1,128,4096]{2,1,0:T(8,128)(2,1)S(1)}, bf16[1,128,4096]{2,1,0:T(8,128)(2,1)}, u32[]{:S(2)}) copy-start(bf16[1,128,4096]{2,1,0:T(8,128)(2,1)} %param.7) | copy-start | bytes 3145732
  100.3 6.1 %collective-permute-start.14 = (bf16[16,512,128]{2,1,0:T(8,128)(2,1)S(1)}, bf16[16,512,128]{2,1,0:T(8,128)(2,1)S(1)}, u32[]{:S(2)}, u32[]{:S(2)}) collective-permute-start(bf16[16,512,128]{2,1,0:T(8,128)(2,1)S(1)} %shard_map.65), channel_id=1, source_target_pairs={{0,32},{32,0},{1,33},{33,1},{2,34},{34,2},{3,35},{35,3},{4,36},{36... | collective-permute-start | bytes 6291464 | tf_op jit(solution)/shard_map/ppermute | solution.py:252
  106.4 8.4 %collective-permute-start.19 = (bf16[512,128]{1,0:T(8,128)(2,1)S(1)}, bf16[512,128]{1,0:T(8,128)(2,1)S(1)}, u32[]{:S(2)}, u32[]{:S(2)}) collective-permute-start(bf16[512,128]{1,0:T(8,128)(2,1)S(1)} %get-tuple-element.23), channel_id=1, source_target_pairs={{0,448},{64,0},{128,64},{192,128},{256,192},{320,256},{384,320},{4... | collective-permute-start | bytes 393224 | tf_op jit(solution)/shard_map/ppermute | solution.py:268
  111.8 8.7 %collective-permute-start.15 = (bf16[512,128]{1,0:T(8,128)(2,1)S(1)}, bf16[512,128]{1,0:T(8,128)(2,1)S(1)}, u32[]{:S(2)}, u32[]{:S(2)}) collective-permute-start(bf16[512,128]{1,0:T(8,128)(2,1)S(1)} %get-tuple-element.22), channel_id=1, source_target_pairs={{0,64},{64,128},{128,192},{192,256},{256,320},{320,384},{384,448},... | collective-permute-start | bytes 393224 | tf_op jit(solution)/shard_map/ppermute | solution.py:268
  114.9 10.6 %collective-permute-start.20 = (bf16[2,512,128]{2,1,0:T(8,128)(2,1)S(1)}, bf16[2,512,128]{2,1,0:T(8,128)(2,1)S(1)}, u32[]{:S(2)}, u32[]{:S(2)}) collective-permute-start(bf16[2,512,128]{2,1,0:T(8,128)(2,1)S(1)} %shard_map.70), channel_id=1, source_target_pairs={{0,448},{64,0},{128,64},{192,128},{256,192},{320,256},{384,320},{4... | collective-permute-start | bytes 786440 | tf_op jit(solution)/shard_map/ppermute | solution.py:268
  120.6 10.6 %collective-permute-start.16 = (bf16[2,512,128]{2,1,0:T(8,128)(2,1)S(1)}, bf16[2,512,128]{2,1,0:T(8,128)(2,1)S(1)}, u32[]{:S(2)}, u32[]{:S(2)}) collective-permute-start(bf16[2,512,128]{2,1,0:T(8,128)(2,1)S(1)} %shard_map.67), channel_id=1, source_target_pairs={{0,64},{64,128},{128,192},{192,256},{256,320},{320,384},{384,448},... | collective-permute-start | bytes 786440 | tf_op jit(solution)/shard_map/ppermute | solution.py:268
  125.6 9.7 %collective-permute-start.21 = (bf16[2,512,128]{2,1,0:T(8,128)(2,1)S(1)}, bf16[2,512,128]{2,1,0:T(8,128)(2,1)S(1)}, u32[]{:S(2)}, u32[]{:S(2)}) collective-permute-start(bf16[2,512,128]{2,1,0:T(8,128)(2,1)S(1)} %shard_map.71), channel_id=1, source_target_pairs={{0,448},{64,0},{128,64},{192,128},{256,192},{320,256},{384,320},{4... | collective-permute-start | bytes 786440 | tf_op jit(solution)/shard_map/ppermute | solution.py:268
  131.3 9.7 %collective-permute-start.17 = (bf16[2,512,128]{2,1,0:T(8,128)(2,1)S(1)}, bf16[2,512,128]{2,1,0:T(8,128)(2,1)S(1)}, u32[]{:S(2)}, u32[]{:S(2)}) collective-permute-start(bf16[2,512,128]{2,1,0:T(8,128)(2,1)S(1)} %shard_map.68), channel_id=1, source_target_pairs={{0,64},{64,128},{128,192},{192,256},{256,320},{320,384},{384,448},... | collective-permute-start | bytes 786440 | tf_op jit(solution)/shard_map/ppermute | solution.py:268
  135.4 9.5 %collective-permute-start.22 = (bf16[2,512,128]{2,1,0:T(8,128)(2,1)S(1)}, bf16[2,512,128]{2,1,0:T(8,128)(2,1)S(1)}, u32[]{:S(2)}, u32[]{:S(2)}) collective-permute-start(bf16[2,512,128]{2,1,0:T(8,128)(2,1)S(1)} %shard_map.72), channel_id=1, source_target_pairs={{0,448},{64,0},{128,64},{192,128},{256,192},{320,256},{384,320},{4... | collective-permute-start | bytes 786440 | tf_op jit(solution)/shard_map/ppermute | solution.py:268
  141.1 9.5 %collective-permute-start.18 = (bf16[2,512,128]{2,1,0:T(8,128)(2,1)S(1)}, bf16[2,512,128]{2,1,0:T(8,128)(2,1)S(1)}, u32[]{:S(2)}, u32[]{:S(2)}) collective-permute-start(bf16[2,512,128]{2,1,0:T(8,128)(2,1)S(1)} %shard_map.69), channel_id=1, source_target_pairs={{0,64},{64,128},{128,192},{192,256},{256,320},{320,384},{384,448},... | collective-permute-start | bytes 786440 | tf_op jit(solution)/shard_map/ppermute | solution.py:268
  150.7 21.5 %collective-permute-start.23 = (bf16[512,128]{1,0:T(8,128)(2,1)S(1)}, bf16[512,128]{1,0:T(8,128)(2,1)S(1)}, u32[]{:S(2)}, u32[]{:S(2)}) collective-permute-start(bf16[512,128]{1,0:T(8,128)(2,1)S(1)} %shard_map.73), channel_id=1, source_target_pairs={{0,512},{512,0},{1,513},{513,1},{2,514},{514,2},{3,515},{515,3},{4... | collective-permute-start | bytes 393224 | tf_op jit(solution)/shard_map/ppermute | solution.py:277

commit v10 on v8

--- a/solution.py
+++ b/solution.py
@@ -119,18 +119,24 @@
             out_ref[slot * far + i, split:, :] = low[:, i * width : (i + 1) * width].astype(BF16)
 
 
-def first_kernel(own_ref, theirs_ref, up_ref, down_ref):
-    for at, out_ref in enumerate((up_ref, down_ref)):
-        out_ref[...] = (own_ref[at, :, :].astype(F32) + theirs_ref[at, :, :].astype(F32)).astype(BF16)
-
-
-def sum_kernel(own_ref, theirs_ref, came_ref, out_ref, *, at, half):
+def first_kernel(own_ref, theirs_ref, up_ref, down_ref, far_up_ref, far_down_ref):
+    def term(at):
+        return (own_ref[at, :, :].astype(F32) + theirs_ref[at, :, :].astype(F32)).astype(BF16)
+
+    far_up_ref[...] = term(0)
+    far_down_ref[...] = term(1)
+    for out_ref, distance in ((up_ref, 3), (down_ref, -3)):
+        for i in range(2):
+            out_ref[i, :, :] = term(ORDER.index(distance) * 2 + i)
+
+
+def sum_kernel(own_ref, theirs_ref, came_ref, *rest, at, half):
+    *far_ref, out_ref = rest
     for i in range(2):
         total = own_ref[at + i, :, :].astype(F32) + theirs_ref[at + i, :, :].astype(F32)
-        if half is None:
-            total = total + came_ref[i, :, :].astype(F32)
-        elif half == i:
-            total = total + came_ref[...].astype(F32)
+        total = total + came_ref[i, :, :].astype(F32)
+        if far_ref and half == i:
+            total = total + far_ref[0][...].astype(F32)
         out_ref[i, :, :] = total.astype(BF16)
 
 
@@ -262,15 +268,20 @@
             compiler_params=PARAMS,
         )(mine, theirs, *came)
 
-    goes = list(call(first_kernel, [one, one]))
-    for distance in (3, 2, 1, 0):
+    *goes, far_up, far_down = call(first_kernel, [two, two, one, one])
+    jumps = [[], []]
+    for distance in (2, 1, 0):
         goes = [lax.ppermute(m, "y", turn(near, way)) for m, way in zip(goes, (1, -1))]
+        if distance == 2:
+            jumps = [
+                [lax.ppermute(m, "y", turn(near, way))] for m, way in ((far_up, 2), (far_down, -2))
+            ]
         if distance == 0:
             break
         for i, way in enumerate((1, -1)):
             at = ORDER.index(distance * way) * far
-            half = i if distance == 3 else None
-            (goes[i],) = call(functools.partial(sum_kernel, at=at, half=half), [two], goes[i])
+            came = [goes[i]] + (jumps[i] if distance == 2 else [])
+            (goes[i],) = call(functools.partial(sum_kernel, at=at, half=i), [two], *came)
     at = ORDER.index(0) * far
     (away,) = call(functools.partial(away_kernel, at=at), [one], *goes)
     other = lax.ppermute(away, "zh", swap(far, 1))

time: 168 us -> 169 us (level)
  waiting for transfers between devices: 44.9 us -> 47.3 us
  starting transfers between devices: 104 us -> 102 us
    ppermute x8, starting transfers between devices: 29.9 us -> 27.8 us  [local(): lax.ppermute(m, 'y', turn(near, way))]
    ppermute x1, waiting for transfers between devices: 4.86 us -> 6.88 us  [local(): other = lax.ppermute(away, 'zh', swap(far, 1))]
  transfers between devices with their start and end apart: 24 -> 24, of which waited for: 13 -> 14; matrix products, arithmetic and copies ran while one was open for 1% -> 1% of each run, Pallas kernels for 6% -> 6%
where the time goes in v10:
time: 169 us; the launch traced here: 167 us
  starting transfers between devices  102 us (60%)
  waiting for transfers between devices  47.3 us (28%)
  Pallas kernels  15.2 us (9%)
  other arithmetic  1.93 us (1%)
    ppermute x8, starting transfers between devices, local(): lax.ppermute(m, 'y', turn(near, way))  27.8 us
    ppermute x6, starting transfers between devices, within(): return [lax.ppermute(rows, 'zl', swap(n_z, s)) for s in (2, 3, 1)]  27.1 us
    ppermute x1, starting transfers between devices, local(): other = lax.ppermute(away, 'zh', swap(far, 1))  14.3 us
    ppermute x8, waiting for transfers between devices, local(): lax.ppermute(m, 'y', turn(near, way))  14.1 us
    ppermute x1, starting transfers between devices, gather(): t_other = lax.ppermute(tokens, 'zl', swap(n_z, 4))  10.9 us
    ppermute x1, waiting for transfers between devices, gather(): t_right = lax.ppermute(t, 'x', down)  8.33 us
    ppermute x6, waiting for transfers between devices, within(): return [lax.ppermute(rows, 'zl', swap(n_z, s)) for s in (2, 3, 1)]  7.26 us
    ppermute x1, waiting for transfers between devices, local(): other = lax.ppermute(away, 'zh', swap(far, 1))  6.88 us
  transfers between devices with their start and end apart: 24, of which 14 were waited for; matrix products, arithmetic and copies ran while one was open for 1% of the time, Pallas kernels for 6%

profile of v10, /device:TPU:6, one launch (start us, length us, event | category | flops | bytes accessed | tf_op | source)
XLA Modules:
  0.0 167.2 jit_solution(12381627211943651483)
XLA Ops:
  0.6 10.9 %collective-permute-start = (bf16[8,4096]{1,0:T(8,128)(2,1)}, bf16[8,4096]{1,0:T(8,128)(2,1)S(1)}, u32[]{:S(2)}, u32[]{:S(2)}) collective-permute-start(bf16[8,4096]{1,0:T(8,128)(2,1)} %param.4), channel_id=1, source_target_pairs={{0,16},{4,20},{8,24},{12,28},{16,0},{20,4},{24,8},{28,12},{1,17},{... | collective-permute-start | bytes 196616 | tf_op jit(solution)/shard_map/ppermute | solution.py:192
  11.6 1.9 %collective-permute-start.7 = (bf16[8,4096]{1,0:T(8,128)(2,1)}, bf16[8,4096]{1,0:T(8,128)(2,1)S(1)}, u32[]{:S(2)}, u32[]{:S(2)}) collective-permute-start(bf16[8,4096]{1,0:T(8,128)(2,1)} %param.5), channel_id=1, source_target_pairs={{0,16},{4,20},{8,24},{12,28},{16,0},{20,4},{24,8},{28,12},{1,17},{... | collective-permute-start | bytes 196616 | tf_op jit(solution)/shard_map/ppermute | solution.py:195
  14.8 6.0 %collective-permute-start.3 = (bf16[16,4096]{1,0:T(8,128)(2,1)S(1)}, bf16[16,4096]{1,0:T(8,128)(2,1)S(1)}, u32[]{:S(2)}, u32[]{:S(2)}) collective-permute-start(bf16[16,4096]{1,0:T(8,128)(2,1)S(1)} %pad_maximum_fusion.2), channel_id=1, source_target_pairs={{0,4},{4,0},{8,12},{12,8},{16,20},{20,16},{24,28},{28,24},{1,5},{5... | collective-permute-start | bytes 393224 | tf_op jit(solution)/shard_map/ppermute | solution.py:190
  20.8 9.1 %collective-permute-start.2 = (bf16[16,4096]{1,0:T(8,128)(2,1)S(1)}, bf16[16,4096]{1,0:T(8,128)(2,1)S(1)}, u32[]{:S(2)}, u32[]{:S(2)}) collective-permute-start(bf16[16,4096]{1,0:T(8,128)(2,1)S(1)} %pad_maximum_fusion.2), channel_id=1, source_target_pairs={{0,12},{4,8},{8,4},{12,0},{16,28},{20,24},{24,20},{28,16},{1,13},{... | collective-permute-start | bytes 393224 | tf_op jit(solution)/shard_map/ppermute | solution.py:190
  29.9 2.5 %collective-permute-start.1 = (bf16[16,4096]{1,0:T(8,128)(2,1)S(1)}, bf16[16,4096]{1,0:T(8,128)(2,1)S(1)}, u32[]{:S(2)}, u32[]{:S(2)}) collective-permute-start(bf16[16,4096]{1,0:T(8,128)(2,1)S(1)} %pad_maximum_fusion.2), channel_id=1, source_target_pairs={{0,8},{4,12},{8,0},{12,4},{16,24},{20,28},{24,16},{28,20},{1,9},{5... | collective-permute-start | bytes 393224 | tf_op jit(solution)/shard_map/ppermute | solution.py:190
  33.2 2.5 %collective-permute-start.10 = (bf16[16,4096]{1,0:T(8,128)(2,1)S(1)}, bf16[16,4096]{1,0:T(8,128)(2,1)S(1)}, u32[]{:S(2)}, u32[]{:S(2)}) collective-permute-start(bf16[16,4096]{1,0:T(8,128)(2,1)S(1)} %pad_maximum_fusion.3), channel_id=1, source_target_pairs={{0,4},{4,0},{8,12},{12,8},{16,20},{20,16},{24,28},{28,24},{1,5},{5... | collective-permute-start | bytes 393224 | tf_op jit(solution)/shard_map/ppermute | solution.py:190
  35.7 5.2 %collective-permute-start.9 = (bf16[16,4096]{1,0:T(8,128)(2,1)S(1)}, bf16[16,4096]{1,0:T(8,128)(2,1)S(1)}, u32[]{:S(2)}, u32[]{:S(2)}) collective-permute-start(bf16[16,4096]{1,0:T(8,128)(2,1)S(1)} %pad_maximum_fusion.3), channel_id=1, source_target_pairs={{0,12},{4,8},{8,4},{12,0},{16,28},{20,24},{24,20},{28,16},{1,13},{... | collective-permute-start | bytes 393224 | tf_op jit(solution)/shard_map/ppermute | solution.py:190
  42.8 3.9 %collective-permute-done.1 = bf16[16,4096]{1,0:T(8,128)(2,1)S(1)} collective-permute-done((bf16[16,4096]{1,0:T(8,128)(2,1)S(1)}, bf16[16,4096]{1,0:T(8,128)(2,1)S(1)}, u32[]{:S(2)}, u32[]{:S(2)}) %collective-permute-start.1) | collective-permute-done | bytes 131104 | tf_op jit(solution)/shard_map/ppermute | solution.py:190
  46.8 3.0 %collective-permute-start.4 = (bf16[64,4096]{1,0:T(8,128)(2,1)S(1)}, bf16[64,4096]{1,0:T(8,128)(2,1)S(1)}, u32[]{:S(2)}, u32[]{:S(2)}) collective-permute-start(bf16[64,4096]{1,0:T(8,128)(2,1)S(1)} %pad_maximum_fusion.refs_0_), channel_id=1, source_target_pairs={{0,1},{1,2},{2,3},{3,0},{4,5},{5,6},{6,7},{7,4},{8,9},{9,10},{10,1... | collective-permute-start | bytes 1572872 | tf_op jit(solution)/shard_map/ppermute | solution.py:197
  49.8 3.3 %collective-permute-done.8 = bf16[16,4096]{1,0:T(8,128)(2,1)S(1)} collective-permute-done((bf16[16,4096]{1,0:T(8,128)(2,1)S(1)}, bf16[16,4096]{1,0:T(8,128)(2,1)S(1)}, u32[]{:S(2)}, u32[]{:S(2)}) %collective-permute-start.8) | collective-permute-done | bytes 131104 | tf_op jit(solution)/shard_map/ppermute | solution.py:190
  53.2 2.7 %collective-permute-start.12 = (bf16[64,4096]{1,0:T(8,128)(2,1)S(1)}, bf16[64,4096]{1,0:T(8,128)(2,1)S(1)}, u32[]{:S(2)}, u32[]{:S(2)}) collective-permute-start(bf16[64,4096]{1,0:T(8,128)(2,1)S(1)} %pad_maximum_fusion.1.refs_0_.refs_3_), channel_id=1, source_target_pairs={{0,3},{1,0},{2,1},{3,2},{4,7},{5,4},{6,5},{7,6},{8,11},{9,8},{10,9... | collective-permute-start | bytes 1572872 | tf_op jit(solution)/shard_map/ppermute | solution.py:203
  55.9 2.4 %collective-permute-start.5 = (bf16[64,4096]{1,0:T(8,128)(2,1)S(1)}, bf16[64,4096]{1,0:T(8,128)(2,1)}, u32[]{:S(2)}, u32[]{:S(2)}) collective-permute-start(bf16[64,4096]{1,0:T(8,128)(2,1)S(1)} %pad_maximum_fusion.refs_0_), channel_id=1, source_target_pairs={{0,3},{1,0},{2,1},{3,2},{4,7},{5,4},{6,5},{7,6},{8,11},{9,8},{10,9... | collective-permute-start | bytes 1572872 | tf_op jit(solution)/shard_map/ppermute | solution.py:198
  58.4 4.6 %collective-permute-start.6 = (bf16[64,4096]{1,0:T(8,128)(2,1)S(1)}, bf16[64,4096]{1,0:T(8,128)(2,1)}, u32[]{:S(2)}, u32[]{:S(2)}) collective-permute-start(bf16[64,4096]{1,0:T(8,128)(2,1)S(1)} %collective-permute-done.4.refs_0_), channel_id=1, source_target_pairs={{0,1},{1,2},{2,3},{3,0},{4,5},{5,6},{6,7},{7,4},{8,9},{9,10},{10,1... | collective-permute-start | bytes 1572872 | tf_op jit(solution)/shard_map/ppermute | solution.py:202
  63.0 3.1 %collective-permute-start.11 = (bf16[64,4096]{1,0:T(8,128)(2,1)S(1)}, bf16[64,4096]{1,0:T(8,128)(2,1)S(1)}, u32[]{:S(2)}, u32[]{:S(2)}) collective-permute-start(bf16[64,4096]{1,0:T(8,128)(2,1)S(1)} %pad_maximum_fusion.1.refs_0_.refs_3_), channel_id=1, source_target_pairs={{0,1},{1,2},{2,3},{3,0},{4,5},{5,6},{6,7},{7,4},{8,9},{9,10},{10,1... | collective-permute-start | bytes 1572872 | tf_op jit(solution)/shard_map/ppermute | solution.py:204
  66.1 5.0 %collective-permute-done.12.refs_2_.refs_5_ = bf16[64,4096]{1,0:T(8,128)(2,1)S(1)} collective-permute-done((bf16[64,4096]{1,0:T(8,128)(2,1)S(1)}, bf16[64,4096]{1,0:T(8,128)(2,1)S(1)}, u32[]{:S(2)}, u32[]{:S(2)}) %collective-permute-start.12) | collective-permute-done | bytes 524320 | tf_op jit(solution)/shard_map/ppermute | solution.py:203
  74.2 8.3 %collective-permute-done.5.refs_1_ = bf16[64,4096]{1,0:T(8,128)(2,1)} collective-permute-done((bf16[64,4096]{1,0:T(8,128)(2,1)S(1)}, bf16[64,4096]{1,0:T(8,128)(2,1)}, u32[]{:S(2)}, u32[]{:S(2)}) %collective-permute-start.5) | collective-permute-done | bytes 524320 | tf_op jit(solution)/shard_map/ppermute | solution.py:198
  82.5 4.2 %shard_map.60.refs_1_.refs_2_ = bf16[192,4096]{1,0:T(8,128)(2,1)S(1)} custom-call(bf16[64,4096]{1,0:T(8,128)(2,1)S(1)} %collective-permute-done.4.refs_0_, bf16[64,4096]{1,0:T(8,128)(2,1)} %collective-permute-done.5.refs_1_, bf16[64,4096]{1,0:T(8,128)(2,1)} %collective-permute-done.6.refs_2_), custom_call_target="tpu_custom_call" | custom-call | tf_op jit(solution)/shard_map/pallas_call | solution.py:174
  86.7 2.7 %shard_map.61 = (bf16[128,256]{1,0:T(8,128)(2,1)S(1)}, f32[256,128]{1,0:T(8,128)S(1)}, f32[256,128]{1,0:T(8,128)S(1)}, f32[256,128]{1,0:T(8,128)S(1)}, f32[256,2...) custom-call(bf16[64,4096]{1,0:T(8,128)(2,1)S(1)} %shard_map.59.refs_0_.refs_1_, ...), custom_call_target="tpu_custom_call" | custom-call | tf_op jit(solution)/shard_map/pallas_call | solution.py:218
  89.4 2.6 %collective-permute-done.13.refs_3_.refs_6_ = bf16[64,4096]{1,0:T(8,128)(2,1)S(1)} collective-permute-done((bf16[64,4096]{1,0:T(8,128)(2,1)S(1)}, bf16[64,4096]{1,0:T(8,128)(2,1)S(1)}, u32[]{:S(2)}, u32[]{:S(2)}) %collective-permute-start.13) | collective-permute-done | bytes 524320 | tf_op jit(solution)/shard_map/ppermute | solution.py:206
  92.1 2.9 %shard_map.62.refs_7_ = bf16[384,256]{1,0:T(8,128)(2,1)S(1)} custom-call(bf16[64,4096]{1,0:T(8,128)(2,1)S(1)} %pad_maximum_fusion.1.refs_0_.refs_3_, bf16[64,4096]{1,0:T(8,128)(2,1)S(1)} %collective-permute-done.11.refs_1_.refs_4_, bf16[64,4096]{1,0:T(8,128)(2,1)S(1)} %collective-permute-done.12.refs_2_.refs_5_, ...), custom_call_target="tpu_custom_call" | custom-call | tf_op jit(solution)/shard_map/pallas_call | solution.py:233
  99.9 2.6 %collective-permute-done.14.theirs_ref = bf16[16,512,128]{2,1,0:T(8,128)(2,1)S(1)} collective-permute-done((bf16[16,512,128]{2,1,0:T(8,128)(2,1)S(1)}, bf16[16,512,128]{2,1,0:T(8,128)(2,1)S(1)}, u32[]{:S(2)}, u32[]{:S(2)}) %collective-permute-start.14) | collective-permute-done | bytes 2097184 | tf_op jit(solution)/shard_map/ppermute | solution.py:257
  102.7 3.5 %collective-permute-start.15 = (bf16[2,512,128]{2,1,0:T(8,128)(2,1)S(1)}, bf16[2,512,128]{2,1,0:T(8,128)(2,1)S(1)}, u32[]{:S(2)}, u32[]{:S(2)}) collective-permute-start(bf16[2,512,128]{2,1,0:T(8,128)(2,1)S(1)} %get-tuple-element.22), channel_id=1, source_target_pairs={{0,64},{64,128},{128,192},{192,256},{256,320},{320,384},{384,448},... | collective-permute-start | bytes 786440 | tf_op jit(solution)/shard_map/ppermute | solution.py:274
  106.2 3.8 %collective-permute-start.19 = (bf16[2,512,128]{2,1,0:T(8,128)(2,1)S(1)}, bf16[2,512,128]{2,1,0:T(8,128)(2,1)S(1)}, u32[]{:S(2)}, u32[]{:S(2)}) collective-permute-start(bf16[2,512,128]{2,1,0:T(8,128)(2,1)S(1)} %get-tuple-element.24), channel_id=1, source_target_pairs={{0,448},{64,0},{128,64},{192,128},{256,192},{320,256},{384,320},{4... | collective-permute-start | bytes 786440 | tf_op jit(solution)/shard_map/ppermute | solution.py:274
  110.0 3.0 %collective-permute-start.16 = (bf16[512,128]{1,0:T(8,128)(2,1)S(1)}, bf16[512,128]{1,0:T(8,128)(2,1)S(1)}, u32[]{:S(2)}, u32[]{:S(2)}) collective-permute-start(bf16[512,128]{1,0:T(8,128)(2,1)S(1)} %get-tuple-element.23), channel_id=1, source_target_pairs={{0,128},{64,192},{128,256},{192,320},{256,384},{320,448},{384,0},{... | collective-permute-start | bytes 393224 | tf_op jit(solution)/shard_map/ppermute | solution.py:277
  113.0 4.9 %collective-permute-start.20 = (bf16[512,128]{1,0:T(8,128)(2,1)S(1)}, bf16[512,128]{1,0:T(8,128)(2,1)S(1)}, u32[]{:S(2)}, u32[]{:S(2)}) collective-permute-start(bf16[512,128]{1,0:T(8,128)(2,1)S(1)} %get-tuple-element.25), channel_id=1, source_target_pairs={{0,384},{64,448},{128,0},{192,64},{256,128},{320,192},{384,256},{4... | collective-permute-start | bytes 393224 | tf_op jit(solution)/shard_map/ppermute | solution.py:277
  118.0 4.1 %collective-permute-done.16.rest_0_ = bf16[512,128]{1,0:T(8,128)(2,1)S(1)} collective-permute-done((bf16[512,128]{1,0:T(8,128)(2,1)S(1)}, bf16[512,128]{1,0:T(8,128)(2,1)S(1)}, u32[]{:S(2)}, u32[]{:S(2)}) %collective-permute-start.16) | collective-permute-done | bytes 131104 | tf_op jit(solution)/shard_map/ppermute | solution.py:277
  125.5 3.9 %collective-permute-start.21 = (bf16[2,512,128]{2,1,0:T(8,128)(2,1)S(1)}, bf16[2,512,128]{2,1,0:T(8,128)(2,1)S(1)}, u32[]{:S(2)}, u32[]{:S(2)}) collective-permute-start(bf16[2,512,128]{2,1,0:T(8,128)(2,1)S(1)} %shard_map.68), channel_id=1, source_target_pairs={{0,448},{64,0},{128,64},{192,128},{256,192},{320,256},{384,320},{4... | collective-permute-start | bytes 786440 | tf_op jit(solution)/shard_map/ppermute | solution.py:274
  129.4 3.9 %collective-permute-done.17.came_ref = bf16[2,512,128]{2,1,0:T(8,128)(2,1)S(1)} collective-permute-done((bf16[2,512,128]{2,1,0:T(8,128)(2,1)S(1)}, bf16[2,512,128]{2,1,0:T(8,128)(2,1)S(1)}, u32[]{:S(2)}, u32[]{:S(2)}) %collective-permute-start.17) | collective-permute-done | bytes 262176 | tf_op jit(solution)/shard_map/ppermute | solution.py:274
  135.8 4.9 %collective-permute-start.22 = (bf16[2,512,128]{2,1,0:T(8,128)(2,1)S(1)}, bf16[2,512,128]{2,1,0:T(8,128)(2,1)S(1)}, u32[]{:S(2)}, u32[]{:S(2)}) collective-permute-start(bf16[2,512,128]{2,1,0:T(8,128)(2,1)S(1)} %shard_map.69), channel_id=1, source_target_pairs={{0,448},{64,0},{128,64},{192,128},{256,192},{320,256},{384,320},{4... | collective-permute-start | bytes 786440 | tf_op jit(solution)/shard_map/ppermute | solution.py:274
  140.6 3.1 %collective-permute-done.18.up_ref = bf16[2,512,128]{2,1,0:T(8,128)(2,1)S(1)} collective-permute-done((bf16[2,512,128]{2,1,0:T(8,128)(2,1)S(1)}, bf16[2,512,128]{2,1,0:T(8,128)(2,1)S(1)}, u32[]{:S(2)}, u32[]{:S(2)}) %collective-permute-start.18) | collective-permute-done | bytes 262176 | tf_op jit(solution)/shard_map/ppermute | solution.py:274
  145.1 14.3 %collective-permute-start.23 = (bf16[512,128]{1,0:T(8,128)(2,1)S(1)}, bf16[512,128]{1,0:T(8,128)(2,1)S(1)}, u32[]{:S(2)}, u32[]{:S(2)}) collective-permute-start(bf16[512,128]{1,0:T(8,128)(2,1)S(1)} %shard_map.70), channel_id=1, source_target_pairs={{0,512},{512,0},{1,513},{513,1},{2,514},{514,2},{3,515},{515,3},{4... | collective-permute-start | bytes 393224 | tf_op jit(solution)/shard_map/ppermute | solution.py:287
  159.5 6.9 %collective-permute-done.23.other_ref = bf16[512,128]{1,0:T(8,128)(2,1)S(1)} collective-permute-done((bf16[512,128]{1,0:T(8,128)(2,1)S(1)}, bf16[512,128]{1,0:T(8,128)(2,1)S(1)}, u32[]{:S(2)}, u32[]{:S(2)}) %collective-permute-start.23) | collective-permute-done | bytes 131104 | tf_op jit(solution)/shard_map/ppermute | solution.py:287
  (39 shorter events, 20.4 us)
Async XLA Ops:
  0.6 13.4 %collective-permute-start = (bf16[8,4096]{1,0:T(8,128)(2,1)}, bf16[8,4096]{1,0:T(8,128)(2,1)S(1)}, u32[]{:S(2)}, u32[]{:S(2)}) collective-permute-start(bf16[8,4096]{1,0:T(8,128)(2,1)} %param.4), channel_id=1, source_target_pairs={{0,16},{4,20},{8,24},{12,28},{16,0},{20,4},{24,8},{28,12},{1,17},{... | collective-permute-start | bytes 196616 | tf_op jit(solution)/shard_map/ppermute | solution.py:192
  11.6 20.8 %collective-permute-start.7 = (bf16[8,4096]{1,0:T(8,128)(2,1)}, bf16[8,4096]{1,0:T(8,128)(2,1)S(1)}, u32[]{:S(2)}, u32[]{:S(2)}) collective-permute-start(bf16[8,4096]{1,0:T(8,128)(2,1)} %param.5), channel_id=1, source_target_pairs={{0,16},{4,20},{8,24},{12,28},{16,0},{20,4},{24,8},{28,12},{1,17},{... | collective-permute-start | bytes 196616 | tf_op jit(solution)/shard_map/ppermute | solution.py:195
  14.8 26.0 %collective-permute-start.3 = (bf16[16,4096]{1,0:T(8,128)(2,1)S(1)}, bf16[16,4096]{1,0:T(8,128)(2,1)S(1)}, u32[]{:S(2)}, u32[]{:S(2)}) collective-permute-start(bf16[16,4096]{1,0:T(8,128)(2,1)S(1)} %pad_maximum_fusion.2), channel_id=1, source_target_pairs={{0,4},{4,0},{8,12},{12,8},{16,20},{20,16},{24,28},{28,24},{1,5},{5... | collective-permute-start | bytes 393224 | tf_op jit(solution)/shard_map/ppermute | solution.py:190
  20.8 22.0 %collective-permute-start.2 = (bf16[16,4096]{1,0:T(8,128)(2,1)S(1)}, bf16[16,4096]{1,0:T(8,128)(2,1)S(1)}, u32[]{:S(2)}, u32[]{:S(2)}) collective-permute-start(bf16[16,4096]{1,0:T(8,128)(2,1)S(1)} %pad_maximum_fusion.2), channel_id=1, source_target_pairs={{0,12},{4,8},{8,4},{12,0},{16,28},{20,24},{24,20},{28,16},{1,13},{... | collective-permute-start | bytes 393224 | tf_op jit(solution)/shard_map/ppermute | solution.py:190
  29.9 16.9 %collective-permute-start.1 = (bf16[16,4096]{1,0:T(8,128)(2,1)S(1)}, bf16[16,4096]{1,0:T(8,128)(2,1)S(1)}, u32[]{:S(2)}, u32[]{:S(2)}) collective-permute-start(bf16[16,4096]{1,0:T(8,128)(2,1)S(1)} %pad_maximum_fusion.2), channel_id=1, source_target_pairs={{0,8},{4,12},{8,0},{12,4},{16,24},{20,28},{24,16},{28,20},{1,9},{5... | collective-permute-start | bytes 393224 | tf_op jit(solution)/shard_map/ppermute | solution.py:190
  33.2 16.6 %collective-permute-start.10 = (bf16[16,4096]{1,0:T(8,128)(2,1)S(1)}, bf16[16,4096]{1,0:T(8,128)(2,1)S(1)}, u32[]{:S(2)}, u32[]{:S(2)}) collective-permute-start(bf16[16,4096]{1,0:T(8,128)(2,1)S(1)} %pad_maximum_fusion.3), channel_id=1, source_target_pairs={{0,4},{4,0},{8,12},{12,8},{16,20},{20,16},{24,28},{28,24},{1,5},{5... | collective-permute-start | bytes 393224 | tf_op jit(solution)/shard_map/ppermute | solution.py:190
  35.7 14.1 %collective-permute-start.9 = (bf16[16,4096]{1,0:T(8,128)(2,1)S(1)}, bf16[16,4096]{1,0:T(8,128)(2,1)S(1)}, u32[]{:S(2)}, u32[]{:S(2)}) collective-permute-start(bf16[16,4096]{1,0:T(8,128)(2,1)S(1)} %pad_maximum_fusion.3), channel_id=1, source_target_pairs={{0,12},{4,8},{8,4},{12,0},{16,28},{20,24},{24,20},{28,16},{1,13},{... | collective-permute-start | bytes 393224 | tf_op jit(solution)/shard_map/ppermute | solution.py:190
  40.9 12.3 %collective-permute-start.8 = (bf16[16,4096]{1,0:T(8,128)(2,1)S(1)}, bf16[16,4096]{1,0:T(8,128)(2,1)S(1)}, u32[]{:S(2)}, u32[]{:S(2)}) collective-permute-start(bf16[16,4096]{1,0:T(8,128)(2,1)S(1)} %pad_maximum_fusion.3), channel_id=1, source_target_pairs={{0,8},{4,12},{8,0},{12,4},{16,24},{20,28},{24,16},{28,20},{1,9},{5... | collective-permute-start | bytes 393224 | tf_op jit(solution)/shard_map/ppermute | solution.py:190
  46.8 11.6 %collective-permute-start.4 = (bf16[64,4096]{1,0:T(8,128)(2,1)S(1)}, bf16[64,4096]{1,0:T(8,128)(2,1)S(1)}, u32[]{:S(2)}, u32[]{:S(2)}) collective-permute-start(bf16[64,4096]{1,0:T(8,128)(2,1)S(1)} %pad_maximum_fusion.refs_0_), channel_id=1, source_target_pairs={{0,1},{1,2},{2,3},{3,0},{4,5},{5,6},{6,7},{7,4},{8,9},{9,10},{10,1... | collective-permute-start | bytes 1572872 | tf_op jit(solution)/shard_map/ppermute | solution.py:197
  53.2 18.0 %collective-permute-start.12 = (bf16[64,4096]{1,0:T(8,128)(2,1)S(1)}, bf16[64,4096]{1,0:T(8,128)(2,1)S(1)}, u32[]{:S(2)}, u32[]{:S(2)}) collective-permute-start(bf16[64,4096]{1,0:T(8,128)(2,1)S(1)} %pad_maximum_fusion.1.refs_0_.refs_3_), channel_id=1, source_target_pairs={{0,3},{1,0},{2,1},{3,2},{4,7},{5,4},{6,5},{7,6},{8,11},{9,8},{10,9... | collective-permute-start | bytes 1572872 | tf_op jit(solution)/shard_map/ppermute | solution.py:203
  55.9 26.6 %collective-permute-start.5 = (bf16[64,4096]{1,0:T(8,128)(2,1)S(1)}, bf16[64,4096]{1,0:T(8,128)(2,1)}, u32[]{:S(2)}, u32[]{:S(2)}) collective-permute-start(bf16[64,4096]{1,0:T(8,128)(2,1)S(1)} %pad_maximum_fusion.refs_0_), channel_id=1, source_target_pairs={{0,3},{1,0},{2,1},{3,2},{4,7},{5,4},{6,5},{7,6},{8,11},{9,8},{10,9... | collective-permute-start | bytes 1572872 | tf_op jit(solution)/shard_map/ppermute | solution.py:198
  58.4 24.1 %collective-permute-start.6 = (bf16[64,4096]{1,0:T(8,128)(2,1)S(1)}, bf16[64,4096]{1,0:T(8,128)(2,1)}, u32[]{:S(2)}, u32[]{:S(2)}) collective-permute-start(bf16[64,4096]{1,0:T(8,128)(2,1)S(1)} %collective-permute-done.4.refs_0_), channel_id=1, source_target_pairs={{0,1},{1,2},{2,3},{3,0},{4,5},{5,6},{6,7},{7,4},{8,9},{9,10},{10,1... | collective-permute-start | bytes 1572872 | tf_op jit(solution)/shard_map/ppermute | solution.py:202
  63.0 26.4 %collective-permute-start.11 = (bf16[64,4096]{1,0:T(8,128)(2,1)S(1)}, bf16[64,4096]{1,0:T(8,128)(2,1)S(1)}, u32[]{:S(2)}, u32[]{:S(2)}) collective-permute-start(bf16[64,4096]{1,0:T(8,128)(2,1)S(1)} %pad_maximum_fusion.1.refs_0_.refs_3_), channel_id=1, source_target_pairs={{0,1},{1,2},{2,3},{3,0},{4,5},{5,6},{6,7},{7,4},{8,9},{9,10},{10,1... | collective-permute-start | bytes 1572872 | tf_op jit(solution)/shard_map/ppermute | solution.py:204
  71.2 20.9 %collective-permute-start.13 = (bf16[64,4096]{1,0:T(8,128)(2,1)S(1)}, bf16[64,4096]{1,0:T(8,128)(2,1)S(1)}, u32[]{:S(2)}, u32[]{:S(2)}) collective-permute-start(bf16[64,4096]{1,0:T(8,128)(2,1)S(1)} %collective-permute-done.12.refs_2_.refs_5_), channel_id=1, source_target_pairs={{0,3},{1,0},{2,1},{3,2},{4,7},{5,4},{6,5},{7,6},{8,11},{9,8},{10,9... | collective-permute-start | bytes 1572872 | tf_op jit(solution)/shard_map/ppermute | solution.py:206
  73.2 13.6 %copy-start = (bf16[4096,1,384]{2,0,1:T(8,128)(2,1)S(1)}, bf16[4096,1,384]{2,0,1:T(8,128)(2,1)}, u32[]{:S(2)}) copy-start(bf16[4096,1,384]{2,0,1:T(8,128)(2,1)} %param.6) | copy-start | bytes 9437188
  86.7 5.4 %copy-start.1 = (bf16[1,128,4096]{2,1,0:T(8,128)(2,1)S(1)}, bf16[1,128,4096]{2,1,0:T(8,128)(2,1)}, u32[]{:S(2)}) copy-start(bf16[1,128,4096]{2,1,0:T(8,128)(2,1)} %param.7) | copy-start | bytes 3145732
  96.4 6.1 %collective-permute-start.14 = (bf16[16,512,128]{2,1,0:T(8,128)(2,1)S(1)}, bf16[16,512,128]{2,1,0:T(8,128)(2,1)S(1)}, u32[]{:S(2)}, u32[]{:S(2)}) collective-permute-start(bf16[16,512,128]{2,1,0:T(8,128)(2,1)S(1)} %shard_map.64), channel_id=1, source_target_pairs={{0,32},{32,0},{1,33},{33,1},{2,34},{34,2},{3,35},{35,3},{4,36},{36... | collective-permute-start | bytes 6291464 | tf_op jit(solution)/shard_map/ppermute | solution.py:257
  102.7 19.4 %collective-permute-start.15 = (bf16[2,512,128]{2,1,0:T(8,128)(2,1)S(1)}, bf16[2,512,128]{2,1,0:T(8,128)(2,1)S(1)}, u32[]{:S(2)}, u32[]{:S(2)}) collective-permute-start(bf16[2,512,128]{2,1,0:T(8,128)(2,1)S(1)} %get-tuple-element.22), channel_id=1, source_target_pairs={{0,64},{64,128},{128,192},{192,256},{256,320},{320,384},{384,448},... | collective-permute-start | bytes 786440 | tf_op jit(solution)/shard_map/ppermute | solution.py:274
  106.2 19.2 %collective-permute-start.19 = (bf16[2,512,128]{2,1,0:T(8,128)(2,1)S(1)}, bf16[2,512,128]{2,1,0:T(8,128)(2,1)S(1)}, u32[]{:S(2)}, u32[]{:S(2)}) collective-permute-start(bf16[2,512,128]{2,1,0:T(8,128)(2,1)S(1)} %get-tuple-element.24), channel_id=1, source_target_pairs={{0,448},{64,0},{128,64},{192,128},{256,192},{320,256},{384,320},{4... | collective-permute-start | bytes 786440 | tf_op jit(solution)/shard_map/ppermute | solution.py:274
  110.0 12.1 %collective-permute-start.16 = (bf16[512,128]{1,0:T(8,128)(2,1)S(1)}, bf16[512,128]{1,0:T(8,128)(2,1)S(1)}, u32[]{:S(2)}, u32[]{:S(2)}) collective-permute-start(bf16[512,128]{1,0:T(8,128)(2,1)S(1)} %get-tuple-element.23), channel_id=1, source_target_pairs={{0,128},{64,192},{128,256},{192,320},{256,384},{320,448},{384,0},{... | collective-permute-start | bytes 393224 | tf_op jit(solution)/shard_map/ppermute | solution.py:277
  113.0 12.4 %collective-permute-start.20 = (bf16[512,128]{1,0:T(8,128)(2,1)S(1)}, bf16[512,128]{1,0:T(8,128)(2,1)S(1)}, u32[]{:S(2)}, u32[]{:S(2)}) collective-permute-start(bf16[512,128]{1,0:T(8,128)(2,1)S(1)} %get-tuple-element.25), channel_id=1, source_target_pairs={{0,384},{64,448},{128,0},{192,64},{256,128},{320,192},{384,256},{4... | collective-permute-start | bytes 393224 | tf_op jit(solution)/shard_map/ppermute | solution.py:277
  122.2 11.2 %collective-permute-start.17 = (bf16[2,512,128]{2,1,0:T(8,128)(2,1)S(1)}, bf16[2,512,128]{2,1,0:T(8,128)(2,1)S(1)}, u32[]{:S(2)}, u32[]{:S(2)}) collective-permute-start(bf16[2,512,128]{2,1,0:T(8,128)(2,1)S(1)} %shard_map.66), channel_id=1, source_target_pairs={{0,64},{64,128},{128,192},{192,256},{256,320},{320,384},{384,448},... | collective-permute-start | bytes 786440 | tf_op jit(solution)/shard_map/ppermute | solution.py:274
  125.5 10.1 %collective-permute-start.21 = (bf16[2,512,128]{2,1,0:T(8,128)(2,1)S(1)}, bf16[2,512,128]{2,1,0:T(8,128)(2,1)S(1)}, u32[]{:S(2)}, u32[]{:S(2)}) collective-permute-start(bf16[2,512,128]{2,1,0:T(8,128)(2,1)S(1)} %shard_map.68), channel_id=1, source_target_pairs={{0,448},{64,0},{128,64},{192,128},{256,192},{320,256},{384,320},{4... | collective-permute-start | bytes 786440 | tf_op jit(solution)/shard_map/ppermute | solution.py:274
  133.4 10.3 %collective-permute-start.18 = (bf16[2,512,128]{2,1,0:T(8,128)(2,1)S(1)}, bf16[2,512,128]{2,1,0:T(8,128)(2,1)S(1)}, u32[]{:S(2)}, u32[]{:S(2)}) collective-permute-start(bf16[2,512,128]{2,1,0:T(8,128)(2,1)S(1)} %shard_map.67), channel_id=1, source_target_pairs={{0,64},{64,128},{128,192},{192,256},{256,320},{320,384},{384,448},... | collective-permute-start | bytes 786440 | tf_op jit(solution)/shard_map/ppermute | solution.py:274
  135.8 9.3 %collective-permute-start.22 = (bf16[2,512,128]{2,1,0:T(8,128)(2,1)S(1)}, bf16[2,512,128]{2,1,0:T(8,128)(2,1)S(1)}, u32[]{:S(2)}, u32[]{:S(2)}) collective-permute-start(bf16[2,512,128]{2,1,0:T(8,128)(2,1)S(1)} %shard_map.69), channel_id=1, source_target_pairs={{0,448},{64,0},{128,64},{192,128},{256,192},{320,256},{384,320},{4... | collective-permute-start | bytes 786440 | tf_op jit(solution)/shard_map/ppermute | solution.py:274
  145.1 21.2 %collective-permute-start.23 = (bf16[512,128]{1,0:T(8,128)(2,1)S(1)}, bf16[512,128]{1,0:T(8,128)(2,1)S(1)}, u32[]{:S(2)}, u32[]{:S(2)}) collective-permute-start(bf16[512,128]{1,0:T(8,128)(2,1)S(1)} %shard_map.70), channel_id=1, source_target_pairs={{0,512},{512,0},{1,513},{513,1},{2,514},{514,2},{3,515},{515,3},{4... | collective-permute-start | bytes 393224 | tf_op jit(solution)/shard_map/ppermute | solution.py:287

commit v11 on v9

--- a/solution.py
+++ b/solution.py
@@ -186,7 +186,7 @@
     t_other = lax.ppermute(tokens, "zl", swap(n_z, 4))
     t = join(tokens, t_other)
     t_near = within(t)
-    c = join(cotangent, lax.ppermute(after(cotangent, t), "zl", swap(n_z, 4)))
+    c = join(cotangent, lax.ppermute(cotangent, "zl", swap(n_z, 4)))
     t = join(t, *t_near)
     t_left = lax.ppermute(t, "x", up)
     t_right = lax.ppermute(t, "x", down)

time: 174 us -> 168 us (0.966)
  starting transfers between devices: 107 us -> 104 us
  waiting for transfers between devices: 47.5 us -> 44.6 us
    ppermute x1, starting transfers between devices: 7.95 us -> 1.92 us  [gather(): c = join(cotangent, lax.ppermute(cotangent, 'zl', swap(n_z, 4)))]
    ppermute x6, starting transfers between devices: 23 us -> 27.1 us  [within(): return [lax.ppermute(rows, 'zl', swap(n_z, s)) for s in (2, 3, 1)]]
    ppermute x1, waiting for transfers between devices: 7.28 us -> 4.86 us  [local(): other = lax.ppermute(away, 'zh', swap(far, 1))]
    ppermute x1, waiting for transfers between devices: 2.44 us -> 0.51 us  [gather(): t_other = lax.ppermute(tokens, 'zl', swap(n_z, 4))]
where the time goes in v11:
time: 168 us; the launch traced here: 167 us
  starting transfers between devices  104 us (62%)
  waiting for transfers between devices  44.6 us (27%)
  Pallas kernels  15.5 us (9%)
  other arithmetic  1.93 us (1%)
    ppermute x8, starting transfers between devices, local(): lax.ppermute(m, 'y', turn(near, way))  29.9 us
    ppermute x6, starting transfers between devices, within(): return [lax.ppermute(rows, 'zl', swap(n_z, s)) for s in (2, 3, 1)]  27.1 us
    ppermute x1, starting transfers between devices, local(): other = lax.ppermute(away, 'zh', swap(far, 1))  14.3 us
    ppermute x8, waiting for transfers between devices, local(): lax.ppermute(m, 'y', turn(near, way))  13.7 us
    ppermute x1, starting transfers between devices, gather(): t_other = lax.ppermute(tokens, 'zl', swap(n_z, 4))  10.9 us
    ppermute x1, waiting for transfers between devices, gather(): t_right = lax.ppermute(t, 'x', down)  7.31 us
    ppermute x6, waiting for transfers between devices, within(): return [lax.ppermute(rows, 'zl', swap(n_z, s)) for s in (2, 3, 1)]  7.26 us
    pallas_call x3, Pallas kernels, normalized(): pl.pallas_call(normalize_kernel, out_shape=jax.ShapeDtypeStruct((rows, pi...  5.21 us
  transfers between devices with their start and end apart: 24, of which 13 were waited for; matrix products, arithmetic and copies ran while one was open for 1% of the time, Pallas kernels for 6%

profile of v11, /device:TPU:6, one launch (start us, length us, event | category | flops | bytes accessed | tf_op | source)
XLA Modules:
  0.0 166.9 jit_solution(10942943705935618626)
XLA Ops:
  0.6 10.9 %collective-permute-start = (bf16[8,4096]{1,0:T(8,128)(2,1)}, bf16[8,4096]{1,0:T(8,128)(2,1)S(1)}, u32[]{:S(2)}, u32[]{:S(2)}) collective-permute-start(bf16[8,4096]{1,0:T(8,128)(2,1)} %param.4), channel_id=1, source_target_pairs={{0,16},{4,20},{8,24},{12,28},{16,0},{20,4},{24,8},{28,12},{1,17},{... | collective-permute-start | bytes 196616 | tf_op jit(solution)/shard_map/ppermute | solution.py:186
  11.6 1.9 %collective-permute-start.7 = (bf16[8,4096]{1,0:T(8,128)(2,1)}, bf16[8,4096]{1,0:T(8,128)(2,1)S(1)}, u32[]{:S(2)}, u32[]{:S(2)}) collective-permute-start(bf16[8,4096]{1,0:T(8,128)(2,1)} %param.5), channel_id=1, source_target_pairs={{0,16},{4,20},{8,24},{12,28},{16,0},{20,4},{24,8},{28,12},{1,17},{... | collective-permute-start | bytes 196616 | tf_op jit(solution)/shard_map/ppermute | solution.py:189
  14.8 6.0 %collective-permute-start.3 = (bf16[16,4096]{1,0:T(8,128)(2,1)S(1)}, bf16[16,4096]{1,0:T(8,128)(2,1)S(1)}, u32[]{:S(2)}, u32[]{:S(2)}) collective-permute-start(bf16[16,4096]{1,0:T(8,128)(2,1)S(1)} %pad_maximum_fusion.2), channel_id=1, source_target_pairs={{0,4},{4,0},{8,12},{12,8},{16,20},{20,16},{24,28},{28,24},{1,5},{5... | collective-permute-start | bytes 393224 | tf_op jit(solution)/shard_map/ppermute | solution.py:184
  20.8 9.1 %collective-permute-start.2 = (bf16[16,4096]{1,0:T(8,128)(2,1)S(1)}, bf16[16,4096]{1,0:T(8,128)(2,1)S(1)}, u32[]{:S(2)}, u32[]{:S(2)}) collective-permute-start(bf16[16,4096]{1,0:T(8,128)(2,1)S(1)} %pad_maximum_fusion.2), channel_id=1, source_target_pairs={{0,12},{4,8},{8,4},{12,0},{16,28},{20,24},{24,20},{28,16},{1,13},{... | collective-permute-start | bytes 393224 | tf_op jit(solution)/shard_map/ppermute | solution.py:184
  29.9 2.5 %collective-permute-start.1 = (bf16[16,4096]{1,0:T(8,128)(2,1)S(1)}, bf16[16,4096]{1,0:T(8,128)(2,1)S(1)}, u32[]{:S(2)}, u32[]{:S(2)}) collective-permute-start(bf16[16,4096]{1,0:T(8,128)(2,1)S(1)} %pad_maximum_fusion.2), channel_id=1, source_target_pairs={{0,8},{4,12},{8,0},{12,4},{16,24},{20,28},{24,16},{28,20},{1,9},{5... | collective-permute-start | bytes 393224 | tf_op jit(solution)/shard_map/ppermute | solution.py:184
  33.2 2.5 %collective-permute-start.10 = (bf16[16,4096]{1,0:T(8,128)(2,1)S(1)}, bf16[16,4096]{1,0:T(8,128)(2,1)S(1)}, u32[]{:S(2)}, u32[]{:S(2)}) collective-permute-start(bf16[16,4096]{1,0:T(8,128)(2,1)S(1)} %pad_maximum_fusion.3), channel_id=1, source_target_pairs={{0,4},{4,0},{8,12},{12,8},{16,20},{20,16},{24,28},{28,24},{1,5},{5... | collective-permute-start | bytes 393224 | tf_op jit(solution)/shard_map/ppermute | solution.py:184
  35.7 5.2 %collective-permute-start.9 = (bf16[16,4096]{1,0:T(8,128)(2,1)S(1)}, bf16[16,4096]{1,0:T(8,128)(2,1)S(1)}, u32[]{:S(2)}, u32[]{:S(2)}) collective-permute-start(bf16[16,4096]{1,0:T(8,128)(2,1)S(1)} %pad_maximum_fusion.3), channel_id=1, source_target_pairs={{0,12},{4,8},{8,4},{12,0},{16,28},{20,24},{24,20},{28,16},{1,13},{... | collective-permute-start | bytes 393224 | tf_op jit(solution)/shard_map/ppermute | solution.py:184
  40.9 1.9 %collective-permute-start.8 = (bf16[16,4096]{1,0:T(8,128)(2,1)S(1)}, bf16[16,4096]{1,0:T(8,128)(2,1)S(1)}, u32[]{:S(2)}, u32[]{:S(2)}) collective-permute-start(bf16[16,4096]{1,0:T(8,128)(2,1)S(1)} %pad_maximum_fusion.3), channel_id=1, source_target_pairs={{0,8},{4,12},{8,0},{12,4},{16,24},{20,28},{24,16},{28,20},{1,9},{5... | collective-permute-start | bytes 393224 | tf_op jit(solution)/shard_map/ppermute | solution.py:184
  42.8 3.9 %collective-permute-done.1 = bf16[16,4096]{1,0:T(8,128)(2,1)S(1)} collective-permute-done((bf16[16,4096]{1,0:T(8,128)(2,1)S(1)}, bf16[16,4096]{1,0:T(8,128)(2,1)S(1)}, u32[]{:S(2)}, u32[]{:S(2)}) %collective-permute-start.1) | collective-permute-done | bytes 131104 | tf_op jit(solution)/shard_map/ppermute | solution.py:184
  46.8 3.0 %collective-permute-start.4 = (bf16[64,4096]{1,0:T(8,128)(2,1)S(1)}, bf16[64,4096]{1,0:T(8,128)(2,1)S(1)}, u32[]{:S(2)}, u32[]{:S(2)}) collective-permute-start(bf16[64,4096]{1,0:T(8,128)(2,1)S(1)} %pad_maximum_fusion.refs_0_), channel_id=1, source_target_pairs={{0,1},{1,2},{2,3},{3,0},{4,5},{5,6},{6,7},{7,4},{8,9},{9,10},{10,1... | collective-permute-start | bytes 1572872 | tf_op jit(solution)/shard_map/ppermute | solution.py:191
  49.8 3.3 %collective-permute-done.8 = bf16[16,4096]{1,0:T(8,128)(2,1)S(1)} collective-permute-done((bf16[16,4096]{1,0:T(8,128)(2,1)S(1)}, bf16[16,4096]{1,0:T(8,128)(2,1)S(1)}, u32[]{:S(2)}, u32[]{:S(2)}) %collective-permute-start.8) | collective-permute-done | bytes 131104 | tf_op jit(solution)/shard_map/ppermute | solution.py:184
  53.2 2.7 %collective-permute-start.12 = (bf16[64,4096]{1,0:T(8,128)(2,1)S(1)}, bf16[64,4096]{1,0:T(8,128)(2,1)S(1)}, u32[]{:S(2)}, u32[]{:S(2)}) collective-permute-start(bf16[64,4096]{1,0:T(8,128)(2,1)S(1)} %pad_maximum_fusion.1.refs_0_.refs_4_), channel_id=1, source_target_pairs={{0,3},{1,0},{2,1},{3,2},{4,7},{5,4},{6,5},{7,6},{8,11},{9,8},{10,9... | collective-permute-start | bytes 1572872 | tf_op jit(solution)/shard_map/ppermute | solution.py:197
  55.9 2.4 %collective-permute-start.5 = (bf16[64,4096]{1,0:T(8,128)(2,1)S(1)}, bf16[64,4096]{1,0:T(8,128)(2,1)}, u32[]{:S(2)}, u32[]{:S(2)}) collective-permute-start(bf16[64,4096]{1,0:T(8,128)(2,1)S(1)} %pad_maximum_fusion.refs_0_), channel_id=1, source_target_pairs={{0,3},{1,0},{2,1},{3,2},{4,7},{5,4},{6,5},{7,6},{8,11},{9,8},{10,9... | collective-permute-start | bytes 1572872 | tf_op jit(solution)/shard_map/ppermute | solution.py:192
  58.4 4.6 %collective-permute-start.6 = (bf16[64,4096]{1,0:T(8,128)(2,1)S(1)}, bf16[64,4096]{1,0:T(8,128)(2,1)}, u32[]{:S(2)}, u32[]{:S(2)}) collective-permute-start(bf16[64,4096]{1,0:T(8,128)(2,1)S(1)} %collective-permute-done.4.refs_0_), channel_id=1, source_target_pairs={{0,1},{1,2},{2,3},{3,0},{4,5},{5,6},{6,7},{7,4},{8,9},{9,10},{10,1... | collective-permute-start | bytes 1572872 | tf_op jit(solution)/shard_map/ppermute | solution.py:196
  63.0 3.1 %collective-permute-start.11 = (bf16[64,4096]{1,0:T(8,128)(2,1)S(1)}, bf16[64,4096]{1,0:T(8,128)(2,1)S(1)}, u32[]{:S(2)}, u32[]{:S(2)}) collective-permute-start(bf16[64,4096]{1,0:T(8,128)(2,1)S(1)} %pad_maximum_fusion.1.refs_0_.refs_4_), channel_id=1, source_target_pairs={{0,1},{1,2},{2,3},{3,0},{4,5},{5,6},{6,7},{7,4},{8,9},{9,10},{10,1... | collective-permute-start | bytes 1572872 | tf_op jit(solution)/shard_map/ppermute | solution.py:198
  66.1 5.0 %collective-permute-done.12.refs_2_.refs_6_ = bf16[64,4096]{1,0:T(8,128)(2,1)S(1)} collective-permute-done((bf16[64,4096]{1,0:T(8,128)(2,1)S(1)}, bf16[64,4096]{1,0:T(8,128)(2,1)S(1)}, u32[]{:S(2)}, u32[]{:S(2)}) %collective-permute-start.12) | collective-permute-done | bytes 524320 | tf_op jit(solution)/shard_map/ppermute | solution.py:197
  75.2 7.3 %collective-permute-done.5.refs_0_ = bf16[64,4096]{1,0:T(8,128)(2,1)} collective-permute-done((bf16[64,4096]{1,0:T(8,128)(2,1)S(1)}, bf16[64,4096]{1,0:T(8,128)(2,1)}, u32[]{:S(2)}, u32[]{:S(2)}) %collective-permute-start.5) | collective-permute-done | bytes 524320 | tf_op jit(solution)/shard_map/ppermute | solution.py:192
  82.5 3.2 %shard_map.61.refs_2_.refs_3_ = bf16[128,4096]{1,0:T(8,128)(2,1)S(1)} custom-call(bf16[64,4096]{1,0:T(8,128)(2,1)} %collective-permute-done.5.refs_0_, bf16[64,4096]{1,0:T(8,128)(2,1)} %collective-permute-done.6.refs_1_), custom_call_target="tpu_custom_call" | custom-call | tf_op jit(solution)/shard_map/pallas_call | solution.py:168
  85.7 3.0 %shard_map.62 = (bf16[128,256]{1,0:T(8,128)(2,1)S(1)}, f32[256,128]{1,0:T(8,128)S(1)}, f32[256,128]{1,0:T(8,128)S(1)}, f32[256,128]{1,0:T(8,128)S(1)}, f32[256,2...) custom-call(bf16[64,4096]{1,0:T(8,128)(2,1)S(1)} %shard_map.59.refs_0_.refs_1_, ...), custom_call_target="tpu_custom_call" | custom-call | tf_op jit(solution)/shard_map/pallas_call | solution.py:213
  88.8 3.3 %collective-permute-done.13.refs_3_.refs_7_ = bf16[64,4096]{1,0:T(8,128)(2,1)S(1)} collective-permute-done((bf16[64,4096]{1,0:T(8,128)(2,1)S(1)}, bf16[64,4096]{1,0:T(8,128)(2,1)S(1)}, u32[]{:S(2)}, u32[]{:S(2)}) %collective-permute-start.13) | collective-permute-done | bytes 524320 | tf_op jit(solution)/shard_map/ppermute | solution.py:201
  92.1 2.9 %shard_map.63.refs_8_ = bf16[384,256]{1,0:T(8,128)(2,1)S(1)} custom-call(bf16[64,4096]{1,0:T(8,128)(2,1)S(1)} %pad_maximum_fusion.1.refs_0_.refs_4_, bf16[64,4096]{1,0:T(8,128)(2,1)S(1)} %collective-permute-done.11.refs_1_.refs_5_, bf16[64,4096]{1,0:T(8,128)(2,1)S(1)} %collective-permute-done.12.refs_2_.refs_6_, ...), custom_call_target="tpu_custom_call" | custom-call | tf_op jit(solution)/shard_map/pallas_call | solution.py:228
  96.4 1.9 %collective-permute-start.14 = (bf16[16,512,128]{2,1,0:T(8,128)(2,1)S(1)}, bf16[16,512,128]{2,1,0:T(8,128)(2,1)S(1)}, u32[]{:S(2)}, u32[]{:S(2)}) collective-permute-start(bf16[16,512,128]{2,1,0:T(8,128)(2,1)S(1)} %shard_map.65), channel_id=1, source_target_pairs={{0,32},{32,0},{1,33},{33,1},{2,34},{34,2},{3,35},{35,3},{4,36},{36... | collective-permute-start | bytes 6291464 | tf_op jit(solution)/shard_map/ppermute | solution.py:252
  99.9 2.6 %collective-permute-done.14.theirs_ref = bf16[16,512,128]{2,1,0:T(8,128)(2,1)S(1)} collective-permute-done((bf16[16,512,128]{2,1,0:T(8,128)(2,1)S(1)}, bf16[16,512,128]{2,1,0:T(8,128)(2,1)S(1)}, u32[]{:S(2)}, u32[]{:S(2)}) %collective-permute-start.14) | collective-permute-done | bytes 2097184 | tf_op jit(solution)/shard_map/ppermute | solution.py:252
  102.6 5.4 %collective-permute-start.19 = (bf16[512,128]{1,0:T(8,128)(2,1)S(1)}, bf16[512,128]{1,0:T(8,128)(2,1)S(1)}, u32[]{:S(2)}, u32[]{:S(2)}) collective-permute-start(bf16[512,128]{1,0:T(8,128)(2,1)S(1)} %get-tuple-element.21), channel_id=1, source_target_pairs={{0,448},{64,0},{128,64},{192,128},{256,192},{320,256},{384,320},{4... | collective-permute-start | bytes 393224 | tf_op jit(solution)/shard_map/ppermute | solution.py:268
  111.1 5.6 %collective-permute-start.20 = (bf16[2,512,128]{2,1,0:T(8,128)(2,1)S(1)}, bf16[2,512,128]{2,1,0:T(8,128)(2,1)S(1)}, u32[]{:S(2)}, u32[]{:S(2)}) collective-permute-start(bf16[2,512,128]{2,1,0:T(8,128)(2,1)S(1)} %shard_map.70), channel_id=1, source_target_pairs={{0,448},{64,0},{128,64},{192,128},{256,192},{320,256},{384,320},{4... | collective-permute-start | bytes 786440 | tf_op jit(solution)/shard_map/ppermute | solution.py:268
  118.7 3.0 %collective-permute-done.20.came_ref = bf16[2,512,128]{2,1,0:T(8,128)(2,1)S(1)} collective-permute-done((bf16[2,512,128]{2,1,0:T(8,128)(2,1)S(1)}, bf16[2,512,128]{2,1,0:T(8,128)(2,1)S(1)}, u32[]{:S(2)}, u32[]{:S(2)}) %collective-permute-start.20) | collective-permute-done | bytes 262176 | tf_op jit(solution)/shard_map/ppermute | solution.py:268
  121.8 5.6 %collective-permute-start.21 = (bf16[2,512,128]{2,1,0:T(8,128)(2,1)S(1)}, bf16[2,512,128]{2,1,0:T(8,128)(2,1)S(1)}, u32[]{:S(2)}, u32[]{:S(2)}) collective-permute-start(bf16[2,512,128]{2,1,0:T(8,128)(2,1)S(1)} %shard_map.71), channel_id=1, source_target_pairs={{0,448},{64,0},{128,64},{192,128},{256,192},{320,256},{384,320},{4... | collective-permute-start | bytes 786440 | tf_op jit(solution)/shard_map/ppermute | solution.py:268
  129.4 2.0 %collective-permute-done.21.came_ref = bf16[2,512,128]{2,1,0:T(8,128)(2,1)S(1)} collective-permute-done((bf16[2,512,128]{2,1,0:T(8,128)(2,1)S(1)}, bf16[2,512,128]{2,1,0:T(8,128)(2,1)S(1)}, u32[]{:S(2)}, u32[]{:S(2)}) %collective-permute-start.21) | collective-permute-done | bytes 262176 | tf_op jit(solution)/shard_map/ppermute | solution.py:268
  131.6 5.6 %collective-permute-start.22 = (bf16[2,512,128]{2,1,0:T(8,128)(2,1)S(1)}, bf16[2,512,128]{2,1,0:T(8,128)(2,1)S(1)}, u32[]{:S(2)}, u32[]{:S(2)}) collective-permute-start(bf16[2,512,128]{2,1,0:T(8,128)(2,1)S(1)} %shard_map.72), channel_id=1, source_target_pairs={{0,448},{64,0},{128,64},{192,128},{256,192},{320,256},{384,320},{4... | collective-permute-start | bytes 786440 | tf_op jit(solution)/shard_map/ppermute | solution.py:268
  141.1 5.7 %collective-permute-done.18.up_ref = bf16[2,512,128]{2,1,0:T(8,128)(2,1)S(1)} collective-permute-done((bf16[2,512,128]{2,1,0:T(8,128)(2,1)S(1)}, bf16[2,512,128]{2,1,0:T(8,128)(2,1)S(1)}, u32[]{:S(2)}, u32[]{:S(2)}) %collective-permute-start.18) | collective-permute-done | bytes 262176 | tf_op jit(solution)/shard_map/ppermute | solution.py:268
  146.9 14.3 %collective-permute-start.23 = (bf16[512,128]{1,0:T(8,128)(2,1)S(1)}, bf16[512,128]{1,0:T(8,128)(2,1)S(1)}, u32[]{:S(2)}, u32[]{:S(2)}) collective-permute-start(bf16[512,128]{1,0:T(8,128)(2,1)S(1)} %shard_map.73), channel_id=1, source_target_pairs={{0,512},{512,0},{1,513},{513,1},{2,514},{514,2},{3,515},{515,3},{4... | collective-permute-start | bytes 393224 | tf_op jit(solution)/shard_map/ppermute | solution.py:277
  161.2 4.9 %collective-permute-done.23.other_ref = bf16[512,128]{1,0:T(8,128)(2,1)S(1)} collective-permute-done((bf16[512,128]{1,0:T(8,128)(2,1)S(1)}, bf16[512,128]{1,0:T(8,128)(2,1)S(1)}, u32[]{:S(2)}, u32[]{:S(2)}) %collective-permute-start.23) | collective-permute-done | bytes 131104 | tf_op jit(solution)/shard_map/ppermute | solution.py:277
  (42 shorter events, 21.4 us)
Async XLA Ops:
  0.6 13.4 %collective-permute-start = (bf16[8,4096]{1,0:T(8,128)(2,1)}, bf16[8,4096]{1,0:T(8,128)(2,1)S(1)}, u32[]{:S(2)}, u32[]{:S(2)}) collective-permute-start(bf16[8,4096]{1,0:T(8,128)(2,1)} %param.4), channel_id=1, source_target_pairs={{0,16},{4,20},{8,24},{12,28},{16,0},{20,4},{24,8},{28,12},{1,17},{... | collective-permute-start | bytes 196616 | tf_op jit(solution)/shard_map/ppermute | solution.py:186
  11.6 20.8 %collective-permute-start.7 = (bf16[8,4096]{1,0:T(8,128)(2,1)}, bf16[8,4096]{1,0:T(8,128)(2,1)S(1)}, u32[]{:S(2)}, u32[]{:S(2)}) collective-permute-start(bf16[8,4096]{1,0:T(8,128)(2,1)} %param.5), channel_id=1, source_target_pairs={{0,16},{4,20},{8,24},{12,28},{16,0},{20,4},{24,8},{28,12},{1,17},{... | collective-permute-start | bytes 196616 | tf_op jit(solution)/shard_map/ppermute | solution.py:189
  14.8 26.0 %collective-permute-start.3 = (bf16[16,4096]{1,0:T(8,128)(2,1)S(1)}, bf16[16,4096]{1,0:T(8,128)(2,1)S(1)}, u32[]{:S(2)}, u32[]{:S(2)}) collective-permute-start(bf16[16,4096]{1,0:T(8,128)(2,1)S(1)} %pad_maximum_fusion.2), channel_id=1, source_target_pairs={{0,4},{4,0},{8,12},{12,8},{16,20},{20,16},{24,28},{28,24},{1,5},{5... | collective-permute-start | bytes 393224 | tf_op jit(solution)/shard_map/ppermute | solution.py:184
  20.8 22.0 %collective-permute-start.2 = (bf16[16,4096]{1,0:T(8,128)(2,1)S(1)}, bf16[16,4096]{1,0:T(8,128)(2,1)S(1)}, u32[]{:S(2)}, u32[]{:S(2)}) collective-permute-start(bf16[16,4096]{1,0:T(8,128)(2,1)S(1)} %pad_maximum_fusion.2), channel_id=1, source_target_pairs={{0,12},{4,8},{8,4},{12,0},{16,28},{20,24},{24,20},{28,16},{1,13},{... | collective-permute-start | bytes 393224 | tf_op jit(solution)/shard_map/ppermute | solution.py:184
  29.9 16.9 %collective-permute-start.1 = (bf16[16,4096]{1,0:T(8,128)(2,1)S(1)}, bf16[16,4096]{1,0:T(8,128)(2,1)S(1)}, u32[]{:S(2)}, u32[]{:S(2)}) collective-permute-start(bf16[16,4096]{1,0:T(8,128)(2,1)S(1)} %pad_maximum_fusion.2), channel_id=1, source_target_pairs={{0,8},{4,12},{8,0},{12,4},{16,24},{20,28},{24,16},{28,20},{1,9},{5... | collective-permute-start | bytes 393224 | tf_op jit(solution)/shard_map/ppermute | solution.py:184
  33.2 16.6 %collective-permute-start.10 = (bf16[16,4096]{1,0:T(8,128)(2,1)S(1)}, bf16[16,4096]{1,0:T(8,128)(2,1)S(1)}, u32[]{:S(2)}, u32[]{:S(2)}) collective-permute-start(bf16[16,4096]{1,0:T(8,128)(2,1)S(1)} %pad_maximum_fusion.3), channel_id=1, source_target_pairs={{0,4},{4,0},{8,12},{12,8},{16,20},{20,16},{24,28},{28,24},{1,5},{5... | collective-permute-start | bytes 393224 | tf_op jit(solution)/shard_map/ppermute | solution.py:184
  35.7 14.1 %collective-permute-start.9 = (bf16[16,4096]{1,0:T(8,128)(2,1)S(1)}, bf16[16,4096]{1,0:T(8,128)(2,1)S(1)}, u32[]{:S(2)}, u32[]{:S(2)}) collective-permute-start(bf16[16,4096]{1,0:T(8,128)(2,1)S(1)} %pad_maximum_fusion.3), channel_id=1, source_target_pairs={{0,12},{4,8},{8,4},{12,0},{16,28},{20,24},{24,20},{28,16},{1,13},{... | collective-permute-start | bytes 393224 | tf_op jit(solution)/shard_map/ppermute | solution.py:184
  40.9 12.3 %collective-permute-start.8 = (bf16[16,4096]{1,0:T(8,128)(2,1)S(1)}, bf16[16,4096]{1,0:T(8,128)(2,1)S(1)}, u32[]{:S(2)}, u32[]{:S(2)}) collective-permute-start(bf16[16,4096]{1,0:T(8,128)(2,1)S(1)} %pad_maximum_fusion.3), channel_id=1, source_target_pairs={{0,8},{4,12},{8,0},{12,4},{16,24},{20,28},{24,16},{28,20},{1,9},{5... | collective-permute-start | bytes 393224 | tf_op jit(solution)/shard_map/ppermute | solution.py:184
  46.8 11.6 %collective-permute-start.4 = (bf16[64,4096]{1,0:T(8,128)(2,1)S(1)}, bf16[64,4096]{1,0:T(8,128)(2,1)S(1)}, u32[]{:S(2)}, u32[]{:S(2)}) collective-permute-start(bf16[64,4096]{1,0:T(8,128)(2,1)S(1)} %pad_maximum_fusion.refs_0_), channel_id=1, source_target_pairs={{0,1},{1,2},{2,3},{3,0},{4,5},{5,6},{6,7},{7,4},{8,9},{9,10},{10,1... | collective-permute-start | bytes 1572872 | tf_op jit(solution)/shard_map/ppermute | solution.py:191
  53.2 18.0 %collective-permute-start.12 = (bf16[64,4096]{1,0:T(8,128)(2,1)S(1)}, bf16[64,4096]{1,0:T(8,128)(2,1)S(1)}, u32[]{:S(2)}, u32[]{:S(2)}) collective-permute-start(bf16[64,4096]{1,0:T(8,128)(2,1)S(1)} %pad_maximum_fusion.1.refs_0_.refs_4_), channel_id=1, source_target_pairs={{0,3},{1,0},{2,1},{3,2},{4,7},{5,4},{6,5},{7,6},{8,11},{9,8},{10,9... | collective-permute-start | bytes 1572872 | tf_op jit(solution)/shard_map/ppermute | solution.py:197
  55.9 26.6 %collective-permute-start.5 = (bf16[64,4096]{1,0:T(8,128)(2,1)S(1)}, bf16[64,4096]{1,0:T(8,128)(2,1)}, u32[]{:S(2)}, u32[]{:S(2)}) collective-permute-start(bf16[64,4096]{1,0:T(8,128)(2,1)S(1)} %pad_maximum_fusion.refs_0_), channel_id=1, source_target_pairs={{0,3},{1,0},{2,1},{3,2},{4,7},{5,4},{6,5},{7,6},{8,11},{9,8},{10,9... | collective-permute-start | bytes 1572872 | tf_op jit(solution)/shard_map/ppermute | solution.py:192
  58.4 24.1 %collective-permute-start.6 = (bf16[64,4096]{1,0:T(8,128)(2,1)S(1)}, bf16[64,4096]{1,0:T(8,128)(2,1)}, u32[]{:S(2)}, u32[]{:S(2)}) collective-permute-start(bf16[64,4096]{1,0:T(8,128)(2,1)S(1)} %collective-permute-done.4.refs_0_), channel_id=1, source_target_pairs={{0,1},{1,2},{2,3},{3,0},{4,5},{5,6},{6,7},{7,4},{8,9},{9,10},{10,1... | collective-permute-start | bytes 1572872 | tf_op jit(solution)/shard_map/ppermute | solution.py:196
  63.0 25.8 %collective-permute-start.11 = (bf16[64,4096]{1,0:T(8,128)(2,1)S(1)}, bf16[64,4096]{1,0:T(8,128)(2,1)S(1)}, u32[]{:S(2)}, u32[]{:S(2)}) collective-permute-start(bf16[64,4096]{1,0:T(8,128)(2,1)S(1)} %pad_maximum_fusion.1.refs_0_.refs_4_), channel_id=1, source_target_pairs={{0,1},{1,2},{2,3},{3,0},{4,5},{5,6},{6,7},{7,4},{8,9},{9,10},{10,1... | collective-permute-start | bytes 1572872 | tf_op jit(solution)/shard_map/ppermute | solution.py:198
  71.2 20.9 %collective-permute-start.13 = (bf16[64,4096]{1,0:T(8,128)(2,1)S(1)}, bf16[64,4096]{1,0:T(8,128)(2,1)S(1)}, u32[]{:S(2)}, u32[]{:S(2)}) collective-permute-start(bf16[64,4096]{1,0:T(8,128)(2,1)S(1)} %collective-permute-done.12.refs_2_.refs_6_), channel_id=1, source_target_pairs={{0,3},{1,0},{2,1},{3,2},{4,7},{5,4},{6,5},{7,6},{8,11},{9,8},{10,9... | collective-permute-start | bytes 1572872 | tf_op jit(solution)/shard_map/ppermute | solution.py:201
  73.2 12.6 %copy-start = (bf16[4096,1,384]{2,0,1:T(8,128)(2,1)S(1)}, bf16[4096,1,384]{2,0,1:T(8,128)(2,1)}, u32[]{:S(2)}) copy-start(bf16[4096,1,384]{2,0,1:T(8,128)(2,1)} %param.6) | copy-start | bytes 9437188
  85.7 6.4 %copy-start.1 = (bf16[1,128,4096]{2,1,0:T(8,128)(2,1)S(1)}, bf16[1,128,4096]{2,1,0:T(8,128)(2,1)}, u32[]{:S(2)}) copy-start(bf16[1,128,4096]{2,1,0:T(8,128)(2,1)} %param.7) | copy-start | bytes 3145732
  96.4 6.1 %collective-permute-start.14 = (bf16[16,512,128]{2,1,0:T(8,128)(2,1)S(1)}, bf16[16,512,128]{2,1,0:T(8,128)(2,1)S(1)}, u32[]{:S(2)}, u32[]{:S(2)}) collective-permute-start(bf16[16,512,128]{2,1,0:T(8,128)(2,1)S(1)} %shard_map.65), channel_id=1, source_target_pairs={{0,32},{32,0},{1,33},{33,1},{2,34},{34,2},{3,35},{35,3},{4,36},{36... | collective-permute-start | bytes 6291464 | tf_op jit(solution)/shard_map/ppermute | solution.py:252
  102.6 8.4 %collective-permute-start.19 = (bf16[512,128]{1,0:T(8,128)(2,1)S(1)}, bf16[512,128]{1,0:T(8,128)(2,1)S(1)}, u32[]{:S(2)}, u32[]{:S(2)}) collective-permute-start(bf16[512,128]{1,0:T(8,128)(2,1)S(1)} %get-tuple-element.21), channel_id=1, source_target_pairs={{0,448},{64,0},{128,64},{192,128},{256,192},{320,256},{384,320},{4... | collective-permute-start | bytes 393224 | tf_op jit(solution)/shard_map/ppermute | solution.py:268
  107.9 8.7 %collective-permute-start.15 = (bf16[512,128]{1,0:T(8,128)(2,1)S(1)}, bf16[512,128]{1,0:T(8,128)(2,1)S(1)}, u32[]{:S(2)}, u32[]{:S(2)}) collective-permute-start(bf16[512,128]{1,0:T(8,128)(2,1)S(1)} %get-tuple-element.20), channel_id=1, source_target_pairs={{0,64},{64,128},{128,192},{192,256},{256,320},{320,384},{384,448},... | collective-permute-start | bytes 393224 | tf_op jit(solution)/shard_map/ppermute | solution.py:268
  111.1 10.6 %collective-permute-start.20 = (bf16[2,512,128]{2,1,0:T(8,128)(2,1)S(1)}, bf16[2,512,128]{2,1,0:T(8,128)(2,1)S(1)}, u32[]{:S(2)}, u32[]{:S(2)}) collective-permute-start(bf16[2,512,128]{2,1,0:T(8,128)(2,1)S(1)} %shard_map.70), channel_id=1, source_target_pairs={{0,448},{64,0},{128,64},{192,128},{256,192},{320,256},{384,320},{4... | collective-permute-start | bytes 786440 | tf_op jit(solution)/shard_map/ppermute | solution.py:268
  116.8 10.6 %collective-permute-start.16 = (bf16[2,512,128]{2,1,0:T(8,128)(2,1)S(1)}, bf16[2,512,128]{2,1,0:T(8,128)(2,1)S(1)}, u32[]{:S(2)}, u32[]{:S(2)}) collective-permute-start(bf16[2,512,128]{2,1,0:T(8,128)(2,1)S(1)} %shard_map.67), channel_id=1, source_target_pairs={{0,64},{64,128},{128,192},{192,256},{256,320},{320,384},{384,448},... | collective-permute-start | bytes 786440 | tf_op jit(solution)/shard_map/ppermute | solution.py:268
  121.8 9.7 %collective-permute-start.21 = (bf16[2,512,128]{2,1,0:T(8,128)(2,1)S(1)}, bf16[2,512,128]{2,1,0:T(8,128)(2,1)S(1)}, u32[]{:S(2)}, u32[]{:S(2)}) collective-permute-start(bf16[2,512,128]{2,1,0:T(8,128)(2,1)S(1)} %shard_map.71), channel_id=1, source_target_pairs={{0,448},{64,0},{128,64},{192,128},{256,192},{320,256},{384,320},{4... | collective-permute-start | bytes 786440 | tf_op jit(solution)/shard_map/ppermute | solution.py:268
  127.5 9.7 %collective-permute-start.17 = (bf16[2,512,128]{2,1,0:T(8,128)(2,1)S(1)}, bf16[2,512,128]{2,1,0:T(8,128)(2,1)S(1)}, u32[]{:S(2)}, u32[]{:S(2)}) collective-permute-start(bf16[2,512,128]{2,1,0:T(8,128)(2,1)S(1)} %shard_map.68), channel_id=1, source_target_pairs={{0,64},{64,128},{128,192},{192,256},{256,320},{320,384},{384,448},... | collective-permute-start | bytes 786440 | tf_op jit(solution)/shard_map/ppermute | solution.py:268
  131.6 9.5 %collective-permute-start.22 = (bf16[2,512,128]{2,1,0:T(8,128)(2,1)S(1)}, bf16[2,512,128]{2,1,0:T(8,128)(2,1)S(1)}, u32[]{:S(2)}, u32[]{:S(2)}) collective-permute-start(bf16[2,512,128]{2,1,0:T(8,128)(2,1)S(1)} %shard_map.72), channel_id=1, source_target_pairs={{0,448},{64,0},{128,64},{192,128},{256,192},{320,256},{384,320},{4... | collective-permute-start | bytes 786440 | tf_op jit(solution)/shard_map/ppermute | solution.py:268
  137.3 9.5 %collective-permute-start.18 = (bf16[2,512,128]{2,1,0:T(8,128)(2,1)S(1)}, bf16[2,512,128]{2,1,0:T(8,128)(2,1)S(1)}, u32[]{:S(2)}, u32[]{:S(2)}) collective-permute-start(bf16[2,512,128]{2,1,0:T(8,128)(2,1)S(1)} %shard_map.69), channel_id=1, source_target_pairs={{0,64},{64,128},{128,192},{192,256},{256,320},{320,384},{384,448},... | collective-permute-start | bytes 786440 | tf_op jit(solution)/shard_map/ppermute | solution.py:268
  146.9 19.2 %collective-permute-start.23 = (bf16[512,128]{1,0:T(8,128)(2,1)S(1)}, bf16[512,128]{1,0:T(8,128)(2,1)S(1)}, u32[]{:S(2)}, u32[]{:S(2)}) collective-permute-start(bf16[512,128]{1,0:T(8,128)(2,1)S(1)} %shard_map.73), channel_id=1, source_target_pairs={{0,512},{512,0},{1,513},{513,1},{2,514},{514,2},{3,515},{515,3},{4... | collective-permute-start | bytes 393224 | tf_op jit(solution)/shard_map/ppermute | solution.py:277
